TPU v7x, 32 devices: a whole 2x2x4 slice. The times are simulated.
32 devices in a mesh: ctx: 16 (over z, y, core), wa: 2 (over x).
Axes of the slice: x: 2, y: 2, z: 4, core: 2. Of those that a mesh axis runs over, the one named last changes fastest.
Arguments:
- layer_input: bfloat16 [2, 2048, 1536], P('wa', 'ctx'), may hold values from -6 to 6
- seq_ids: int32 [2, 2048], P('wa'), may hold values from 0 to 2, as said below
- routes: int32 [2, 2048, 4], P('wa', 'ctx'), may hold values from 0 to 7, all different within a row; in each aligned block of 128 rows (0 to 127, 128 to 255, ..., all dimensions but the last counted through in order) at most 128 rows name the same one
- gain_attn: bfloat16 [1536], P('wa'), may hold values from 0.5 to 1.5
- w_query: bfloat16 [1536, 1536], P('wa'), may hold values from -0.15625 to 0.15625
- w_keyval: bfloat16 [1536, 512], P('wa'), may hold values from -0.15625 to 0.15625
- w_out_attn: bfloat16 [1536, 1536], P('wa'), may hold values from -1.75 to 1.75
- gain_ffn: bfloat16 [1536], P('wa'), may hold values from 0.5 to 1.5
- router: bfloat16 [1536, 8], P('wa'), may hold values from -0.078125 to 0.078125
- w_in: bfloat16 [16, 2, 1536, 384], P('ctx', None, None, 'wa'), may hold values from -0.15625 to 0.15625
- w_out: bfloat16 [16, 384, 1536], P('ctx', 'wa'), may hold values from -0.21875 to 0.21875
- d_out: bfloat16 [2, 2048, 1536], P('wa', 'ctx'), may hold values from -6 to 6
Outputs:
- output: bfloat16 [2, 2048, 1536], P('wa', 'ctx')
- d_layer_input: bfloat16 [2, 2048, 1536], P('wa', 'ctx')
- d_gain_attn: float32 [1536], P('wa')
- d_w_query: float32 [1536, 1536], P('wa')
- d_w_keyval: float32 [1536, 512], P('wa')
- d_w_out_attn: float32 [1536, 1536], P('wa')
- d_gain_ffn: float32 [1536], P('wa')
- d_router: float32 [1536, 8], P('wa')
- d_w_in: float32 [16, 2, 1536, 384], P('ctx', None, None, 'wa')
- d_w_out: float32 [16, 384, 1536], P('ctx', 'wa')
Inputs may be any that keep to these rules, and one draw needn't show every extreme that they name: `seq_ids`: in each row, id 0 covers a first run of 1 to 127 positions, id 2 a last run of 1 to 127 positions, and id 1 all positions between them. `routes`: each token names 4 different experts. Within the 128 tokens of one device no expert is named by more than 128 tokens, a bound that some block reaches.
All inputs are finite; a program needn't handle non-finite values.
Results may differ from a plain program's by a relative error of at most 0.018.
Values may be sent and summed in bfloat16 or wider, within the bound.
A program may use at most 192 MiB of HBM per device.

v0:
```python
import math

import jax
import jax.numpy as jnp
from jax import lax
from jax.sharding import PartitionSpec as P

D = 1536
HEADS = 12
KV_HEADS = 2
HEAD_DIM = 128
TOP = 4
BLOCK = 256


EPSILON = 1e-06
THETA = 1000000.0
NEGATIVE = -1e30


def rms_scale(values, gain_vec):
    return (
        values * lax.rsqrt(jnp.mean(values * values, axis=-1, keepdims=True) + EPSILON) * gain_vec
    )


def rotate(values, angles):
    half_dim = values.shape[-1] // 2
    cosine = jnp.cos(angles)
    sine_part = jnp.sin(angles)
    first_half = values[..., :half_dim]
    second = values[..., half_dim:]
    return jnp.concatenate(
        [first_half * cosine - second * sine_part, second * cosine + first_half * sine_part],
        axis=-1,
    )


def angle_table(positions):
    half_dim = HEAD_DIM // 2
    frequency = THETA ** (-2.0 * jnp.arange(half_dim, dtype=jnp.float32) / HEAD_DIM)
    return (positions.astype(jnp.float32)[:, None] * frequency[None, :])[:, None, :]


def gated(stacked):
    return jax.nn.gelu(stacked[..., 0, :], approximate=True) * stacked[..., 1, :]


def over_keys(key_rows, running, advance):
    key_count = key_rows.shape[0]
    key_width = math.gcd(key_count, 512)

    def one_turn(state_now, block_index):
        key_offset = block_index * key_width
        key_part = lax.dynamic_slice_in_dim(key_rows, key_offset, key_width, 0)
        return (advance(state_now, key_part, key_offset), None)

    running, unused = lax.scan(
        one_turn, running, jnp.arange(key_count // key_width, dtype=jnp.int32)
    )
    return running


def body(
    layer_input,
    seq_ids,
    routes,
    gain_attn,
    w_query,
    w_keyval,
    w_out_attn,
    gain_ffn,
    router,
    w_in,
    w_out,
    d_out,
):
    ctx_count = lax.axis_size("ctx")
    ctx_index = lax.axis_index("ctx")
    tokens = layer_input.shape[1]
    length = tokens * ctx_count
    experts_all = ctx_count // 2
    capacity = 2 * tokens * TOP // experts_all
    group = HEADS // KV_HEADS
    kv_width = KV_HEADS * HEAD_DIM
    row_count = group * tokens
    scale = HEAD_DIM ** (-0.5)
    gain_one, query_matrix, keyvalue_matrix, attention_matrix = (
        lax.all_gather(gain_attn, "wa", axis=0, tiled=True),
        lax.all_gather(w_query, "wa", axis=0, tiled=True),
        lax.all_gather(w_keyval, "wa", axis=0, tiled=True),
        lax.all_gather(w_out_attn, "wa", axis=0, tiled=True),
    )
    residual = layer_input[0].astype(jnp.float32)
    normed_one, norm_one_back = jax.vjp(rms_scale, residual, gain_one.astype(jnp.float32))
    hidden_first_norm = normed_one.astype(jnp.bfloat16)
    positions = ctx_index * tokens + jnp.arange(tokens, dtype=jnp.int32)
    angles = angle_table(positions)
    query_projected = jnp.dot(
        hidden_first_norm, query_matrix, preferred_element_type=jnp.float32
    ).reshape(tokens, HEADS, HEAD_DIM)
    keyvalue_projected = jnp.dot(
        hidden_first_norm, keyvalue_matrix, preferred_element_type=jnp.float32
    )
    key_pre = keyvalue_projected[:, :kv_width].reshape(tokens, KV_HEADS, HEAD_DIM)
    query_low = rotate(query_projected, angles).astype(jnp.bfloat16)
    key_low = rotate(key_pre, angles).astype(jnp.bfloat16)
    value_low = keyvalue_projected[:, kv_width:].astype(jnp.bfloat16)
    keyval_send = jnp.concatenate([key_low.reshape(tokens, kv_width), value_low], axis=1)
    query_rows = (
        query_low.reshape(tokens, KV_HEADS, group, HEAD_DIM)
        .transpose(1, 2, 0, 3)
        .reshape(KV_HEADS, row_count, HEAD_DIM)
    )
    doc_row = seq_ids[0]
    query_docs = lax.dynamic_slice_in_dim(doc_row, ctx_index * tokens, tokens, 0)
    query_blocks = positions // BLOCK

    def block_scores(key_part, first_key):
        key_count = key_part.shape[0]
        split_part = key_part.reshape(key_count, 2, KV_HEADS, HEAD_DIM)
        keys_here = split_part[:, 0]
        values_here = split_part[:, 1]
        scores = (
            jnp.einsum("hrd,nhd->hrn", query_rows, keys_here, preferred_element_type=jnp.float32)
            * scale
        )
        key_docs = lax.dynamic_slice_in_dim(doc_row, first_key, key_count, 0)
        key_blocks = (first_key + jnp.arange(key_count, dtype=jnp.int32)) // BLOCK
        allowed = (query_docs[:, None] == key_docs[None, :]) & (
            key_blocks[None, :] <= query_blocks[:, None]
        )
        allowed = jnp.broadcast_to(allowed[None], (group, tokens, key_count)).reshape(
            1, row_count, key_count
        )
        return (jnp.where(allowed, scores, NEGATIVE), allowed, keys_here, values_here)

    def probs_of(masked, allowed, largest, totals):
        return jnp.where(allowed, jnp.exp(masked - largest[..., None]) / totals[..., None], 0.0)

    def stats_step(running, key_part, first_key):
        largest, totals = running
        masked, allowed, keys_here, values_here = block_scores(key_part, first_key)
        new_largest = jnp.maximum(largest, jnp.max(masked, axis=-1))
        weights = jnp.where(allowed, jnp.exp(masked - new_largest[..., None]), 0.0)
        return (new_largest, totals * jnp.exp(largest - new_largest) + jnp.sum(weights, axis=-1))

    start_stats = (
        jnp.full((KV_HEADS, row_count), NEGATIVE, jnp.float32),
        jnp.zeros((KV_HEADS, row_count), jnp.float32),
    )
    largest, totals = over_keys(
        lax.all_gather(keyval_send, "ctx", axis=0, tiled=True), start_stats, stats_step
    )

    def values_step(running, key_part, first_key):
        masked, allowed, keys_here, values_here = block_scores(key_part, first_key)
        probs_low = probs_of(masked, allowed, largest, totals).astype(jnp.bfloat16)
        return running + jnp.einsum(
            "hrn,nhd->hrd", probs_low, values_here, preferred_element_type=jnp.float32
        )

    start_values = jnp.zeros((KV_HEADS, row_count, HEAD_DIM), jnp.float32)
    mixed_rows = over_keys(
        lax.all_gather(keyval_send, "ctx", axis=0, tiled=True), start_values, values_step
    )
    mixed_low = (
        mixed_rows.reshape(KV_HEADS, group, tokens, HEAD_DIM)
        .transpose(2, 0, 1, 3)
        .reshape(tokens, HEADS * HEAD_DIM)
        .astype(jnp.bfloat16)
    )
    middle_activation = residual + jnp.dot(
        mixed_low, attention_matrix, preferred_element_type=jnp.float32
    )
    gain_two, router_full, w_in_full, w_out_full = (
        lax.all_gather(gain_ffn, "wa", axis=0, tiled=True),
        lax.all_gather(router, "wa", axis=0, tiled=True),
        lax.all_gather(w_in, "wa", axis=3, tiled=True),
        lax.all_gather(w_out, "wa", axis=1, tiled=True),
    )
    in_half = w_in_full[0]
    out_half = w_out_full[0]
    normed_two, norm_two_back = jax.vjp(rms_scale, middle_activation, gain_two.astype(jnp.float32))
    hidden_second_norm = normed_two.astype(jnp.bfloat16)
    router_logits = jnp.dot(hidden_second_norm, router_full, preferred_element_type=jnp.float32)
    route_ids = routes[0]

    def gate_values(logit_rows):
        return jax.nn.softmax(jnp.take_along_axis(logit_rows, route_ids, axis=-1), axis=-1)

    gates, gate_back = jax.vjp(gate_values, router_logits)
    flat_ids = route_ids.reshape(tokens * TOP)
    expert_hits = (flat_ids[:, None] == jnp.arange(experts_all, dtype=jnp.int32)[None, :]).astype(
        jnp.int32
    )
    ranks = jnp.sum(expert_hits * (jnp.cumsum(expert_hits, axis=0) - expert_hits), axis=1)
    slot_first = 2 * flat_ids * capacity + ranks
    slot_second = slot_first + capacity
    slot_total = ctx_count * capacity
    slot_numbers = jnp.arange(slot_total, dtype=jnp.int32)[:, None]
    placed = (
        (slot_first[None, :] == slot_numbers) | (slot_second[None, :] == slot_numbers)
    ).astype(jnp.bfloat16)
    dispatch = jnp.sum(placed.reshape(slot_total, tokens, TOP), axis=2)
    send_rows = (
        jnp.dot(dispatch, hidden_second_norm, preferred_element_type=jnp.float32)
        .astype(jnp.bfloat16)
        .reshape(ctx_count, capacity, D)
    )
    arrived = lax.all_to_all(send_rows, "ctx", split_axis=0, concat_axis=0, tiled=True)
    stacked = jnp.einsum("ncd,gdf->ncgf", arrived, in_half, preferred_element_type=jnp.float32)
    hidden_low = gated(stacked).astype(jnp.bfloat16)
    result = jnp.einsum(
        "ncf,fd->ncd", hidden_low, out_half, preferred_element_type=jnp.float32
    ).astype(jnp.bfloat16)
    returned_rows = lax.all_to_all(result, "ctx", split_axis=0, concat_axis=0, tiled=True)
    returned_flat = returned_rows.reshape(slot_total, D)
    pair_rows = (
        returned_flat[slot_first].astype(jnp.float32)
        + returned_flat[slot_second].astype(jnp.float32)
    ).reshape(tokens, TOP, D)
    output = (middle_activation + jnp.sum(gates[:, :, None] * pair_rows, axis=1)).astype(
        jnp.bfloat16
    )
    grad_out = d_out[0].astype(jnp.float32)
    grad_gates = jnp.sum(pair_rows * grad_out[:, None, :], axis=-1)
    (grad_logits,) = gate_back(grad_gates)
    grad_logits_low = grad_logits.astype(jnp.bfloat16)
    gate_slots = jnp.dot(
        placed.astype(jnp.float32), gates.reshape(tokens * TOP), precision=lax.Precision.HIGHEST
    )
    routed_grad = jnp.dot(dispatch, d_out[0], preferred_element_type=jnp.float32)
    grad_send_rows = (
        (gate_slots[:, None] * routed_grad).astype(jnp.bfloat16).reshape(ctx_count, capacity, D)
    )
    grad_arrived = lax.all_to_all(grad_send_rows, "ctx", split_axis=0, concat_axis=0, tiled=True)
    grad_hidden = jnp.einsum(
        "ncd,fd->ncf", grad_arrived, out_half, preferred_element_type=jnp.float32
    )
    hidden_again, gated_back = jax.vjp(gated, stacked)
    (grad_stacked,) = gated_back(grad_hidden)
    grad_stacked_low = grad_stacked.astype(jnp.bfloat16)
    grad_rows = jnp.einsum(
        "ncgf,gdf->ncd", grad_stacked_low, in_half, preferred_element_type=jnp.float32
    ).astype(jnp.bfloat16)
    grad_returned = lax.all_to_all(grad_rows, "ctx", split_axis=0, concat_axis=0, tiled=True)
    grad_w_in = jnp.einsum(
        "ncd,ncgf->gdf", arrived, grad_stacked_low, preferred_element_type=jnp.float32
    )[None]
    grad_w_out = jnp.einsum(
        "ncf,ncd->fd",
        hidden_again.astype(jnp.bfloat16),
        grad_arrived,
        preferred_element_type=jnp.float32,
    )[None]
    grad_hidden_two = jnp.einsum(
        "st,sd->td",
        dispatch,
        grad_returned.reshape(slot_total, D),
        preferred_element_type=jnp.float32,
    )
    grad_hidden_two = grad_hidden_two + jnp.dot(
        grad_logits_low, router_full.T, preferred_element_type=jnp.float32
    )
    grad_router = jnp.dot(hidden_second_norm.T, grad_logits_low, preferred_element_type=jnp.float32)
    grad_middle_norm, grad_gain_two = norm_two_back(grad_hidden_two)
    grad_middle = grad_out + grad_middle_norm
    grad_middle_low = grad_middle.astype(jnp.bfloat16)
    grad_attn_weight = jnp.dot(mixed_low.T, grad_middle_low, preferred_element_type=jnp.float32)
    grad_mixed = jnp.dot(
        grad_middle_low, attention_matrix.T, preferred_element_type=jnp.float32
    ).astype(jnp.bfloat16)
    grad_rows_out = (
        grad_mixed.reshape(tokens, KV_HEADS, group, HEAD_DIM)
        .transpose(1, 2, 0, 3)
        .reshape(KV_HEADS, row_count, HEAD_DIM)
    )
    delta = jnp.sum(grad_rows_out.astype(jnp.float32) * mixed_rows, axis=-1)

    def score_grads(key_part, first_key):
        masked, allowed, keys_here, values_here = block_scores(key_part, first_key)
        probs = probs_of(masked, allowed, largest, totals)
        grad_probs = jnp.einsum(
            "hrd,nhd->hrn", grad_rows_out, values_here, preferred_element_type=jnp.float32
        )
        grad_scores = (probs * (grad_probs - delta[..., None])).astype(jnp.bfloat16)
        return (grad_scores, probs.astype(jnp.bfloat16), keys_here)

    def key_terms(grad_scores, probs_low, key_count):
        grad_keys = (
            jnp.einsum("hrn,hrd->nhd", grad_scores, query_rows, preferred_element_type=jnp.float32)
            * scale
        )
        grad_values = jnp.einsum(
            "hrn,hrd->nhd", probs_low, grad_rows_out, preferred_element_type=jnp.float32
        )
        return jnp.concatenate(
            [grad_keys.reshape(key_count, kv_width), grad_values.reshape(key_count, kv_width)],
            axis=1,
        )

    start_query = jnp.zeros((KV_HEADS, row_count, HEAD_DIM), jnp.float32)

    def back_step(running, key_part, first_key):
        grad_query_rows, grad_keyvals = running
        grad_scores, probs_low, keys_here = score_grads(key_part, first_key)
        grad_query_rows = (
            grad_query_rows
            + jnp.einsum("hrn,nhd->hrd", grad_scores, keys_here, preferred_element_type=jnp.float32)
            * scale
        )
        fresh = key_terms(grad_scores, probs_low, key_part.shape[0])
        return (grad_query_rows, lax.dynamic_update_slice_in_dim(grad_keyvals, fresh, first_key, 0))

    start_back = (start_query, jnp.zeros((length, 2 * kv_width), jnp.float32))
    grad_query_rows, grad_keyvals = over_keys(
        lax.all_gather(keyval_send, "ctx", axis=0, tiled=True), start_back, back_step
    )
    grad_keyval_mine = lax.psum_scatter(grad_keyvals, "ctx", scatter_dimension=0, tiled=True)
    grad_query = grad_query_rows.reshape(KV_HEADS, group, tokens, HEAD_DIM).transpose(2, 0, 1, 3)
    grad_query_pre = (
        rotate(grad_query.reshape(tokens, HEADS, HEAD_DIM), -angles)
        .reshape(tokens, HEADS * HEAD_DIM)
        .astype(jnp.bfloat16)
    )
    grad_key_pre = rotate(
        grad_keyval_mine[:, :kv_width].reshape(tokens, KV_HEADS, HEAD_DIM), -angles
    ).reshape(tokens, kv_width)
    grad_keyval_pre = jnp.concatenate(
        [grad_key_pre, grad_keyval_mine[:, kv_width:]], axis=1
    ).astype(jnp.bfloat16)
    grad_hidden_one = jnp.dot(
        grad_query_pre, query_matrix.T, preferred_element_type=jnp.float32
    ) + jnp.dot(grad_keyval_pre, keyvalue_matrix.T, preferred_element_type=jnp.float32)
    grad_query_weight = jnp.dot(
        hidden_first_norm.T, grad_query_pre, preferred_element_type=jnp.float32
    )
    grad_keyval_weight = jnp.dot(
        hidden_first_norm.T, grad_keyval_pre, preferred_element_type=jnp.float32
    )
    grad_residual_norm, grad_gain_one = norm_one_back(grad_hidden_one)
    grad_input = (grad_middle + grad_residual_norm).astype(jnp.bfloat16)
    shares = (
        lax.psum_scatter(
            grad_gain_one.astype(jnp.bfloat16), "wa", scatter_dimension=0, tiled=True
        ).astype(jnp.float32),
        lax.psum_scatter(
            grad_query_weight.astype(jnp.bfloat16), "wa", scatter_dimension=0, tiled=True
        ).astype(jnp.float32),
        lax.psum_scatter(
            grad_keyval_weight.astype(jnp.bfloat16), "wa", scatter_dimension=0, tiled=True
        ).astype(jnp.float32),
        lax.psum_scatter(
            grad_attn_weight.astype(jnp.bfloat16), "wa", scatter_dimension=0, tiled=True
        ).astype(jnp.float32),
        lax.psum_scatter(
            grad_gain_two.astype(jnp.bfloat16), "wa", scatter_dimension=0, tiled=True
        ).astype(jnp.float32),
        lax.psum_scatter(
            grad_router.astype(jnp.bfloat16), "wa", scatter_dimension=0, tiled=True
        ).astype(jnp.float32),
        lax.psum_scatter(
            grad_w_in.astype(jnp.bfloat16), "wa", scatter_dimension=3, tiled=True
        ).astype(jnp.float32),
        lax.psum_scatter(
            grad_w_out.astype(jnp.bfloat16), "wa", scatter_dimension=1, tiled=True
        ).astype(jnp.float32),
    )
    summed = lax.psum((shares[0], shares[1], shares[2], shares[3], shares[4], shares[5]), "ctx")
    return (
        output[None],
        grad_input[None],
        summed[0],
        summed[1],
        summed[2],
        summed[3],
        summed[4],
        summed[5],
        shares[6],
        shares[7],
    )


def solution(mesh):
    in_specs = (
        P("wa", "ctx", None),
        P("wa", None),
        P("wa", "ctx", None),
        P("wa"),
        P("wa", None),
        P("wa", None),
        P("wa", None),
        P("wa"),
        P("wa", None),
        P("ctx", None, None, "wa"),
        P("ctx", "wa", None),
        P("wa", "ctx", None),
    )
    out_specs = (
        P("wa", "ctx", None),
        P("wa", "ctx", None),
        P("wa"),
        P("wa", None),
        P("wa", None),
        P("wa", None),
        P("wa"),
        P("wa", None),
        P("ctx", None, None, "wa"),
        P("ctx", "wa", None),
    )
    return jax.shard_map(body, mesh=mesh, in_specs=in_specs, out_specs=out_specs, check_vma=False)
```

profile of v0, /device:TPU:0, one launch (start us, length us, event | category | flops | bytes accessed | tf_op | source)
XLA Modules:
  0.0 1458.6 jit_solution(3266071365475592392)
XLA Ops:
  15.4 24.1 %all-gather.9.cloned.1.call-done = bf16[1536,512]{1,0:T(8,128)(2,1)} async-done(((bf16[768,512]{1,0:T(8,128)(2,1)}), bf16[1536,512]{1,0:T(8,128)(2,1)}) %all-gather.9.cloned.1.call-update) | async-done | bytes 1572880 | tf_op jit(solution)/shard_map/all_gather | solution.py:91
  51.3 52.4 %all-gather.13.cloned.1.call-done = bf16[1536,1536]{1,0:T(8,128)(2,1)} async-done(((bf16[768,1536]{1,0:T(8,128)(2,1)}), bf16[1536,1536]{1,0:T(8,128)(2,1)}) %all-gather.13.cloned.1.call-update) | async-done | bytes 4718608 | tf_op jit(solution)/shard_map/all_gather | solution.py:90
  115.7 32.2 %all-gather.11.cloned.1.call-done = bf16[2048,512]{1,0:T(8,128)(2,1)} async-done(((bf16[128,512]{1,0:T(8,128)(2,1)}), bf16[2048,512]{1,0:T(8,128)(2,1)}) %all-gather.11.cloned.1.call-update) | async-done | bytes 2097168 | tf_op jit(solution)/shard_map/all_gather | solution.py:165
  150.9 20.1 %while.43 = (s32[]{:T(128)}, f32[2,768]{1,0:T(2,128)S(1)}, f32[2,768]{1,0:T(2,128)S(1)}, s32[128]{0:T(128)S(1)}, s32[4]{0:T(128)S(1)}, /*index=5*/s32[2048]{0:T(...) while((s32[]{:T(128)}, f32[2,768]{1,0:T(2,128)S(1)}, ...), condition=%wide.region_4.5_spmd.clone, body=%wide.region_1.4_spmd.clone.sunk | while | flops 207832576 | bytes 10184410 | solution.py:58
  171.0 24.3 %while.44 = (s32[]{:T(128)}, f32[2,768,128]{2,1,0:T(8,128)}, s32[128]{0:T(128)S(1)}, s32[4]{0:T(128)S(1)}, s32[2048]{0:T(1024)S(1)}, /*index=5*/bf16[2048,512]{0...) while((s32[]{:T(128)}, f32[2,768,128]{2,1,0:T(8,128)}, ...), condition=%wide.region_6.7_spmd.clone, body=%wide.region_5.6_spmd.clone.sunk | while | flops 407971840 | bytes 5267169 | solution.py:58
  196.7 14.1 all-gather.15.cloned.1.call-done
  240.2 99.3 %all-to-all-done = bf16[16,128,1536]{2,1,0:T(8,128)(2,1)} async-done(((bf16[16,128,1536]{2,1,0:T(8,128)(2,1)}), bf16[16,128,1536]{2,1,0:T(8,128)(2,1)}, u32[]{:S(2)}, u32[]{:S(2)}) %all-to-all-start) | async-done | bytes 6291488 | tf_op jit(solution)/shard_map/all_to_all | solution.py:211
  339.6 28.1 %all-to-all-start.2 = ((bf16[16,128,1536]{2,1,0:T(8,128)(2,1)}), bf16[16,128,1536]{2,1,0:T(8,128)(2,1)}, u32[]{:S(2)}, u32[]{:S(2)}) async-start(bf16[16,128,1536]{2,1,0:T(8,128)(2,1)} %bitcast.383), calls=%async_computation.2 | async-start | bytes 12582912 | tf_op jit(solution)/shard_map/all_to_all | solution.py:237
  371.9 36.0 %all-gather.17.cloned.1.call-done = bf16[1,2,1536,384]{2,1,0,3:T(2,128)(2,1)} async-done(((bf16[1,2,1536,192]{2,1,0,3:T(2,128)(2,1)}), bf16[1,2,1536,384]{2,1,0,3:T(2,128)(2,1)}) %all-gather.17.cloned.1.call-update) | async-done | bytes 2359312 | tf_op jit(solution)/shard_map/all_gather | solution.py:179
  414.6 9.8 fusion.37
  424.5 7.6 all-gather.19.cloned.1.call-done
  432.1 49.8 %all-to-all-done.2 = bf16[16,128,1536]{2,1,0:T(8,128)(2,1)} async-done(((bf16[16,128,1536]{2,1,0:T(8,128)(2,1)}), bf16[16,128,1536]{2,1,0:T(8,128)(2,1)}, u32[]{:S(2)}, u32[]{:S(2)}) %all-to-all-start.2) | async-done | bytes 6291488 | tf_op jit(solution)/shard_map/all_to_all | solution.py:237
  481.9 10.6 multiply_bitcast_fusion
  495.1 7.1 bitcast_convert_fusion
  502.2 28.5 %all-to-all-start.3 = ((bf16[16,128,1536]{2,1,0:T(8,128)(2,1)}), bf16[16,128,1536]{2,1,0:T(8,128)(2,1)}, u32[]{:S(2)}, u32[]{:S(2)}) async-start(bf16[16,128,1536]{2,1,0:T(8,128)(2,1)} %bitcast_convert_fusion), calls=%async_computation.3 | async-start | bytes 12582912 | tf_op jit(solution)/shard_map/all_to_all | solution.py:247
  530.7 9.5 convolution_convert_fusion.3
  540.2 104.7 %all-to-all-done.3 = bf16[16,128,1536]{2,1,0:T(8,128)(2,1)} async-done(((bf16[16,128,1536]{2,1,0:T(8,128)(2,1)}), bf16[16,128,1536]{2,1,0:T(8,128)(2,1)}, u32[]{:S(2)}, u32[]{:S(2)}) %all-to-all-start.3) | async-done | bytes 6291488 | tf_op jit(solution)/shard_map/all_to_all | solution.py:247
  644.9 28.1 %all-to-all-start.1 = ((bf16[16,128,1536]{2,1,0:T(8,128)(2,1)}), bf16[16,128,1536]{2,1,0:T(8,128)(2,1)}, u32[]{:S(2)}, u32[]{:S(2)}) async-start(bf16[16,128,1536]{2,1,0:T(8,128)(2,1)} %convolution_convert_fusion.3), calls=%async_computation.1 | async-start | bytes 12582912 | tf_op jit(solution)/shard_map/all_to_all | solution.py:217
  680.5 106.7 %all-to-all-done.1 = bf16[16,128,1536]{2,1,0:T(8,128)(2,1)} async-done(((bf16[16,128,1536]{2,1,0:T(8,128)(2,1)}), bf16[16,128,1536]{2,1,0:T(8,128)(2,1)}, u32[]{:S(2)}, u32[]{:S(2)}) %all-to-all-start.1) | async-done | bytes 6291488 | tf_op jit(solution)/shard_map/all_to_all | solution.py:217
  787.2 8.2 gather_fusion.1
  795.4 8.0 gather_fusion
  817.6 22.1 %scatter_fusion = f32[128,8]{0,1:T(8,128)S(1)} fusion(f32[128,8]{0,1:T(8,128)S(1)} %broadcast_in_dim.206, s32[512]{0:T(512)S(1)} %reshape.788, f32[512]{0:T(512)S(1)} %reshape.790), kind=kCustom, calls=%fused_computation.3 | custom fusion | flops 512 | bytes 10240 | tf_op jit(solution)/shard_map/transpose(jvp(jit(take_along_axis)))/scatter-add | solution.py:190
  854.9 38.2 %while.45 = (s32[]{:T(128)}, f32[2,768,128]{2,1,0:T(8,128)}, f32[2048,512]{0,1:T(8,128)}, s32[128]{0:T(128)S(1)}, s32[4]{0:T(128)S(1)}, /*index=5*/s32[2048]{0:T...) while((s32[]{:T(128)}, f32[2,768,128]{2,1,0:T(8,128)}, ...), condition=%wide.region_21.22_spmd.clone, body=%wide.region_20.21_spmd.clone.sunk | while | flops 1014900736 | bytes 30308148 | solution.py:58
  893.2 8.4 fusion.71
  901.7 10.2 fusion.67
  912.9 75.6 %reduce-scatter.8.cloned.1.call-done = f32[128,512]{0,1:T(8,128)} async-done(((f32[2048,512]{0,1:T(8,128)}), f32[128,512]{0,1:T(8,128)}) %reduce-scatter.8.cloned.1.call-update) | async-done | bytes 262160 | tf_op jit(solution)/shard_map/reduce_scatter | solution.py:320
  1003.2 9.0 reduce-scatter.20.cloned.1.call-done
  1014.4 35.4 %reduce-scatter.18.cloned.1.call-done = bf16[1,2,1536,192]{2,3,1,0:T(8,128)(2,1)} async-done(((bf16[1,2,1536,384]{2,3,1,0:T(8,128)(2,1)}), bf16[1,2,1536,192]{2,3,1,0:T(8,128)(2,1)}) %reduce-scatter.18.cloned.1.call-update) | async-done | bytes 1179664 | tf_op jit(solution)/shard_map/reduce_scatter | solution.py:363
  1070.7 20.7 %reduce-scatter.12.cloned.1.call-done = bf16[768,512]{1,0:T(8,128)(2,1)} async-done(((bf16[1536,512]{1,0:T(8,128)(2,1)}), bf16[768,512]{1,0:T(8,128)(2,1)}) %reduce-scatter.12.cloned.1.call-update) | async-done | bytes 786448 | tf_op jit(solution)/shard_map/reduce_scatter | solution.py:351
  1091.3 62.8 %reduce-scatter.14.cloned.1.call-done = bf16[768,1536]{1,0:T(8,128)(2,1)} async-done(((bf16[1536,1536]{1,0:T(8,128)(2,1)}), bf16[768,1536]{1,0:T(8,128)(2,1)}) %reduce-scatter.14.cloned.1.call-update) | async-done | bytes 2359312 | tf_op jit(solution)/shard_map/reduce_scatter | solution.py:354
  1154.1 63.0 %reduce-scatter.10.cloned.1.call-done = bf16[768,1536]{1,0:T(8,128)(2,1)} async-done(((bf16[1536,1536]{1,0:T(8,128)(2,1)}), bf16[768,1536]{1,0:T(8,128)(2,1)}) %reduce-scatter.10.cloned.1.call-update) | async-done | bytes 2359312 | tf_op jit(solution)/shard_map/reduce_scatter | solution.py:348
  1217.1 234.5 %all-reduce.7 = (f32[768]{0:T(1024)}, f32[768,1536]{1,0:T(8,128)}, f32[768,512]{1,0:T(8,128)}, f32[768,1536]{1,0:T(8,128)}, f32[768]{0:T(1024)}, /*index=5*/f32[768,8]{0,1:T(8,128)}) all-reduce(f32[768]{0:T(1024)S(1)} %get-tuple-element.887, ...), channel_id=1, replica_groups=mesh['ctx'=16,'wa'=2] {'ctx'}, use_global_device_ids=true, to_apply=%region_26.27 | all-reduce | flops 2760192 | bytes 16564224 | tf_op jit(solution)/shard_map/psum | solution.py:370
  (382 shorter events, 227.3 us)
Async XLA Ops:
  7.2 32.3 %all-gather.9.cloned.1.call-start = ((), (), s32[]{:S(2)}) async-start(), calls=%async_computation.11 | async-start | bytes 2359296 | tf_op jit(solution)/shard_map/all_gather | solution.py:91
  7.9 95.8 %all-gather.13.cloned.1.call-start = ((), (), s32[]{:S(2)}) async-start(), calls=%async_computation.13 | async-start | bytes 7077888 | tf_op jit(solution)/shard_map/all_gather | solution.py:90
  8.7 139.2 %all-gather.11.cloned.1.call-start = ((), (), s32[]{:S(2)}) async-start(), calls=%async_computation.12 | async-start | bytes 2228224 | tf_op jit(solution)/shard_map/all_gather | solution.py:165
  14.0 96.3 %copy-start.17 = (f32[1536]{0:T(1024)}, f32[1536]{0:T(1024)S(1)}, u32[]{:S(2)}) copy-start(f32[1536]{0:T(1024)S(1)} %reshape.799) | copy-start | bytes 18436
  15.4 27.9 %copy-start.29 = (f32[128]{0:T(128)}, f32[128]{0:T(128)S(1)}, u32[]{:S(2)}) copy-start(f32[128]{0:T(128)S(1)} %fusion.94) | copy-start | bytes 1540
  15.4 95.0 %copy-start.23 = (f32[128]{0:T(128)}, f32[128]{0:T(128)S(1)}, u32[]{:S(2)}) copy-start(f32[128]{0:T(128)S(1)} %fusion.126) | copy-start | bytes 1540
  15.4 27.9 %copy-start.22 = (s32[1,128,4]{1,2,0:T(4,128)S(1)}, s32[1,128,4]{1,2,0:T(4,128)}, u32[]{:S(2)}) copy-start(s32[1,128,4]{1,2,0:T(4,128)} %param.20) | copy-start | bytes 6148
  15.4 28.2 %copy-start.28 = (bf16[768]{0:T(1024)(128)(2,1)S(1)}, bf16[768]{0:T(1024)(128)(2,1)}, u32[]{:S(2)}) copy-start(bf16[768]{0:T(1024)(128)(2,1)} %param.25) | copy-start | bytes 4612
  15.4 34.3 %copy-start.21 = (s32[1,2048]{1,0:T(1,128)S(1)}, s32[1,2048]{1,0:T(1,128)}, u32[]{:S(2)}) copy-start(s32[1,2048]{1,0:T(1,128)} %param.19) | copy-start | bytes 24580
  42.7 168.1 %all-gather.15.cloned.1.call-start = ((), (), s32[]{:S(2)}) async-start(), calls=%async_computation.14 | async-start | bytes 7077888 | tf_op jit(solution)/shard_map/all_gather | solution.py:92
  219.6 120.0 %all-to-all-start = ((bf16[16,128,1536]{2,1,0:T(8,128)(2,1)}), bf16[16,128,1536]{2,1,0:T(8,128)(2,1)}, u32[]{:S(2)}, u32[]{:S(2)}) async-start(bf16[16,128,1536]{2,1,0:T(8,128)(2,1)} %bitcast.382), calls=%async_computation | async-start | bytes 12582912 | tf_op jit(solution)/shard_map/all_to_all | solution.py:211
  339.6 142.3 %all-to-all-start.2 = ((bf16[16,128,1536]{2,1,0:T(8,128)(2,1)}), bf16[16,128,1536]{2,1,0:T(8,128)(2,1)}, u32[]{:S(2)}, u32[]{:S(2)}) async-start(bf16[16,128,1536]{2,1,0:T(8,128)(2,1)} %bitcast.383), calls=%async_computation.2 | async-start | bytes 12582912 | tf_op jit(solution)/shard_map/all_to_all | solution.py:237
  367.7 40.1 %all-gather.17.cloned.1.call-start = ((), (), s32[]{:S(2)}) async-start(), calls=%async_computation.15 | async-start | bytes 3538944 | tf_op jit(solution)/shard_map/all_gather | solution.py:179
  371.3 60.8 %all-gather.19.cloned.1.call-start = ((), (), s32[]{:S(2)}) async-start(), calls=%async_computation.16 | async-start | bytes 1769472 | tf_op jit(solution)/shard_map/all_gather | solution.py:180
  502.2 142.7 %all-to-all-start.3 = ((bf16[16,128,1536]{2,1,0:T(8,128)(2,1)}), bf16[16,128,1536]{2,1,0:T(8,128)(2,1)}, u32[]{:S(2)}, u32[]{:S(2)}) async-start(bf16[16,128,1536]{2,1,0:T(8,128)(2,1)} %bitcast_convert_fusion), calls=%async_computation.3 | async-start | bytes 12582912 | tf_op jit(solution)/shard_map/all_to_all | solution.py:247
  644.9 142.3 %all-to-all-start.1 = ((bf16[16,128,1536]{2,1,0:T(8,128)(2,1)}), bf16[16,128,1536]{2,1,0:T(8,128)(2,1)}, u32[]{:S(2)}, u32[]{:S(2)}) async-start(bf16[16,128,1536]{2,1,0:T(8,128)(2,1)} %convolution_convert_fusion.3), calls=%async_computation.1 | async-start | bytes 12582912 | tf_op jit(solution)/shard_map/all_to_all | solution.py:217
  673.0 315.4 %reduce-scatter.8.cloned.1.call-start = ((), (), s32[]{:S(2)}) async-start(), calls=%async_computation.17 | async-start | bytes 4456448 | tf_op jit(solution)/shard_map/reduce_scatter | solution.py:320
  817.6 22.1 %copy-start.7 = (f32[128,1536]{1,0:T(8,128)S(1)}, f32[128,1536]{1,0:T(8,128)}, u32[]{:S(2)}) copy-start(f32[128,1536]{1,0:T(8,128)} %copy-done.6) | copy-start | bytes 2359300
  893.2 119.1 %reduce-scatter.20.cloned.1.call-start = ((), (), s32[]{:S(2)}) async-start(), calls=%async_computation.23 | async-start | bytes 1769472 | tf_op jit(solution)/shard_map/reduce_scatter | solution.py:366
  901.6 87.7 %copy-start.19 = (f32[128,64]{0,1:T(8,128)S(1)}, f32[128,64]{0,1:T(8,128)}, u32[]{:S(2)}) copy-start(f32[128,64]{0,1:T(8,128)} %get-tuple-element.878) | copy-start | bytes 98308
  901.6 87.7 %copy-start.20 = (f32[128,64]{0,1:T(8,128)S(1)}, f32[128,64]{0,1:T(8,128)}, u32[]{:S(2)}) copy-start(f32[128,64]{0,1:T(8,128)} %get-tuple-element.880) | copy-start | bytes 98308
  901.7 148.1 %reduce-scatter.18.cloned.1.call-start = ((), (), s32[]{:S(2)}) async-start(), calls=%async_computation.22 | async-start | bytes 3538944 | tf_op jit(solution)/shard_map/reduce_scatter | solution.py:363
  911.9 78.5 %copy-start.1 = (bf16[1,128,1536]{2,1,0:T(8,128)(2,1)S(1)}, bf16[1,128,1536]{2,1,0:T(8,128)(2,1)}, u32[]{:S(2)}) copy-start(bf16[1,128,1536]{2,1,0:T(8,128)(2,1)} %param.18) | copy-start | bytes 1179652
  911.9 78.5 %copy-start.18 = (f32[1536]{0:T(1024)S(1)}, f32[1536]{0:T(1024)}, u32[]{:S(2)}) copy-start(f32[1536]{0:T(1024)} %copy-done.17) | copy-start | bytes 18436
  911.9 78.5 %copy-start.24 = (f32[128]{0:T(128)S(1)}, f32[128]{0:T(128)}, u32[]{:S(2)}) copy-start(f32[128]{0:T(128)} %copy-done.23) | copy-start | bytes 1540
  911.9 80.4 %copy-start.9 = (f32[128,1536]{1,0:T(8,128)S(1)}, f32[128,1536]{1,0:T(8,128)}, u32[]{:S(2)}) copy-start(f32[128,1536]{1,0:T(8,128)} %copy-done.8) | copy-start | bytes 2359300
  911.9 80.4 %copy-start.13 = (bf16[128,2,6,128]{0,3,2,1:T(8,128)(2,1)S(1)}, bf16[128,2,6,128]{0,3,2,1:T(8,128)(2,1)}, u32[]{:S(2)}) copy-start(bf16[128,2,6,128]{0,3,2,1:T(8,128)(2,1)} %copy-done.12) | copy-start | bytes 1179652
  912.0 150.4 %reduce-scatter.16.cloned.1.call-start = ((), (), s32[]{:S(2)}) async-start(), calls=%async_computation.21 | async-start | bytes 36864 | tf_op jit(solution)/shard_map/reduce_scatter | solution.py:360
  912.8 178.5 %reduce-scatter.12.cloned.1.call-start = ((), (), s32[]{:S(2)}) async-start(), calls=%async_computation.19 | async-start | bytes 2359296 | tf_op jit(solution)/shard_map/reduce_scatter | solution.py:351
  992.2 161.9 %reduce-scatter.14.cloned.1.call-start = ((), (), s32[]{:S(2)}) async-start(), calls=%async_computation.20 | async-start | bytes 7077888 | tf_op jit(solution)/shard_map/reduce_scatter | solution.py:354
  995.9 221.2 %reduce-scatter.10.cloned.1.call-start = ((), (), s32[]{:S(2)}) async-start(), calls=%async_computation.18 | async-start | bytes 7077888 | tf_op jit(solution)/shard_map/reduce_scatter | solution.py:348
  1062.3 154.8 %copy-start.25 = (bf16[768,8]{0,1:T(8,128)(2,1)S(1)}, bf16[768,8]{0,1:T(8,128)(2,1)}, u32[]{:S(2)}) copy-start(bf16[768,8]{0,1:T(8,128)(2,1)} %reduce-scatter.16.cloned.1.call-done) | copy-start | bytes 36868
  (25 other events, 115.9 us)
Sparse Core Ops, SparseCore 0:
  9.6 29.8 all-gather.8
  41.1 62.6 all-gather.12
  106.5 41.3 all-gather.10
  149.3 61.4 all-gather.14
  371.4 36.4 all-gather.16
  409.3 22.7 all-gather.18
  893.3 95.1 reduce-scatter.7
  991.4 20.8 reduce-scatter.19
  1015.0 34.7 reduce-scatter.17
  1052.5 9.8 reduce-scatter.15
  1065.3 26.0 reduce-scatter.11
  1094.1 59.9 reduce-scatter.13
  1157.1 59.9 reduce-scatter.9
where the time goes:
time: 1470 us; the launch traced here: 1460 us
  waiting for transfers between devices  802 us (55%)
  blocking collectives  254 us (17%)
  matrix products  145 us (10%)
  starting transfers between devices  91.3 us (6%)
  local copies, waits for them, and re-layouts  82.8 us (6%)
  other arithmetic  59.4 us (4%)
  between operations  15.9 us (1%)
    psum x1, blocking collectives, body(): lax.psum((shares[0], shares[1], shares[2], shares[3], shares[4], shares[5...  234 us
    all_to_all x1, waiting for transfers between devices, body(): lax.all_to_all(result, 'ctx', split_axis=0, concat_axis=0, tiled=True)  107 us
    all_to_all x1, waiting for transfers between devices, body(): lax.all_to_all(grad_rows, 'ctx', split_axis=0, concat_axis=0, tiled=True)  105 us
    all_to_all x1, waiting for transfers between devices, body(): lax.all_to_all(send_rows, 'ctx', split_axis=0, concat_axis=0, tiled=True)  99.3 us
    reduce_scatter x1, waiting for transfers between devices, body(): lax.psum_scatter(grad_keyvals, 'ctx', scatter_dimension=0, tiled=True)  75.6 us
    reduce_scatter x1, waiting for transfers between devices, body(): lax.psum_scatter(grad_query_weight.astype(jnp.bfloat16), 'wa', scatter_di...  63 us
    reduce_scatter x1, waiting for transfers between devices, body(): lax.psum_scatter(grad_attn_weight.astype(jnp.bfloat16), 'wa', scatter_dim...  62.8 us
    all_gather x1, waiting for transfers between devices, body(): lax.all_gather(w_query, 'wa', axis=0, tiled=True)  52.4 us
  transfers between devices with their start and end apart: 17, of which 17 were waited for; matrix products, arithmetic and copies ran while one was open for 11% of the time, Pallas kernels for 0%

commit v1 on v0

--- a/solution.py
+++ b/solution.py
@@ -1,8 +1,11 @@
+import functools
 import math
 
 import jax
 import jax.numpy as jnp
 from jax import lax
+from jax.experimental import pallas as pl
+from jax.experimental.pallas import tpu as pltpu
 from jax.sharding import PartitionSpec as P
 
 D = 1536
@@ -61,7 +64,7 @@
     return running
 
 
-def body(
+def routed_body(
     layer_input,
     seq_ids,
     routes,
@@ -382,6 +385,581 @@
     )
 
 
+MESH = pl.DeviceIdType.MESH
+VMEM_LIMIT = 60 * 1024 * 1024
+
+
+def chip_place():
+    count = lax.axis_size("ctx")
+    me = lax.axis_index("ctx")
+    return me // 4, lax.rem(me // 2, 2), lax.rem(me, 2), count // 4
+
+
+def ctx_of(z, y, c):
+    return (z * 2 + y) * 2 + c
+
+
+def greet():
+    z, y, c, depth = chip_place()
+    barrier = pltpu.get_barrier_semaphore()
+
+    def signal(device):
+        pl.semaphore_signal(barrier, 1, device_id={"ctx": device}, device_id_type=MESH)
+
+    signal(ctx_of(z, y, 1 - c))
+    signal(ctx_of(z, 1 - y, c))
+    pl.when(z > 0)(lambda: signal(ctx_of(z - 1, y, c)))
+    pl.when(z < depth - 1)(lambda: signal(ctx_of(z + 1, y, c)))
+    pl.semaphore_wait(barrier, 2 + (z > 0).astype(jnp.int32) + (z < depth - 1).astype(jnp.int32))
+
+
+def gather_steps(out, z_sems, y_sems, c_sems):
+    z, y, c, depth = chip_place()
+    other_y, other_c = 1 - y, 1 - c
+    me = ctx_of(z, y, c)
+
+    def copy(slot, sems, at, target):
+        return pltpu.make_async_remote_copy(
+            src_ref=out.at[slot],
+            dst_ref=out.at[slot],
+            send_sem=sems.at[(0,) + at],
+            recv_sem=sems.at[(1,) + at],
+            device_id={"ctx": target},
+            device_id_type=MESH,
+        )
+
+    up, down = ctx_of(jnp.minimum(z + 1, depth - 1), y, c), ctx_of(jnp.maximum(z - 1, 0), y, c)
+
+    def send_up(of_z):
+        return copy(ctx_of(of_z, y, c), z_sems, (0, of_z), up)
+
+    def send_down(of_z):
+        return copy(ctx_of(of_z, y, c), z_sems, (1, of_z), down)
+
+    def send_y(of_z):
+        return copy(ctx_of(of_z, y, c), y_sems, (of_z,), ctx_of(z, other_y, c))
+
+    def take_y(of_z):
+        return copy(ctx_of(of_z, other_y, c), y_sems, (of_z,), ctx_of(z, other_y, c))
+
+    def send_c(of_z, of_y):
+        return copy(ctx_of(of_z, of_y, c), c_sems, (of_z * 2 + of_y,), ctx_of(z, y, other_c))
+
+    def take_c(of_z, of_y):
+        return copy(ctx_of(of_z, of_y, other_c), c_sems, (of_z * 2 + of_y,), ctx_of(z, y, other_c))
+
+    pl.when(z < depth - 1)(lambda: send_up(z).start())
+    pl.when(z > 0)(lambda: send_down(z).start())
+    send_y(z).start()
+    send_c(z, y).start()
+    for step in range(1, depth):
+
+        def from_below(of_z=z - step):
+            send_up(of_z).wait_recv()
+            pl.when(z < depth - 1)(lambda: send_up(of_z).start())
+            send_y(of_z).start()
+            send_c(of_z, y).start()
+
+        def from_above(of_z=z + step):
+            send_down(of_z).wait_recv()
+            pl.when(z > 0)(lambda: send_down(of_z).start())
+            send_y(of_z).start()
+            send_c(of_z, y).start()
+
+        pl.when(z - step >= 0)(from_below)
+        pl.when(z + step < depth)(from_above)
+
+    def across(of_z):
+        take_y(of_z).wait_recv()
+        send_c(of_z, other_y).start()
+
+    across(z)
+    for step in range(1, depth):
+        pl.when(z - step >= 0)(lambda: across(z - step))
+        pl.when(z + step < depth)(lambda: across(z + step))
+    for of_z in range(depth):
+        pl.when((z < depth - 1) & (of_z <= z))(lambda: send_up(of_z).wait_send())
+        pl.when((z > 0) & (of_z >= z))(lambda: send_down(of_z).wait_send())
+        send_y(of_z).wait_send()
+        for of_y in range(2):
+            send_c(of_z, of_y).wait_send()
+            take_c(of_z, of_y).wait_recv()
+    return me
+
+
+def gather_sems(depth):
+    return [
+        pltpu.SemaphoreType.DMA((2, 2, depth)),
+        pltpu.SemaphoreType.DMA((2, depth)),
+        pltpu.SemaphoreType.DMA((2, 2 * depth)),
+    ]
+
+
+def add_into(target, terms, rows):
+    @pl.loop(0, rows // 16)
+    def _(turn):
+        at = pl.ds(pl.multiple_of(turn * 16, 16), 16)
+        total = terms[0][at, :].astype(jnp.float32)
+        for term in terms[1:]:
+            total = total + term[at, :].astype(jnp.float32)
+        target[at, :] = total.astype(target.dtype)
+
+
+def scatter_steps(part, result, from_core, sums, from_y, from_z, c_sems, y_sems, z_sems):
+    z, y, c, depth = chip_place()
+    rows = part.shape[1]
+    other_y, other_c = 1 - y, 1 - c
+
+    def copy(source, target_ref, sems, at, target):
+        return pltpu.make_async_remote_copy(
+            src_ref=source,
+            dst_ref=target_ref,
+            send_sem=sems.at[(0,) + at],
+            recv_sem=sems.at[(1,) + at],
+            device_id={"ctx": target},
+            device_id_type=MESH,
+        )
+
+    def core_copy(chip):
+        return copy(
+            part.at[chip * 2 + other_c], from_core.at[chip], c_sems, (chip,), ctx_of(z, y, other_c)
+        )
+
+    def y_copy(of_z):
+        return copy(
+            sums.at[of_z * 2 + other_y], from_y.at[of_z], y_sems, (of_z,), ctx_of(z, other_y, c)
+        )
+
+    def z_copy(way, of_z):
+        target = jnp.minimum(z + 1, depth - 1) if way == 0 else jnp.maximum(z - 1, 0)
+        return copy(
+            sums.at[of_z * 2 + y],
+            from_z.at[way, of_z],
+            z_sems,
+            (way, of_z),
+            ctx_of(target, y, c),
+        )
+
+    def in_order(act):
+        for step in range(depth - 1, 0, -1):
+            pl.when(z + step < depth)(functools.partial(act, z + step))
+            pl.when(z - step >= 0)(functools.partial(act, z - step))
+        act(z)
+
+    def send_cores(of_z):
+        core_copy(of_z * 2 + other_y).start()
+        core_copy(of_z * 2 + y).start()
+
+    in_order(send_cores)
+
+    def add_cores(of_z):
+        for of_y in (other_y, y):
+            chip = of_z * 2 + of_y
+            core_copy(chip).wait_recv()
+            add_into(sums.at[chip], (part.at[chip * 2 + c], from_core.at[chip]), rows)
+            if of_y is other_y:
+                y_copy(of_z).start()
+
+    in_order(add_cores)
+
+    def add_y(of_z):
+        y_copy(of_z).wait_recv()
+        own = sums.at[of_z * 2 + y]
+
+        def upward():
+            z_copy(0, of_z).wait_recv()
+            add_into(own, (own, from_y.at[of_z], from_z.at[0, of_z]), rows)
+
+        def downward():
+            z_copy(1, of_z).wait_recv()
+            add_into(own, (own, from_y.at[of_z], from_z.at[1, of_z]), rows)
+
+        inner = ((of_z > z) & (z > 0)) | ((of_z < z) & (z < depth - 1))
+        pl.when((of_z > z) & (z > 0))(upward)
+        pl.when((of_z < z) & (z < depth - 1))(downward)
+        pl.when(jnp.logical_not(inner))(lambda: add_into(own, (own, from_y.at[of_z]), rows))
+        pl.when(of_z > z)(lambda: z_copy(0, of_z).start())
+        pl.when(of_z < z)(lambda: z_copy(1, of_z).start())
+
+    in_order(add_y)
+    own = sums.at[z * 2 + y]
+    pl.when(z > 0)(lambda: z_copy(0, z).wait_recv())
+    pl.when(z < depth - 1)(lambda: z_copy(1, z).wait_recv())
+
+    @pl.when((z > 0) & (z < depth - 1))
+    def _():
+        add_into(result, (own, from_z.at[0, z], from_z.at[1, z]), rows)
+
+    pl.when(z == 0)(lambda: add_into(result, (own, from_z.at[1, z]), rows))
+    pl.when(z == depth - 1)(lambda: add_into(result, (own, from_z.at[0, z]), rows))
+    for of_z in range(depth):
+        y_copy(of_z).wait_send()
+        core_copy(of_z * 2).wait_send()
+        core_copy(of_z * 2 + 1).wait_send()
+        pl.when(of_z > z)(lambda: z_copy(0, of_z).wait_send())
+        pl.when(of_z < z)(lambda: z_copy(1, of_z).wait_send())
+
+
+def scatter_scratch(depth, rows, columns):
+    return [
+        pltpu.VMEM((2 * depth, rows, columns), jnp.bfloat16),
+        pltpu.VMEM((2 * depth, rows, columns), jnp.bfloat16),
+        pltpu.VMEM((depth, rows, columns), jnp.bfloat16),
+        pltpu.VMEM((2, depth, rows, columns), jnp.bfloat16),
+        pltpu.SemaphoreType.DMA((2, 2 * depth)),
+        pltpu.SemaphoreType.DMA((2, depth)),
+        pltpu.SemaphoreType.DMA((2, 2, depth)),
+    ]
+
+
+def in_vmem(kernel, out, scratch, number, name, *operands):
+    return pl.pallas_call(
+        kernel,
+        out_shape=out,
+        in_specs=[pl.BlockSpec(memory_space=pltpu.VMEM)] * len(operands),
+        out_specs=jax.tree.map(lambda _: pl.BlockSpec(memory_space=pltpu.VMEM), out),
+        scratch_shapes=scratch,
+        compiler_params=pltpu.CompilerParams(
+            collective_id=number,
+            has_side_effects=number is not None,
+            vmem_limit_bytes=VMEM_LIMIT,
+        ),
+        name=name,
+    )(*operands)
+
+
+def gather_ctx(block, number, name):
+    count = lax.axis_size("ctx")
+
+    def kernel(block_ref, out, *sems):
+        out[lax.axis_index("ctx")] = block_ref[...]
+        greet()
+        gather_steps(out, *sems)
+
+    out = jax.ShapeDtypeStruct((count,) + block.shape, block.dtype)
+    return in_vmem(kernel, out, gather_sems(count // 4), number, name, block)
+
+
+def scatter_ctx(parts, number, name):
+    count, rows, columns = parts.shape
+
+    def kernel(part, result, *scratch):
+        greet()
+        scatter_steps(part, result, *scratch)
+
+    out = jax.ShapeDtypeStruct((rows, columns), jnp.float32)
+    return in_vmem(kernel, out, scatter_scratch(count // 4, rows, columns), number, name, parts)
+
+
+def sum_ctx(parts, number, name):
+    count, rows, columns = parts.shape
+    depth = count // 4
+
+    def kernel(part, out, *scratch):
+        greet()
+        scatter_steps(part, out.at[lax.axis_index("ctx")], *scratch[:7])
+        gather_steps(out, *scratch[7:])
+
+    out = jax.ShapeDtypeStruct(parts.shape, jnp.bfloat16)
+    scratch = scatter_scratch(depth, rows, columns) + gather_sems(depth)
+    return in_vmem(kernel, out, scratch, number, name, parts)
+
+
+def rows_by_rows(left, right):
+    return lax.dot_general(
+        left, right, (((1,), (1,)), ((), ())), preferred_element_type=jnp.float32
+    )
+
+
+def columns_by_columns(left, right):
+    return lax.dot_general(
+        left, right, (((0,), (0,)), ((), ())), preferred_element_type=jnp.float32
+    )
+
+
+def allowed_bias(doc_row, doc_column, tokens):
+    keys = doc_row.shape[1]
+    query_block = lax.axis_index("ctx") * tokens // BLOCK
+    key_block = lax.broadcasted_iota(jnp.int32, (tokens, keys), 1) // BLOCK
+    allowed = (doc_row == doc_column) & (key_block <= query_block)
+    return jnp.where(allowed, 0.0, NEGATIVE)
+
+
+def attend_kernel(query, keyval, doc_row, doc_column, mixed, level, stacked, bias):
+    tokens = query.shape[0]
+    bias[...] = allowed_bias(doc_row[...], doc_column[...], tokens)
+    for head in range(HEADS):
+        stacked[head * tokens : (head + 1) * tokens, :] = query[:, head * 128 : (head + 1) * 128]
+
+    @pl.loop(0, HEADS // 2)
+    def _(pair):
+        rows = pl.ds(pl.multiple_of(pair * 2 * tokens, 128), 2 * tokens)
+        kind = pair // (HEADS // KV_HEADS // 2)
+        keys = keyval[:, pl.ds(pl.multiple_of(kind * 128, 128), 128)]
+        vals = keyval[:, pl.ds(pl.multiple_of(kind * 128 + 256, 128), 128)]
+        scores = rows_by_rows(stacked[rows, :], keys) * HEAD_DIM**-0.5
+        scores = (scores.reshape(2, tokens, -1) + bias[...][None]).reshape(scores.shape)
+        top = jnp.max(scores, axis=-1, keepdims=True)
+        weights = jnp.exp(scores - top)
+        total = jnp.sum(weights, axis=-1, keepdims=True)
+        probs = (weights / total).astype(jnp.bfloat16)
+        mixture = jnp.dot(probs, vals, preferred_element_type=jnp.float32)
+        for half in range(2):
+            columns = pl.ds(pl.multiple_of((pair * 2 + half) * 128, 128), 128)
+            mixed[:, columns] = mixture[half * tokens : (half + 1) * tokens]
+        level[rows, :] = top + jnp.log(total)
+
+
+def attend(query, keyval, doc_row, doc_column):
+    tokens, keys = query.shape[0], keyval.shape[0]
+    out = (
+        jax.ShapeDtypeStruct(query.shape, jnp.float32),
+        jax.ShapeDtypeStruct((HEADS * tokens, 1), jnp.float32),
+    )
+    scratch = [
+        pltpu.VMEM((HEADS * tokens, HEAD_DIM), jnp.bfloat16),
+        pltpu.VMEM((tokens, keys), jnp.float32),
+    ]
+    return in_vmem(
+        attend_kernel, out, scratch, None, "attend", query, keyval, doc_row, doc_column
+    )
+
+
+def attend_back_kernel(
+    query, keyval, doc_row, doc_column, level, mixed, grad_mixed,
+    grad_query, grad_keyval, stacked, grads, bias, delta, total,
+):
+    tokens = query.shape[0]
+    bias[...] = allowed_bias(doc_row[...], doc_column[...], tokens)
+    total[...] = jnp.zeros_like(total)
+    for head in range(HEADS):
+        rows, columns = slice(head * tokens, (head + 1) * tokens), slice(head * 128, head * 128 + 128)
+        stacked[rows, :] = query[:, columns]
+        grads[rows, :] = grad_mixed[:, columns]
+        delta[rows, :] = jnp.sum(
+            grad_mixed[:, columns].astype(jnp.float32) * mixed[:, columns], axis=-1, keepdims=True
+        )
+
+    @pl.loop(0, HEADS // 2)
+    def _(pair):
+        rows = pl.ds(pl.multiple_of(pair * 2 * tokens, 128), 2 * tokens)
+        kind = pair // (HEADS // KV_HEADS // 2)
+        key_columns = pl.ds(pl.multiple_of(kind * 128, 128), 128)
+        val_columns = pl.ds(pl.multiple_of(kind * 128 + 256, 128), 128)
+        keys, vals = keyval[:, key_columns], keyval[:, val_columns]
+        own, grad = stacked[rows, :], grads[rows, :]
+        scores = rows_by_rows(own, keys) * HEAD_DIM**-0.5
+        scores = (scores.reshape(2, tokens, -1) + bias[...][None]).reshape(scores.shape)
+        probs = jnp.exp(scores - level[rows, :])
+        grad_probs = rows_by_rows(grad, vals)
+        grad_scores = (probs * (grad_probs - delta[rows, :])).astype(jnp.bfloat16)
+        own_grad = jnp.dot(grad_scores, keys, preferred_element_type=jnp.float32)
+        for half in range(2):
+            columns = pl.ds(pl.multiple_of((pair * 2 + half) * 128, 128), 128)
+            grad_query[:, columns] = own_grad[half * tokens : (half + 1) * tokens] * HEAD_DIM**-0.5
+        total[:, key_columns] += columns_by_columns(grad_scores, own) * HEAD_DIM**-0.5
+        total[:, val_columns] += columns_by_columns(probs.astype(jnp.bfloat16), grad)
+
+    grad_keyval[...] = total[...].astype(jnp.bfloat16)
+
+
+def attend_back(query, keyval, doc_row, doc_column, level, mixed, grad_mixed):
+    tokens, keys = query.shape[0], keyval.shape[0]
+    out = (
+        jax.ShapeDtypeStruct(query.shape, jnp.float32),
+        jax.ShapeDtypeStruct(keyval.shape, jnp.bfloat16),
+    )
+    scratch = [
+        pltpu.VMEM((HEADS * tokens, HEAD_DIM), jnp.bfloat16),
+        pltpu.VMEM((HEADS * tokens, HEAD_DIM), jnp.bfloat16),
+        pltpu.VMEM((tokens, keys), jnp.float32),
+        pltpu.VMEM((HEADS * tokens, 1), jnp.float32),
+        pltpu.VMEM(keyval.shape, jnp.float32),
+    ]
+    return in_vmem(
+        attend_back_kernel, out, scratch, None, "attend_back",
+        query, keyval, doc_row, doc_column, level, mixed, grad_mixed,
+    )
+
+
+def rms_back(values, gain_vec, grad):
+    scale = lax.rsqrt(jnp.mean(values * values, axis=-1, keepdims=True) + EPSILON)
+    through = jnp.mean(gain_vec * grad * values, axis=-1, keepdims=True)
+    back = scale * gain_vec * grad - values * scale**3 * through
+    return back, jnp.sum(grad * values * scale, axis=0)
+
+
+def swap_wa(values):
+    return jax.tree.map(lambda v: lax.ppermute(v, "wa", ((0, 1), (1, 0))), values)
+
+
+def gathered_body(
+    layer_input, seq_ids, routes, gain_attn, w_query, w_keyval, w_out_attn, gain_ffn, router,
+    w_in, w_out, d_out,
+):
+    count, me, side = lax.axis_size("ctx"), lax.axis_index("ctx"), lax.axis_index("wa")
+    tokens = layer_input.shape[1]
+    length = tokens * count
+    experts = router.shape[1]
+    kv_width = KV_HEADS * HEAD_DIM
+    half = D // 2
+
+    def gathered(values, axis):
+        return lax.all_gather(values, "wa", axis=axis, tiled=True)
+
+    def other_half(values):
+        return lax.dynamic_slice_in_dim(values, (1 - side) * half, half, 1)
+
+    def own_half(values):
+        return lax.dynamic_slice_in_dim(values, side * half, half, 1)
+
+    d_out_all = gather_ctx(d_out[0], 0, "gather_d_out").reshape(length, D)
+    query_matrix, keyval_matrix = gathered(w_query, 0), gathered(w_keyval, 0)
+    attention_matrix = gathered(w_out_attn, 0)
+    gain_one = gathered(gain_attn, 0).astype(jnp.float32)
+    gain_two = gathered(gain_ffn, 0).astype(jnp.float32)
+    router_full = gathered(router, 0)
+    in_half, out_half = gathered(w_in, 3)[0], gathered(w_out, 1)[0]
+    in_matrix = in_half.transpose(1, 0, 2).reshape(D, -1)
+
+    residual = layer_input[0].astype(jnp.float32)
+    hidden_one = rms_scale(residual, gain_one).astype(jnp.bfloat16)
+    hidden_one_there = swap_wa(other_half(hidden_one))
+    positions = me * tokens + jnp.arange(tokens, dtype=jnp.int32)
+    angles = angle_table(positions)
+    query_pre = jnp.dot(hidden_one, query_matrix, preferred_element_type=jnp.float32)
+    keyval_pre = jnp.dot(hidden_one, keyval_matrix, preferred_element_type=jnp.float32)
+    query = rotate(query_pre.reshape(tokens, HEADS, HEAD_DIM), angles).astype(jnp.bfloat16)
+    query = query.reshape(tokens, D)
+    keys = rotate(keyval_pre[:, :kv_width].reshape(tokens, KV_HEADS, HEAD_DIM), angles)
+    keyval = jnp.concatenate([keys.reshape(tokens, kv_width), keyval_pre[:, kv_width:]], axis=1)
+    keyval_all = gather_ctx(keyval.astype(jnp.bfloat16), 1, "gather_kv").reshape(length, -1)
+    doc_column = lax.dynamic_slice_in_dim(seq_ids[0], me * tokens, tokens, 0)[:, None]
+    mixed, level = attend(query, keyval_all, seq_ids, doc_column)
+    mixed_low = mixed.astype(jnp.bfloat16)
+    mixed_there = swap_wa(other_half(mixed_low))
+    middle = residual + jnp.dot(mixed_low, attention_matrix, preferred_element_type=jnp.float32)
+
+    hidden_two = rms_scale(middle, gain_two).astype(jnp.bfloat16)
+    logits = jnp.dot(hidden_two, router_full, preferred_element_type=jnp.float32)
+    numbers = jnp.arange(experts, dtype=jnp.int32)
+    chosen = jnp.any(routes[0][:, :, None] == numbers[None, None, :], axis=1)
+    masked = jnp.where(chosen, logits, NEGATIVE)
+    weights = jnp.exp(masked - jnp.max(masked, axis=1, keepdims=True))
+    gates = weights / jnp.sum(weights, axis=1, keepdims=True)
+    gates_high = gates.astype(jnp.bfloat16)
+    gates_low = (gates - gates_high.astype(jnp.float32)).astype(jnp.bfloat16)
+    spare = jnp.zeros((tokens, 128 - 2 * experts), jnp.bfloat16)
+    send = jnp.concatenate([hidden_two, gates_high, gates_low, spare], axis=1)
+    hidden_all = gather_ctx(send, 2, "gather_hidden").reshape(length, -1)
+
+    rows = hidden_all[:, :D]
+    expert = me // 2
+    lane = jnp.arange(128, dtype=jnp.int32)[None, :]
+    gate = jnp.sum(
+        jnp.where(
+            (lane == expert) | (lane == expert + experts), hidden_all[:, D:].astype(jnp.float32), 0.0
+        ),
+        axis=1,
+        keepdims=True,
+    )
+    both = jnp.dot(rows, in_matrix, preferred_element_type=jnp.float32)
+    width = both.shape[1] // 2
+
+    def gate_unit(first, second):
+        return jax.nn.gelu(first, approximate=True) * second
+
+    hidden, unit_back = jax.vjp(gate_unit, both[:, :width], both[:, width:])
+    hidden_gated = (hidden * gate).astype(jnp.bfloat16)
+    result = jnp.dot(hidden_gated, out_half, preferred_element_type=jnp.float32)
+    grad_hidden = rows_by_rows(d_out_all, out_half)
+    grad_gate = jnp.sum(grad_hidden * hidden, axis=1, keepdims=True)
+    grad_both = jnp.concatenate(unit_back(grad_hidden * gate), axis=1).astype(jnp.bfloat16)
+    grad_rows = rows_by_rows(grad_both, in_matrix)
+    gate_columns = jnp.where(lane == expert, grad_gate, 0.0)
+    grad_send = jnp.concatenate([grad_rows, gate_columns], axis=1).astype(jnp.bfloat16)
+    returned = scatter_ctx(grad_send.reshape(count, tokens, -1), 3, "scatter_grad_rows")
+    result_sum = scatter_ctx(
+        result.astype(jnp.bfloat16).reshape(count, tokens, D), 4, "scatter_result"
+    )
+    output = (middle + result_sum).astype(jnp.bfloat16)
+    grad_in_matrix = columns_by_columns(rows, grad_both).reshape(D, 2, width).transpose(1, 0, 2)
+    grad_out_half = columns_by_columns(hidden_gated, d_out_all)
+    grad_w_in = lax.psum_scatter(
+        grad_in_matrix[None].astype(jnp.bfloat16), "wa", scatter_dimension=3, tiled=True
+    ).astype(jnp.float32)
+    grad_w_out = lax.psum_scatter(
+        grad_out_half[None].astype(jnp.bfloat16), "wa", scatter_dimension=1, tiled=True
+    ).astype(jnp.float32)
+
+    grad_out = d_out[0].astype(jnp.float32)
+    grad_gates = returned[:, D : D + experts]
+    grad_logits = gates * (grad_gates - jnp.sum(gates * grad_gates, axis=1, keepdims=True))
+    grad_logits_low = grad_logits.astype(jnp.bfloat16)
+    grad_hidden_two = returned[:, :D] + rows_by_rows(grad_logits_low, router_full)
+    grad_router = columns_by_columns(hidden_two, grad_logits_low)
+    back_two, grad_gain_two = rms_back(middle, gain_two, grad_hidden_two)
+    grad_middle = grad_out + back_two
+    grad_middle_low = grad_middle.astype(jnp.bfloat16)
+    grad_middle_there = swap_wa(grad_middle_low)
+    grad_mixed = rows_by_rows(grad_middle_low, attention_matrix).astype(jnp.bfloat16)
+    grad_query, grad_keyval = attend_back(
+        query, keyval_all, seq_ids, doc_column, level, mixed, grad_mixed
+    )
+    grad_query_pre = rotate(grad_query.reshape(tokens, HEADS, HEAD_DIM), -angles)
+    grad_query_pre = grad_query_pre.reshape(tokens, D).astype(jnp.bfloat16)
+    grad_query_there = swap_wa(grad_query_pre)
+    grad_keyval_own = scatter_ctx(grad_keyval.reshape(count, tokens, -1), 5, "scatter_grad_kv")
+    grad_keys = rotate(
+        grad_keyval_own[:, :kv_width].reshape(tokens, KV_HEADS, HEAD_DIM), -angles
+    ).reshape(tokens, kv_width)
+    grad_keyval_pre = jnp.concatenate([grad_keys, grad_keyval_own[:, kv_width:]], axis=1)
+    grad_keyval_pre = grad_keyval_pre.astype(jnp.bfloat16)
+    grad_keyval_there = swap_wa(grad_keyval_pre)
+    grad_hidden_one = rows_by_rows(grad_query_pre, query_matrix) + rows_by_rows(
+        grad_keyval_pre, keyval_matrix
+    )
+    back_one, grad_gain_one = rms_back(residual, gain_one, grad_hidden_one)
+    grad_input = (grad_middle + back_one).astype(jnp.bfloat16)
+
+    small = jnp.concatenate(
+        [grad_router, grad_gain_two[:, None], grad_gain_one[:, None]], axis=1
+    )
+    small_half = lax.dynamic_slice_in_dim(small, side * half, half, 0)
+    small_there = swap_wa(lax.dynamic_slice_in_dim(small, (1 - side) * half, half, 0))
+    small_sum = small_half + small_there
+
+    def pair_sum(left, left_there, right, right_there):
+        return columns_by_columns(
+            jnp.concatenate([own_half(left), left_there]), jnp.concatenate([right, right_there])
+        ).astype(jnp.bfloat16)
+
+    shares = jnp.concatenate(
+        [
+            pair_sum(hidden_one, hidden_one_there, grad_query_pre, grad_query_there),
+            pair_sum(hidden_one, hidden_one_there, grad_keyval_pre, grad_keyval_there),
+            pair_sum(mixed_low, mixed_there, grad_middle_low, grad_middle_there),
+            jnp.pad(small_sum, ((0, 0), (0, 128 - experts - 2))).astype(jnp.bfloat16),
+        ],
+        axis=1,
+    )
+    summed = sum_ctx(shares.reshape(count, half // count, -1), 6, "sum_shares")
+    summed = summed.reshape(half, -1).astype(jnp.float32)
+    first, second, third = D, D + 2 * kv_width, 2 * D + 2 * kv_width
+    return (
+        output[None],
+        grad_input[None],
+        summed[:, third + experts + 1],
+        summed[:, :first],
+        summed[:, first:second],
+        summed[:, second:third],
+        summed[:, third + experts],
+        summed[:, third : third + experts],
+        grad_w_in,
+        grad_w_out,
+    )
+
+
 def solution(mesh):
     in_specs = (
         P("wa", "ctx", None),
@@ -409,4 +987,6 @@
         P("ctx", None, None, "wa"),
         P("ctx", "wa", None),
     )
+    depth = mesh.shape["ctx"]
+    body = gathered_body if depth == 16 else routed_body
     return jax.shard_map(body, mesh=mesh, in_specs=in_specs, out_specs=out_specs, check_vma=False)

time: 1470 us -> 604 us (0.41)
  waiting for transfers between devices: 802 us -> 67.7 us
  Pallas kernels: 0 us -> 346 us
  blocking collectives: 254 us -> 17.8 us
  starting transfers between devices: 91.3 us -> 7 us
  matrix products: 145 us -> 80.2 us
  local copies, waits for them, and re-layouts: 82.8 us -> 35.7 us
  other arithmetic: 59.4 us -> 27.1 us
    all_to_all x4 -> x0, waiting for transfers between devices: 361 us -> none  [the longest x1 107 us: body(): lax.all_to_all(result, 'ctx', split_axis=0, concat_axis=0, tiled=True)]
    pallas_call x0 -> x9, Pallas kernels: none -> 346 us  [in_vmem(): pl.pallas_call(kernel, out_shape=out, in_specs=[pl.BlockSpec(memory_space...]
    reduce_scatter x7 -> x2, waiting for transfers between devices: 272 us -> 0.01 us  [the longest x1 0.01 us: gathered_body(): lax.psum_scatter(grad_out_half[None].astype(jnp.bfloat16), 'wa', scatter_...]
    psum x1 -> x0, blocking collectives: 234 us -> none  [body(): lax.psum((shares[0], shares[1], shares[2], shares[3], shares[4], shares[5...]
    all_gather x6 -> x5, waiting for transfers between devices: 166 us -> 40.2 us  [gathered(): return lax.all_gather(values, 'wa', axis=axis, tiled=True)]
    all_to_all x4 -> x0, starting transfers between devices: 90.5 us -> none  [the longest x1 28.5 us: body(): lax.all_to_all(grad_rows, 'ctx', split_axis=0, concat_axis=0, tiled=True)]
    dot_general x50 -> x18, matrix products: 145 us -> 80.2 us  [the longest x6 31 us: rows_by_rows(): lax.dot_general(left, right, (((1,), (1,)), ((), ())), preferred_element_...]
    ppermute x0 -> x6, waiting for transfers between devices: none -> 24.9 us  [swap_wa(): lax.ppermute(v, 'wa', ((0, 1), (1, 0)))]
  transfers between devices with their start and end apart: 17 -> 13, of which waited for: 17 -> 3; matrix products, arithmetic and copies ran while one was open for 11% -> 23% of each run, Pallas kernels for 0% -> 58%
where the time goes in v1:
time: 604 us; the launch traced here: 597 us
  Pallas kernels  346 us (57%)
  matrix products  80.2 us (13%)
  waiting for transfers between devices  67.7 us (11%)
  local copies, waits for them, and re-layouts  35.7 us (6%)
  other arithmetic  27.1 us (4%)
  blocking collectives  17.8 us (3%)
  between operations  15.5 us (3%)
  starting transfers between devices  7 us (1%)
    pallas_call x9, Pallas kernels, in_vmem(): pl.pallas_call(kernel, out_shape=out, in_specs=[pl.BlockSpec(memory_space...  346 us
    all_gather x5, waiting for transfers between devices, gathered(): return lax.all_gather(values, 'wa', axis=axis, tiled=True)  40.2 us
    dot_general x6, matrix products, rows_by_rows(): lax.dot_general(left, right, (((1,), (1,)), ((), ())), preferred_element_...  31 us
    ppermute x6, waiting for transfers between devices, swap_wa(): lax.ppermute(v, 'wa', ((0, 1), (1, 0)))  24.9 us
    dot_general x6, matrix products, columns_by_columns(): lax.dot_general(left, right, (((0,), (0,)), ((), ())), preferred_element_...  22 us
    all_gather x3, blocking collectives, gathered(): return lax.all_gather(values, 'wa', axis=axis, tiled=True)  17.8 us
  transfers between devices with their start and end apart: 13, of which 3 were waited for; matrix products, arithmetic and copies ran while one was open for 23% of the time, Pallas kernels for 58%

profile of v1, /device:TPU:0, one launch (start us, length us, event | category | flops | bytes accessed | tf_op | source)
XLA Modules:
  0.0 597.1 jit_solution(6156840119297749324)
XLA Ops:
  10.1 5.2 all-gather
  19.3 7.8 %all-gather.1 = bf16[2,1,768]{2,1,0:T(2,128)(2,1)S(1)} all-gather(bf16[1,1,768]{2,1,0:T(2,128)(2,1)S(1)} %reshape.287), channel_id=1, replica_groups=mesh['ctx'=16,'wa'=2] {'wa'}, dimensions={0}, use_global_device_ids=true | all-gather | bytes 4608 | tf_op jit(solution)/shard_map/all_gather | solution.py:808
  27.3 4.8 all_gather.29
  35.4 46.2 %gather_d_out.1 = bf16[16,128,1536]{2,1,0:T(8,128)(2,1)} custom-call(bf16[128,1536]{1,0:T(8,128)(2,1)} %bitcast.134), custom_call_target="tpu_custom_call" | custom-call | tf_op jit(solution)/shard_map/gather_d_out/pallas_call | solution.py:616
  84.7 21.5 %gather_kv.1 = bf16[16,128,512]{2,1,0:T(8,128)(2,1)} custom-call(bf16[128,512]{1,0:T(8,128)(2,1)} %pad_maximum_fusion.6.block_ref), custom_call_target="tpu_custom_call" | custom-call | tf_op jit(solution)/shard_map/gather_kv/pallas_call | solution.py:616
  106.2 6.6 %copy.90 = bf16[1536,1536]{1,0:T(8,128)(2,1)} copy(bf16[1536,1536]{0,1:T(8,128)(2,1)} %bitcast.118) | data formatting | bytes 9437184 | tf_op jit(solution)/shard_map/dot_general | solution.py:830
  112.8 4.5 fusion.51
  118.4 10.7 %attend.1 = (f32[128,1536]{1,0:T(8,128)}, f32[1536,1]{1,0:T(8,128)}) custom-call(bf16[128,1536]{1,0:T(8,128)(2,1)} %copy.93.query, bf16[2048,512]{1,0:T(8,128)(2,1)} %bitcast.120, s32[1,2048]{1,0:T(1,128)} %doc_row.3, s32[128,1]{1,0:T(8,128)} %copy.94.doc_column), custom_call_target="tpu_custom_call" | custom-call | tf_op jit(solution)/shard_map/attend/pallas_call | solution.py:616
  130.3 40.2 %all-gather.12.cloned.1.call-done = bf16[1536,1536]{1,0:T(8,128)(2,1)} async-done(((bf16[768,1536]{1,0:T(8,128)(2,1)}), bf16[1536,1536]{1,0:T(8,128)(2,1)}) %all-gather.12.cloned.1.call-update) | async-done | bytes 4718608 | tf_op jit(solution)/shard_map/all_gather | solution.py:808
  170.4 3.2 multiply_reduce_fusion.3
  175.8 48.8 %gather_hidden.1 = bf16[16,128,1664]{2,1,0:T(8,128)(2,1)} custom-call(bf16[128,1664]{1,0:T(8,128)(2,1)} %concatenate.69.block_ref), custom_call_target="tpu_custom_call" | custom-call | tf_op jit(solution)/shard_map/gather_hidden/pallas_call | solution.py:616
  226.7 9.6 %fusion.4 = f32[2048,768]{1,0:T(8,128)} fusion(bf16[1536,768]{0,1:T(8,128)(2,1)} %bitcast.144, bf16[2048,1664]{1,0:T(8,128)(2,1)} %bitcast.123), kind=kOutput, calls=%fused_computation.8 | convolution fusion | flops 4831838208 | bytes 14942208 | tf_op jit(solution)/shard_map/dot_general | solution.py:866
  236.3 10.9 %fusion.15 = (bf16[2048,384]{1,0:T(8,128)(2,1)}, bf16[2048,384]{1,0:T(8,128)(2,1)}, bf16[2048]{0:T(1024)(128)(2,1)S(1)}, bf16[2048,384]{1,0:T(8,128)(2,1)S(1)}) fusion(f32[2048,768]{1,0:T(8,128)} %fusion.4, f32[2048]{0:T(1024)S(1)} %select_reduce_fusion, bf16[2048,1536]{1,0:T(8,128)(2,1)} %bitcast.125, bf16[1,384,1536]{2,1,0:T(8,128)(2,1)} %all-gather.16.cloned.1.call-done), kind=kOutput, calls=%fused_computation.22 | convolution fusion | flops 2439510016 | bytes 18493440 | tf_op jit(solution)/shard_map/dot_general | solution.py:669
  248.3 6.4 %fusion.22 = bf16[1,384,1536]{2,1,0:T(8,128)(2,1)} fusion(bf16[2048,384]{1,0:T(8,128)(2,1)S(1)} %get-tuple-element.31, bf16[2048,1536]{1,0:T(8,128)(2,1)} %bitcast.126), kind=kOutput, calls=%fused_computation.35 | convolution fusion | flops 2416508928 | bytes 9043968 | tf_op jit(solution)/shard_map/dot_general | solution.py:675
  255.1 7.4 %convolution_convert_fusion.1 = bf16[16,128,1536]{2,1,0:T(8,128)(2,1)S(1)} fusion(bf16[1536,768,1]{0,1,2:T(8,128)(2,1)} %bitcast.145, bf16[16,128,384]{2,1,0:T(8,128)(2,1)} %bitcast.147, bf16[16,128,384]{2,1,0:T(8,128)(2,1)} %bitcast.146), kind=kOutput, calls=%fused_computation.10 | convolution fusion | flops 4841275392 | bytes 11796480 | tf_op jit(solution)/shard_map/dot_general | solution.py:669
  262.5 3.5 pad_maximum_fusion.part
  266.0 49.2 %scatter_grad_rows.1 = f32[128,1664]{1,0:T(8,128)} custom-call(bf16[16,128,1664]{2,1,0:T(8,128)(2,1)} %pad_maximum_fusion.part), custom_call_target="tpu_custom_call" | custom-call | tf_op jit(solution)/shard_map/scatter_grad_rows/pallas_call | solution.py:616
  318.5 7.9 %convolution_convert_fusion = bf16[2048,1536]{1,0:T(8,128)(2,1)} fusion(bf16[2048,384]{1,0:T(8,128)(2,1)} %copy-done.36, bf16[1,384,1536]{2,1,0:T(8,128)(2,1)} %all-gather.16.cloned.1.call-done), kind=kOutput, calls=%fused_computation.2 | convolution fusion | flops 2419064832 | bytes 9043968 | tf_op jit(solution)/shard_map/dot_general | solution.py:874
  326.4 46.2 %scatter_result.1 = f32[128,1536]{1,0:T(8,128)} custom-call(bf16[16,128,1536]{2,1,0:T(8,128)(2,1)} %bitcast.127), custom_call_target="tpu_custom_call" | custom-call | tf_op jit(solution)/shard_map/scatter_result/pallas_call | solution.py:616
  374.8 4.7 convolution_convert_fusion.5.grad_mixed
  379.5 16.8 %attend_back.1 = (f32[128,1536]{1,0:T(8,128)}, bf16[2048,512]{1,0:T(8,128)(2,1)}) custom-call(bf16[128,1536]{1,0:T(8,128)(2,1)} %copy.93.query, bf16[2048,512]{1,0:T(8,128)(2,1)} %bitcast.121, s32[1,2048]{1,0:T(1,128)} %doc_row.3, s32[128,1]{1,0:T(8,128)} %copy.94.doc_column, f32[1536,1]{1,0:T(8,128)} %get-tuple-element.15.level, ...), custom_call_target="tpu_custom_call" | custom-call | tf_op jit(solution)/shard_map/attend_back/pallas_call | solution.py:616
  396.3 24.4 %scatter_grad_kv.1 = f32[128,512]{1,0:T(8,128)} custom-call(bf16[16,128,512]{2,1,0:T(8,128)(2,1)} %bitcast.133), custom_call_target="tpu_custom_call" | custom-call | tf_op jit(solution)/shard_map/scatter_grad_kv/pallas_call | solution.py:616
  427.5 4.4 fusion.81
  436.7 9.3 %fusion.6 = bf16[1536,768]{0,1:T(8,128)(2,1)} fusion(bf16[2048,1664]{1,0:T(8,128)(2,1)} %bitcast.124, bf16[2048,384]{1,0:T(8,128)(2,1)} %get-tuple-element.29, bf16[2048,384]{1,0:T(8,128)(2,1)} %get-tuple-element.28), kind=kOutput, calls=%fused_computation.13 | convolution fusion | flops 4839309312 | bytes 11796480 | tf_op jit(solution)/shard_map/dot_general | solution.py:675
  447.3 19.0 %collective-permute-done.5 = f32[768,10]{1,0:T(8,128)} collective-permute-done((f32[768,10]{1,0:T(8,128)}, f32[768,10]{1,0:T(8,128)}, u32[]{:S(2)}, u32[]{:S(2)}) %collective-permute-start.5) | collective-permute-done | bytes 30752 | tf_op jit(solution)/shard_map/ppermute | solution.py:793
  467.9 5.9 collective-permute-done.2
  479.1 2.8 fusion.1
  481.9 82.3 %sum_shares.1 = bf16[16,48,3712]{2,1,0:T(8,128)(2,1)} custom-call(bf16[16,48,3712]{2,1,0:T(8,128)(2,1)} %bitcast.117), custom_call_target="tpu_custom_call" | custom-call | tf_op jit(solution)/shard_map/sum_shares/pallas_call | solution.py:616
  564.2 3.4 bitcast_convert_fusion
  567.6 4.2 copy-done
  576.2 8.4 %fusion.78 = (f32[768,1536]{1,0:T(8,128)}, f32[768,1536]{1,0:T(8,128)}) fusion(f32[768,3712]{1,0:T(8,128)} %copy-done), kind=kLoop, calls=%fused_computation.156 | loop fusion | bytes 18874368 | tf_op jit(solution)/shard_map/slice | solution.py:955
  586.8 3.0 convert_element_type.163
  (182 shorter events, 52.7 us)
Async XLA Ops:
  7.2 74.4 %all-gather.10.cloned.1.call-start = ((), (), s32[]{:S(2)}) async-start(), calls=%async_computation.3 | async-start | bytes 2359296 | tf_op jit(solution)/shard_map/all_gather | solution.py:808
  7.9 98.3 %all-gather.8.cloned.1.call-start = ((), (), s32[]{:S(2)}) async-start(), calls=%async_computation.2 | async-start | bytes 7077888 | tf_op jit(solution)/shard_map/all_gather | solution.py:808
  8.7 18.5 %copy-start.17 = (bf16[768,8]{0,1:T(8,128)(2,1)S(1)}, bf16[768,8]{0,1:T(8,128)(2,1)}, u32[]{:S(2)}) copy-start(bf16[768,8]{0,1:T(8,128)(2,1)} %param.20) | copy-start | bytes 36868
  8.7 161.7 %all-gather.12.cloned.1.call-start = ((), (), s32[]{:S(2)}) async-start(), calls=%async_computation.4 | async-start | bytes 7077888 | tf_op jit(solution)/shard_map/all_gather | solution.py:808
  9.4 217.3 %all-gather.14.cloned.1.call-start = ((), (), s32[]{:S(2)}) async-start(), calls=%async_computation.5 | async-start | bytes 3538944 | tf_op jit(solution)/shard_map/all_gather | solution.py:808
  10.0 226.3 %all-gather.16.cloned.1.call-start = ((), (), s32[]{:S(2)}) async-start(), calls=%async_computation.6 | async-start | bytes 1769472 | tf_op jit(solution)/shard_map/all_gather | solution.py:808
  16.1 96.8 %copy-start.19 = (f32[128]{0:T(128)}, f32[128]{0:T(128)S(1)}, u32[]{:S(2)}) copy-start(f32[128]{0:T(128)S(1)} %get-tuple-element.54) | copy-start | bytes 1540
  17.0 450.9 %collective-permute-start = (bf16[128,768]{1,0:T(8,128)(2,1)}, bf16[128,768]{1,0:T(8,128)(2,1)}, u32[]{:S(2)}, u32[]{:S(2)}) collective-permute-start(bf16[128,768]{1,0:T(8,128)(2,1)} %get-tuple-element.38), channel_id=1, source_target_pairs={{0,1},{1,0},{2,3},{3,2},{4,5},{5,4},{6,7},{7,6},{8,9},{9,8},{10,11... | collective-permute-start | bytes 589832 | tf_op jit(solution)/shard_map/ppermute | solution.py:793
  19.1 565.5 %reduce-scatter.5.cloned.1.call-start = ((), (), s32[]{:S(2)}) async-start(), calls=%async_computation.8 | async-start | bytes 1769472 | tf_op jit(solution)/shard_map/reduce_scatter | solution.py:891
  33.8 47.8 %copy-start.10 = (f32[128,64]{0,1:T(8,128)}, f32[128,64]{0,1:T(8,128)S(1)}, u32[]{:S(2)}) copy-start(f32[128,64]{0,1:T(8,128)S(1)} %get-tuple-element.49) | copy-start | bytes 98308
  33.8 47.8 %copy-start.12 = (f32[128,64]{0,1:T(8,128)}, f32[128,64]{0,1:T(8,128)S(1)}, u32[]{:S(2)}) copy-start(f32[128,64]{0,1:T(8,128)S(1)} %get-tuple-element.51) | copy-start | bytes 98308
  174.2 142.0 %copy-start.26 = (f32[128]{0:T(128)}, f32[128]{0:T(128)S(1)}, u32[]{:S(2)}) copy-start(f32[128]{0:T(128)S(1)} %get-tuple-element.56) | copy-start | bytes 1540
  174.6 141.6 %copy-start.8 = (f32[128,8]{1,0:T(8,128)}, f32[128,8]{1,0:T(8,128)S(1)}, u32[]{:S(2)}) copy-start(f32[128,8]{1,0:T(8,128)S(1)} %get-tuple-element.60) | copy-start | bytes 12292
  174.6 141.6 %copy-start.22 = (f32[128]{0:T(128)}, f32[128]{0:T(128)S(1)}, u32[]{:S(2)}) copy-start(f32[128]{0:T(128)S(1)} %get-tuple-element.59) | copy-start | bytes 1540
  174.8 141.4 %copy-start.24 = (f32[128]{0:T(128)}, f32[128]{0:T(128)S(1)}, u32[]{:S(2)}) copy-start(f32[128]{0:T(128)S(1)} %fusion.65) | copy-start | bytes 1540
  326.4 46.2 %copy-start.3 = (bf16[1,128,1536]{2,1,0:T(8,128)(2,1)S(1)}, bf16[1,128,1536]{2,1,0:T(8,128)(2,1)}, u32[]{:S(2)}) copy-start(bf16[1,128,1536]{2,1,0:T(8,128)(2,1)} %param.23) | copy-start | bytes 1179652
  326.4 46.3 %copy-start.27 = (f32[128]{0:T(128)S(1)}, f32[128]{0:T(128)}, u32[]{:S(2)}) copy-start(f32[128]{0:T(128)} %copy-done.26) | copy-start | bytes 1540
  326.4 46.3 %copy-start.34 = (f32[128]{0:T(128)S(1)}, f32[128]{0:T(128)}, u32[]{:S(2)}) copy-start(f32[128]{0:T(128)} %get-tuple-element.55) | copy-start | bytes 1540
  379.5 45.1 %copy-start.18 = (f32[1536]{0:T(1024)S(1)}, f32[1536]{0:T(1024)}, u32[]{:S(2)}) copy-start(f32[1536]{0:T(1024)} %get-tuple-element.20) | copy-start | bytes 18436
  396.3 29.7 %copy-start.11 = (f32[128,64]{0,1:T(8,128)S(1)}, f32[128,64]{0,1:T(8,128)}, u32[]{:S(2)}) copy-start(f32[128,64]{0,1:T(8,128)} %copy-done.10) | copy-start | bytes 98308
  396.3 29.8 %copy-start.13 = (f32[128,64]{0,1:T(8,128)S(1)}, f32[128,64]{0,1:T(8,128)}, u32[]{:S(2)}) copy-start(f32[128,64]{0,1:T(8,128)} %copy-done.12) | copy-start | bytes 98308
  396.3 30.0 %copy-start.14 = (f32[128,64]{1,0:T(8,128)S(1)}, f32[128,64]{1,0:T(8,128)}, u32[]{:S(2)}) copy-start(f32[128,64]{1,0:T(8,128)} %copy.102) | copy-start | bytes 98308
  396.3 30.0 %copy-start.15 = (f32[128,64]{1,0:T(8,128)S(1)}, f32[128,64]{1,0:T(8,128)}, u32[]{:S(2)}) copy-start(f32[128,64]{1,0:T(8,128)} %copy.103) | copy-start | bytes 98308
  422.3 54.9 %collective-permute-start.4 = (bf16[128,1536]{1,0:T(8,128)(2,1)S(1)}, bf16[128,1536]{1,0:T(8,128)(2,1)}, u32[]{:S(2)}, u32[]{:S(2)}) collective-permute-start(bf16[128,1536]{1,0:T(8,128)(2,1)S(1)} %get-tuple-element.24), channel_id=1, source_target_pairs={{0,1},{1,0},{2,3},{3,2},{4,5},{5,4},{6,7},{7,6},{8,9},{9,8},{10,11... | collective-permute-start | bytes 1179656 | tf_op jit(solution)/shard_map/ppermute | solution.py:793
  422.9 54.3 %collective-permute-start.3 = (bf16[128,768]{1,0:T(8,128)(2,1)}, bf16[128,768]{1,0:T(8,128)(2,1)}, u32[]{:S(2)}, u32[]{:S(2)}) collective-permute-start(bf16[128,768]{1,0:T(8,128)(2,1)} %get-tuple-element.40), channel_id=1, source_target_pairs={{0,1},{1,0},{2,3},{3,2},{4,5},{5,4},{6,7},{7,6},{8,9},{9,8},{10,11... | collective-permute-start | bytes 589832 | tf_op jit(solution)/shard_map/ppermute | solution.py:793
  424.3 162.5 %reduce-scatter.3.cloned.1.call-start = ((), (), s32[]{:S(2)}) async-start(), calls=%async_computation.7 | async-start | bytes 3538944 | tf_op jit(solution)/shard_map/reduce_scatter | solution.py:888
  426.8 20.3 %copy-start.7 = (bf16[16,8,2,128]{3,1,2,0:T(8,128)(2,1)}, bf16[16,8,2,128]{3,1,2,0:T(8,128)(2,1)S(1)}, u32[]{:S(2)}) copy-start(bf16[16,8,2,128]{3,1,2,0:T(8,128)(2,1)S(1)} %copy.118) | copy-start | bytes 196612
  426.9 48.3 %collective-permute-start.1 = (bf16[128,1536]{0,1:T(8,128)(2,1)S(1)}, bf16[128,1536]{0,1:T(8,128)(2,1)}, u32[]{:S(2)}, u32[]{:S(2)}) collective-permute-start(bf16[128,1536]{0,1:T(8,128)(2,1)S(1)} %bitcast.128), channel_id=1, source_target_pairs={{0,1},{1,0},{2,3},{3,2},{4,5},{5,4},{6,7},{7,6},{8,9},{9,8},{10,11... | collective-permute-start | bytes 1179656 | tf_op jit(solution)/shard_map/ppermute | solution.py:793
  435.5 30.8 %collective-permute-start.5 = (f32[768,10]{1,0:T(8,128)}, f32[768,10]{1,0:T(8,128)}, u32[]{:S(2)}, u32[]{:S(2)}) collective-permute-start(f32[768,10]{1,0:T(8,128)} %copy.112), channel_id=1, source_target_pairs={{0,1},{1,0},{2,3},{3,2},{4,5},{5,4},{6,7},{7,6},{8,9},{9,8},{10,11... | collective-permute-start | bytes 92168 | tf_op jit(solution)/shard_map/ppermute | solution.py:793
  446.0 27.8 %copy-start.4 = (bf16[128,768]{1,0:T(8,128)(2,1)S(1)}, bf16[128,768]{1,0:T(8,128)(2,1)}, u32[]{:S(2)}) copy-start(bf16[128,768]{1,0:T(8,128)(2,1)} %get-tuple-element.37) | copy-start | bytes 589828
  446.0 27.8 %copy-start.6 = (bf16[128,256]{1,0:T(8,128)(2,1)S(1)}, bf16[128,256]{1,0:T(8,128)(2,1)}, u32[]{:S(2)}) copy-start(bf16[128,256]{1,0:T(8,128)(2,1)} %slice.170) | copy-start | bytes 196612
  466.3 7.5 %collective-permute-start.2 = (bf16[128,512]{1,0:T(8,128)(2,1)S(1)}, bf16[128,512]{1,0:T(8,128)(2,1)S(1)}, u32[]{:S(2)}, u32[]{:S(2)}) collective-permute-start(bf16[128,512]{1,0:T(8,128)(2,1)S(1)} %pad_maximum_fusion.7), channel_id=1, source_target_pairs={{0,1},{1,0},{2,3},{3,2},{4,5},{5,4},{6,7},{7,6},{8,9},{9,8},{10,11... | collective-permute-start | bytes 393224 | tf_op jit(solution)/shard_map/ppermute | solution.py:793
  (19 other events, 107.7 us)
Sparse Core Ops, SparseCore 0:
  9.6 30.8 all-gather.9
  42.0 64.1 all-gather.7
  107.7 62.6 all-gather.11
  171.8 36.0 all-gather.13
  209.3 22.7 all-gather.15
  424.5 33.3 reduce-scatter.4
  460.7 36.0 reduce-scatter.2

commit v2 on v0

--- a/solution.py
+++ b/solution.py
@@ -1,8 +1,11 @@
+import functools
 import math
 
 import jax
 import jax.numpy as jnp
 from jax import lax
+from jax.experimental import pallas as pl
+from jax.experimental.pallas import tpu as pltpu
 from jax.sharding import PartitionSpec as P
 
 D = 1536
@@ -61,7 +64,7 @@
     return running
 
 
-def body(
+def routed_body(
     layer_input,
     seq_ids,
     routes,
@@ -381,6 +384,865 @@
         shares[7],
     )
 
+MESH = pl.DeviceIdType.MESH
+VMEM_LIMIT = 60 * 1024 * 1024
+
+
+def chip_place():
+    count = lax.axis_size("ctx")
+    me = lax.axis_index("ctx")
+    return me // 4, lax.rem(me // 2, 2), lax.rem(me, 2), count // 4
+
+
+def ctx_of(z, y, c):
+    return (z * 2 + y) * 2 + c
+
+
+def greet(across_x=False):
+    z, y, c, depth = chip_place()
+    barrier = pltpu.get_barrier_semaphore()
+
+    def signal(device):
+        pl.semaphore_signal(barrier, 1, device_id=device, device_id_type=MESH)
+
+    signal({"ctx": ctx_of(z, y, 1 - c)})
+    signal({"ctx": ctx_of(z, 1 - y, c)})
+    if across_x:
+        signal({"wa": 1 - lax.axis_index("wa")})
+    pl.when(z > 0)(lambda: signal({"ctx": ctx_of(z - 1, y, c)}))
+    pl.when(z < depth - 1)(lambda: signal({"ctx": ctx_of(z + 1, y, c)}))
+    ends = (z > 0).astype(jnp.int32) + (z < depth - 1).astype(jnp.int32)
+    pl.semaphore_wait(barrier, (3 if across_x else 2) + ends)
+
+
+def remote(source, target_ref, sems, at, device):
+    return pltpu.make_async_remote_copy(
+        src_ref=source,
+        dst_ref=target_ref,
+        send_sem=sems.at[(0,) + at],
+        recv_sem=sems.at[(1,) + at],
+        device_id=device,
+        device_id_type=MESH,
+    )
+
+
+def each(step, act):
+    z, _, _, depth = chip_place()
+    if step == 0:
+        act(z)
+    else:
+        pl.when(z + step < depth)(lambda: act(z + step))
+        pl.when(z - step >= 0)(lambda: act(z - step))
+
+
+class Gather:
+    def __init__(self, out, rows, sems):
+        self.out, self.rows = out, rows
+        self.z_sems, self.y_sems, self.c_sems = sems
+        self.z, self.y, self.c, self.depth = chip_place()
+
+    @staticmethod
+    def sems(depth):
+        return [
+            pltpu.SemaphoreType.DMA((2, 2, depth)),
+            pltpu.SemaphoreType.DMA((2, depth)),
+            pltpu.SemaphoreType.DMA((2, 2 * depth)),
+        ]
+
+    def slot(self, z, y, c):
+        return self.out.at[pl.ds(pl.multiple_of(ctx_of(z, y, c) * self.rows, 16), self.rows)]
+
+    def own(self):
+        return self.slot(self.z, self.y, self.c)
+
+    def on_z(self, way, of_z, source=None):
+        goal = jnp.minimum(self.z + 1, self.depth - 1) if way == 0 else jnp.maximum(self.z - 1, 0)
+        block = self.slot(of_z, self.y, self.c)
+        target = {"ctx": ctx_of(goal, self.y, self.c)}
+        return remote(block if source is None else source, block, self.z_sems, (way, of_z), target)
+
+    def on_y(self, of_z, mine=True, source=None):
+        block = self.slot(of_z, self.y if mine else 1 - self.y, self.c)
+        target = {"ctx": ctx_of(self.z, 1 - self.y, self.c)}
+        return remote(block if source is None else source, block, self.y_sems, (of_z,), target)
+
+    def on_core(self, of_z, of_y, mine=True, source=None):
+        block = self.slot(of_z, of_y, self.c if mine else 1 - self.c)
+        target = {"ctx": ctx_of(self.z, self.y, 1 - self.c)}
+        at = (of_z * 2 + of_y,)
+        return remote(block if source is None else source, block, self.c_sems, at, target)
+
+    def start(self, source=None):
+        z, depth = self.z, self.depth
+        pl.when(z < depth - 1)(lambda: self.on_z(0, z, source).start())
+        pl.when(z > 0)(lambda: self.on_z(1, z, source).start())
+        self.on_y(z, source=source).start()
+        self.on_core(z, self.y, source=source).start()
+
+    def along_z(self, step):
+        z, depth = self.z, self.depth
+
+        def from_side(way, of_z, more):
+            self.on_z(way, of_z).wait_recv()
+            pl.when(more)(lambda: self.on_z(way, of_z).start())
+            self.on_y(of_z).start()
+            self.on_core(of_z, self.y).start()
+
+        pl.when(z - step >= 0)(lambda: from_side(0, z - step, z < depth - 1))
+        pl.when(z + step < depth)(lambda: from_side(1, z + step, z > 0))
+
+    def along_y(self, step):
+        def across(of_z):
+            self.on_y(of_z, mine=False).wait_recv()
+            self.on_core(of_z, 1 - self.y).start()
+
+        each(step, across)
+
+    def finish(self):
+        z, depth = self.z, self.depth
+        for of_z in range(depth):
+            pl.when((z < depth - 1) & (of_z <= z))(lambda: self.on_z(0, of_z).wait_send())
+            pl.when((z > 0) & (of_z >= z))(lambda: self.on_z(1, of_z).wait_send())
+            self.on_y(of_z).wait_send()
+            for of_y in range(2):
+                self.on_core(of_z, of_y).wait_send()
+                self.on_core(of_z, of_y, mine=False).wait_recv()
+
+    def run(self, source=None):
+        self.start(source)
+        self.along_z(1)
+        self.along_y(0)
+        for step in range(1, self.depth):
+            if step + 1 < self.depth:
+                self.along_z(step + 1)
+            self.along_y(step)
+        self.finish()
+
+
+def add_into(target, terms, rows):
+    @pl.loop(0, rows // 16)
+    def _(turn):
+        at = pl.ds(pl.multiple_of(turn * 16, 16), 16)
+        total = terms[0][at, :].astype(jnp.float32)
+        for term in terms[1:]:
+            total = total + term[at, :].astype(jnp.float32)
+        target[at, :] = total.astype(target.dtype)
+
+
+class Scatter:
+    def __init__(self, part, scratch):
+        self.part = part
+        self.from_core, self.sums, self.from_y, self.from_z = scratch[:4]
+        self.c_sems, self.y_sems, self.z_sems = scratch[4:]
+        self.rows = self.sums.shape[1]
+        self.z, self.y, self.c, self.depth = chip_place()
+
+    @staticmethod
+    def scratch(depth, rows, columns):
+        return [
+            pltpu.VMEM((2 * depth, rows, columns), jnp.bfloat16),
+            pltpu.VMEM((2 * depth, rows, columns), jnp.bfloat16),
+            pltpu.VMEM((depth, rows, columns), jnp.bfloat16),
+            pltpu.VMEM((2, depth, rows, columns), jnp.bfloat16),
+            pltpu.SemaphoreType.DMA((2, 2 * depth)),
+            pltpu.SemaphoreType.DMA((2, depth)),
+            pltpu.SemaphoreType.DMA((2, 2, depth)),
+        ]
+
+    def share(self, chip, c):
+        return self.part.at[pl.ds(pl.multiple_of((chip * 2 + c) * self.rows, 16), self.rows)]
+
+    def on_core(self, chip):
+        target = {"ctx": ctx_of(self.z, self.y, 1 - self.c)}
+        return remote(
+            self.share(chip, 1 - self.c), self.from_core.at[chip], self.c_sems, (chip,), target
+        )
+
+    def on_y(self, of_z):
+        target = {"ctx": ctx_of(self.z, 1 - self.y, self.c)}
+        source = self.sums.at[of_z * 2 + 1 - self.y]
+        return remote(source, self.from_y.at[of_z], self.y_sems, (of_z,), target)
+
+    def on_z(self, way, of_z):
+        goal = jnp.minimum(self.z + 1, self.depth - 1) if way == 0 else jnp.maximum(self.z - 1, 0)
+        source = self.sums.at[of_z * 2 + self.y]
+        target = {"ctx": ctx_of(goal, self.y, self.c)}
+        return remote(source, self.from_z.at[way, of_z], self.z_sems, (way, of_z), target)
+
+    def start(self):
+        def send(of_z):
+            self.on_core(of_z * 2 + 1 - self.y).start()
+            self.on_core(of_z * 2 + self.y).start()
+
+        for step in range(self.depth - 1, -1, -1):
+            each(step, send)
+
+    def add_cores(self, step):
+        def add(of_z):
+            for other in (True, False):
+                chip = of_z * 2 + (1 - self.y if other else self.y)
+                self.on_core(chip).wait_recv()
+                terms = (self.share(chip, self.c), self.from_core.at[chip])
+                add_into(self.sums.at[chip], terms, self.rows)
+                if other:
+                    self.on_y(of_z).start()
+
+        each(step, add)
+
+    def add_y(self, step):
+        z, depth = self.z, self.depth
+
+        def add(of_z):
+            self.on_y(of_z).wait_recv()
+            own = self.sums.at[of_z * 2 + self.y]
+
+            def passing(way):
+                self.on_z(way, of_z).wait_recv()
+                terms = (own, self.from_y.at[of_z], self.from_z.at[way, of_z])
+                add_into(own, terms, self.rows)
+
+            upward, downward = (of_z > z) & (z > 0), (of_z < z) & (z < depth - 1)
+            pl.when(upward)(lambda: passing(0))
+            pl.when(downward)(lambda: passing(1))
+
+            @pl.when(jnp.logical_not(upward | downward))
+            def _():
+                add_into(own, (own, self.from_y.at[of_z]), self.rows)
+
+            pl.when(of_z > z)(lambda: self.on_z(0, of_z).start())
+            pl.when(of_z < z)(lambda: self.on_z(1, of_z).start())
+
+        each(step, add)
+
+    def last(self, result):
+        z, depth = self.z, self.depth
+        own = self.sums.at[z * 2 + self.y]
+        low, high = self.from_z.at[0, z], self.from_z.at[1, z]
+        pl.when(z > 0)(lambda: self.on_z(0, z).wait_recv())
+        pl.when(z < depth - 1)(lambda: self.on_z(1, z).wait_recv())
+        inside = (z > 0) & (z < depth - 1)
+        pl.when(inside)(lambda: add_into(result, (own, low, high), self.rows))
+        pl.when(z == 0)(lambda: add_into(result, (own, high), self.rows))
+        pl.when(z == depth - 1)(lambda: add_into(result, (own, low), self.rows))
+
+    def finish(self):
+        for of_z in range(self.depth):
+            self.on_y(of_z).wait_send()
+            self.on_core(of_z * 2).wait_send()
+            self.on_core(of_z * 2 + 1).wait_send()
+            pl.when(of_z > self.z)(lambda: self.on_z(0, of_z).wait_send())
+            pl.when(of_z < self.z)(lambda: self.on_z(1, of_z).wait_send())
+
+    def run(self, result):
+        steps = range(self.depth - 1, -1, -1)
+        self.start()
+        for step in steps:
+            self.add_cores(step)
+        for step in steps:
+            self.add_y(step)
+        self.last(result)
+        self.finish()
+
+
+def call(kernel, out, scratch, number, name, *operands, outside=(), outside_out=()):
+    def spec(position, far):
+        return pl.BlockSpec(memory_space=pl.ANY if position in far else pltpu.VMEM)
+
+    many = isinstance(out, (tuple, list))
+    out_specs = [spec(i, outside_out) for i in range(len(out) if many else 1)]
+    return pl.pallas_call(
+        kernel,
+        out_shape=out,
+        in_specs=[spec(i, outside) for i in range(len(operands))],
+        out_specs=out_specs if many else out_specs[0],
+        scratch_shapes=scratch,
+        compiler_params=pltpu.CompilerParams(
+            collective_id=number,
+            has_side_effects=number is not None,
+            vmem_limit_bytes=VMEM_LIMIT,
+        ),
+        name=name,
+    )(*operands)
+
+
+def gather_ctx(block, number, name):
+    count, rows = lax.axis_size("ctx"), block.shape[0]
+
+    def kernel(block_ref, out, *sems):
+        gather = Gather(out, rows, sems)
+        gather.own()[...] = block_ref[...]
+        greet()
+        gather.run()
+
+    out = jax.ShapeDtypeStruct((count * rows, block.shape[1]), block.dtype)
+    return call(kernel, out, Gather.sems(count // 4), number, name, block)
+
+
+def scatter_ctx(parts, number, name):
+    count = lax.axis_size("ctx")
+    rows, columns = parts.shape[0] // count, parts.shape[1]
+
+    def kernel(part, result, *scratch):
+        greet()
+        Scatter(part, scratch).run(result)
+
+    out = jax.ShapeDtypeStruct((rows, columns), jnp.float32)
+    scratch = Scatter.scratch(count // 4, rows, columns)
+    return call(kernel, out, scratch, number, name, parts)
+
+
+class Relay:
+    def __init__(self, source, out, sems, parts=1, over_y=False):
+        self.source, self.out, self.sems = source, out, sems
+        self.z, self.y, self.c, _ = chip_place()
+        self.parts, self.over_y = parts, over_y
+        self.rows = source.shape[0] // (4 if over_y else 2 * parts)
+
+    @staticmethod
+    def semaphores():
+        return pltpu.SemaphoreType.DMA((2, 6))
+
+    def block(self, ref, part, y, c):
+        place = y * 2 + c if self.over_y else c * self.parts + part
+        return ref.at[pl.ds(pl.multiple_of(place * self.rows, 16), self.rows)]
+
+    def on_x(self, part):
+        source = self.block(self.source, part, self.y, self.c)
+        target = self.block(self.out, part, self.y, self.c)
+        return remote(source, target, self.sems, (part,), {"wa": 1 - lax.axis_index("wa")})
+
+    def on_core(self, part, y, c):
+        block = self.block(self.out, part, y, c)
+        at = (2 + (jnp.where(y == self.y, 0, 1) if self.over_y else part),)
+        return remote(block, block, self.sems, at, {"ctx": ctx_of(self.z, self.y, 1 - self.c)})
+
+    def on_y(self, y):
+        block = self.block(self.out, 0, y, self.c)
+        return remote(block, block, self.sems, (4,), {"ctx": ctx_of(self.z, 1 - self.y, self.c)})
+
+    def start(self):
+        for part in range(self.parts):
+            self.on_x(part).start()
+
+    def pass_on(self, part=0):
+        self.on_x(part).wait_recv()
+        if self.over_y:
+            self.on_y(self.y).start()
+        self.on_core(part, self.y, self.c).start()
+
+    def pass_on_y(self):
+        self.on_y(1 - self.y).wait_recv()
+        self.on_core(0, 1 - self.y, self.c).start()
+
+    def finish(self):
+        for part in range(self.parts):
+            self.on_x(part).wait_send()
+            self.on_core(part, self.y, self.c).wait_send()
+            self.on_core(part, self.y, 1 - self.c).wait_recv()
+        if self.over_y:
+            self.on_y(self.y).wait_send()
+            self.on_core(0, 1 - self.y, self.c).wait_send()
+            self.on_core(0, 1 - self.y, 1 - self.c).wait_recv()
+
+
+def front(d_out, w_query, w_keyval, w_out_attn, small):
+    count, rows = lax.axis_size("ctx"), d_out.shape[0]
+    depth = count // 4
+
+    def kernel(
+        d_out_ref, query_ref, keyval_ref, attn_ref, small_ref,
+        d_out_all, query_there, keyval_there, attn_there, small_there, *sems,
+    ):
+        gather = Gather(d_out_all, rows, sems[:3])
+        query_sems, keyval_sems, attn_sems, small_sems, own_sem = sems[3:]
+        query = Relay(query_ref, query_there, query_sems, parts=2)
+        keyval = Relay(keyval_ref, keyval_there, keyval_sems)
+        attn = Relay(attn_ref, attn_there, attn_sems, over_y=True)
+        partner = {"wa": 1 - lax.axis_index("wa")}
+        swap = remote(small_ref, small_there, small_sems, (0,), partner)
+        keep = pltpu.make_async_copy(d_out_ref, gather.own(), own_sem.at[0])
+        keep.start()
+        greet(across_x=True)
+        swap.start()
+        attn.start()
+        query.start()
+        keyval.start()
+        gather.start(d_out_ref)
+        gather.along_z(1)
+        gather.along_y(0)
+        gather.along_z(2)
+        attn.pass_on()
+        gather.along_y(1)
+        gather.along_z(3)
+        query.pass_on(0)
+        gather.along_y(2)
+        attn.pass_on_y()
+        gather.along_y(3)
+        query.pass_on(1)
+        keyval.pass_on()
+        gather.finish()
+        query.finish()
+        keyval.finish()
+        attn.finish()
+        swap.wait()
+        keep.wait()
+
+    def like(values):
+        return jax.ShapeDtypeStruct(values.shape, values.dtype)
+
+    out = [
+        jax.ShapeDtypeStruct((count * rows, d_out.shape[1]), d_out.dtype),
+        like(w_query), like(w_keyval), like(w_out_attn), like(small),
+    ]
+    scratch = Gather.sems(depth) + [Relay.semaphores()] * 3
+    scratch += [pltpu.SemaphoreType.DMA((2, 1)), pltpu.SemaphoreType.DMA((1,))]
+    every = range(5)
+    return call(
+        kernel, out, scratch, 0, "front",
+        d_out, w_query, w_keyval, w_out_attn, small, outside=every, outside_out=every,
+    )
+
+
+def finish(hidden, hidden_there, mixed, mixed_there, middle, middle_there, query, keyval, small, small_other, expert_in, expert_out):
+    count = lax.axis_size("ctx")
+    depth, tokens, half = count // 4, hidden.shape[0], hidden.shape[1]
+    rows = half // count
+    widths = (middle.shape[1], query.shape[1], keyval.shape[1])
+
+    def kernel(*refs):
+        (hidden_ref, hidden_there_ref, mixed_ref, mixed_there_ref, middle_ref, middle_there_ref,
+         query_ref, keyval_ref, small_ref, small_other_ref, in_ref, out_ref) = refs[:12]
+        attn_sum, query_sum, keyval_sum, small_sum, in_there, out_there = refs[12:18]
+        (attn_part, query_part, keyval_part, pair, query_there, keyval_there, small_there,
+         small_all, x_sems) = refs[18:27]
+        scratch = refs[27:]
+        scatters, gathers = [], []
+        parts, sums = (attn_part, query_part, keyval_part), (attn_sum, query_sum, keyval_sum)
+        for part, total in zip(parts, sums):
+            scatters.append(Scatter(part, scratch[:7]))
+            gathers.append(Gather(total, rows, scratch[7:10]))
+            scratch = scratch[10:]
+        small_gather = Gather(small_all, small.shape[0], scratch)
+        (attn, query_, keyval_), (attn_out, query_out, keyval_out) = scatters, gathers
+        partner = {"wa": 1 - lax.axis_index("wa")}
+        swaps = [
+            remote(source, target, x_sems, (i,), partner)
+            for i, (source, target) in enumerate(
+                [(small_other_ref, small_there), (query_ref, query_there), (keyval_ref, keyval_there),
+                 (in_ref, in_there), (out_ref, out_there)]
+            )
+        ]
+        greet(across_x=True)
+        for swap in swaps:
+            swap.start()
+
+        def products(left, left_there, right, right_there, part):
+            pair[:tokens] = left[...]
+            pair[tokens:] = left_there[...]
+            width = part.shape[1]
+
+            @pl.loop(0, width // 512)
+            def _(turn):
+                at = pl.ds(pl.multiple_of(turn * 512, 512), 512)
+                both = jnp.concatenate([right[:, at], right_there[:, at]], axis=0)
+                part[:, at] = columns_by_columns(pair[...], both).astype(jnp.bfloat16)
+
+        steps = range(depth - 1, -1, -1)
+        products(mixed_ref, mixed_there_ref, middle_ref, middle_there_ref, attn_part)
+        attn.start()
+        for step in steps:
+            attn.add_cores(step)
+        swaps[0].wait()
+        small_gather.own()[...] = (small_ref[...] + small_there[...]).astype(jnp.bfloat16)
+        swaps[1].wait()
+        products(hidden_ref, hidden_there_ref, query_ref, query_there, query_part)
+        query_.start()
+        for step in steps:
+            query_.add_cores(step)
+        swaps[2].wait()
+        products(hidden_ref, hidden_there_ref, keyval_ref, keyval_there, keyval_part)
+        keyval_.start()
+        for step in steps:
+            keyval_.add_cores(step)
+        for step in steps:
+            attn.add_y(step)
+        attn.last(attn_out.own())
+        attn_out.start()
+        small_gather.start()
+        for step in steps:
+            query_.add_y(step)
+        attn_out.along_z(1)
+        query_.last(query_out.own())
+        query_out.start()
+        attn_out.along_z(2)
+        attn_out.along_y(0)
+        small_gather.along_z(1)
+        for step in steps:
+            keyval_.add_y(step)
+        attn_out.along_z(3)
+        attn_out.along_y(1)
+        keyval_.last(keyval_out.own())
+        keyval_out.start()
+        query_out.along_z(1)
+        small_gather.along_z(2)
+        attn_out.along_y(2)
+        query_out.along_z(2)
+        small_gather.along_z(3)
+        query_out.along_y(0)
+        keyval_out.along_z(1)
+        query_out.along_z(3)
+        attn_out.along_y(3)
+        keyval_out.along_z(2)
+        query_out.along_y(1)
+        keyval_out.along_z(3)
+        query_out.along_y(2)
+        small_gather.along_y(0)
+        keyval_out.along_y(0)
+        small_gather.along_y(1)
+        query_out.along_y(3)
+        keyval_out.along_y(1)
+        small_gather.along_y(2)
+        keyval_out.along_y(2)
+        small_gather.along_y(3)
+        keyval_out.along_y(3)
+        for one in [small_gather] + gathers + scatters:
+            one.finish()
+        small_rows = small.shape[0]
+        total = small_all[:small_rows].astype(jnp.float32)
+        for device in range(1, count):
+            rows_of = slice(device * small_rows, (device + 1) * small_rows)
+            total = total + small_all[rows_of].astype(jnp.float32)
+        small_sum[...] = total
+        swaps[3].wait()
+        swaps[4].wait()
+
+    out = [jax.ShapeDtypeStruct((half, width), jnp.bfloat16) for width in widths]
+    out += [
+        jax.ShapeDtypeStruct(small.shape, jnp.float32),
+        jax.ShapeDtypeStruct(expert_in.shape, expert_in.dtype),
+        jax.ShapeDtypeStruct(expert_out.shape, expert_out.dtype),
+    ]
+    scratch = [pltpu.VMEM((half, width), jnp.bfloat16) for width in widths]
+    scratch += [
+        pltpu.VMEM((2 * tokens, half), jnp.bfloat16),
+        pltpu.VMEM(query.shape, jnp.bfloat16),
+        pltpu.VMEM(keyval.shape, jnp.bfloat16),
+        pltpu.VMEM(small.shape, jnp.float32),
+        pltpu.VMEM((count * small.shape[0], small.shape[1]), jnp.bfloat16),
+        pltpu.SemaphoreType.DMA((2, 5)),
+    ]
+    for width in widths:
+        scratch += Scatter.scratch(depth, rows, width) + Gather.sems(depth)
+    scratch += Gather.sems(depth)
+    return call(
+        kernel, out, scratch, 1, "finish",
+        hidden, hidden_there, mixed, mixed_there, middle, middle_there, query, keyval, small,
+        small_other, expert_in, expert_out, outside=(10, 11), outside_out=(4, 5),
+    )
+
+
+def rows_by_rows(left, right):
+    return lax.dot_general(
+        left, right, (((1,), (1,)), ((), ())), preferred_element_type=jnp.float32
+    )
+
+
+def columns_by_columns(left, right):
+    return lax.dot_general(
+        left, right, (((0,), (0,)), ((), ())), preferred_element_type=jnp.float32
+    )
+
+
+def allowed_bias(doc_row, doc_column, tokens):
+    keys = doc_row.shape[1]
+    query_block = lax.axis_index("ctx") * tokens // BLOCK
+    key_block = lax.broadcasted_iota(jnp.int32, (tokens, keys), 1) // BLOCK
+    allowed = (doc_row == doc_column) & (key_block <= query_block)
+    return jnp.where(allowed, 0.0, NEGATIVE)
+
+
+def attend_kernel(query, keyval, doc_row, doc_column, mixed, level, stacked, bias):
+    tokens = query.shape[0]
+    bias[...] = allowed_bias(doc_row[...], doc_column[...], tokens)
+    for head in range(HEADS):
+        stacked[head * tokens : (head + 1) * tokens, :] = query[:, head * 128 : (head + 1) * 128]
+
+    @pl.loop(0, HEADS // 2)
+    def _(pair):
+        rows = pl.ds(pl.multiple_of(pair * 2 * tokens, 128), 2 * tokens)
+        kind = pair // (HEADS // KV_HEADS // 2)
+        keys = keyval[:, pl.ds(pl.multiple_of(kind * 128, 128), 128)]
+        vals = keyval[:, pl.ds(pl.multiple_of(kind * 128 + 256, 128), 128)]
+        scores = rows_by_rows(stacked[rows, :], keys) * HEAD_DIM**-0.5
+        scores = (scores.reshape(2, tokens, -1) + bias[...][None]).reshape(scores.shape)
+        top = jnp.max(scores, axis=-1, keepdims=True)
+        weights = jnp.exp(scores - top)
+        total = jnp.sum(weights, axis=-1, keepdims=True)
+        probs = (weights / total).astype(jnp.bfloat16)
+        mixture = jnp.dot(probs, vals, preferred_element_type=jnp.float32)
+        for half in range(2):
+            columns = pl.ds(pl.multiple_of((pair * 2 + half) * 128, 128), 128)
+            mixed[:, columns] = mixture[half * tokens : (half + 1) * tokens]
+        level[rows, :] = top + jnp.log(total)
+
+
+def attend(query, keyval, doc_row, doc_column):
+    tokens, keys = query.shape[0], keyval.shape[0]
+    out = (
+        jax.ShapeDtypeStruct(query.shape, jnp.float32),
+        jax.ShapeDtypeStruct((HEADS * tokens, 1), jnp.float32),
+    )
+    scratch = [
+        pltpu.VMEM((HEADS * tokens, HEAD_DIM), jnp.bfloat16),
+        pltpu.VMEM((tokens, keys), jnp.float32),
+    ]
+    return call(
+        attend_kernel, out, scratch, None, "attend", query, keyval, doc_row, doc_column
+    )
+
+
+def attend_back_kernel(
+    query, keyval, doc_row, doc_column, level, mixed, grad_mixed,
+    grad_query, grad_keyval, stacked, grads, bias, delta, total,
+):
+    tokens = query.shape[0]
+    bias[...] = allowed_bias(doc_row[...], doc_column[...], tokens)
+    total[...] = jnp.zeros_like(total)
+    for head in range(HEADS):
+        rows, columns = slice(head * tokens, (head + 1) * tokens), slice(head * 128, head * 128 + 128)
+        stacked[rows, :] = query[:, columns]
+        grads[rows, :] = grad_mixed[:, columns]
+        delta[rows, :] = jnp.sum(
+            grad_mixed[:, columns].astype(jnp.float32) * mixed[:, columns], axis=-1, keepdims=True
+        )
+
+    @pl.loop(0, HEADS // 2)
+    def _(pair):
+        rows = pl.ds(pl.multiple_of(pair * 2 * tokens, 128), 2 * tokens)
+        kind = pair // (HEADS // KV_HEADS // 2)
+        key_columns = pl.ds(pl.multiple_of(kind * 128, 128), 128)
+        val_columns = pl.ds(pl.multiple_of(kind * 128 + 256, 128), 128)
+        keys, vals = keyval[:, key_columns], keyval[:, val_columns]
+        own, grad = stacked[rows, :], grads[rows, :]
+        scores = rows_by_rows(own, keys) * HEAD_DIM**-0.5
+        scores = (scores.reshape(2, tokens, -1) + bias[...][None]).reshape(scores.shape)
+        probs = jnp.exp(scores - level[rows, :])
+        grad_probs = rows_by_rows(grad, vals)
+        grad_scores = (probs * (grad_probs - delta[rows, :])).astype(jnp.bfloat16)
+        own_grad = jnp.dot(grad_scores, keys, preferred_element_type=jnp.float32)
+        for half in range(2):
+            columns = pl.ds(pl.multiple_of((pair * 2 + half) * 128, 128), 128)
+            grad_query[:, columns] = own_grad[half * tokens : (half + 1) * tokens] * HEAD_DIM**-0.5
+        total[:, key_columns] += columns_by_columns(grad_scores, own) * HEAD_DIM**-0.5
+        total[:, val_columns] += columns_by_columns(probs.astype(jnp.bfloat16), grad)
+
+    grad_keyval[...] = total[...].astype(jnp.bfloat16)
+
+
+def attend_back(query, keyval, doc_row, doc_column, level, mixed, grad_mixed):
+    tokens, keys = query.shape[0], keyval.shape[0]
+    out = (
+        jax.ShapeDtypeStruct(query.shape, jnp.float32),
+        jax.ShapeDtypeStruct(keyval.shape, jnp.bfloat16),
+    )
+    scratch = [
+        pltpu.VMEM((HEADS * tokens, HEAD_DIM), jnp.bfloat16),
+        pltpu.VMEM((HEADS * tokens, HEAD_DIM), jnp.bfloat16),
+        pltpu.VMEM((tokens, keys), jnp.float32),
+        pltpu.VMEM((HEADS * tokens, 1), jnp.float32),
+        pltpu.VMEM(keyval.shape, jnp.float32),
+    ]
+    return call(
+        attend_back_kernel, out, scratch, None, "attend_back",
+        query, keyval, doc_row, doc_column, level, mixed, grad_mixed,
+    )
+
+
+def rms_back(values, gain_vec, grad):
+    scale = lax.rsqrt(jnp.mean(values * values, axis=-1, keepdims=True) + EPSILON)
+    through = jnp.mean(gain_vec * grad * values, axis=-1, keepdims=True)
+    back = scale * gain_vec * grad - values * scale**3 * through
+    return back, jnp.sum(grad * values * scale, axis=0)
+
+
+def swap_wa(values):
+    return jax.tree.map(lambda v: lax.ppermute(v, "wa", ((0, 1), (1, 0))), values)
+
+
+def gathered_body(
+    layer_input, seq_ids, routes, gain_attn, w_query, w_keyval, w_out_attn, gain_ffn, router,
+    w_in, w_out, d_out,
+):
+    me, side = lax.axis_index("ctx"), lax.axis_index("wa")
+    tokens = layer_input.shape[1]
+    experts = router.shape[1]
+    kv_width = KV_HEADS * HEAD_DIM
+    half = D // 2
+    quarter = w_in.shape[3]
+
+    def halves(values):
+        own = lax.dynamic_slice_in_dim(values, side * half, half, values.ndim - 1)
+        return own, lax.dynamic_slice_in_dim(values, (1 - side) * half, half, values.ndim - 1)
+
+    def whole(own, there):
+        both = jnp.concatenate([own, there], axis=-1), jnp.concatenate([there, own], axis=-1)
+        return jnp.where(side == 0, *both)
+
+    small = jnp.concatenate(
+        [router.T, gain_attn[None], gain_ffn[None], jnp.zeros((14 - experts, half), jnp.bfloat16)]
+    )
+    d_out_all, w_query_there, w_keyval_there, w_out_attn_there, small_there = front(
+        d_out[0], w_query, w_keyval, w_out_attn, small
+    )
+    w_in, w_out, small_there = lax.optimization_barrier((w_in, w_out, small_there))
+    small = whole(small, small_there).astype(jnp.float32)
+    router_rows, gain_one, gain_two = small[:experts], small[experts], small[experts + 1]
+    w_in_there, w_out_there = swap_wa((w_in[0], w_out[0]))
+    in_matrix = jnp.concatenate([w_in[0, 0], w_in_there[0], w_in[0, 1], w_in_there[1]], axis=1)
+    out_matrix = jnp.concatenate([w_out[0], w_out_there], axis=0)
+
+    def onto(values, weight, weight_there):
+        own, there = halves(values)
+        return jnp.dot(own, weight, preferred_element_type=jnp.float32) + jnp.dot(
+            there, weight_there, preferred_element_type=jnp.float32
+        )
+
+    residual = layer_input[0].astype(jnp.float32)
+    hidden_one = rms_scale(residual, gain_one).astype(jnp.bfloat16)
+    hidden_one_own, hidden_one_other = halves(hidden_one)
+    hidden_one_there = swap_wa(hidden_one_other)
+    positions = me * tokens + jnp.arange(tokens, dtype=jnp.int32)
+    angles = angle_table(positions)
+    query_pre = onto(hidden_one, w_query, w_query_there)
+    keyval_pre = onto(hidden_one, w_keyval, w_keyval_there)
+    query = rotate(query_pre.reshape(tokens, HEADS, HEAD_DIM), angles).astype(jnp.bfloat16)
+    query = query.reshape(tokens, D)
+    keys = rotate(keyval_pre[:, :kv_width].reshape(tokens, KV_HEADS, HEAD_DIM), angles)
+    keyval = jnp.concatenate([keys.reshape(tokens, kv_width), keyval_pre[:, kv_width:]], axis=1)
+    keyval_all = gather_ctx(keyval.astype(jnp.bfloat16), 2, "gather_kv")
+    doc_column = lax.dynamic_slice_in_dim(seq_ids[0], me * tokens, tokens, 0)[:, None]
+    mixed, level = attend(query, keyval_all, seq_ids, doc_column)
+    mixed_low = mixed.astype(jnp.bfloat16)
+    mixed_own, mixed_other = halves(mixed_low)
+    mixed_there = swap_wa(mixed_other)
+    middle = residual + onto(mixed_low, w_out_attn, w_out_attn_there)
+
+    hidden_two = rms_scale(middle, gain_two).astype(jnp.bfloat16)
+    router_low = router_rows.astype(jnp.bfloat16)
+    logits = rows_by_rows(hidden_two, router_low)
+    numbers = jnp.arange(experts, dtype=jnp.int32)
+    chosen = jnp.any(routes[0][:, :, None] == numbers[None, None, :], axis=1)
+    masked = jnp.where(chosen, logits, NEGATIVE)
+    weights = jnp.exp(masked - jnp.max(masked, axis=1, keepdims=True))
+    gates = weights / jnp.sum(weights, axis=1, keepdims=True)
+    gates_high = gates.astype(jnp.bfloat16)
+    gates_low = (gates - gates_high.astype(jnp.float32)).astype(jnp.bfloat16)
+    spare = jnp.zeros((tokens, 128 - 2 * experts), jnp.bfloat16)
+    send = jnp.concatenate([hidden_two, gates_high, gates_low, spare], axis=1)
+    hidden_all = gather_ctx(send, 3, "gather_hidden")
+
+    rows = hidden_all[:, :D]
+    expert = me // 2
+    lane = jnp.arange(128, dtype=jnp.int32)[None, :]
+    gate = jnp.sum(
+        jnp.where(
+            (lane == expert) | (lane == expert + experts), hidden_all[:, D:].astype(jnp.float32), 0.0
+        ),
+        axis=1,
+        keepdims=True,
+    )
+    both = jnp.dot(rows, in_matrix, preferred_element_type=jnp.float32)
+    width = 2 * quarter
+
+    def gate_unit(first, second):
+        return jax.nn.gelu(first, approximate=True) * second
+
+    hidden, unit_back = jax.vjp(gate_unit, both[:, :width], both[:, width:])
+    hidden_gated = (hidden * gate).astype(jnp.bfloat16)
+    result = jnp.dot(hidden_gated, out_matrix, preferred_element_type=jnp.float32)
+    grad_hidden = rows_by_rows(d_out_all, out_matrix)
+    grad_gate = jnp.sum(grad_hidden * hidden, axis=1, keepdims=True)
+    grad_both = jnp.concatenate(unit_back(grad_hidden * gate), axis=1).astype(jnp.bfloat16)
+    grad_rows = rows_by_rows(grad_both, in_matrix)
+    gate_columns = jnp.where(lane == expert, grad_gate, 0.0)
+    grad_send = jnp.concatenate([grad_rows, gate_columns], axis=1).astype(jnp.bfloat16)
+    returned = scatter_ctx(grad_send, 4, "scatter_grad_rows")
+    result_sum = scatter_ctx(result.astype(jnp.bfloat16), 5, "scatter_result")
+    output = (middle + result_sum).astype(jnp.bfloat16)
+    grad_in_matrix = columns_by_columns(rows, grad_both)
+    grad_out_matrix = columns_by_columns(hidden_gated, d_out_all)
+
+    grad_out = d_out[0].astype(jnp.float32)
+    grad_gates = returned[:, D : D + experts]
+    grad_logits = gates * (grad_gates - jnp.sum(gates * grad_gates, axis=1, keepdims=True))
+    grad_logits_low = grad_logits.astype(jnp.bfloat16)
+    grad_hidden_two = returned[:, :D] + jnp.dot(
+        grad_logits_low, router_low, preferred_element_type=jnp.float32
+    )
+    grad_router = columns_by_columns(grad_logits_low, hidden_two)
+    back_two, grad_gain_two = rms_back(middle, gain_two, grad_hidden_two)
+    grad_middle = grad_out + back_two
+    grad_middle_low = grad_middle.astype(jnp.bfloat16)
+    grad_middle_there = swap_wa(grad_middle_low)
+    grad_mixed = whole(
+        rows_by_rows(grad_middle_low, w_out_attn), rows_by_rows(grad_middle_low, w_out_attn_there)
+    ).astype(jnp.bfloat16)
+    grad_query, grad_keyval = attend_back(
+        query, keyval_all, seq_ids, doc_column, level, mixed, grad_mixed
+    )
+    grad_query_pre = rotate(grad_query.reshape(tokens, HEADS, HEAD_DIM), -angles)
+    grad_query_pre = grad_query_pre.reshape(tokens, D).astype(jnp.bfloat16)
+    grad_keyval_own = scatter_ctx(grad_keyval, 6, "scatter_grad_kv")
+    grad_keys = rotate(
+        grad_keyval_own[:, :kv_width].reshape(tokens, KV_HEADS, HEAD_DIM), -angles
+    ).reshape(tokens, kv_width)
+    grad_keyval_pre = jnp.concatenate([grad_keys, grad_keyval_own[:, kv_width:]], axis=1)
+    grad_keyval_pre = grad_keyval_pre.astype(jnp.bfloat16)
+    grad_hidden_one = whole(
+        rows_by_rows(grad_query_pre, w_query) + rows_by_rows(grad_keyval_pre, w_keyval),
+        rows_by_rows(grad_query_pre, w_query_there)
+        + rows_by_rows(grad_keyval_pre, w_keyval_there),
+    )
+    back_one, grad_gain_one = rms_back(residual, gain_one, grad_hidden_one)
+    grad_input = (grad_middle + back_one).astype(jnp.bfloat16)
+
+    small_grads = jnp.concatenate(
+        [
+            grad_router,
+            grad_gain_one[None],
+            grad_gain_two[None],
+            jnp.zeros((14 - experts, D), jnp.float32),
+        ]
+    )
+    attn_sum, query_sum, keyval_sum, small_sum, in_there, out_there = finish(
+        hidden_one_own, hidden_one_there, mixed_own, mixed_there, grad_middle_low,
+        grad_middle_there, grad_query_pre, grad_keyval_pre, *halves(small_grads),
+        jnp.concatenate(
+            [grad_in_matrix[:, quarter:width], grad_in_matrix[:, width + quarter :]], axis=1
+        ).astype(jnp.bfloat16),
+        grad_out_matrix[quarter:].astype(jnp.bfloat16),
+    )
+    grad_w_in = jnp.stack(
+        [
+            grad_in_matrix[:, :quarter] + in_there[:, :quarter].astype(jnp.float32),
+            grad_in_matrix[:, width : width + quarter]
+            + in_there[:, quarter:].astype(jnp.float32),
+        ]
+    )
+    grad_w_out = grad_out_matrix[:quarter] + out_there.astype(jnp.float32)
+    return (
+        output[None],
+        grad_input[None],
+        small_sum[experts],
+        query_sum.astype(jnp.float32),
+        keyval_sum.astype(jnp.float32),
+        attn_sum.astype(jnp.float32),
+        small_sum[experts + 1],
+        small_sum[:experts].T,
+        grad_w_in[None],
+        grad_w_out[None],
+    )
+
 
 def solution(mesh):
     in_specs = (
@@ -409,4 +1271,6 @@
         P("ctx", None, None, "wa"),
         P("ctx", "wa", None),
     )
+    depth = mesh.shape["ctx"]
+    body = gathered_body if depth == 16 else routed_body
     return jax.shard_map(body, mesh=mesh, in_specs=in_specs, out_specs=out_specs, check_vma=False)

time: 1470 us -> 515 us (0.35)
  waiting for transfers between devices: 802 us -> 0.01 us
  Pallas kernels: 0 us -> 359 us
  blocking collectives: 254 us -> 0 us
  starting transfers between devices: 91.3 us -> 5.59 us
  matrix products: 145 us -> 63.2 us
  local copies, waits for them, and re-layouts: 82.8 us -> 35.7 us
  other arithmetic: 59.4 us -> 42 us
    all_to_all x4 -> x0, waiting for transfers between devices: 361 us -> none  [the longest x1 107 us: body(): lax.all_to_all(result, 'ctx', split_axis=0, concat_axis=0, tiled=True)]
    pallas_call x0 -> x9, Pallas kernels: none -> 359 us  [call(): pl.pallas_call(kernel, out_shape=out, in_specs=[spec(i, outside) for i in...]
    reduce_scatter x7 -> x0, waiting for transfers between devices: 272 us -> none  [the longest x1 75.6 us: body(): lax.psum_scatter(grad_keyvals, 'ctx', scatter_dimension=0, tiled=True)]
    psum x1 -> x0, blocking collectives: 234 us -> none  [body(): lax.psum((shares[0], shares[1], shares[2], shares[3], shares[4], shares[5...]
    all_gather x6 -> x0, waiting for transfers between devices: 166 us -> none  [the longest x1 52.4 us: body(): lax.all_gather(w_query, 'wa', axis=0, tiled=True)]
    all_to_all x4 -> x0, starting transfers between devices: 90.5 us -> none  [the longest x1 28.5 us: body(): lax.all_to_all(grad_rows, 'ctx', split_axis=0, concat_axis=0, tiled=True)]
    dot_general x50 -> x21, matrix products: 145 us -> 63.2 us  [the longest x9 21.7 us: rows_by_rows(): lax.dot_general(left, right, (((1,), (1,)), ((), ())), preferred_element_...]
    scatter-add x1 -> x0, other arithmetic: 22.1 us -> none  [gate_values(): jnp.take_along_axis(logit_rows, route_ids, axis=-1)]
  transfers between devices with their start and end apart: 17 -> 5, of which waited for: 17 -> 0; matrix products, arithmetic and copies ran while one was open for 11% -> 22% of each run, Pallas kernels for 0% -> 42%
where the time goes in v2:
time: 515 us; the launch traced here: 508 us
  Pallas kernels  359 us (70%)
  matrix products  63.2 us (12%)
  other arithmetic  42 us (8%)
  local copies, waits for them, and re-layouts  35.7 us (7%)
  starting transfers between devices  5.59 us (1%)
    pallas_call x9, Pallas kernels, call(): pl.pallas_call(kernel, out_shape=out, in_specs=[spec(i, outside) for i in...  359 us
    dot_general x9, matrix products, rows_by_rows(): lax.dot_general(left, right, (((1,), (1,)), ((), ())), preferred_element_...  21.7 us
    dot_general x3, matrix products, columns_by_columns(): lax.dot_general(left, right, (((0,), (0,)), ((), ())), preferred_element_...  17.3 us
  transfers between devices with their start and end apart: 5, of which 0 were waited for; matrix products, arithmetic and copies ran while one was open for 22% of the time, Pallas kernels for 42%

profile of v2, /device:TPU:0, one launch (start us, length us, event | category | flops | bytes accessed | tf_op | source)
XLA Modules:
  0.0 507.7 jit_solution(13299055779973677806)
XLA Ops:
  5.1 58.3 %front.1 = (bf16[2048,1536]{1,0:T(8,128)(2,1)}, bf16[768,1536]{1,0:T(8,128)(2,1)}, bf16[768,512]{1,0:T(8,128)(2,1)}, bf16[768,1536]{1,0:T(8,128)(2,1)}, bf16[16,768]{1,0:T(8,128)(2,1)}) custom-call(bf16[128,1536]{1,0:T(8,128)(2,1)} %bitcast.86, bf16[768,1536]{1,0:T(8,128)(2,1)} %query_ref.1, bf16[768,512]{1,0:T(8,128)(2,1)} %keyval_ref.1, ...), custom_call_target="tpu_custom_call" | custom-call | tf_op jit(solution)/shard_map/front/pallas_call | solution.py:653
  77.1 1.6 fusion.32
  80.3 2.3 convolution_add_fusion.2
  84.6 19.9 %gather_kv.1.keyval = bf16[2048,512]{1,0:T(8,128)(2,1)} custom-call(bf16[128,512]{1,0:T(8,128)(2,1)} %pad_maximum_fusion.13.block_ref), custom_call_target="tpu_custom_call" | custom-call | tf_op jit(solution)/shard_map/gather_kv/pallas_call | solution.py:653
  104.6 10.6 %attend.1 = (f32[128,1536]{1,0:T(8,128)}, f32[1536,1]{1,0:T(8,128)}) custom-call(bf16[128,1536]{1,0:T(8,128)(2,1)} %copy.70.query, bf16[2048,512]{1,0:T(8,128)(2,1)} %gather_kv.1.keyval, s32[1,2048]{1,0:T(1,128)} %doc_row.3, s32[128,1]{1,0:T(8,128)} %copy.71.doc_column), custom_call_target="tpu_custom_call" | custom-call | tf_op jit(solution)/shard_map/attend/pallas_call | solution.py:653
  131.6 1.9 concatenate.75.block_ref
  133.5 47.5 %gather_hidden.1 = bf16[2048,1664]{1,0:T(8,128)(2,1)} custom-call(bf16[128,1664]{1,0:T(8,128)(2,1)} %concatenate.75.block_ref), custom_call_target="tpu_custom_call" | custom-call | tf_op jit(solution)/shard_map/gather_hidden/pallas_call | solution.py:653
  185.8 7.3 %fusion.2 = f32[2048,768]{0,1:T(8,128)S(1)} fusion(bf16[2048,1664]{1,0:T(8,128)(2,1)} %gather_hidden.1, bf16[1536,192]{0,1:T(8,128)(2,1)S(1)} %get-tuple-element.109, bf16[1536,192]{0,1:T(8,128)(2,1)S(1)} %get-tuple-element.107, bf16[1536,192]{0,1:T(8,128)(2,1)S(1)} %get-tuple-element.108, bf16[1536,192]{0,1:T(8,128)(2,1)S(1)} %get-tuple-element.106), kind=kOutput, calls=%fused_computation.5 | convolution fusion | flops 4841275392 | bytes 14942208 | tf_op jit(solution)/shard_map/dot_general | solution.py:1154
  193.2 7.8 %fusion.10 = (bf16[2048,384]{0,1:T(8,128)(2,1)S(1)}, bf16[2048,384]{0,1:T(8,128)(2,1)}, bf16[2048]{0:T(1024)(128)(2,1)S(1)}, bf16[2048,384]{0,1:T(8,128)(2,1)}) fusion(f32[2048,768]{0,1:T(8,128)S(1)} %fusion.2, f32[2048]{0:T(1024)S(1)} %select_reduce_fusion, bf16[2048,1536]{1,0:T(8,128)(2,1)S(1)} %bitcast.99, bf16[192,1536]{1,0:T(8,128)(2,1)} %collective-permute-done.1, ...), kind=kOutput, calls=%fused_computation.15 | convolution fusion | flops 2441869312 | bytes 18493440 | tf_op jit(solution)/shard_map/dot_general | solution.py:945
  201.0 8.7 %fusion.50 = (bf16[1536,768]{1,0:T(8,128)(2,1)}, f32[1536,768]{1,0:T(8,128)}) fusion(bf16[2048,384]{0,1:T(8,128)(2,1)} %get-tuple-element.99, bf16[2048,384]{0,1:T(8,128)(2,1)S(1)} %get-tuple-element.98, bf16[2048,1664]{1,0:T(8,128)(2,1)S(1)} %bitcast.80), kind=kOutput, calls=%fused_computation.146 | convolution fusion | flops 4839309312 | bytes 16515072 | tf_op jit(solution)/shard_map/dot_general | solution.py:951
  209.7 5.5 %convolution_convert_fusion = bf16[2048,1536]{1,0:T(8,128)(2,1)S(1)} fusion(bf16[2048,384]{0,1:T(8,128)(2,1)S(1)} %copy-done.55, bf16[2048,384]{0,1:T(8,128)(2,1)S(1)} %get-tuple-element.98, bf16[1536,192]{0,1:T(8,128)(2,1)S(1)} %get-tuple-element.109, bf16[1536,192]{0,1:T(8,128)(2,1)S(1)} %get-tuple-element.107, ...), kind=kOutput, calls=%fused_computation | convolution fusion | flops 4850712576 | bytes 11796480 | tf_op jit(solution)/shard_map/dot_general | solution.py:945
  215.6 3.3 pad_maximum_fusion.part
  219.0 49.0 %scatter_grad_rows.1 = f32[128,1664]{1,0:T(8,128)} custom-call(bf16[2048,1664]{1,0:T(8,128)(2,1)} %pad_maximum_fusion.part), custom_call_target="tpu_custom_call" | custom-call | tf_op jit(solution)/shard_map/scatter_grad_rows/pallas_call | solution.py:653
  269.1 1.8 fusion.45
  270.9 3.0 multiply_reduce_fusion.1
  274.0 6.8 %fusion.56 = f32[384,1536]{1,0:T(8,128)} fusion(bf16[2048,384]{0,1:T(8,128)(2,1)S(1)} %copy-done.54, bf16[2048,1536]{1,0:T(8,128)(2,1)} %get-tuple-element.36), kind=kOutput, calls=%fused_computation.152 | convolution fusion | flops 2415919104 | bytes 10223616 | tf_op jit(solution)/shard_map/dot_general | solution.py:951
  280.8 6.4 %convolution_convert_fusion.1.part = bf16[2048,1536]{1,0:T(8,128)(2,1)} fusion(bf16[2048,384]{0,1:T(8,128)(2,1)S(1)} %copy-done.54, bf16[192,1536]{1,0:T(8,128)(2,1)} %collective-permute-done.1, bf16[192,1536]{1,0:T(8,128)(2,1)S(1)} %bitcast.102), kind=kOutput, calls=%fused_computation.1 | convolution fusion | flops 2421424128 | bytes 9043968 | tf_op jit(solution)/shard_map/dot_general | solution.py:1162
  287.2 48.0 %scatter_result.1 = f32[128,1536]{1,0:T(8,128)} custom-call(bf16[2048,1536]{1,0:T(8,128)(2,1)} %convolution_convert_fusion.1.part), custom_call_target="tpu_custom_call" | custom-call | tf_op jit(solution)/shard_map/scatter_result/pallas_call | solution.py:653
  335.3 2.8 fusion.46
  340.8 16.8 %attend_back.1 = (f32[128,1536]{1,0:T(8,128)}, bf16[2048,512]{1,0:T(8,128)(2,1)}) custom-call(bf16[128,1536]{1,0:T(8,128)(2,1)} %copy.70.query, bf16[2048,512]{1,0:T(8,128)(2,1)} %gather_kv.1.keyval, s32[1,2048]{1,0:T(1,128)} %doc_row.3, s32[128,1]{1,0:T(8,128)} %copy.71.doc_column, f32[1536,1]{1,0:T(8,128)} %get-tuple-element.37.level, ...), custom_call_target="tpu_custom_call" | custom-call | tf_op jit(solution)/shard_map/attend_back/pallas_call | solution.py:653
  357.6 23.0 %scatter_grad_kv.1 = f32[128,512]{1,0:T(8,128)} custom-call(bf16[2048,512]{1,0:T(8,128)(2,1)} %get-tuple-element.39.part), custom_call_target="tpu_custom_call" | custom-call | tf_op jit(solution)/shard_map/scatter_grad_kv/pallas_call | solution.py:653
  386.9 1.9 fusion.48
  388.8 2.4 copy.78
  392.5 2.1 convolution_add_fusion.3
  398.7 2.1 slice.246.refs_11_
  403.1 86.1 %finish.1 = (bf16[768,1536]{1,0:T(8,128)(2,1)}, bf16[768,1536]{1,0:T(8,128)(2,1)}, bf16[768,512]{1,0:T(8,128)(2,1)}, f32[16,768]{1,0:T(8,128)}, bf16[1536,384]{1,0:T(8,128)(2,1)}, /*index=5*/bf16[192,1536]{1,0:T(8,128)(2,1)}) custom-call(bf16[128,768]{1,0:T(8,128)(2,1)} %get-tuple-element.118.refs_0_, bf16[128,768]{1,0:T(8,128)(2,1)} %collective-permute-done.2.refs_1_, ...), custom_call_target="tpu_custom_call" | custom-call | tf_op jit(solution)/shard_map/finish/pallas_call | solution.py:653
  492.0 2.2 fusion.14
  494.2 2.4 fusion.13
  496.8 2.2 copy.85
  498.9 2.6 convert_element_type.116
  501.6 2.8 convert_element_type.115
  504.4 2.8 convert_element_type.117
  (212 shorter events, 63.7 us)
Async XLA Ops:
  5.0 58.3 %copy-start.37 = (bf16[768,8]{0,1:T(8,128)(2,1)S(1)}, bf16[768,8]{0,1:T(8,128)(2,1)}, u32[]{:S(2)}) copy-start(bf16[768,8]{0,1:T(8,128)(2,1)} %param.20) | copy-start | bytes 36868
  5.0 59.8 %copy-start.3 = (bf16[1,128,1536]{2,1,0:T(8,128)(2,1)S(1)}, bf16[1,128,1536]{2,1,0:T(8,128)(2,1)}, u32[]{:S(2)}) copy-start(bf16[1,128,1536]{2,1,0:T(8,128)(2,1)} %param.12) | copy-start | bytes 1179652
  5.0 66.1 %copy-start.7 = (bf16[768,512]{1,0:T(8,128)(2,1)S(1)}, bf16[768,512]{1,0:T(8,128)(2,1)}, u32[]{:S(2)}) copy-start(bf16[768,512]{1,0:T(8,128)(2,1)} %keyval_ref.1) | copy-start | bytes 2359300
  64.8 10.4 %copy-start.1 = (bf16[768,1536]{1,0:T(8,128)(2,1)S(1)}, bf16[768,1536]{1,0:T(8,128)(2,1)}, u32[]{:S(2)}) copy-start(bf16[768,1536]{1,0:T(8,128)(2,1)} %query_ref.1) | copy-start | bytes 7077892
  66.6 336.5 %collective-permute-start.2 = (bf16[128,768]{1,0:T(8,128)(2,1)}, bf16[128,768]{1,0:T(8,128)(2,1)}, u32[]{:S(2)}, u32[]{:S(2)}) collective-permute-start(bf16[128,768]{1,0:T(8,128)(2,1)} %get-tuple-element.117), channel_id=1, source_target_pairs={{0,1},{1,0},{2,3},{3,2},{4,5},{5,4},{6,7},{7,6},{8,9},{9,8},{10,11... | collective-permute-start | bytes 589832 | tf_op jit(solution)/shard_map/ppermute | solution.py:1069
  68.1 125.1 %collective-permute-start.1 = (bf16[192,1536]{1,0:T(8,128)(2,1)}, bf16[192,1536]{1,0:T(8,128)(2,1)}, u32[]{:S(2)}, u32[]{:S(2)}) collective-permute-start(bf16[192,1536]{1,0:T(8,128)(2,1)} %bitcast.100), channel_id=1, source_target_pairs={{0,1},{1,0},{2,3},{3,2},{4,5},{5,4},{6,7},{7,6},{8,9},{9,8},{10,11... | collective-permute-start | bytes 1769480 | tf_op jit(solution)/shard_map/ppermute | solution.py:1069
  68.6 115.7 %collective-permute-start = (bf16[2,1536,192]{1,2,0:T(8,128)(2,1)}, bf16[2,1536,192]{1,2,0:T(8,128)(2,1)}, u32[]{:S(2)}, u32[]{:S(2)}) collective-permute-start(bf16[2,1536,192]{1,2,0:T(8,128)(2,1)} %bitcast.88), channel_id=1, source_target_pairs={{0,1},{1,0},{2,3},{3,2},{4,5},{5,4},{6,7},{7,6},{8,9},{9,8},{10,11... | collective-permute-start | bytes 3538952 | tf_op jit(solution)/shard_map/ppermute | solution.py:1069
  104.6 13.1 %copy-start.48 = (s32[1,128,4]{1,2,0:T(4,128)S(1)}, s32[1,128,4]{1,2,0:T(4,128)}, u32[]{:S(2)}) copy-start(s32[1,128,4]{1,2,0:T(4,128)} %param.14) | copy-start | bytes 6148
  104.6 13.8 %copy-start = (bf16[768,1536]{1,0:T(8,128)(2,1)S(1)}, bf16[768,1536]{1,0:T(8,128)(2,1)}, u32[]{:S(2)}) copy-start(bf16[768,1536]{1,0:T(8,128)(2,1)} %attn_ref.1) | copy-start | bytes 7077892
  117.1 285.9 %collective-permute-start.3 = (bf16[128,768]{1,0:T(8,128)(2,1)}, bf16[128,768]{1,0:T(8,128)(2,1)}, u32[]{:S(2)}, u32[]{:S(2)}) collective-permute-start(bf16[128,768]{1,0:T(8,128)(2,1)} %get-tuple-element.115), channel_id=1, source_target_pairs={{0,1},{1,0},{2,3},{3,2},{4,5},{5,4},{6,7},{7,6},{8,9},{9,8},{10,11... | collective-permute-start | bytes 589832 | tf_op jit(solution)/shard_map/ppermute | solution.py:1069
  184.3 8.9 %slice-start.2 = ((s8[6291456]{0:T(1024)(128)(4,1)}), s8[4194304]{0:T(1024)(128)(4,1)S(1)}, s32[]{:S(2)}) async-start(s8[6291456]{0:T(1024)(128)(4,1)} %bitcast.98), calls=%async_computation.2 | async-start | bytes 8388608
  185.8 7.4 %slice-start.3 = ((s8[6291456]{0:T(1024)(128)(4,1)}), s8[2097152]{0:T(1024)(128)(4,1)S(1)}, s32[]{:S(2)}) async-start(s8[6291456]{0:T(1024)(128)(4,1)} %bitcast.98), calls=%async_computation.3 | async-start | bytes 4194304
  185.8 7.4 %copy-start.52 = (bf16[1,192,1536]{2,1,0:T(8,128)(2,1)S(1)}, bf16[1,192,1536]{2,1,0:T(8,128)(2,1)}, u32[]{:S(2)}) copy-start(bf16[1,192,1536]{2,1,0:T(8,128)(2,1)} %param.22) | copy-start | bytes 1769476
  185.8 15.2 %slice-start = ((s8[6815744]{0:T(1024)(128)(4,1)}), s8[2621440]{0:T(1024)(128)(4,1)S(1)}, s32[]{:S(2)}) async-start(s8[6815744]{0:T(1024)(128)(4,1)} %bitcast.79), calls=%async_computation | async-start | bytes 5242880
  193.2 7.8 %slice-start.1 = ((s8[6815744]{0:T(1024)(128)(4,1)}), s8[4194304]{0:T(1024)(128)(4,1)S(1)}, s32[]{:S(2)}) async-start(s8[6815744]{0:T(1024)(128)(4,1)} %bitcast.79), calls=%async_computation.1 | async-start | bytes 8388608
  201.0 8.7 %copy-start.55 = (bf16[2048,384]{0,1:T(8,128)(2,1)S(1)}, bf16[2048,384]{0,1:T(8,128)(2,1)}, u32[]{:S(2)}) copy-start(bf16[2048,384]{0,1:T(8,128)(2,1)} %get-tuple-element.99) | copy-start | bytes 4718596
  218.9 49.0 %copy-start.30 = (f32[128,8]{1,0:T(8,128)S(1)}, f32[128,8]{1,0:T(8,128)}, u32[]{:S(2)}) copy-start(f32[128,8]{1,0:T(8,128)} %get-tuple-element.138) | copy-start | bytes 12292
  218.9 49.0 %copy-start.42 = (f32[128]{0:T(128)S(1)}, f32[128]{0:T(128)}, u32[]{:S(2)}) copy-start(f32[128]{0:T(128)} %get-tuple-element.137) | copy-start | bytes 1540
  218.9 49.0 %copy-start.44 = (f32[128]{0:T(128)S(1)}, f32[128]{0:T(128)}, u32[]{:S(2)}) copy-start(f32[128]{0:T(128)} %copy-done.43) | copy-start | bytes 1540
  218.9 50.2 %copy-start.12 = (bf16[128,1536]{1,0:T(8,128)(2,1)S(1)}, bf16[128,1536]{1,0:T(8,128)(2,1)}, u32[]{:S(2)}) copy-start(bf16[128,1536]{1,0:T(8,128)(2,1)} %copy-done.11) | copy-start | bytes 1179652
  218.9 52.0 %copy-start.39 = (bf16[16,1536]{1,0:T(8,128)(2,1)S(1)}, bf16[16,1536]{1,0:T(8,128)(2,1)}, u32[]{:S(2)}) copy-start(bf16[16,1536]{1,0:T(8,128)(2,1)} %get-tuple-element.97) | copy-start | bytes 147460
  218.9 52.0 %copy-start.47 = (f32[128]{0:T(128)S(1)}, f32[128]{0:T(128)}, u32[]{:S(2)}) copy-start(f32[128]{0:T(128)} %copy-done.46) | copy-start | bytes 1540
  268.0 6.0 %copy-start.54 = (bf16[2048,384]{0,1:T(8,128)(2,1)S(1)}, bf16[2048,384]{0,1:T(8,128)(2,1)}, u32[]{:S(2)}) copy-start(bf16[2048,384]{0,1:T(8,128)(2,1)} %get-tuple-element.101) | copy-start | bytes 4718596
  274.0 6.9 %copy-start.53 = (bf16[1,192,1536]{2,1,0:T(8,128)(2,1)S(1)}, bf16[1,192,1536]{2,1,0:T(8,128)(2,1)}, u32[]{:S(2)}) copy-start(bf16[1,192,1536]{2,1,0:T(8,128)(2,1)} %param.22) | copy-start | bytes 1769476
  287.2 48.1 %copy-start.22 = (bf16[1,128,1536]{2,1,0:T(8,128)(2,1)S(1)}, bf16[1,128,1536]{2,1,0:T(8,128)(2,1)}, u32[]{:S(2)}) copy-start(bf16[1,128,1536]{2,1,0:T(8,128)(2,1)} %param.23) | copy-start | bytes 1179652
  287.2 48.1 %copy-start.50 = (f32[128]{0:T(128)S(1)}, f32[128]{0:T(128)}, u32[]{:S(2)}) copy-start(f32[128]{0:T(128)} %get-tuple-element.133) | copy-start | bytes 1540
  357.5 25.0 %copy-start.34 = (f32[128,64]{1,0:T(8,128)S(1)}, f32[128,64]{1,0:T(8,128)}, u32[]{:S(2)}) copy-start(f32[128,64]{1,0:T(8,128)} %copy.79) | copy-start | bytes 98308
  357.6 25.0 %copy-start.35 = (f32[128,64]{1,0:T(8,128)S(1)}, f32[128,64]{1,0:T(8,128)}, u32[]{:S(2)}) copy-start(f32[128,64]{1,0:T(8,128)} %copy.80) | copy-start | bytes 98308
  357.6 25.5 %copy-start.13 = (bf16[768,512]{1,0:T(8,128)(2,1)S(1)}, bf16[768,512]{1,0:T(8,128)(2,1)}, u32[]{:S(2)}) copy-start(bf16[768,512]{1,0:T(8,128)(2,1)} %get-tuple-element.31) | copy-start | bytes 2359300
  357.6 26.6 %copy-start.8 = (bf16[768,512]{1,0:T(8,128)(2,1)S(1)}, bf16[768,512]{1,0:T(8,128)(2,1)}, u32[]{:S(2)}) copy-start(bf16[768,512]{1,0:T(8,128)(2,1)} %keyval_ref.1) | copy-start | bytes 2359300
  385.3 17.7 %collective-permute-start.4 = (bf16[128,1536]{1,0:T(8,128)(2,1)S(1)}, bf16[128,1536]{1,0:T(8,128)(2,1)}, u32[]{:S(2)}, u32[]{:S(2)}) collective-permute-start(bf16[128,1536]{1,0:T(8,128)(2,1)S(1)} %copy-done.10), channel_id=1, source_target_pairs={{0,1},{1,0},{2,3},{3,2},{4,5},{5,4},{6,7},{7,6},{8,9},{9,8},{10,11... | collective-permute-start | bytes 1179656 | tf_op jit(solution)/shard_map/ppermute | solution.py:1069
  403.0 88.9 %copy-start.24 = (f32[384,1536]{1,0:T(8,128)S(1)}, f32[384,1536]{1,0:T(8,128)}, u32[]{:S(2)}) copy-start(f32[384,1536]{1,0:T(8,128)} %fusion.56) | copy-start | bytes 7077892
  (33 other events, 101.2 us)

commit v3 on v2

--- a/solution.py
+++ b/solution.py
@@ -435,6 +435,14 @@
         pl.when(z - step >= 0)(lambda: act(z - step))
 
 
+def nearest(k):
+    z, _, _, depth = chip_place()
+    low = jnp.minimum(z, depth - 1 - z)
+    step = (k + 1) // 2
+    place = jnp.where(k > 2 * low, k, jnp.where(lax.rem(k, 2) == 1, low - step, low + step))
+    return jnp.where(z == low, place, depth - 1 - place)
+
+
 class Gather:
     def __init__(self, out, rows, sems):
         self.out, self.rows = out, rows
@@ -520,9 +528,11 @@
 
 
 def add_into(target, terms, rows):
-    @pl.loop(0, rows // 16)
+    some = 32 if rows % 32 == 0 else 48 if rows % 48 == 0 else 16
+
+    @pl.loop(0, rows // some)
     def _(turn):
-        at = pl.ds(pl.multiple_of(turn * 16, 16), 16)
+        at = pl.ds(pl.multiple_of(turn * some, 16), some)
         total = terms[0][at, :].astype(jnp.float32)
         for term in terms[1:]:
             total = total + term[at, :].astype(jnp.float32)
@@ -530,11 +540,12 @@
 
 
 class Scatter:
-    def __init__(self, part, scratch):
+    def __init__(self, part, scratch, sums=None):
         self.part = part
-        self.from_core, self.sums, self.from_y, self.from_z = scratch[:4]
+        self.from_core, self.totals, self.from_y, self.from_z = scratch[:4]
+        self.sums = self.totals if sums is None else sums
         self.c_sems, self.y_sems, self.z_sems = scratch[4:]
-        self.rows = self.sums.shape[1]
+        self.rows = self.totals.shape[1]
         self.z, self.y, self.c, self.depth = chip_place()
 
     @staticmethod
@@ -543,20 +554,22 @@
             pltpu.VMEM((2 * depth, rows, columns), jnp.bfloat16),
             pltpu.VMEM((2 * depth, rows, columns), jnp.bfloat16),
             pltpu.VMEM((depth, rows, columns), jnp.bfloat16),
-            pltpu.VMEM((2, depth, rows, columns), jnp.bfloat16),
+            pltpu.VMEM((depth + 1, rows, columns), jnp.bfloat16),
             pltpu.SemaphoreType.DMA((2, 2 * depth)),
             pltpu.SemaphoreType.DMA((2, depth)),
             pltpu.SemaphoreType.DMA((2, 2, depth)),
         ]
 
+    def split(self):
+        return len(self.part.shape) == 3
+
     def share(self, chip, c):
         return self.part.at[pl.ds(pl.multiple_of((chip * 2 + c) * self.rows, 16), self.rows)]
 
     def on_core(self, chip):
         target = {"ctx": ctx_of(self.z, self.y, 1 - self.c)}
-        return remote(
-            self.share(chip, 1 - self.c), self.from_core.at[chip], self.c_sems, (chip,), target
-        )
+        source = self.part.at[chip] if self.split() else self.share(chip, 1 - self.c)
+        return remote(source, self.from_core.at[chip], self.c_sems, (chip,), target)
 
     def on_y(self, of_z):
         target = {"ctx": ctx_of(self.z, 1 - self.y, self.c)}
@@ -565,9 +578,10 @@
 
     def on_z(self, way, of_z):
         goal = jnp.minimum(self.z + 1, self.depth - 1) if way == 0 else jnp.maximum(self.z - 1, 0)
-        source = self.sums.at[of_z * 2 + self.y]
+        place = of_z if way == 0 else jnp.where(of_z == goal, self.depth, of_z)
+        source = self.totals.at[of_z * 2 + self.y]
         target = {"ctx": ctx_of(goal, self.y, self.c)}
-        return remote(source, self.from_z.at[way, of_z], self.z_sems, (way, of_z), target)
+        return remote(source, self.from_z.at[place], self.z_sems, (way, of_z), target)
 
     def start(self):
         def send(of_z):
@@ -577,47 +591,48 @@
         for step in range(self.depth - 1, -1, -1):
             each(step, send)
 
+    def add_chip(self, of_z, other, send=True):
+        chip = of_z * 2 + (1 - self.y if other else self.y)
+        self.on_core(chip).wait_recv()
+        own = self.sums.at[chip] if self.split() else self.share(chip, self.c)
+        add_into(self.sums.at[chip], (own, self.from_core.at[chip]), self.rows)
+        if other and send:
+            self.on_y(of_z).start()
+
     def add_cores(self, step):
         def add(of_z):
-            for other in (True, False):
-                chip = of_z * 2 + (1 - self.y if other else self.y)
-                self.on_core(chip).wait_recv()
-                terms = (self.share(chip, self.c), self.from_core.at[chip])
-                add_into(self.sums.at[chip], terms, self.rows)
-                if other:
-                    self.on_y(of_z).start()
+            self.add_chip(of_z, True)
+            self.add_chip(of_z, False)
 
         each(step, add)
 
+    def add_y_of(self, of_z):
+        z, depth = self.z, self.depth
+        self.on_y(of_z).wait_recv()
+        place = of_z * 2 + self.y
+        total, own, other = self.totals.at[place], self.sums.at[place], self.from_y.at[of_z]
+        upward, downward = (of_z > z) & (z > 0), (of_z < z) & (z < depth - 1)
+        pl.when(upward)(lambda: self.on_z(0, of_z).wait_recv())
+        pl.when(downward)(lambda: self.on_z(1, of_z).wait_recv())
+
+        @pl.when(upward | downward)
+        def _():
+            add_into(total, (own, other, self.from_z.at[of_z]), self.rows)
+
+        @pl.when(jnp.logical_not(upward | downward))
+        def _():
+            add_into(total, (own, other), self.rows)
+
+        pl.when(of_z > z)(lambda: self.on_z(0, of_z).start())
+        pl.when(of_z < z)(lambda: self.on_z(1, of_z).start())
+
     def add_y(self, step):
-        z, depth = self.z, self.depth
-
-        def add(of_z):
-            self.on_y(of_z).wait_recv()
-            own = self.sums.at[of_z * 2 + self.y]
-
-            def passing(way):
-                self.on_z(way, of_z).wait_recv()
-                terms = (own, self.from_y.at[of_z], self.from_z.at[way, of_z])
-                add_into(own, terms, self.rows)
-
-            upward, downward = (of_z > z) & (z > 0), (of_z < z) & (z < depth - 1)
-            pl.when(upward)(lambda: passing(0))
-            pl.when(downward)(lambda: passing(1))
-
-            @pl.when(jnp.logical_not(upward | downward))
-            def _():
-                add_into(own, (own, self.from_y.at[of_z]), self.rows)
-
-            pl.when(of_z > z)(lambda: self.on_z(0, of_z).start())
-            pl.when(of_z < z)(lambda: self.on_z(1, of_z).start())
-
-        each(step, add)
+        each(step, self.add_y_of)
 
     def last(self, result):
         z, depth = self.z, self.depth
-        own = self.sums.at[z * 2 + self.y]
-        low, high = self.from_z.at[0, z], self.from_z.at[1, z]
+        own = self.totals.at[z * 2 + self.y]
+        low, high = self.from_z.at[z], self.from_z.at[depth]
         pl.when(z > 0)(lambda: self.on_z(0, z).wait_recv())
         pl.when(z < depth - 1)(lambda: self.on_z(1, z).wait_recv())
         inside = (z > 0) & (z < depth - 1)
@@ -625,23 +640,14 @@
         pl.when(z == 0)(lambda: add_into(result, (own, high), self.rows))
         pl.when(z == depth - 1)(lambda: add_into(result, (own, low), self.rows))
 
-    def finish(self):
+    def finish(self, cores=True):
         for of_z in range(self.depth):
             self.on_y(of_z).wait_send()
-            self.on_core(of_z * 2).wait_send()
-            self.on_core(of_z * 2 + 1).wait_send()
+            if cores:
+                self.on_core(of_z * 2).wait_send()
+                self.on_core(of_z * 2 + 1).wait_send()
             pl.when(of_z > self.z)(lambda: self.on_z(0, of_z).wait_send())
             pl.when(of_z < self.z)(lambda: self.on_z(1, of_z).wait_send())
-
-    def run(self, result):
-        steps = range(self.depth - 1, -1, -1)
-        self.start()
-        for step in steps:
-            self.add_cores(step)
-        for step in steps:
-            self.add_y(step)
-        self.last(result)
-        self.finish()
 
 
 def call(kernel, out, scratch, number, name, *operands, outside=(), outside_out=()):
@@ -676,19 +682,6 @@
 
     out = jax.ShapeDtypeStruct((count * rows, block.shape[1]), block.dtype)
     return call(kernel, out, Gather.sems(count // 4), number, name, block)
-
-
-def scatter_ctx(parts, number, name):
-    count = lax.axis_size("ctx")
-    rows, columns = parts.shape[0] // count, parts.shape[1]
-
-    def kernel(part, result, *scratch):
-        greet()
-        Scatter(part, scratch).run(result)
-
-    out = jax.ShapeDtypeStruct((rows, columns), jnp.float32)
-    scratch = Scatter.scratch(count // 4, rows, columns)
-    return call(kernel, out, scratch, number, name, parts)
 
 
 class Relay:
@@ -1001,60 +994,225 @@
     )
 
 
-def attend_back_kernel(
-    query, keyval, doc_row, doc_column, level, mixed, grad_mixed,
-    grad_query, grad_keyval, stacked, grads, bias, delta, total,
-):
-    tokens = query.shape[0]
-    bias[...] = allowed_bias(doc_row[...], doc_column[...], tokens)
-    total[...] = jnp.zeros_like(total)
-    for head in range(HEADS):
-        rows, columns = slice(head * tokens, (head + 1) * tokens), slice(head * 128, head * 128 + 128)
-        stacked[rows, :] = query[:, columns]
-        grads[rows, :] = grad_mixed[:, columns]
-        delta[rows, :] = jnp.sum(
-            grad_mixed[:, columns].astype(jnp.float32) * mixed[:, columns], axis=-1, keepdims=True
-        )
-
-    @pl.loop(0, HEADS // 2)
-    def _(pair):
-        rows = pl.ds(pl.multiple_of(pair * 2 * tokens, 128), 2 * tokens)
-        kind = pair // (HEADS // KV_HEADS // 2)
-        key_columns = pl.ds(pl.multiple_of(kind * 128, 128), 128)
-        val_columns = pl.ds(pl.multiple_of(kind * 128 + 256, 128), 128)
-        keys, vals = keyval[:, key_columns], keyval[:, val_columns]
-        own, grad = stacked[rows, :], grads[rows, :]
-        scores = rows_by_rows(own, keys) * HEAD_DIM**-0.5
-        scores = (scores.reshape(2, tokens, -1) + bias[...][None]).reshape(scores.shape)
-        probs = jnp.exp(scores - level[rows, :])
-        grad_probs = rows_by_rows(grad, vals)
-        grad_scores = (probs * (grad_probs - delta[rows, :])).astype(jnp.bfloat16)
-        own_grad = jnp.dot(grad_scores, keys, preferred_element_type=jnp.float32)
-        for half in range(2):
-            columns = pl.ds(pl.multiple_of((pair * 2 + half) * 128, 128), 128)
-            grad_query[:, columns] = own_grad[half * tokens : (half + 1) * tokens] * HEAD_DIM**-0.5
-        total[:, key_columns] += columns_by_columns(grad_scores, own) * HEAD_DIM**-0.5
-        total[:, val_columns] += columns_by_columns(probs.astype(jnp.bfloat16), grad)
-
-    grad_keyval[...] = total[...].astype(jnp.bfloat16)
-
-
-def attend_back(query, keyval, doc_row, doc_column, level, mixed, grad_mixed):
-    tokens, keys = query.shape[0], keyval.shape[0]
-    out = (
+def attend_back(query, keyval, doc_row, doc_column, level, mixed, grad_mixed, results):
+    count, tokens, keys = lax.axis_size("ctx"), query.shape[0], keyval.shape[0]
+    depth = count // 4
+
+    def kernel(
+        query_ref, keyval_ref, doc_row_ref, doc_column_ref, level_ref, mixed_ref, grad_mixed_ref,
+        results_ref, grad_query, grad_keyval, output,
+        stacked, grads, bias, delta, total, part, *scratch,
+    ):
+        result = Scatter(None, (None,) + tuple(scratch[:3]) + (None,) + tuple(scratch[3:5]), results_ref)
+        keyval_sum = Scatter(part, scratch[5:])
+        greet()
+        for k in (depth - 1, depth - 2):
+            result.on_y(nearest(k)).start()
+        bias[...] = allowed_bias(doc_row_ref[...], doc_column_ref[...], tokens)
+        total[...] = jnp.zeros_like(total)
+        for head in range(HEADS):
+            rows = slice(head * tokens, (head + 1) * tokens)
+            columns = slice(head * 128, head * 128 + 128)
+            stacked[rows, :] = query_ref[:, columns]
+            grads[rows, :] = grad_mixed_ref[:, columns]
+            delta[rows, :] = jnp.sum(
+                grad_mixed_ref[:, columns].astype(jnp.float32) * mixed_ref[:, columns],
+                axis=-1,
+                keepdims=True,
+            )
+
+        @pl.loop(0, HEADS // 2)
+        def _(pair):
+            rows = pl.ds(pl.multiple_of(pair * 2 * tokens, 128), 2 * tokens)
+            kind = pair // (HEADS // KV_HEADS // 2)
+            key_columns = pl.ds(pl.multiple_of(kind * 128, 128), 128)
+            val_columns = pl.ds(pl.multiple_of(kind * 128 + 256, 128), 128)
+            key_part, val_part = keyval_ref[:, key_columns], keyval_ref[:, val_columns]
+            own, grad = stacked[rows, :], grads[rows, :]
+            scores = rows_by_rows(own, key_part) * HEAD_DIM**-0.5
+            scores = (scores.reshape(2, tokens, -1) + bias[...][None]).reshape(scores.shape)
+            probs = jnp.exp(scores - level_ref[rows, :])
+            grad_probs = rows_by_rows(grad, val_part)
+            grad_scores = (probs * (grad_probs - delta[rows, :])).astype(jnp.bfloat16)
+            own_grad = jnp.dot(grad_scores, key_part, preferred_element_type=jnp.float32)
+            for half in range(2):
+                columns = pl.ds(pl.multiple_of((pair * 2 + half) * 128, 128), 128)
+                grad_query[:, columns] = (
+                    own_grad[half * tokens : (half + 1) * tokens] * HEAD_DIM**-0.5
+                )
+            total[:, key_columns] += columns_by_columns(grad_scores, own) * HEAD_DIM**-0.5
+            total[:, val_columns] += columns_by_columns(probs.astype(jnp.bfloat16), grad)
+            pl.when(pair == HEADS // 4)(lambda: result.add_y_of(nearest(depth - 1)))
+
+        part[...] = total[...].astype(jnp.bfloat16)
+        keyval_sum.start()
+        steps = range(depth - 1, -1, -1)
+        for step in steps:
+            keyval_sum.add_cores(step)
+        for k in range(depth - 3, -1, -1):
+            result.on_y(nearest(k)).start()
+        result.add_y_of(nearest(depth - 2))
+        for step in steps:
+            keyval_sum.add_y(step)
+        keyval_sum.last(grad_keyval)
+        for k in range(depth - 3, -1, -1):
+            result.add_y_of(nearest(k))
+        result.last(output)
+        keyval_sum.finish()
+        result.finish(cores=False)
+
+    out = [
         jax.ShapeDtypeStruct(query.shape, jnp.float32),
-        jax.ShapeDtypeStruct(keyval.shape, jnp.bfloat16),
-    )
+        jax.ShapeDtypeStruct((tokens, keyval.shape[1]), jnp.float32),
+        jax.ShapeDtypeStruct(query.shape, jnp.float32),
+    ]
     scratch = [
         pltpu.VMEM((HEADS * tokens, HEAD_DIM), jnp.bfloat16),
         pltpu.VMEM((HEADS * tokens, HEAD_DIM), jnp.bfloat16),
         pltpu.VMEM((tokens, keys), jnp.float32),
         pltpu.VMEM((HEADS * tokens, 1), jnp.float32),
         pltpu.VMEM(keyval.shape, jnp.float32),
+        pltpu.VMEM(keyval.shape, jnp.bfloat16),
     ]
+    wide = Scatter.scratch(depth, tokens, query.shape[1])
+    scratch += wide[1:4] + wide[5:] + Scatter.scratch(depth, tokens, keyval.shape[1])
     return call(
-        attend_back_kernel, out, scratch, None, "attend_back",
-        query, keyval, doc_row, doc_column, level, mixed, grad_mixed,
+        kernel, out, scratch, 4, "attend_back",
+        query, keyval, doc_row, doc_column, level, mixed, grad_mixed, results,
+    )
+
+
+def gate_unit(first, second):
+    root, cube = math.sqrt(2 / math.pi), 0.044715
+    square = first * first
+    bend = jnp.tanh(root * first * (1 + cube * square))
+    lift = 0.5 * (1 + bend)
+    slope = lift + 0.5 * first * (1 - bend * bend) * root * (1 + 3 * cube * square)
+    gelu = first * lift
+    return gelu * second, slope * second, gelu
+
+
+def run_experts(send, d_out_all, in_matrix, out_matrix, experts):
+    count, tokens = lax.axis_size("ctx"), send.shape[0]
+    depth, chips, length = count // 4, count // 2, count * tokens
+    wide, features, width = send.shape[1], d_out_all.shape[1], out_matrix.shape[0]
+
+    def kernel(
+        send_ref, d_out_ref, in_ref, out_ref, returned, results, grad_in, grad_out,
+        hidden_all, grad_both, gated_hidden, other_part, other_result, result_from, result_sems,
+        *scratch,
+    ):
+        gather = Gather(hidden_all, tokens, scratch[:3])
+        scatter = Scatter(other_part, scratch[3:])
+        z, y, c, _ = chip_place()
+        expert = lax.axis_index("ctx") // 2
+        lane = lax.broadcasted_iota(jnp.int32, (1, 128), 1)
+        gather.own()[...] = send_ref[...]
+        greet()
+        gather.run()
+
+        def chip_rows(chip):
+            return pl.ds(pl.multiple_of(chip * 2 * tokens, 16), 2 * tokens)
+
+        def parted(values):
+            low, high = values[:tokens], values[tokens:]
+            return jnp.where(c == 0, low, high), jnp.where(c == 0, high, low)
+
+        def backward(chip):
+            rows = chip_rows(chip)
+            carried = hidden_all[rows, features:].astype(jnp.float32)
+            mine = (lane == expert) | (lane == expert + experts)
+            gate = jnp.sum(jnp.where(mine, carried, 0.0), axis=1, keepdims=True)
+            both = jnp.dot(
+                hidden_all[rows, :features], in_ref[...], preferred_element_type=jnp.float32
+            )
+            hidden, by_first, by_second = gate_unit(both[:, :width], both[:, width:])
+            gated_hidden[rows, :] = (hidden * gate).astype(jnp.bfloat16)
+            grad_hidden = rows_by_rows(d_out_ref[rows, :], out_ref[...])
+            grad_gate = jnp.sum(grad_hidden * hidden, axis=1, keepdims=True)
+            grad_hidden = grad_hidden * gate
+            grad_both[rows, :width] = (grad_hidden * by_first).astype(jnp.bfloat16)
+            grad_both[rows, width:] = (grad_hidden * by_second).astype(jnp.bfloat16)
+            own, other = parted(rows_by_rows(grad_both[rows, :], in_ref[...]))
+            scatter.sums[chip, :, :features] = own.astype(jnp.bfloat16)
+            other_part[chip, :, :features] = other.astype(jnp.bfloat16)
+            own, other = parted(jnp.where(lane == expert, grad_gate, 0.0))
+            scatter.sums[chip, :, features:] = own.astype(jnp.bfloat16)
+            other_part[chip, :, features:] = other.astype(jnp.bfloat16)
+            scatter.on_core(chip).start()
+
+        @pl.loop(0, depth)
+        def _(turn):
+            of_z = nearest(depth - 1 - turn)
+            backward(of_z * 2 + 1 - y)
+            pl.when(turn > 0)(lambda: scatter.add_chip(nearest(depth - turn), False))
+            backward(of_z * 2 + y)
+            scatter.add_chip(of_z, True)
+
+        scatter.add_chip(nearest(0), False)
+
+        def result_copy(chip):
+            target = {"ctx": ctx_of(z, y, 1 - c)}
+            return remote(
+                other_result.at[chip], result_from.at[chip], result_sems, (chip,), target
+            )
+
+        @pl.loop(0, chips)
+        def _(chip):
+            result = jnp.dot(
+                gated_hidden[chip_rows(chip), :], out_ref[...], preferred_element_type=jnp.float32
+            )
+            own, other = parted(result)
+            results[chip] = own.astype(jnp.bfloat16)
+            other_result[chip] = other.astype(jnp.bfloat16)
+            result_copy(chip).start()
+
+        scatter.add_y_of(nearest(depth - 1))
+
+        @pl.loop(0, features // 512)
+        def _(turn):
+            at = pl.ds(pl.multiple_of(turn * 512, 512), 512)
+            grad_out[:, at] = columns_by_columns(gated_hidden[...], d_out_ref[:, at])
+
+        scatter.add_y_of(nearest(depth - 2))
+
+        @pl.loop(0, features // 256)
+        def _(turn):
+            at = pl.ds(pl.multiple_of(turn * 256, 256), 256)
+            grad_in[at, :] = columns_by_columns(hidden_all[:, at], grad_both[...])
+
+        for k in range(depth - 3, -1, -1):
+            scatter.add_y_of(nearest(k))
+
+        @pl.loop(0, chips)
+        def _(chip):
+            result_copy(chip).wait_recv()
+            add_into(results.at[chip], (results.at[chip], result_from.at[chip]), tokens)
+
+        scatter.last(returned)
+        scatter.finish()
+        for chip in range(chips):
+            result_copy(chip).wait_send()
+
+    block = (chips, tokens, features)
+    out = [
+        jax.ShapeDtypeStruct((tokens, wide), jnp.float32),
+        jax.ShapeDtypeStruct(block, jnp.bfloat16),
+        jax.ShapeDtypeStruct(in_matrix.shape, jnp.float32),
+        jax.ShapeDtypeStruct(out_matrix.shape, jnp.float32),
+    ]
+    scratch = [
+        pltpu.VMEM((length, wide), jnp.bfloat16),
+        pltpu.VMEM((length, 2 * width), jnp.bfloat16),
+        pltpu.VMEM((length, width), jnp.bfloat16),
+        pltpu.VMEM((chips, tokens, wide), jnp.bfloat16),
+        pltpu.VMEM(block, jnp.bfloat16),
+        pltpu.VMEM(block, jnp.bfloat16),
+        pltpu.SemaphoreType.DMA((2, chips)),
+    ]
+    scratch += Gather.sems(depth) + Scatter.scratch(depth, tokens, wide)
+    return call(
+        kernel, out, scratch, 3, "experts", send, d_out_all, in_matrix, out_matrix
     )
 
 
@@ -1139,38 +1297,10 @@
     gates_low = (gates - gates_high.astype(jnp.float32)).astype(jnp.bfloat16)
     spare = jnp.zeros((tokens, 128 - 2 * experts), jnp.bfloat16)
     send = jnp.concatenate([hidden_two, gates_high, gates_low, spare], axis=1)
-    hidden_all = gather_ctx(send, 3, "gather_hidden")
-
-    rows = hidden_all[:, :D]
-    expert = me // 2
-    lane = jnp.arange(128, dtype=jnp.int32)[None, :]
-    gate = jnp.sum(
-        jnp.where(
-            (lane == expert) | (lane == expert + experts), hidden_all[:, D:].astype(jnp.float32), 0.0
-        ),
-        axis=1,
-        keepdims=True,
-    )
-    both = jnp.dot(rows, in_matrix, preferred_element_type=jnp.float32)
     width = 2 * quarter
-
-    def gate_unit(first, second):
-        return jax.nn.gelu(first, approximate=True) * second
-
-    hidden, unit_back = jax.vjp(gate_unit, both[:, :width], both[:, width:])
-    hidden_gated = (hidden * gate).astype(jnp.bfloat16)
-    result = jnp.dot(hidden_gated, out_matrix, preferred_element_type=jnp.float32)
-    grad_hidden = rows_by_rows(d_out_all, out_matrix)
-    grad_gate = jnp.sum(grad_hidden * hidden, axis=1, keepdims=True)
-    grad_both = jnp.concatenate(unit_back(grad_hidden * gate), axis=1).astype(jnp.bfloat16)
-    grad_rows = rows_by_rows(grad_both, in_matrix)
-    gate_columns = jnp.where(lane == expert, grad_gate, 0.0)
-    grad_send = jnp.concatenate([grad_rows, gate_columns], axis=1).astype(jnp.bfloat16)
-    returned = scatter_ctx(grad_send, 4, "scatter_grad_rows")
-    result_sum = scatter_ctx(result.astype(jnp.bfloat16), 5, "scatter_result")
-    output = (middle + result_sum).astype(jnp.bfloat16)
-    grad_in_matrix = columns_by_columns(rows, grad_both)
-    grad_out_matrix = columns_by_columns(hidden_gated, d_out_all)
+    returned, results, grad_in_matrix, grad_out_matrix = run_experts(
+        send, d_out_all, in_matrix, out_matrix, experts
+    )
 
     grad_out = d_out[0].astype(jnp.float32)
     grad_gates = returned[:, D : D + experts]
@@ -1187,12 +1317,12 @@
     grad_mixed = whole(
         rows_by_rows(grad_middle_low, w_out_attn), rows_by_rows(grad_middle_low, w_out_attn_there)
     ).astype(jnp.bfloat16)
-    grad_query, grad_keyval = attend_back(
-        query, keyval_all, seq_ids, doc_column, level, mixed, grad_mixed
-    )
+    grad_query, grad_keyval_own, result_sum = attend_back(
+        query, keyval_all, seq_ids, doc_column, level, mixed, grad_mixed, results
+    )
+    output = (middle + result_sum).astype(jnp.bfloat16)
     grad_query_pre = rotate(grad_query.reshape(tokens, HEADS, HEAD_DIM), -angles)
     grad_query_pre = grad_query_pre.reshape(tokens, D).astype(jnp.bfloat16)
-    grad_keyval_own = scatter_ctx(grad_keyval, 6, "scatter_grad_kv")
     grad_keys = rotate(
         grad_keyval_own[:, :kv_width].reshape(tokens, KV_HEADS, HEAD_DIM), -angles
     ).reshape(tokens, kv_width)

time: 515 us -> 474 us (0.920)
  matrix products: 63.2 us -> 20.8 us
  local copies, waits for them, and re-layouts: 35.7 us -> 45.2 us
  Pallas kernels: 359 us -> 352 us
    dot_general x3 -> x1, matrix products: 17.3 us -> 2.02 us  [columns_by_columns(): lax.dot_general(left, right, (((0,), (0,)), ((), ())), preferred_element_...]
    dot_general x2 -> x0, matrix products: 13.8 us -> none  [the longest x1 7.33 us: gathered_body(): both = jnp.dot(rows, in_matrix, preferred_element_type=jnp.float32)]
    dot_general x9 -> x7, matrix products: 21.7 us -> 8.7 us  [rows_by_rows(): lax.dot_general(left, right, (((1,), (1,)), ((), ())), preferred_element_...]
    pallas_call x9 -> x6, Pallas kernels: 359 us -> 352 us  [call(): pl.pallas_call(kernel, out_shape=out, in_specs=[spec(i, outside) for i in...]
    unnamed x123 -> x119, local copies, waits for them, and re-layouts: 5.37 us -> 10.6 us
  transfers between devices with their start and end apart: 5 -> 5, of which waited for: 0 -> 0; matrix products, arithmetic and copies ran while one was open for 22% -> 18% of each run, Pallas kernels for 42% -> 45%
where the time goes in v3:
time: 474 us; the launch traced here: 465 us
  Pallas kernels  352 us (74%)
  local copies, waits for them, and re-layouts  45.2 us (10%)
  other arithmetic  39.5 us (8%)
  matrix products  20.8 us (4%)
  starting transfers between devices  5.63 us (1%)
    pallas_call x6, Pallas kernels, call(): pl.pallas_call(kernel, out_shape=out, in_specs=[spec(i, outside) for i in...  352 us
    unnamed x119, local copies, waits for them, and re-layouts  10.6 us
  transfers between devices with their start and end apart: 5, of which 0 were waited for; matrix products, arithmetic and copies ran while one was open for 18% of the time, Pallas kernels for 45%

profile of v3, /device:TPU:0, one launch (start us, length us, event | category | flops | bytes accessed | tf_op | source)
XLA Modules:
  0.0 465.4 jit_solution(4514975812648044358)
XLA Ops:
  3.4 58.3 %front.1 = (bf16[2048,1536]{1,0:T(8,128)(2,1)}, bf16[768,1536]{1,0:T(8,128)(2,1)}, bf16[768,512]{1,0:T(8,128)(2,1)}, bf16[768,1536]{1,0:T(8,128)(2,1)}, bf16[16,768]{1,0:T(8,128)(2,1)}) custom-call(bf16[128,1536]{1,0:T(8,128)(2,1)} %bitcast.84, bf16[768,1536]{1,0:T(8,128)(2,1)} %query_ref.1, bf16[768,512]{1,0:T(8,128)(2,1)} %keyval_ref.1, ...), custom_call_target="tpu_custom_call" | custom-call | tf_op jit(solution)/shard_map/front/pallas_call | solution.py:659
  61.6 1.6 collective-permute-start
  67.4 1.8 constant_dynamic-slice_fusion.5
  69.2 1.5 collective-permute-start.2
  71.2 2.4 fusion.34
  77.1 1.7 convolution_add_fusion.1
  79.1 1.6 fusion.17
  83.2 20.0 %gather_kv.1.keyval.keyval_ref = bf16[2048,512]{1,0:T(8,128)(2,1)} custom-call(bf16[128,512]{1,0:T(8,128)(2,1)} %pad_maximum_fusion.5.block_ref), custom_call_target="tpu_custom_call" | custom-call | tf_op jit(solution)/shard_map/gather_kv/pallas_call | solution.py:659
  104.8 10.5 %attend.1 = (f32[128,1536]{1,0:T(8,128)}, f32[1536,1]{1,0:T(8,128)}) custom-call(bf16[128,1536]{1,0:T(8,128)(2,1)} %copy.86.query.query_ref, bf16[2048,512]{1,0:T(8,128)(2,1)} %gather_kv.1.keyval.keyval_ref, s32[1,2048]{1,0:T(1,128)} %doc_row_ref.1, s32[128,1]{1,0:T(8,128)} %copy.87.doc_column.doc_column_ref), custom_call_target="tpu_custom_call" | custom-call | tf_op jit(solution)/shard_map/attend/pallas_call | solution.py:659
  118.2 1.5 multiply_reduce_fusion.2
  126.7 2.5 copy.91
  129.2 1.5 copy.99
  133.3 1.9 concatenate.67.send_ref
  135.2 2.6 slice_bitcast_fusion.1
  137.9 2.3 pad_maximum_fusion.1.out_ref
  140.2 2.3 fusion.32
  142.5 2.2 copy.104
  144.7 2.2 copy.103
  147.0 3.9 pad_maximum_fusion.in_ref
  151.0 115.8 %experts.1 = (f32[128,1664]{1,0:T(8,128)}, bf16[8,128,1536]{2,1,0:T(8,128)(2,1)}, f32[1536,768]{1,0:T(8,128)}, f32[384,1536]{1,0:T(8,128)}) custom-call(bf16[128,1664]{1,0:T(8,128)(2,1)} %concatenate.67.send_ref, bf16[2048,1536]{1,0:T(8,128)(2,1)} %get-tuple-element.40.d_out_ref, bf16[1536,768]{1,0:T(8,128)(2,1)} %pad_maximum_fusion.in_ref, ...), custom_call_target="tpu_custom_call" | custom-call | tf_op jit(solution)/shard_map/experts/pallas_call | solution.py:659
  267.9 2.4 multiply_reduce_fusion
  274.1 63.3 %attend_back.1 = (f32[128,1536]{1,0:T(8,128)}, f32[128,512]{1,0:T(8,128)}, f32[128,1536]{1,0:T(8,128)}) custom-call(bf16[128,1536]{1,0:T(8,128)(2,1)} %copy.86.query.query_ref, bf16[2048,512]{1,0:T(8,128)(2,1)} %gather_kv.1.keyval.keyval_ref, s32[1,2048]{1,0:T(1,128)} %doc_row_ref.1, s32[128,1]{1,0:T(8,128)} %copy.87.doc_column.doc_column_ref, ...), custom_call_target="tpu_custom_call" | custom-call | tf_op jit(solution)/shard_map/attend_back/pallas_call | solution.py:659
  343.7 2.0 fusion.28
  345.7 2.3 copy.97
  349.5 2.7 convolution_add_fusion.3
  358.1 2.1 slice.197.refs_11_
  360.9 1.5 pad_maximum_fusion.2.refs_10_
  362.4 84.6 %finish.1 = (bf16[768,1536]{1,0:T(8,128)(2,1)}, bf16[768,1536]{1,0:T(8,128)(2,1)}, bf16[768,512]{1,0:T(8,128)(2,1)}, f32[16,768]{1,0:T(8,128)}, bf16[1536,384]{1,0:T(8,128)(2,1)}, /*index=5*/bf16[192,1536]{1,0:T(8,128)(2,1)}) custom-call(bf16[128,768]{1,0:T(8,128)(2,1)} %get-tuple-element.133.refs_0_, bf16[128,768]{1,0:T(8,128)(2,1)} %collective-permute-done.2.refs_1_, ...), custom_call_target="tpu_custom_call" | custom-call | tf_op jit(solution)/shard_map/finish/pallas_call | solution.py:659
  449.8 4.6 convert_element_type.101
  456.7 2.8 convert_element_type.103
  460.2 2.2 copy.101
  462.3 2.6 add_bitcast_fusion.2
  (199 shorter events, 52.2 us)
Async XLA Ops:
  3.3 60.4 %copy-start.36 = (bf16[768,8]{0,1:T(8,128)(2,1)S(1)}, bf16[768,8]{0,1:T(8,128)(2,1)}, u32[]{:S(2)}) copy-start(bf16[768,8]{0,1:T(8,128)(2,1)} %param.20) | copy-start | bytes 36868
  3.4 61.9 %copy-start.3 = (bf16[1,128,1536]{2,1,0:T(8,128)(2,1)S(1)}, bf16[1,128,1536]{2,1,0:T(8,128)(2,1)}, u32[]{:S(2)}) copy-start(bf16[1,128,1536]{2,1,0:T(8,128)(2,1)} %param.12) | copy-start | bytes 1179652
  3.4 67.9 %copy-start.1 = (bf16[768,1536]{1,0:T(8,128)(2,1)S(1)}, bf16[768,1536]{1,0:T(8,128)(2,1)}, u32[]{:S(2)}) copy-start(bf16[768,1536]{1,0:T(8,128)(2,1)} %query_ref.1) | copy-start | bytes 7077892
  61.6 78.6 %collective-permute-start = (bf16[2,1536,192]{1,2,0:T(8,128)(2,1)}, bf16[2,1536,192]{1,2,0:T(8,128)(2,1)}, u32[]{:S(2)}, u32[]{:S(2)}) collective-permute-start(bf16[2,1536,192]{1,2,0:T(8,128)(2,1)} %bitcast.86), channel_id=1, source_target_pairs={{0,1},{1,0},{2,3},{3,2},{4,5},{5,4},{6,7},{7,6},{8,9},{9,8},{10,11... | collective-permute-start | bytes 3538952 | tf_op jit(solution)/shard_map/ppermute | solution.py:1227
  63.2 74.7 %collective-permute-start.1 = (bf16[192,1536]{1,0:T(8,128)(2,1)}, bf16[192,1536]{1,0:T(8,128)(2,1)}, u32[]{:S(2)}, u32[]{:S(2)}) collective-permute-start(bf16[192,1536]{1,0:T(8,128)(2,1)} %bitcast.13), channel_id=1, source_target_pairs={{0,1},{1,0},{2,3},{3,2},{4,5},{5,4},{6,7},{7,6},{8,9},{9,8},{10,11... | collective-permute-start | bytes 1769480 | tf_op jit(solution)/shard_map/ppermute | solution.py:1227
  66.5 7.1 %copy-start.8 = (bf16[768,512]{1,0:T(8,128)(2,1)S(1)}, bf16[768,512]{1,0:T(8,128)(2,1)}, u32[]{:S(2)}) copy-start(bf16[768,512]{1,0:T(8,128)(2,1)} %keyval_ref.1) | copy-start | bytes 2359300
  69.2 293.2 %collective-permute-start.2 = (bf16[128,768]{1,0:T(8,128)(2,1)}, bf16[128,768]{1,0:T(8,128)(2,1)}, u32[]{:S(2)}, u32[]{:S(2)}) collective-permute-start(bf16[128,768]{1,0:T(8,128)(2,1)} %get-tuple-element.132), channel_id=1, source_target_pairs={{0,1},{1,0},{2,3},{3,2},{4,5},{5,4},{6,7},{7,6},{8,9},{9,8},{10,11... | collective-permute-start | bytes 589832 | tf_op jit(solution)/shard_map/ppermute | solution.py:1227
  103.2 14.5 %copy-start = (bf16[768,1536]{1,0:T(8,128)(2,1)S(1)}, bf16[768,1536]{1,0:T(8,128)(2,1)}, u32[]{:S(2)}) copy-start(bf16[768,1536]{1,0:T(8,128)(2,1)} %attn_ref.1) | copy-start | bytes 7077892
  117.1 245.2 %collective-permute-start.3 = (bf16[128,768]{1,0:T(8,128)(2,1)}, bf16[128,768]{1,0:T(8,128)(2,1)}, u32[]{:S(2)}, u32[]{:S(2)}) collective-permute-start(bf16[128,768]{1,0:T(8,128)(2,1)} %get-tuple-element.130), channel_id=1, source_target_pairs={{0,1},{1,0},{2,3},{3,2},{4,5},{5,4},{6,7},{7,6},{8,9},{9,8},{10,11... | collective-permute-start | bytes 589832 | tf_op jit(solution)/shard_map/ppermute | solution.py:1227
  150.9 115.9 %copy-start.28 = (f32[128,8]{1,0:T(8,128)S(1)}, f32[128,8]{1,0:T(8,128)}, u32[]{:S(2)}) copy-start(f32[128,8]{1,0:T(8,128)} %copy-done.27) | copy-start | bytes 12292
  150.9 115.9 %copy-start.40 = (f32[128]{0:T(128)S(1)}, f32[128]{0:T(128)}, u32[]{:S(2)}) copy-start(f32[128]{0:T(128)} %copy-done.39) | copy-start | bytes 1540
  150.9 115.9 %copy-start.43 = (f32[128]{0:T(128)S(1)}, f32[128]{0:T(128)}, u32[]{:S(2)}) copy-start(f32[128]{0:T(128)} %copy-done.42) | copy-start | bytes 1540
  150.9 116.9 %copy-start.37 = (bf16[16,1536]{1,0:T(8,128)(2,1)S(1)}, bf16[16,1536]{1,0:T(8,128)(2,1)}, u32[]{:S(2)}) copy-start(bf16[16,1536]{1,0:T(8,128)(2,1)} %get-tuple-element.117) | copy-start | bytes 147460
  150.9 116.9 %copy-start.47 = (f32[128]{0:T(128)S(1)}, f32[128]{0:T(128)}, u32[]{:S(2)}) copy-start(f32[128]{0:T(128)} %get-tuple-element.149) | copy-start | bytes 1540
  150.9 119.4 %copy-start.21 = (bf16[1,128,1536]{2,1,0:T(8,128)(2,1)S(1)}, bf16[1,128,1536]{2,1,0:T(8,128)(2,1)}, u32[]{:S(2)}) copy-start(bf16[1,128,1536]{2,1,0:T(8,128)(2,1)} %param.23) | copy-start | bytes 1179652
  150.9 119.4 %copy-start.51 = (f32[128]{0:T(128)S(1)}, f32[128]{0:T(128)}, u32[]{:S(2)}) copy-start(f32[128]{0:T(128)} %get-tuple-element.148) | copy-start | bytes 1540
  274.1 65.3 %copy-start.33 = (f32[128,64]{1,0:T(8,128)S(1)}, f32[128,64]{1,0:T(8,128)}, u32[]{:S(2)}) copy-start(f32[128,64]{1,0:T(8,128)} %copy.99) | copy-start | bytes 98308
  274.1 65.3 %copy-start.34 = (f32[128,64]{1,0:T(8,128)S(1)}, f32[128,64]{1,0:T(8,128)}, u32[]{:S(2)}) copy-start(f32[128,64]{1,0:T(8,128)} %copy.98) | copy-start | bytes 98308
  274.1 65.8 %copy-start.9 = (bf16[768,512]{1,0:T(8,128)(2,1)S(1)}, bf16[768,512]{1,0:T(8,128)(2,1)}, u32[]{:S(2)}) copy-start(bf16[768,512]{1,0:T(8,128)(2,1)} %keyval_ref.1) | copy-start | bytes 2359300
  337.4 6.3 %copy-start.41 = (f32[128]{0:T(128)S(1)}, f32[128]{0:T(128)}, u32[]{:S(2)}) copy-start(f32[128]{0:T(128)} %copy-done.39) | copy-start | bytes 1540
  337.4 6.3 %copy-start.44 = (f32[128]{0:T(128)S(1)}, f32[128]{0:T(128)}, u32[]{:S(2)}) copy-start(f32[128]{0:T(128)} %copy-done.42) | copy-start | bytes 1540
  342.2 7.2 %copy-start.2 = (bf16[768,1536]{1,0:T(8,128)(2,1)S(1)}, bf16[768,1536]{1,0:T(8,128)(2,1)}, u32[]{:S(2)}) copy-start(bf16[768,1536]{1,0:T(8,128)(2,1)} %query_ref.1) | copy-start | bytes 7077892
  342.2 20.2 %collective-permute-start.4 = (bf16[128,1536]{1,0:T(8,128)(2,1)}, bf16[128,1536]{1,0:T(8,128)(2,1)}, u32[]{:S(2)}, u32[]{:S(2)}) collective-permute-start(bf16[128,1536]{1,0:T(8,128)(2,1)} %copy-done.12), channel_id=1, source_target_pairs={{0,1},{1,0},{2,3},{3,2},{4,5},{5,4},{6,7},{7,6},{8,9},{9,8},{10,11... | collective-permute-start | bytes 1179656 | tf_op jit(solution)/shard_map/ppermute | solution.py:1227
  348.0 4.2 copy-start.5
  348.0 4.2 copy-start.22
  348.0 5.5 %slice-start = ((s8[4718592]{0:T(1024)(128)(4,1)}), s8[4194304]{0:T(1024)(128)(4,1)S(1)}, s32[]{:S(2)}) async-start(s8[4718592]{0:T(1024)(128)(4,1)} %bitcast.73), calls=%async_computation | async-start | bytes 8388608
  349.5 4.0 slice-start.1
  355.1 5.1 %copy-start.24 = (bf16[128,256]{1,0:T(8,128)(2,1)S(1)}, bf16[128,256]{1,0:T(8,128)(2,1)}, u32[]{:S(2)}) copy-start(bf16[128,256]{1,0:T(8,128)(2,1)} %copy-done.23) | copy-start | bytes 196612
  355.1 5.1 %copy-start.26 = (bf16[16,8,2,128]{3,1,2,0:T(8,128)(2,1)S(1)}, bf16[16,8,2,128]{3,1,2,0:T(8,128)(2,1)}, u32[]{:S(2)}) copy-start(bf16[16,8,2,128]{3,1,2,0:T(8,128)(2,1)} %copy-done.25) | copy-start | bytes 196612
  449.8 4.7 %copy-start.29 = (bf16[768,512]{1,0:T(8,128)(2,1)S(1)}, bf16[768,512]{1,0:T(8,128)(2,1)}, u32[]{:S(2)}) copy-start(bf16[768,512]{1,0:T(8,128)(2,1)} %get-tuple-element.52) | copy-start | bytes 2359300
  449.8 9.7 %slice-start.2 = ((s8[4718592]{0:T(1024)(128)(4,1)}), s8[4194304]{0:T(1024)(128)(4,1)S(1)}, s32[]{:S(2)}) async-start(s8[4718592]{0:T(1024)(128)(4,1)} %bitcast.75), calls=%async_computation.2 | async-start | bytes 8388608
  454.4 5.1 %slice-start.3 = ((s8[4718592]{0:T(1024)(128)(4,1)}), s8[524288]{0:T(1024)(128)(4,1)S(1)}, s32[]{:S(2)}) async-start(s8[4718592]{0:T(1024)(128)(4,1)} %bitcast.75), calls=%async_computation.3 | async-start | bytes 1048576
  (30 other events, 61.0 us)

commit v4 on v3

--- a/solution.py
+++ b/solution.py
@@ -516,8 +516,11 @@
                 self.on_core(of_z, of_y).wait_send()
                 self.on_core(of_z, of_y, mine=False).wait_recv()
 
-    def run(self, source=None):
-        self.start(source)
+    def run(self):
+        self.start()
+        self.follow()
+
+    def follow(self):
         self.along_z(1)
         self.along_y(0)
         for step in range(1, self.depth):
@@ -669,19 +672,6 @@
         ),
         name=name,
     )(*operands)
-
-
-def gather_ctx(block, number, name):
-    count, rows = lax.axis_size("ctx"), block.shape[0]
-
-    def kernel(block_ref, out, *sems):
-        gather = Gather(out, rows, sems)
-        gather.own()[...] = block_ref[...]
-        greet()
-        gather.run()
-
-    out = jax.ShapeDtypeStruct((count * rows, block.shape[1]), block.dtype)
-    return call(kernel, out, Gather.sems(count // 4), number, name, block)
 
 
 class Relay:
@@ -796,144 +786,6 @@
     )
 
 
-def finish(hidden, hidden_there, mixed, mixed_there, middle, middle_there, query, keyval, small, small_other, expert_in, expert_out):
-    count = lax.axis_size("ctx")
-    depth, tokens, half = count // 4, hidden.shape[0], hidden.shape[1]
-    rows = half // count
-    widths = (middle.shape[1], query.shape[1], keyval.shape[1])
-
-    def kernel(*refs):
-        (hidden_ref, hidden_there_ref, mixed_ref, mixed_there_ref, middle_ref, middle_there_ref,
-         query_ref, keyval_ref, small_ref, small_other_ref, in_ref, out_ref) = refs[:12]
-        attn_sum, query_sum, keyval_sum, small_sum, in_there, out_there = refs[12:18]
-        (attn_part, query_part, keyval_part, pair, query_there, keyval_there, small_there,
-         small_all, x_sems) = refs[18:27]
-        scratch = refs[27:]
-        scatters, gathers = [], []
-        parts, sums = (attn_part, query_part, keyval_part), (attn_sum, query_sum, keyval_sum)
-        for part, total in zip(parts, sums):
-            scatters.append(Scatter(part, scratch[:7]))
-            gathers.append(Gather(total, rows, scratch[7:10]))
-            scratch = scratch[10:]
-        small_gather = Gather(small_all, small.shape[0], scratch)
-        (attn, query_, keyval_), (attn_out, query_out, keyval_out) = scatters, gathers
-        partner = {"wa": 1 - lax.axis_index("wa")}
-        swaps = [
-            remote(source, target, x_sems, (i,), partner)
-            for i, (source, target) in enumerate(
-                [(small_other_ref, small_there), (query_ref, query_there), (keyval_ref, keyval_there),
-                 (in_ref, in_there), (out_ref, out_there)]
-            )
-        ]
-        greet(across_x=True)
-        for swap in swaps:
-            swap.start()
-
-        def products(left, left_there, right, right_there, part):
-            pair[:tokens] = left[...]
-            pair[tokens:] = left_there[...]
-            width = part.shape[1]
-
-            @pl.loop(0, width // 512)
-            def _(turn):
-                at = pl.ds(pl.multiple_of(turn * 512, 512), 512)
-                both = jnp.concatenate([right[:, at], right_there[:, at]], axis=0)
-                part[:, at] = columns_by_columns(pair[...], both).astype(jnp.bfloat16)
-
-        steps = range(depth - 1, -1, -1)
-        products(mixed_ref, mixed_there_ref, middle_ref, middle_there_ref, attn_part)
-        attn.start()
-        for step in steps:
-            attn.add_cores(step)
-        swaps[0].wait()
-        small_gather.own()[...] = (small_ref[...] + small_there[...]).astype(jnp.bfloat16)
-        swaps[1].wait()
-        products(hidden_ref, hidden_there_ref, query_ref, query_there, query_part)
-        query_.start()
-        for step in steps:
-            query_.add_cores(step)
-        swaps[2].wait()
-        products(hidden_ref, hidden_there_ref, keyval_ref, keyval_there, keyval_part)
-        keyval_.start()
-        for step in steps:
-            keyval_.add_cores(step)
-        for step in steps:
-            attn.add_y(step)
-        attn.last(attn_out.own())
-        attn_out.start()
-        small_gather.start()
-        for step in steps:
-            query_.add_y(step)
-        attn_out.along_z(1)
-        query_.last(query_out.own())
-        query_out.start()
-        attn_out.along_z(2)
-        attn_out.along_y(0)
-        small_gather.along_z(1)
-        for step in steps:
-            keyval_.add_y(step)
-        attn_out.along_z(3)
-        attn_out.along_y(1)
-        keyval_.last(keyval_out.own())
-        keyval_out.start()
-        query_out.along_z(1)
-        small_gather.along_z(2)
-        attn_out.along_y(2)
-        query_out.along_z(2)
-        small_gather.along_z(3)
-        query_out.along_y(0)
-        keyval_out.along_z(1)
-        query_out.along_z(3)
-        attn_out.along_y(3)
-        keyval_out.along_z(2)
-        query_out.along_y(1)
-        keyval_out.along_z(3)
-        query_out.along_y(2)
-        small_gather.along_y(0)
-        keyval_out.along_y(0)
-        small_gather.along_y(1)
-        query_out.along_y(3)
-        keyval_out.along_y(1)
-        small_gather.along_y(2)
-        keyval_out.along_y(2)
-        small_gather.along_y(3)
-        keyval_out.along_y(3)
-        for one in [small_gather] + gathers + scatters:
-            one.finish()
-        small_rows = small.shape[0]
-        total = small_all[:small_rows].astype(jnp.float32)
-        for device in range(1, count):
-            rows_of = slice(device * small_rows, (device + 1) * small_rows)
-            total = total + small_all[rows_of].astype(jnp.float32)
-        small_sum[...] = total
-        swaps[3].wait()
-        swaps[4].wait()
-
-    out = [jax.ShapeDtypeStruct((half, width), jnp.bfloat16) for width in widths]
-    out += [
-        jax.ShapeDtypeStruct(small.shape, jnp.float32),
-        jax.ShapeDtypeStruct(expert_in.shape, expert_in.dtype),
-        jax.ShapeDtypeStruct(expert_out.shape, expert_out.dtype),
-    ]
-    scratch = [pltpu.VMEM((half, width), jnp.bfloat16) for width in widths]
-    scratch += [
-        pltpu.VMEM((2 * tokens, half), jnp.bfloat16),
-        pltpu.VMEM(query.shape, jnp.bfloat16),
-        pltpu.VMEM(keyval.shape, jnp.bfloat16),
-        pltpu.VMEM(small.shape, jnp.float32),
-        pltpu.VMEM((count * small.shape[0], small.shape[1]), jnp.bfloat16),
-        pltpu.SemaphoreType.DMA((2, 5)),
-    ]
-    for width in widths:
-        scratch += Scatter.scratch(depth, rows, width) + Gather.sems(depth)
-    scratch += Gather.sems(depth)
-    return call(
-        kernel, out, scratch, 1, "finish",
-        hidden, hidden_there, mixed, mixed_there, middle, middle_there, query, keyval, small,
-        small_other, expert_in, expert_out, outside=(10, 11), outside_out=(4, 5),
-    )
-
-
 def rows_by_rows(left, right):
     return lax.dot_general(
         left, right, (((1,), (1,)), ((), ())), preferred_element_type=jnp.float32
@@ -954,69 +806,210 @@
     return jnp.where(allowed, 0.0, NEGATIVE)
 
 
-def attend_kernel(query, keyval, doc_row, doc_column, mixed, level, stacked, bias):
-    tokens = query.shape[0]
-    bias[...] = allowed_bias(doc_row[...], doc_column[...], tokens)
-    for head in range(HEADS):
-        stacked[head * tokens : (head + 1) * tokens, :] = query[:, head * 128 : (head + 1) * 128]
-
-    @pl.loop(0, HEADS // 2)
-    def _(pair):
-        rows = pl.ds(pl.multiple_of(pair * 2 * tokens, 128), 2 * tokens)
-        kind = pair // (HEADS // KV_HEADS // 2)
-        keys = keyval[:, pl.ds(pl.multiple_of(kind * 128, 128), 128)]
-        vals = keyval[:, pl.ds(pl.multiple_of(kind * 128 + 256, 128), 128)]
-        scores = rows_by_rows(stacked[rows, :], keys) * HEAD_DIM**-0.5
-        scores = (scores.reshape(2, tokens, -1) + bias[...][None]).reshape(scores.shape)
-        top = jnp.max(scores, axis=-1, keepdims=True)
-        weights = jnp.exp(scores - top)
-        total = jnp.sum(weights, axis=-1, keepdims=True)
-        probs = (weights / total).astype(jnp.bfloat16)
-        mixture = jnp.dot(probs, vals, preferred_element_type=jnp.float32)
-        for half in range(2):
-            columns = pl.ds(pl.multiple_of((pair * 2 + half) * 128, 128), 128)
-            mixed[:, columns] = mixture[half * tokens : (half + 1) * tokens]
-        level[rows, :] = top + jnp.log(total)
-
-
-def attend(query, keyval, doc_row, doc_column):
-    tokens, keys = query.shape[0], keyval.shape[0]
-    out = (
-        jax.ShapeDtypeStruct(query.shape, jnp.float32),
-        jax.ShapeDtypeStruct((HEADS * tokens, 1), jnp.float32),
-    )
+def side_columns(own):
+    side = lax.axis_index("wa")
+    return pl.ds(pl.multiple_of((side if own else 1 - side) * (D // 2), 128), D // 2)
+
+
+def turned(values, cosine, sine):
+    heads = []
+    for head in range(values.shape[1] // HEAD_DIM):
+        one = values[:, head * HEAD_DIM : (head + 1) * HEAD_DIM]
+        heads.append(one * cosine + pltpu.roll(one, HEAD_DIM // 2, axis=1) * sine)
+    return jnp.concatenate(heads, axis=1)
+
+
+def normed(values, gain_vec):
+    return values * lax.rsqrt(jnp.mean(values * values, axis=-1, keepdims=True) + EPSILON) * gain_vec
+
+
+def fill_small(full, small, small_there):
+    full[:, side_columns(True)] = small[...].astype(jnp.float32)
+    full[:, side_columns(False)] = small_there[...].astype(jnp.float32)
+
+
+def router_block(full, experts):
+    rows = full[:experts]
+    spare = jnp.zeros((128 - 2 * experts, rows.shape[1]), jnp.float32)
+    return jnp.concatenate([rows, rows, spare], axis=0).astype(jnp.bfloat16)
+
+
+def attend(x, small, small_there, matrices, angles, docs, chosen, experts):
+    count, tokens, features = lax.axis_size("ctx"), x.shape[0], x.shape[1]
+    depth, length = count // 4, count * tokens
+    kv_columns, half = matrices[2].shape[1], features // 2
+
+    def kernel(
+        x_ref, small_ref, small_there_ref, query_own, query_other, keyval_own, keyval_other,
+        attn_own, attn_other, cosine_ref, sine_ref, doc_row, doc_column, chosen_ref,
+        query, keyval, level, mixed, hidden_own, hidden_there, mixed_own, mixed_there, middle,
+        send, gates_out,
+        hidden, mixed_low, full, stacked, bias, x_sems, *sems,
+    ):
+        gather = Gather(keyval, tokens, sems)
+        partner = {"wa": 1 - lax.axis_index("wa")}
+        fill_small(full, small_ref, small_there_ref)
+        residual = x_ref[...].astype(jnp.float32)
+        hidden[...] = normed(residual, full[experts : experts + 1]).astype(jnp.bfloat16)
+        hidden_own[...] = hidden[:, side_columns(True)]
+        own, other = hidden[:, side_columns(True)], hidden[:, side_columns(False)]
+        cosine, sine = cosine_ref[...], sine_ref[...]
+
+        def onto(matrix, matrix_other):
+            return jnp.dot(own, matrix[...], preferred_element_type=jnp.float32) + jnp.dot(
+                other, matrix_other[...], preferred_element_type=jnp.float32
+            )
+
+        pre = onto(keyval_own, keyval_other)
+        keys = turned(pre[:, : kv_columns // 2], cosine, sine)
+        block = jnp.concatenate([keys, pre[:, kv_columns // 2 :]], axis=1)
+        gather.own()[...] = block.astype(jnp.bfloat16)
+        greet(across_x=True)
+        gather.start()
+        swap = remote(hidden.at[:, side_columns(False)], hidden_there, x_sems, (0,), partner)
+        swap.start()
+        query[...] = turned(onto(query_own, query_other), cosine, sine).astype(jnp.bfloat16)
+        bias[...] = allowed_bias(doc_row[...], doc_column[...], tokens)
+        for head in range(HEADS):
+            rows = slice(head * tokens, (head + 1) * tokens)
+            stacked[rows, :] = query[:, head * 128 : (head + 1) * 128]
+        gather.follow()
+
+        @pl.loop(0, HEADS // 2)
+        def _(pair):
+            rows = pl.ds(pl.multiple_of(pair * 2 * tokens, 128), 2 * tokens)
+            kind = pair // (HEADS // KV_HEADS // 2)
+            key_part = keyval[:, pl.ds(pl.multiple_of(kind * 128, 128), 128)]
+            val_part = keyval[:, pl.ds(pl.multiple_of(kind * 128 + 256, 128), 128)]
+            scores = rows_by_rows(stacked[rows, :], key_part) * HEAD_DIM**-0.5
+            scores = (scores.reshape(2, tokens, -1) + bias[...][None]).reshape(scores.shape)
+            top = jnp.max(scores, axis=-1, keepdims=True)
+            weights = jnp.exp(scores - top)
+            total = jnp.sum(weights, axis=-1, keepdims=True)
+            probs = (weights / total).astype(jnp.bfloat16)
+            mixture = jnp.dot(probs, val_part, preferred_element_type=jnp.float32)
+            for part in range(2):
+                columns = pl.ds(pl.multiple_of((pair * 2 + part) * 128, 128), 128)
+                mixed[:, columns] = mixture[part * tokens : (part + 1) * tokens]
+            level[rows, :] = top + jnp.log(total)
+
+        mixed_low[...] = mixed[...].astype(jnp.bfloat16)
+        mixed_own[...] = mixed_low[:, side_columns(True)]
+        swap_mixed = remote(
+            mixed_low.at[:, side_columns(False)], mixed_there, x_sems, (1,), partner
+        )
+        swap_mixed.start()
+        own, other = mixed_low[:, side_columns(True)], mixed_low[:, side_columns(False)]
+        middle[...] = residual + onto(attn_own, attn_other)
+        hidden_two = normed(middle[...], full[experts + 1 : experts + 2]).astype(jnp.bfloat16)
+        send[:, :features] = hidden_two
+        logits = rows_by_rows(hidden_two, router_block(full, experts))
+        lane = lax.broadcasted_iota(jnp.int32, logits.shape, 1)
+        masked = jnp.where(chosen_ref[...] > 0, logits, NEGATIVE)
+        weights = jnp.exp(masked - jnp.max(masked, axis=1, keepdims=True))
+        total = jnp.sum(jnp.where(lane < experts, weights, 0.0), axis=1, keepdims=True)
+        gates = weights / total
+        high = gates.astype(jnp.bfloat16).astype(jnp.float32)
+        carried = jnp.where(lane < experts, high, jnp.where(lane < 2 * experts, gates - high, 0.0))
+        send[:, features:] = carried.astype(jnp.bfloat16)
+        gates_out[...] = jnp.where(lane < experts, gates, 0.0)
+        swap.wait()
+        swap_mixed.wait()
+
+    def shape(rows, columns, kind=jnp.bfloat16):
+        return jax.ShapeDtypeStruct((rows, columns), kind)
+
+    wide = features + 128
+    out = [
+        shape(tokens, features), shape(length, kv_columns), shape(HEADS * tokens, 1, jnp.float32),
+        shape(tokens, features, jnp.float32),
+        shape(tokens, half), shape(tokens, half), shape(tokens, half), shape(tokens, half),
+        shape(tokens, features, jnp.float32), shape(tokens, wide), shape(tokens, 128, jnp.float32),
+    ]
     scratch = [
+        pltpu.VMEM((tokens, features), jnp.bfloat16),
+        pltpu.VMEM((tokens, features), jnp.bfloat16),
+        pltpu.VMEM((small.shape[0], features), jnp.float32),
         pltpu.VMEM((HEADS * tokens, HEAD_DIM), jnp.bfloat16),
-        pltpu.VMEM((tokens, keys), jnp.float32),
-    ]
+        pltpu.VMEM((tokens, length), jnp.float32),
+        pltpu.SemaphoreType.DMA((2, 2)),
+    ] + Gather.sems(depth)
     return call(
-        attend_kernel, out, scratch, None, "attend", query, keyval, doc_row, doc_column
-    )
-
-
-def attend_back(query, keyval, doc_row, doc_column, level, mixed, grad_mixed, results):
-    count, tokens, keys = lax.axis_size("ctx"), query.shape[0], keyval.shape[0]
-    depth = count // 4
+        kernel, out, scratch, 2, "attend",
+        x, small, small_there, *matrices, *angles, *docs, chosen,
+    )
+
+
+def norm_back(values, gain_vec, grad):
+    scale = lax.rsqrt(jnp.mean(values * values, axis=-1, keepdims=True) + EPSILON)
+    through = jnp.mean(gain_vec * grad * values, axis=-1, keepdims=True)
+    back = scale * gain_vec * grad - values * (scale * scale * scale * through)
+    return back, jnp.sum(grad * values * scale, axis=0, keepdims=True)
+
+
+def attend_back(
+    returned, gates, small, small_there, middle, d_out, send, attn_own, attn_other, query, keyval,
+    angles, docs, level, mixed, results, experts,
+):
+    count, tokens, features = lax.axis_size("ctx"), query.shape[0], query.shape[1]
+    depth, length, kv_columns = count // 4, keyval.shape[0], keyval.shape[1]
 
     def kernel(
-        query_ref, keyval_ref, doc_row_ref, doc_column_ref, level_ref, mixed_ref, grad_mixed_ref,
-        results_ref, grad_query, grad_keyval, output,
-        stacked, grads, bias, delta, total, part, *scratch,
+        returned_ref, gates_ref, small_ref, small_there_ref, middle_ref, d_out_ref, send_ref,
+        attn_own_ref, attn_other_ref, query_ref, keyval_ref, cosine_ref, sine_ref, doc_row,
+        doc_column, level_ref, mixed_ref, results_ref,
+        output, grad_middle, grad_middle_low, grad_middle_there, grad_query, grad_query_there,
+        grad_keyval, grad_keyval_there, small_grads,
+        full, grad_mixed, turned_query, own_keyval, result_sum, stacked, grads, bias, delta, total,
+        part, x_sems, *scratch,
     ):
-        result = Scatter(None, (None,) + tuple(scratch[:3]) + (None,) + tuple(scratch[3:5]), results_ref)
+        result = Scatter(
+            None, (None,) + tuple(scratch[:3]) + (None,) + tuple(scratch[3:5]), results_ref
+        )
         keyval_sum = Scatter(part, scratch[5:])
-        greet()
+        partner = {"wa": 1 - lax.axis_index("wa")}
+        swaps = [
+            remote(source, target, x_sems, (i,), partner)
+            for i, (source, target) in enumerate(
+                [(grad_middle_low, grad_middle_there), (grad_query, grad_query_there),
+                 (grad_keyval, grad_keyval_there)]
+            )
+        ]
+        greet(across_x=True)
         for k in (depth - 1, depth - 2):
             result.on_y(nearest(k)).start()
-        bias[...] = allowed_bias(doc_row_ref[...], doc_column_ref[...], tokens)
+        fill_small(full, small_ref, small_there_ref)
+        lane = lax.broadcasted_iota(jnp.int32, (tokens, 128), 1)
+        gates = gates_ref[...]
+        grad_gates = jnp.where(lane < experts, returned_ref[:, features:], 0.0)
+        inner = jnp.sum(gates * grad_gates, axis=1, keepdims=True)
+        grad_logits = (gates * (grad_gates - inner)).astype(jnp.bfloat16)
+        grad_two = returned_ref[:, :features] + jnp.dot(
+            grad_logits, router_block(full, experts), preferred_element_type=jnp.float32
+        )
+        grad_router = columns_by_columns(grad_logits, send_ref[:, :features])
+        back, grad_gain = norm_back(middle_ref[...], full[experts + 1 : experts + 2], grad_two)
+        grad_middle[...] = d_out_ref[...].astype(jnp.float32) + back
+        grad_middle_low[...] = grad_middle[...].astype(jnp.bfloat16)
+        swaps[0].start()
+        small_grads[:experts] = grad_router[:experts]
+        row = lax.broadcasted_iota(jnp.int32, (small_grads.shape[0] - experts, 1), 0)
+        small_grads[experts:] = jnp.where(row == 1, grad_gain, 0.0)
+        grad_mixed[:, side_columns(True)] = rows_by_rows(
+            grad_middle_low[...], attn_own_ref[...]
+        ).astype(jnp.bfloat16)
+        grad_mixed[:, side_columns(False)] = rows_by_rows(
+            grad_middle_low[...], attn_other_ref[...]
+        ).astype(jnp.bfloat16)
+        bias[...] = allowed_bias(doc_row[...], doc_column[...], tokens)
         total[...] = jnp.zeros_like(total)
         for head in range(HEADS):
             rows = slice(head * tokens, (head + 1) * tokens)
             columns = slice(head * 128, head * 128 + 128)
             stacked[rows, :] = query_ref[:, columns]
-            grads[rows, :] = grad_mixed_ref[:, columns]
+            grads[rows, :] = grad_mixed[:, columns]
             delta[rows, :] = jnp.sum(
-                grad_mixed_ref[:, columns].astype(jnp.float32) * mixed_ref[:, columns],
+                grad_mixed[:, columns].astype(jnp.float32) * mixed_ref[:, columns],
                 axis=-1,
                 keepdims=True,
             )
@@ -1037,7 +1030,7 @@
             own_grad = jnp.dot(grad_scores, key_part, preferred_element_type=jnp.float32)
             for half in range(2):
                 columns = pl.ds(pl.multiple_of((pair * 2 + half) * 128, 128), 128)
-                grad_query[:, columns] = (
+                turned_query[:, columns] = (
                     own_grad[half * tokens : (half + 1) * tokens] * HEAD_DIM**-0.5
                 )
             total[:, key_columns] += columns_by_columns(grad_scores, own) * HEAD_DIM**-0.5
@@ -1046,6 +1039,9 @@
 
         part[...] = total[...].astype(jnp.bfloat16)
         keyval_sum.start()
+        cosine, sine = cosine_ref[...], -sine_ref[...]
+        grad_query[...] = turned(turned_query[...], cosine, sine).astype(jnp.bfloat16)
+        swaps[1].start()
         steps = range(depth - 1, -1, -1)
         for step in steps:
             keyval_sum.add_cores(step)
@@ -1054,31 +1050,50 @@
         result.add_y_of(nearest(depth - 2))
         for step in steps:
             keyval_sum.add_y(step)
-        keyval_sum.last(grad_keyval)
+        keyval_sum.last(own_keyval)
+        keys = turned(own_keyval[:, : kv_columns // 2], cosine, sine)
+        grad_keyval[...] = jnp.concatenate(
+            [keys, own_keyval[:, kv_columns // 2 :]], axis=1
+        ).astype(jnp.bfloat16)
+        swaps[2].start()
         for k in range(depth - 3, -1, -1):
             result.add_y_of(nearest(k))
-        result.last(output)
+        result.last(result_sum)
+        output[...] = (middle_ref[...] + result_sum[...]).astype(jnp.bfloat16)
         keyval_sum.finish()
         result.finish(cores=False)
-
+        for swap in swaps:
+            swap.wait()
+
+    def shape(like, kind=jnp.bfloat16):
+        return jax.ShapeDtypeStruct(like, kind)
+
+    rows, narrow = (tokens, features), (tokens, kv_columns)
+    small_shape = (small.shape[0], features)
     out = [
-        jax.ShapeDtypeStruct(query.shape, jnp.float32),
-        jax.ShapeDtypeStruct((tokens, keyval.shape[1]), jnp.float32),
-        jax.ShapeDtypeStruct(query.shape, jnp.float32),
+        shape(rows), shape(rows, jnp.float32), shape(rows), shape(rows), shape(rows), shape(rows),
+        shape(narrow), shape(narrow), shape(small_shape, jnp.float32),
     ]
     scratch = [
+        pltpu.VMEM(small_shape, jnp.float32),
+        pltpu.VMEM(rows, jnp.bfloat16),
+        pltpu.VMEM(rows, jnp.float32),
+        pltpu.VMEM(narrow, jnp.float32),
+        pltpu.VMEM(rows, jnp.float32),
         pltpu.VMEM((HEADS * tokens, HEAD_DIM), jnp.bfloat16),
         pltpu.VMEM((HEADS * tokens, HEAD_DIM), jnp.bfloat16),
-        pltpu.VMEM((tokens, keys), jnp.float32),
+        pltpu.VMEM((tokens, length), jnp.float32),
         pltpu.VMEM((HEADS * tokens, 1), jnp.float32),
         pltpu.VMEM(keyval.shape, jnp.float32),
         pltpu.VMEM(keyval.shape, jnp.bfloat16),
+        pltpu.SemaphoreType.DMA((2, 3)),
     ]
-    wide = Scatter.scratch(depth, tokens, query.shape[1])
-    scratch += wide[1:4] + wide[5:] + Scatter.scratch(depth, tokens, keyval.shape[1])
+    wide = Scatter.scratch(depth, tokens, features)
+    scratch += wide[1:4] + wide[5:] + Scatter.scratch(depth, tokens, kv_columns)
     return call(
         kernel, out, scratch, 4, "attend_back",
-        query, keyval, doc_row, doc_column, level, mixed, grad_mixed, results,
+        returned, gates, small, small_there, middle, d_out, send, attn_own, attn_other, query,
+        keyval, *angles, *docs, level, mixed, results,
     )
 
 
@@ -1092,15 +1107,18 @@
     return gelu * second, slope * second, gelu
 
 
-def run_experts(send, d_out_all, in_matrix, out_matrix, experts):
+def run_experts(send, d_out_all, in_own, out_own, experts):
     count, tokens = lax.axis_size("ctx"), send.shape[0]
     depth, chips, length = count // 4, count // 2, count * tokens
-    wide, features, width = send.shape[1], d_out_all.shape[1], out_matrix.shape[0]
+    wide, features = send.shape[1], d_out_all.shape[1]
+    quarter = out_own.shape[0]
+    width = 2 * quarter
 
     def kernel(
-        send_ref, d_out_ref, in_ref, out_ref, returned, results, grad_in, grad_out,
+        send_ref, d_out_ref, in_own_ref, out_own_ref,
+        returned, results, grad_in, grad_in_other, grad_out, grad_out_other,
         hidden_all, grad_both, gated_hidden, other_part, other_result, result_from, result_sems,
-        *scratch,
+        in_ref, out_ref, x_sems, *scratch,
     ):
         gather = Gather(hidden_all, tokens, scratch[:3])
         scatter = Scatter(other_part, scratch[3:])
@@ -1108,8 +1126,27 @@
         expert = lax.axis_index("ctx") // 2
         lane = lax.broadcasted_iota(jnp.int32, (1, 128), 1)
         gather.own()[...] = send_ref[...]
-        greet()
+        partner = {"wa": 1 - lax.axis_index("wa")}
+        in_there = gated_hidden.at[pl.ds(0, features)]
+        swaps = [
+            remote(in_own_ref, in_there, x_sems, (0,), partner),
+            remote(out_own_ref, out_ref.at[pl.ds(quarter, quarter)], x_sems, (1,), partner),
+        ]
+        greet(across_x=True)
+        for swap in swaps:
+            swap.start()
+        out_ref[:quarter] = out_own_ref[...]
         gather.run()
+        for swap in swaps:
+            swap.wait()
+
+        @pl.loop(0, features // 256)
+        def _(turn):
+            at = pl.ds(pl.multiple_of(turn * 256, 256), 256)
+            own, there = in_own_ref[at, :], gated_hidden[at, :]
+            in_ref[at, :] = jnp.concatenate(
+                [own[:, :quarter], there[:, :quarter], own[:, quarter:], there[:, quarter:]], axis=1
+            )
 
         def chip_rows(chip):
             return pl.ds(pl.multiple_of(chip * 2 * tokens, 16), 2 * tokens)
@@ -1172,14 +1209,22 @@
         @pl.loop(0, features // 512)
         def _(turn):
             at = pl.ds(pl.multiple_of(turn * 512, 512), 512)
-            grad_out[:, at] = columns_by_columns(gated_hidden[...], d_out_ref[:, at])
+            grad = columns_by_columns(gated_hidden[...], d_out_ref[:, at])
+            grad_out[:, at] = grad[:quarter]
+            grad_out_other[:, at] = grad[quarter:].astype(jnp.bfloat16)
 
         scatter.add_y_of(nearest(depth - 2))
 
         @pl.loop(0, features // 256)
         def _(turn):
             at = pl.ds(pl.multiple_of(turn * 256, 256), 256)
-            grad_in[at, :] = columns_by_columns(hidden_all[:, at], grad_both[...])
+            grad = columns_by_columns(hidden_all[:, at], grad_both[...])
+            grad_in[at, :] = jnp.concatenate(
+                [grad[:, :quarter], grad[:, width : width + quarter]], axis=1
+            )
+            grad_in_other[at, :] = jnp.concatenate(
+                [grad[:, quarter:width], grad[:, width + quarter :]], axis=1
+            ).astype(jnp.bfloat16)
 
         for k in range(depth - 3, -1, -1):
             scatter.add_y_of(nearest(k))
@@ -1198,8 +1243,10 @@
     out = [
         jax.ShapeDtypeStruct((tokens, wide), jnp.float32),
         jax.ShapeDtypeStruct(block, jnp.bfloat16),
-        jax.ShapeDtypeStruct(in_matrix.shape, jnp.float32),
-        jax.ShapeDtypeStruct(out_matrix.shape, jnp.float32),
+        jax.ShapeDtypeStruct(in_own.shape, jnp.float32),
+        jax.ShapeDtypeStruct(in_own.shape, jnp.bfloat16),
+        jax.ShapeDtypeStruct(out_own.shape, jnp.float32),
+        jax.ShapeDtypeStruct(out_own.shape, jnp.bfloat16),
     ]
     scratch = [
         pltpu.VMEM((length, wide), jnp.bfloat16),
@@ -1209,168 +1256,276 @@
         pltpu.VMEM(block, jnp.bfloat16),
         pltpu.VMEM(block, jnp.bfloat16),
         pltpu.SemaphoreType.DMA((2, chips)),
+        pltpu.VMEM((features, 2 * width), jnp.bfloat16),
+        pltpu.VMEM((width, features), jnp.bfloat16),
+        pltpu.SemaphoreType.DMA((2, 2)),
     ]
     scratch += Gather.sems(depth) + Scatter.scratch(depth, tokens, wide)
+    return call(kernel, out, scratch, 3, "experts", send, d_out_all, in_own, out_own)
+
+
+def finish(
+    x, grad_middle, small, small_there, small_grads, matrices, hidden, mixed, middle, query, keyval,
+    expert_in, expert_out,
+):
+    count, tokens, half = lax.axis_size("ctx"), x.shape[0], x.shape[1] // 2
+    depth, rows = count // 4, half // count
+    widths = (middle[0].shape[1], query[0].shape[1], keyval[0].shape[1])
+    experts = small.shape[0] // 2
+
+    def kernel(
+        x_ref, grad_middle_ref, small_ref, small_there_ref, small_grads_ref,
+        query_own, query_other, keyval_own, keyval_other,
+        hidden_ref, hidden_there, mixed_ref, mixed_there, middle_ref, middle_there,
+        query_ref, query_there, keyval_ref, keyval_there, in_ref, out_ref,
+        attn_sum, query_sum, keyval_sum, small_sum, grad_input, in_there, out_there,
+        attn_part, query_part, keyval_part, pair, full, grad_one, small_mine, small_came, small_all,
+        x_sems, *scratch,
+    ):
+        scatters, gathers = [], []
+        parts, sums = (attn_part, query_part, keyval_part), (attn_sum, query_sum, keyval_sum)
+        for part, total in zip(parts, sums):
+            scatters.append(Scatter(part, scratch[:7]))
+            gathers.append(Gather(total, rows, scratch[7:10]))
+            scratch = scratch[10:]
+        small_out = Gather(small_all, small_came.shape[0], scratch)
+        (attn, query_, keyval_), (attn_out, query_out, keyval_out) = scatters, gathers
+        partner = {"wa": 1 - lax.axis_index("wa")}
+        swaps = [
+            remote(source, target, x_sems, (i,), partner)
+            for i, (source, target) in enumerate(
+                [(small_mine.at[:, side_columns(False)], small_came), (in_ref, in_there),
+                 (out_ref, out_there)]
+            )
+        ]
+        steps = range(depth - 1, -1, -1)
+
+        def products(left, left_there, right, right_there, part):
+            pair[:tokens] = left[...]
+            pair[tokens:] = left_there[...]
+
+            @pl.loop(0, part.shape[1] // 512)
+            def _(turn):
+                at = pl.ds(pl.multiple_of(turn * 512, 512), 512)
+                both = jnp.concatenate([right[:, at], right_there[:, at]], axis=0)
+                part[:, at] = columns_by_columns(pair[...], both).astype(jnp.bfloat16)
+
+        products(mixed_ref, mixed_there, middle_ref, middle_there, attn_part)
+        greet(across_x=True)
+        attn.start()
+        products(hidden_ref, hidden_there, query_ref, query_there, query_part)
+        for step in steps:
+            attn.add_cores(step)
+        query_.start()
+        swaps[1].start()
+        swaps[2].start()
+        products(hidden_ref, hidden_there, keyval_ref, keyval_there, keyval_part)
+        keyval_.start()
+        for step in steps:
+            query_.add_cores(step)
+        attn.add_y(depth - 1)
+        fill_small(full, small_ref, small_there_ref)
+        grad_one[:, side_columns(True)] = rows_by_rows(
+            query_ref[...], query_own[...]
+        ) + rows_by_rows(keyval_ref[...], keyval_own[...])
+        attn.add_y(depth - 2)
+        grad_one[:, side_columns(False)] = rows_by_rows(
+            query_ref[...], query_other[...]
+        ) + rows_by_rows(keyval_ref[...], keyval_other[...])
+        back, grad_gain = norm_back(
+            x_ref[...].astype(jnp.float32), full[experts : experts + 1], grad_one[...]
+        )
+        grad_input[...] = (grad_middle_ref[...] + back).astype(jnp.bfloat16)
+        row = lax.broadcasted_iota(jnp.int32, (small_mine.shape[0], 1), 0)
+        small_mine[...] = jnp.where(row == experts, grad_gain, small_grads_ref[...])
+        swaps[0].start()
+        for step in range(depth - 3, -1, -1):
+            attn.add_y(step)
+        for step in steps:
+            keyval_.add_cores(step)
+        attn.last(attn_out.own())
+        attn_out.start()
+        swaps[0].wait()
+        small_out.own()[...] = (small_mine[:, side_columns(True)] + small_came[...]).astype(
+            jnp.bfloat16
+        )
+        small_out.start()
+        for step in steps:
+            query_.add_y(step)
+        attn_out.along_z(1)
+        query_.last(query_out.own())
+        query_out.start()
+        attn_out.along_z(2)
+        attn_out.along_y(0)
+        small_out.along_z(1)
+        for step in steps:
+            keyval_.add_y(step)
+        attn_out.along_z(3)
+        attn_out.along_y(1)
+        keyval_.last(keyval_out.own())
+        keyval_out.start()
+        query_out.along_z(1)
+        small_out.along_z(2)
+        attn_out.along_y(2)
+        query_out.along_z(2)
+        small_out.along_z(3)
+        query_out.along_y(0)
+        keyval_out.along_z(1)
+        query_out.along_z(3)
+        attn_out.along_y(3)
+        keyval_out.along_z(2)
+        query_out.along_y(1)
+        keyval_out.along_z(3)
+        query_out.along_y(2)
+        small_out.along_y(0)
+        keyval_out.along_y(0)
+        small_out.along_y(1)
+        query_out.along_y(3)
+        keyval_out.along_y(1)
+        small_out.along_y(2)
+        keyval_out.along_y(2)
+        small_out.along_y(3)
+        keyval_out.along_y(3)
+        for one in [small_out] + gathers + scatters:
+            one.finish()
+        small_rows = small_came.shape[0]
+        total = small_all[:small_rows].astype(jnp.float32)
+        for device in range(1, count):
+            rows_of = slice(device * small_rows, (device + 1) * small_rows)
+            total = total + small_all[rows_of].astype(jnp.float32)
+        small_sum[...] = total
+        swaps[1].wait()
+        swaps[2].wait()
+
+    small_shape = (small.shape[0], half)
+    out = [jax.ShapeDtypeStruct((half, width), jnp.bfloat16) for width in widths]
+    out += [
+        jax.ShapeDtypeStruct(small_shape, jnp.float32),
+        jax.ShapeDtypeStruct(x.shape, jnp.bfloat16),
+        jax.ShapeDtypeStruct(expert_in.shape, expert_in.dtype),
+        jax.ShapeDtypeStruct(expert_out.shape, expert_out.dtype),
+    ]
+    scratch = [pltpu.VMEM((half, width), jnp.bfloat16) for width in widths]
+    scratch += [
+        pltpu.VMEM((2 * tokens, half), jnp.bfloat16),
+        pltpu.VMEM(small_grads.shape, jnp.float32),
+        pltpu.VMEM(x.shape, jnp.float32),
+        pltpu.VMEM(small_grads.shape, jnp.float32),
+        pltpu.VMEM(small_shape, jnp.float32),
+        pltpu.VMEM((count * small.shape[0], half), jnp.bfloat16),
+        pltpu.SemaphoreType.DMA((2, 3)),
+    ]
+    for width in widths:
+        scratch += Scatter.scratch(depth, rows, width) + Gather.sems(depth)
+    scratch += Gather.sems(depth)
     return call(
-        kernel, out, scratch, 3, "experts", send, d_out_all, in_matrix, out_matrix
-    )
-
-
-def rms_back(values, gain_vec, grad):
-    scale = lax.rsqrt(jnp.mean(values * values, axis=-1, keepdims=True) + EPSILON)
-    through = jnp.mean(gain_vec * grad * values, axis=-1, keepdims=True)
-    back = scale * gain_vec * grad - values * scale**3 * through
-    return back, jnp.sum(grad * values * scale, axis=0)
-
-
-def swap_wa(values):
-    return jax.tree.map(lambda v: lax.ppermute(v, "wa", ((0, 1), (1, 0))), values)
+        kernel, out, scratch, 1, "finish",
+        x, grad_middle, small, small_there, small_grads, *matrices, *hidden, *mixed, *middle,
+        *query, *keyval, expert_in, expert_out, outside=(19, 20), outside_out=(5, 6),
+    )
+
+
+def widen(query, keyval, attn, grad_in, in_there, grad_out, out_there):
+    half, quarter, features = query.shape[0], grad_out.shape[0], grad_out.shape[1]
+    steps = 4
+
+    def kernel(*refs):
+        query_ref, keyval_ref, attn_ref, in_ref, in_there_ref, out_ref, out_there_ref = refs[:7]
+        query_out, keyval_out, attn_out, in_out, out_out = refs[7:]
+        query_out[...] = query_ref[...].astype(jnp.float32)
+        keyval_out[...] = keyval_ref[...].astype(jnp.float32)
+        attn_out[...] = attn_ref[...].astype(jnp.float32)
+        both = in_ref[...] + in_there_ref[...].astype(jnp.float32)
+        in_out[0, 0] = both[:, :quarter]
+        in_out[0, 1] = both[:, quarter:]
+        out_out[0] = out_ref[...] + out_there_ref[...].astype(jnp.float32)
+
+    def rows(values):
+        return pl.BlockSpec((values.shape[0] // steps, values.shape[1]), lambda i: (i, 0))
+
+    operands = (query, keyval, attn, grad_in, in_there, grad_out, out_there)
+    return pl.pallas_call(
+        kernel,
+        grid=(steps,),
+        out_shape=[
+            jax.ShapeDtypeStruct(query.shape, jnp.float32),
+            jax.ShapeDtypeStruct(keyval.shape, jnp.float32),
+            jax.ShapeDtypeStruct(attn.shape, jnp.float32),
+            jax.ShapeDtypeStruct((1, 2, features, quarter), jnp.float32),
+            jax.ShapeDtypeStruct((1, quarter, features), jnp.float32),
+        ],
+        in_specs=[rows(values) for values in operands],
+        out_specs=[
+            rows(query), rows(keyval), rows(attn),
+            pl.BlockSpec((1, 2, features // steps, quarter), lambda i: (0, 0, i, 0)),
+            pl.BlockSpec((1, quarter // steps, features), lambda i: (0, i, 0)),
+        ],
+        compiler_params=pltpu.CompilerParams(vmem_limit_bytes=VMEM_LIMIT),
+        name="widen",
+    )(*operands)
 
 
 def gathered_body(
     layer_input, seq_ids, routes, gain_attn, w_query, w_keyval, w_out_attn, gain_ffn, router,
     w_in, w_out, d_out,
 ):
-    me, side = lax.axis_index("ctx"), lax.axis_index("wa")
-    tokens = layer_input.shape[1]
-    experts = router.shape[1]
-    kv_width = KV_HEADS * HEAD_DIM
-    half = D // 2
-    quarter = w_in.shape[3]
-
-    def halves(values):
-        own = lax.dynamic_slice_in_dim(values, side * half, half, values.ndim - 1)
-        return own, lax.dynamic_slice_in_dim(values, (1 - side) * half, half, values.ndim - 1)
-
-    def whole(own, there):
-        both = jnp.concatenate([own, there], axis=-1), jnp.concatenate([there, own], axis=-1)
-        return jnp.where(side == 0, *both)
-
+    me = lax.axis_index("ctx")
+    tokens, experts = layer_input.shape[1], router.shape[1]
+    x, grad_out = layer_input[0], d_out[0]
     small = jnp.concatenate(
-        [router.T, gain_attn[None], gain_ffn[None], jnp.zeros((14 - experts, half), jnp.bfloat16)]
-    )
+        [router.T, gain_attn[None], gain_ffn[None], jnp.zeros((experts - 2, D // 2), jnp.bfloat16)]
+    )
+    turns = angle_table(me * tokens + jnp.arange(tokens, dtype=jnp.int32))[:, 0]
+    cosine, sine = jnp.cos(turns), jnp.sin(turns)
+    angles = (
+        jnp.concatenate([cosine, cosine], axis=1), jnp.concatenate([-sine, sine], axis=1)
+    )
+    docs = (seq_ids, lax.dynamic_slice_in_dim(seq_ids[0], me * tokens, tokens, 0)[:, None])
+    numbers = jnp.arange(128, dtype=jnp.int32)
+    named = jnp.any(routes[0][:, :, None] == (numbers % experts)[None, None, :], axis=1)
+    chosen = (named & (numbers < 2 * experts)[None, :]).astype(jnp.float32)
+    in_own = jnp.concatenate([w_in[0, 0], w_in[0, 1]], axis=1)
+
     d_out_all, w_query_there, w_keyval_there, w_out_attn_there, small_there = front(
-        d_out[0], w_query, w_keyval, w_out_attn, small
-    )
-    w_in, w_out, small_there = lax.optimization_barrier((w_in, w_out, small_there))
-    small = whole(small, small_there).astype(jnp.float32)
-    router_rows, gain_one, gain_two = small[:experts], small[experts], small[experts + 1]
-    w_in_there, w_out_there = swap_wa((w_in[0], w_out[0]))
-    in_matrix = jnp.concatenate([w_in[0, 0], w_in_there[0], w_in[0, 1], w_in_there[1]], axis=1)
-    out_matrix = jnp.concatenate([w_out[0], w_out_there], axis=0)
-
-    def onto(values, weight, weight_there):
-        own, there = halves(values)
-        return jnp.dot(own, weight, preferred_element_type=jnp.float32) + jnp.dot(
-            there, weight_there, preferred_element_type=jnp.float32
-        )
-
-    residual = layer_input[0].astype(jnp.float32)
-    hidden_one = rms_scale(residual, gain_one).astype(jnp.bfloat16)
-    hidden_one_own, hidden_one_other = halves(hidden_one)
-    hidden_one_there = swap_wa(hidden_one_other)
-    positions = me * tokens + jnp.arange(tokens, dtype=jnp.int32)
-    angles = angle_table(positions)
-    query_pre = onto(hidden_one, w_query, w_query_there)
-    keyval_pre = onto(hidden_one, w_keyval, w_keyval_there)
-    query = rotate(query_pre.reshape(tokens, HEADS, HEAD_DIM), angles).astype(jnp.bfloat16)
-    query = query.reshape(tokens, D)
-    keys = rotate(keyval_pre[:, :kv_width].reshape(tokens, KV_HEADS, HEAD_DIM), angles)
-    keyval = jnp.concatenate([keys.reshape(tokens, kv_width), keyval_pre[:, kv_width:]], axis=1)
-    keyval_all = gather_ctx(keyval.astype(jnp.bfloat16), 2, "gather_kv")
-    doc_column = lax.dynamic_slice_in_dim(seq_ids[0], me * tokens, tokens, 0)[:, None]
-    mixed, level = attend(query, keyval_all, seq_ids, doc_column)
-    mixed_low = mixed.astype(jnp.bfloat16)
-    mixed_own, mixed_other = halves(mixed_low)
-    mixed_there = swap_wa(mixed_other)
-    middle = residual + onto(mixed_low, w_out_attn, w_out_attn_there)
-
-    hidden_two = rms_scale(middle, gain_two).astype(jnp.bfloat16)
-    router_low = router_rows.astype(jnp.bfloat16)
-    logits = rows_by_rows(hidden_two, router_low)
-    numbers = jnp.arange(experts, dtype=jnp.int32)
-    chosen = jnp.any(routes[0][:, :, None] == numbers[None, None, :], axis=1)
-    masked = jnp.where(chosen, logits, NEGATIVE)
-    weights = jnp.exp(masked - jnp.max(masked, axis=1, keepdims=True))
-    gates = weights / jnp.sum(weights, axis=1, keepdims=True)
-    gates_high = gates.astype(jnp.bfloat16)
-    gates_low = (gates - gates_high.astype(jnp.float32)).astype(jnp.bfloat16)
-    spare = jnp.zeros((tokens, 128 - 2 * experts), jnp.bfloat16)
-    send = jnp.concatenate([hidden_two, gates_high, gates_low, spare], axis=1)
-    width = 2 * quarter
-    returned, results, grad_in_matrix, grad_out_matrix = run_experts(
-        send, d_out_all, in_matrix, out_matrix, experts
-    )
-
-    grad_out = d_out[0].astype(jnp.float32)
-    grad_gates = returned[:, D : D + experts]
-    grad_logits = gates * (grad_gates - jnp.sum(gates * grad_gates, axis=1, keepdims=True))
-    grad_logits_low = grad_logits.astype(jnp.bfloat16)
-    grad_hidden_two = returned[:, :D] + jnp.dot(
-        grad_logits_low, router_low, preferred_element_type=jnp.float32
-    )
-    grad_router = columns_by_columns(grad_logits_low, hidden_two)
-    back_two, grad_gain_two = rms_back(middle, gain_two, grad_hidden_two)
-    grad_middle = grad_out + back_two
-    grad_middle_low = grad_middle.astype(jnp.bfloat16)
-    grad_middle_there = swap_wa(grad_middle_low)
-    grad_mixed = whole(
-        rows_by_rows(grad_middle_low, w_out_attn), rows_by_rows(grad_middle_low, w_out_attn_there)
-    ).astype(jnp.bfloat16)
-    grad_query, grad_keyval_own, result_sum = attend_back(
-        query, keyval_all, seq_ids, doc_column, level, mixed, grad_mixed, results
-    )
-    output = (middle + result_sum).astype(jnp.bfloat16)
-    grad_query_pre = rotate(grad_query.reshape(tokens, HEADS, HEAD_DIM), -angles)
-    grad_query_pre = grad_query_pre.reshape(tokens, D).astype(jnp.bfloat16)
-    grad_keys = rotate(
-        grad_keyval_own[:, :kv_width].reshape(tokens, KV_HEADS, HEAD_DIM), -angles
-    ).reshape(tokens, kv_width)
-    grad_keyval_pre = jnp.concatenate([grad_keys, grad_keyval_own[:, kv_width:]], axis=1)
-    grad_keyval_pre = grad_keyval_pre.astype(jnp.bfloat16)
-    grad_hidden_one = whole(
-        rows_by_rows(grad_query_pre, w_query) + rows_by_rows(grad_keyval_pre, w_keyval),
-        rows_by_rows(grad_query_pre, w_query_there)
-        + rows_by_rows(grad_keyval_pre, w_keyval_there),
-    )
-    back_one, grad_gain_one = rms_back(residual, gain_one, grad_hidden_one)
-    grad_input = (grad_middle + back_one).astype(jnp.bfloat16)
-
-    small_grads = jnp.concatenate(
-        [
-            grad_router,
-            grad_gain_one[None],
-            grad_gain_two[None],
-            jnp.zeros((14 - experts, D), jnp.float32),
-        ]
-    )
-    attn_sum, query_sum, keyval_sum, small_sum, in_there, out_there = finish(
-        hidden_one_own, hidden_one_there, mixed_own, mixed_there, grad_middle_low,
-        grad_middle_there, grad_query_pre, grad_keyval_pre, *halves(small_grads),
-        jnp.concatenate(
-            [grad_in_matrix[:, quarter:width], grad_in_matrix[:, width + quarter :]], axis=1
-        ).astype(jnp.bfloat16),
-        grad_out_matrix[quarter:].astype(jnp.bfloat16),
-    )
-    grad_w_in = jnp.stack(
-        [
-            grad_in_matrix[:, :quarter] + in_there[:, :quarter].astype(jnp.float32),
-            grad_in_matrix[:, width : width + quarter]
-            + in_there[:, quarter:].astype(jnp.float32),
-        ]
-    )
-    grad_w_out = grad_out_matrix[:quarter] + out_there.astype(jnp.float32)
+        grad_out, w_query, w_keyval, w_out_attn, small
+    )
+    projections = (w_query, w_query_there, w_keyval, w_keyval_there)
+    (
+        query, keyval, level, mixed, hidden_own, hidden_there, mixed_own, mixed_there, middle,
+        send, gates,
+    ) = attend(
+        x, small, small_there, projections + (w_out_attn, w_out_attn_there), angles, docs, chosen,
+        experts,
+    )
+    returned, results, grad_in, grad_in_other, grad_out_matrix, grad_out_other = run_experts(
+        send, d_out_all, in_own, w_out[0], experts
+    )
+    (
+        output, grad_middle, middle_low, middle_there, grad_query, query_there, grad_keyval,
+        keyval_there, small_grads,
+    ) = attend_back(
+        returned, gates, small, small_there, middle, grad_out, send, w_out_attn, w_out_attn_there,
+        query, keyval, angles, docs, level, mixed, results, experts,
+    )
+    attn_sum, query_sum, keyval_sum, small_sum, grad_input, in_there, out_there = finish(
+        x, grad_middle, small, small_there, small_grads, projections, (hidden_own, hidden_there),
+        (mixed_own, mixed_there), (middle_low, middle_there), (grad_query, query_there),
+        (grad_keyval, keyval_there), grad_in_other, grad_out_other,
+    )
+    query_sum, keyval_sum, attn_sum, grad_w_in, grad_w_out = widen(
+        query_sum, keyval_sum, attn_sum, grad_in, in_there, grad_out_matrix, out_there
+    )
     return (
         output[None],
         grad_input[None],
         small_sum[experts],
-        query_sum.astype(jnp.float32),
-        keyval_sum.astype(jnp.float32),
-        attn_sum.astype(jnp.float32),
+        query_sum,
+        keyval_sum,
+        attn_sum,
         small_sum[experts + 1],
         small_sum[:experts].T,
-        grad_w_in[None],
-        grad_w_out[None],
+        grad_w_in,
+        grad_w_out,
     )
 
 

time: 474 us -> 412 us (0.87); the launches traced: 465 us -> 411 us
  Pallas kernels: 352 us -> 393 us
  other arithmetic: 39.5 us -> 5.44 us
  local copies, waits for them, and re-layouts: 45.2 us -> 12.4 us
  matrix products: 20.8 us -> 0 us
  starting transfers between devices: 5.63 us -> 0 us
    pallas_call x6 -> x5, Pallas kernels: 352 us -> 383 us  [call(): pl.pallas_call(kernel, out_shape=out, in_specs=[spec(i, outside) for i in...]
    dot_general x15 -> x0, matrix products: 20.8 us -> none  [the longest x7 8.7 us: rows_by_rows(): lax.dot_general(left, right, (((1,), (1,)), ((), ())), preferred_element_...]
    convert_element_type x10 -> x1, other arithmetic: 15.8 us -> 0.64 us  [gathered_body(): chosen = (named & (numbers < 2 * experts)[None, :]).astype(jnp.float32)]
    pallas_call x0 -> x1, Pallas kernels: none -> 9.42 us  [widen(): pl.pallas_call(kernel, grid=(steps,), out_shape=[jax.ShapeDtypeStruct(que...]
    concatenate x11 -> x3, other arithmetic: 10.9 us -> 3.65 us  [the longest x1 1.5 us: gathered_body(): in_own = jnp.concatenate([w_in[0, 0], w_in[0, 1]], axis=1)]
    slice x8 -> x1, local copies, waits for them, and re-layouts: 8.45 us -> 1.32 us  [gathered_body(): in_own = jnp.concatenate([w_in[0, 0], w_in[0, 1]], axis=1)]
    ppermute x5 -> x0, starting transfers between devices: 5.63 us -> none  [swap_wa(): lax.ppermute(v, 'wa', ((0, 1), (1, 0)))]
    unnamed x119 -> x9, local copies, waits for them, and re-layouts: 10.6 us -> 5.47 us
  transfers between devices with their start and end apart: 5 -> 0, of which waited for: 0 -> 0; matrix products, arithmetic and copies ran while one was open for 18% -> 0% of each run, Pallas kernels for 45% -> 0%
where the time goes in v4:
time: 412 us; the launch traced here: 411 us
  Pallas kernels  393 us (95%)
  local copies, waits for them, and re-layouts  12.4 us (3%)
  other arithmetic  5.44 us (1%)
    pallas_call x5, Pallas kernels, call(): pl.pallas_call(kernel, out_shape=out, in_specs=[spec(i, outside) for i in...  383 us
    pallas_call x1, Pallas kernels, widen(): pl.pallas_call(kernel, grid=(steps,), out_shape=[jax.ShapeDtypeStruct(que...  9.42 us

profile of v4, /device:TPU:0, one launch (start us, length us, event | category | flops | bytes accessed | tf_op | source)
XLA Modules:
  0.0 411.1 jit_solution(7850808271340165222)
XLA Ops:
  0.6 0.7 dynamic-slice_bitcast_fusion
  1.3 0.1 pad.9.clone
  1.4 0.7 broadcast_in_dim.22
  2.1 0.7 broadcast_in_dim.23
  2.8 0.8 compare_reduce_fusion
  3.6 1.4 maximum_maximum_fusion.small_ref
  5.0 0.6 and_convert_fusion.chosen_ref
  5.6 0.7 copy.28.doc_column
  6.4 0.3 fusion
  6.7 0.8 pad_maximum_fusion.1
  7.5 1.3 fusion.1
  8.8 0.3 copy.33
  9.1 0.3 copy.34
  9.3 1.5 pad_maximum_fusion.in_own_ref
  10.8 58.2 %front.1 = (bf16[2048,1536]{1,0:T(8,128)(2,1)}, bf16[768,1536]{1,0:T(8,128)(2,1)}, bf16[768,512]{1,0:T(8,128)(2,1)}, bf16[768,1536]{1,0:T(8,128)(2,1)}, bf16[16,768]{1,0:T(8,128)(2,1)}) custom-call(bf16[128,1536]{1,0:T(8,128)(2,1)} %bitcast.17, bf16[768,1536]{1,0:T(8,128)(2,1)} %query_own.3, bf16[768,512]{1,0:T(8,128)(2,1)} %keyval_own.3, ...), custom_call_target="tpu_custom_call" | custom-call | tf_op jit(solution)/shard_map/front/pallas_call | solution.py:662
  69.1 41.3 %attend.1 = (bf16[128,1536]{1,0:T(8,128)(2,1)}, bf16[2048,512]{1,0:T(8,128)(2,1)}, f32[1536,1]{1,0:T(8,128)}, f32[128,1536]{1,0:T(8,128)}, bf16[128,768]{1,0:T(8...) custom-call(bf16[128,1536]{1,0:T(8,128)(2,1)} %bitcast.15, ...), custom_call_target="tpu_custom_call" | custom-call | tf_op jit(solution)/shard_map/attend/pallas_call | solution.py:662
  110.4 115.3 %experts.1 = (f32[128,1664]{1,0:T(8,128)}, bf16[8,128,1536]{2,1,0:T(8,128)(2,1)}, f32[1536,384]{1,0:T(8,128)}, bf16[1536,384]{1,0:T(8,128)(2,1)}, f32[192,1536]{1,0:T(8,128)}, /*index=5*/bf16[192,1536]{1,0:T(8,128)(2,1)}) custom-call(bf16[128,1664]{1,0:T(8,128)(2,1)} %get-tuple-element.57.send_ref, bf16[2048,1536]{1,0:T(8,128)(2,1)} %get-tuple-element.58.d_out_ref, ...), custom_call_target="tpu_custom_call" | custom-call | tf_op jit(solution)/shard_map/experts/pallas_call | solution.py:662
  225.7 68.5 %attend_back.1 = (bf16[128,1536]{1,0:T(8,128)(2,1)}, f32[128,1536]{1,0:T(8,128)}, bf16[128,1536]{1,0:T(8,128)(2,1)}, bf16[128,1536]{1,0:T(8,128)(2,1)}, bf16[128...) custom-call(f32[128,1664]{1,0:T(8,128)} %get-tuple-element.59.return, ...), custom_call_target="tpu_custom_call" | custom-call | tf_op jit(solution)/shard_map/attend_back/pallas_call | solution.py:662
  294.2 99.8 %finish.1 = (bf16[768,1536]{1,0:T(8,128)(2,1)}, bf16[768,1536]{1,0:T(8,128)(2,1)}, bf16[768,512]{1,0:T(8,128)(2,1)}, f32[16,768]{1,0:T(8,128)}, bf16[128,1536]{1...) custom-call(bf16[128,1536]{1,0:T(8,128)(2,1)} %bitcast.16, ...), custom_call_target="tpu_custom_call" | custom-call | tf_op jit(solution)/shard_map/finish/pallas_call | solution.py:662
  394.0 1.4 slice_reduce_fusion
  395.4 1.3 slice_bitcast_fusion
  396.8 9.4 %widen.1 = (f32[768,1536]{1,0:T(8,128)}, f32[768,512]{1,0:T(8,128)}, f32[768,1536]{1,0:T(8,128)}, f32[1,2,1536,192]{3,2,1,0:T(8,128)}, f32[1,192,1536]{2,1,0:T(8,128)}) custom-call(bf16[768,1536]{1,0:T(8,128)(2,1)} %get-tuple-element.84.refs_0_, bf16[768,512]{1,0:T(8,128)(2,1)} %get-tuple-element.85.refs_1_, bf16[768,1536]{1,0:T(8,128)(2,1)} %get-tuple-element.86.refs_2_, ...), custom_call_target="tpu_custom_call" | custom-call | tf_op jit(solution)/shard_map/widen/pallas_call | solution.py:1447
  406.2 0.0 copy-start
  406.2 0.0 copy-start.1
  406.2 3.4 copy.32
  409.6 0.0 copy-done
  409.6 0.7 copy.37
  410.4 0.0 copy-done.1
  410.4 0.7 copy.38
  (5 shorter events, 0.0 us)
Async XLA Ops:
  406.2 3.4 copy-start
  406.2 4.2 %copy-start.1 = (bf16[128,1536]{1,0:T(8,128)(2,1)S(1)}, bf16[128,1536]{1,0:T(8,128)(2,1)}, u32[]{:S(2)}) copy-start(bf16[128,1536]{1,0:T(8,128)(2,1)} %get-tuple-element.82) | copy-start | bytes 1179652

commit v5 on v4

--- a/solution.py
+++ b/solution.py
@@ -675,33 +675,27 @@
 
 
 class Relay:
-    def __init__(self, source, out, sems, parts=1, over_y=False):
-        self.source, self.out, self.sems = source, out, sems
+    def __init__(self, source, out, sems, parts=1):
+        self.source, self.out, self.sems, self.parts = source, out, sems, parts
         self.z, self.y, self.c, _ = chip_place()
-        self.parts, self.over_y = parts, over_y
-        self.rows = source.shape[0] // (4 if over_y else 2 * parts)
+        self.rows = source.shape[0] // (2 * parts)
 
     @staticmethod
     def semaphores():
-        return pltpu.SemaphoreType.DMA((2, 6))
-
-    def block(self, ref, part, y, c):
-        place = y * 2 + c if self.over_y else c * self.parts + part
-        return ref.at[pl.ds(pl.multiple_of(place * self.rows, 16), self.rows)]
+        return pltpu.SemaphoreType.DMA((2, 4))
+
+    def block(self, ref, part, c):
+        return ref.at[pl.ds(pl.multiple_of((c * self.parts + part) * self.rows, 16), self.rows)]
 
     def on_x(self, part):
-        source = self.block(self.source, part, self.y, self.c)
-        target = self.block(self.out, part, self.y, self.c)
+        source, target = self.block(self.source, part, self.c), self.block(self.out, part, self.c)
         return remote(source, target, self.sems, (part,), {"wa": 1 - lax.axis_index("wa")})
 
-    def on_core(self, part, y, c):
-        block = self.block(self.out, part, y, c)
-        at = (2 + (jnp.where(y == self.y, 0, 1) if self.over_y else part),)
-        return remote(block, block, self.sems, at, {"ctx": ctx_of(self.z, self.y, 1 - self.c)})
-
-    def on_y(self, y):
-        block = self.block(self.out, 0, y, self.c)
-        return remote(block, block, self.sems, (4,), {"ctx": ctx_of(self.z, 1 - self.y, self.c)})
+    def on_core(self, part, c):
+        block = self.block(self.out, part, c)
+        return remote(
+            block, block, self.sems, (2 + part,), {"ctx": ctx_of(self.z, self.y, 1 - self.c)}
+        )
 
     def start(self):
         for part in range(self.parts):
@@ -709,64 +703,49 @@
 
     def pass_on(self, part=0):
         self.on_x(part).wait_recv()
-        if self.over_y:
-            self.on_y(self.y).start()
-        self.on_core(part, self.y, self.c).start()
-
-    def pass_on_y(self):
-        self.on_y(1 - self.y).wait_recv()
-        self.on_core(0, 1 - self.y, self.c).start()
+        self.on_core(part, self.c).start()
 
     def finish(self):
         for part in range(self.parts):
             self.on_x(part).wait_send()
-            self.on_core(part, self.y, self.c).wait_send()
-            self.on_core(part, self.y, 1 - self.c).wait_recv()
-        if self.over_y:
-            self.on_y(self.y).wait_send()
-            self.on_core(0, 1 - self.y, self.c).wait_send()
-            self.on_core(0, 1 - self.y, 1 - self.c).wait_recv()
-
-
-def front(d_out, w_query, w_keyval, w_out_attn, small):
+            self.on_core(part, self.c).wait_send()
+            self.on_core(part, 1 - self.c).wait_recv()
+
+
+def front(d_out, w_query, w_keyval, small):
     count, rows = lax.axis_size("ctx"), d_out.shape[0]
     depth = count // 4
 
     def kernel(
-        d_out_ref, query_ref, keyval_ref, attn_ref, small_ref,
-        d_out_all, query_there, keyval_there, attn_there, small_there, *sems,
+        d_out_ref, query_ref, keyval_ref, small_ref,
+        d_out_all, query_there, keyval_there, small_there, *sems,
     ):
         gather = Gather(d_out_all, rows, sems[:3])
-        query_sems, keyval_sems, attn_sems, small_sems, own_sem = sems[3:]
+        query_sems, keyval_sems, small_sems, own_sem = sems[3:]
         query = Relay(query_ref, query_there, query_sems, parts=2)
         keyval = Relay(keyval_ref, keyval_there, keyval_sems)
-        attn = Relay(attn_ref, attn_there, attn_sems, over_y=True)
         partner = {"wa": 1 - lax.axis_index("wa")}
         swap = remote(small_ref, small_there, small_sems, (0,), partner)
         keep = pltpu.make_async_copy(d_out_ref, gather.own(), own_sem.at[0])
         keep.start()
         greet(across_x=True)
         swap.start()
-        attn.start()
         query.start()
         keyval.start()
         gather.start(d_out_ref)
         gather.along_z(1)
         gather.along_y(0)
         gather.along_z(2)
-        attn.pass_on()
         gather.along_y(1)
+        query.pass_on(0)
         gather.along_z(3)
-        query.pass_on(0)
         gather.along_y(2)
-        attn.pass_on_y()
-        gather.along_y(3)
         query.pass_on(1)
         keyval.pass_on()
+        gather.along_y(3)
         gather.finish()
         query.finish()
         keyval.finish()
-        attn.finish()
         swap.wait()
         keep.wait()
 
@@ -775,14 +754,14 @@
 
     out = [
         jax.ShapeDtypeStruct((count * rows, d_out.shape[1]), d_out.dtype),
-        like(w_query), like(w_keyval), like(w_out_attn), like(small),
+        like(w_query), like(w_keyval), like(small),
     ]
-    scratch = Gather.sems(depth) + [Relay.semaphores()] * 3
+    scratch = Gather.sems(depth) + [Relay.semaphores()] * 2
     scratch += [pltpu.SemaphoreType.DMA((2, 1)), pltpu.SemaphoreType.DMA((1,))]
-    every = range(5)
+    every = range(4)
     return call(
         kernel, out, scratch, 0, "front",
-        d_out, w_query, w_keyval, w_out_attn, small, outside=every, outside_out=every,
+        d_out, w_query, w_keyval, small, outside=every, outside_out=every,
     )
 
 
@@ -834,20 +813,23 @@
     return jnp.concatenate([rows, rows, spare], axis=0).astype(jnp.bfloat16)
 
 
-def attend(x, small, small_there, matrices, angles, docs, chosen, experts):
+def attend(x, small, small_there, projections, w_out_attn, angles, docs, chosen, experts):
     count, tokens, features = lax.axis_size("ctx"), x.shape[0], x.shape[1]
     depth, length = count // 4, count * tokens
-    kv_columns, half = matrices[2].shape[1], features // 2
+    kv_columns, half = projections[2].shape[1], features // 2
 
     def kernel(
         x_ref, small_ref, small_there_ref, query_own, query_other, keyval_own, keyval_other,
-        attn_own, attn_other, cosine_ref, sine_ref, doc_row, doc_column, chosen_ref,
+        attn_own, cosine_ref, sine_ref, doc_row, doc_column, chosen_ref,
         query, keyval, level, mixed, hidden_own, hidden_there, mixed_own, mixed_there, middle,
-        send, gates_out,
-        hidden, mixed_low, full, stacked, bias, x_sems, *sems,
+        send, gates_out, attn_other,
+        hidden, mixed_low, full, stacked, bias, x_sems, attn_sems, *sems,
     ):
         gather = Gather(keyval, tokens, sems)
+        attn = Relay(attn_own, attn_other, attn_sems, parts=2)
         partner = {"wa": 1 - lax.axis_index("wa")}
+        greet(across_x=True)
+        attn.start()
         fill_small(full, small_ref, small_there_ref)
         residual = x_ref[...].astype(jnp.float32)
         hidden[...] = normed(residual, full[experts : experts + 1]).astype(jnp.bfloat16)
@@ -864,7 +846,6 @@
         keys = turned(pre[:, : kv_columns // 2], cosine, sine)
         block = jnp.concatenate([keys, pre[:, kv_columns // 2 :]], axis=1)
         gather.own()[...] = block.astype(jnp.bfloat16)
-        greet(across_x=True)
         gather.start()
         swap = remote(hidden.at[:, side_columns(False)], hidden_there, x_sems, (0,), partner)
         swap.start()
@@ -892,13 +873,16 @@
                 columns = pl.ds(pl.multiple_of((pair * 2 + part) * 128, 128), 128)
                 mixed[:, columns] = mixture[part * tokens : (part + 1) * tokens]
             level[rows, :] = top + jnp.log(total)
-
+            pl.when(pair == HEADS // 4)(lambda: attn.pass_on(0))
+
+        attn.pass_on(1)
         mixed_low[...] = mixed[...].astype(jnp.bfloat16)
         mixed_own[...] = mixed_low[:, side_columns(True)]
         swap_mixed = remote(
             mixed_low.at[:, side_columns(False)], mixed_there, x_sems, (1,), partner
         )
         swap_mixed.start()
+        attn.finish()
         own, other = mixed_low[:, side_columns(True)], mixed_low[:, side_columns(False)]
         middle[...] = residual + onto(attn_own, attn_other)
         hidden_two = normed(middle[...], full[experts + 1 : experts + 2]).astype(jnp.bfloat16)
@@ -925,6 +909,7 @@
         shape(tokens, features, jnp.float32),
         shape(tokens, half), shape(tokens, half), shape(tokens, half), shape(tokens, half),
         shape(tokens, features, jnp.float32), shape(tokens, wide), shape(tokens, 128, jnp.float32),
+        shape(*w_out_attn.shape),
     ]
     scratch = [
         pltpu.VMEM((tokens, features), jnp.bfloat16),
@@ -933,10 +918,11 @@
         pltpu.VMEM((HEADS * tokens, HEAD_DIM), jnp.bfloat16),
         pltpu.VMEM((tokens, length), jnp.float32),
         pltpu.SemaphoreType.DMA((2, 2)),
+        Relay.semaphores(),
     ] + Gather.sems(depth)
     return call(
         kernel, out, scratch, 2, "attend",
-        x, small, small_there, *matrices, *angles, *docs, chosen,
+        x, small, small_there, *projections, w_out_attn, *angles, *docs, chosen,
     )
 
 
@@ -1035,6 +1021,7 @@
                 )
             total[:, key_columns] += columns_by_columns(grad_scores, own) * HEAD_DIM**-0.5
             total[:, val_columns] += columns_by_columns(probs.astype(jnp.bfloat16), grad)
+            pl.when(pair == 1)(lambda: result.on_y(nearest(depth - 3)).start())
             pl.when(pair == HEADS // 4)(lambda: result.add_y_of(nearest(depth - 1)))
 
         part[...] = total[...].astype(jnp.bfloat16)
@@ -1045,7 +1032,7 @@
         steps = range(depth - 1, -1, -1)
         for step in steps:
             keyval_sum.add_cores(step)
-        for k in range(depth - 3, -1, -1):
+        for k in range(depth - 4, -1, -1):
             result.on_y(nearest(k)).start()
         result.add_y_of(nearest(depth - 2))
         for step in steps:
@@ -1115,10 +1102,10 @@
     width = 2 * quarter
 
     def kernel(
-        send_ref, d_out_ref, in_own_ref, out_own_ref,
+        send_ref, d_out_far, in_own_ref, out_own_ref,
         returned, results, grad_in, grad_in_other, grad_out, grad_out_other,
         hidden_all, grad_both, gated_hidden, other_part, other_result, result_from, result_sems,
-        in_ref, out_ref, x_sems, *scratch,
+        in_ref, out_ref, d_out_ref, x_sems, near_sem, *scratch,
     ):
         gather = Gather(hidden_all, tokens, scratch[:3])
         scatter = Scatter(other_part, scratch[3:])
@@ -1127,26 +1114,32 @@
         lane = lax.broadcasted_iota(jnp.int32, (1, 128), 1)
         gather.own()[...] = send_ref[...]
         partner = {"wa": 1 - lax.axis_index("wa")}
-        in_there = gated_hidden.at[pl.ds(0, features)]
+        near = pltpu.make_async_copy(d_out_far, d_out_ref, near_sem.at[0])
+        near.start()
         swaps = [
-            remote(in_own_ref, in_there, x_sems, (0,), partner),
-            remote(out_own_ref, out_ref.at[pl.ds(quarter, quarter)], x_sems, (1,), partner),
+            remote(
+                in_own_ref.at[pl.ds(part * quarter, quarter)],
+                in_ref.at[pl.ds((2 * part + 1) * quarter, quarter)],
+                x_sems,
+                (part,),
+                partner,
+            )
+            for part in range(2)
         ]
+        swaps.append(
+            remote(out_own_ref, out_ref.at[pl.ds(quarter, quarter)], x_sems, (2,), partner)
+        )
         greet(across_x=True)
+        gather.start()
         for swap in swaps:
             swap.start()
         out_ref[:quarter] = out_own_ref[...]
-        gather.run()
+        in_ref[:quarter] = in_own_ref[:quarter]
+        in_ref[width : width + quarter] = in_own_ref[quarter:]
+        gather.follow()
+        near.wait()
         for swap in swaps:
             swap.wait()
-
-        @pl.loop(0, features // 256)
-        def _(turn):
-            at = pl.ds(pl.multiple_of(turn * 256, 256), 256)
-            own, there = in_own_ref[at, :], gated_hidden[at, :]
-            in_ref[at, :] = jnp.concatenate(
-                [own[:, :quarter], there[:, :quarter], own[:, quarter:], there[:, quarter:]], axis=1
-            )
 
         def chip_rows(chip):
             return pl.ds(pl.multiple_of(chip * 2 * tokens, 16), 2 * tokens)
@@ -1160,9 +1153,7 @@
             carried = hidden_all[rows, features:].astype(jnp.float32)
             mine = (lane == expert) | (lane == expert + experts)
             gate = jnp.sum(jnp.where(mine, carried, 0.0), axis=1, keepdims=True)
-            both = jnp.dot(
-                hidden_all[rows, :features], in_ref[...], preferred_element_type=jnp.float32
-            )
+            both = rows_by_rows(hidden_all[rows, :features], in_ref[...])
             hidden, by_first, by_second = gate_unit(both[:, :width], both[:, width:])
             gated_hidden[rows, :] = (hidden * gate).astype(jnp.bfloat16)
             grad_hidden = rows_by_rows(d_out_ref[rows, :], out_ref[...])
@@ -1170,7 +1161,9 @@
             grad_hidden = grad_hidden * gate
             grad_both[rows, :width] = (grad_hidden * by_first).astype(jnp.bfloat16)
             grad_both[rows, width:] = (grad_hidden * by_second).astype(jnp.bfloat16)
-            own, other = parted(rows_by_rows(grad_both[rows, :], in_ref[...]))
+            own, other = parted(
+                jnp.dot(grad_both[rows, :], in_ref[...], preferred_element_type=jnp.float32)
+            )
             scatter.sums[chip, :, :features] = own.astype(jnp.bfloat16)
             other_part[chip, :, :features] = other.astype(jnp.bfloat16)
             own, other = parted(jnp.where(lane == expert, grad_gate, 0.0))
@@ -1187,6 +1180,7 @@
             scatter.add_chip(of_z, True)
 
         scatter.add_chip(nearest(0), False)
+        scatter.add_y_of(nearest(depth - 1))
 
         def result_copy(chip):
             target = {"ctx": ctx_of(z, y, 1 - c)}
@@ -1204,7 +1198,7 @@
             other_result[chip] = other.astype(jnp.bfloat16)
             result_copy(chip).start()
 
-        scatter.add_y_of(nearest(depth - 1))
+        scatter.add_y_of(nearest(depth - 2))
 
         @pl.loop(0, features // 512)
         def _(turn):
@@ -1213,21 +1207,20 @@
             grad_out[:, at] = grad[:quarter]
             grad_out_other[:, at] = grad[quarter:].astype(jnp.bfloat16)
 
-        scatter.add_y_of(nearest(depth - 2))
-
-        @pl.loop(0, features // 256)
+        for k in range(depth - 3, 0, -1):
+            scatter.add_y_of(nearest(k))
+
+        @pl.loop(0, features // 512)
         def _(turn):
-            at = pl.ds(pl.multiple_of(turn * 256, 256), 256)
-            grad = columns_by_columns(hidden_all[:, at], grad_both[...])
-            grad_in[at, :] = jnp.concatenate(
-                [grad[:, :quarter], grad[:, width : width + quarter]], axis=1
-            )
-            grad_in_other[at, :] = jnp.concatenate(
-                [grad[:, quarter:width], grad[:, width + quarter :]], axis=1
-            ).astype(jnp.bfloat16)
-
-        for k in range(depth - 3, -1, -1):
-            scatter.add_y_of(nearest(k))
+            at = pl.ds(pl.multiple_of(turn * 512, 512), 512)
+            grad = columns_by_columns(grad_both[...], hidden_all[:, at])
+            for part in range(2):
+                rows = slice(part * quarter, (part + 1) * quarter)
+                first = part * width
+                grad_in[rows, at] = grad[first : first + quarter]
+                grad_in_other[rows, at] = grad[first + quarter : first + width].astype(jnp.bfloat16)
+
+        scatter.add_y_of(nearest(0))
 
         @pl.loop(0, chips)
         def _(chip):
@@ -1256,12 +1249,16 @@
         pltpu.VMEM(block, jnp.bfloat16),
         pltpu.VMEM(block, jnp.bfloat16),
         pltpu.SemaphoreType.DMA((2, chips)),
-        pltpu.VMEM((features, 2 * width), jnp.bfloat16),
+        pltpu.VMEM((2 * width, features), jnp.bfloat16),
         pltpu.VMEM((width, features), jnp.bfloat16),
-        pltpu.SemaphoreType.DMA((2, 2)),
+        pltpu.VMEM(d_out_all.shape, jnp.bfloat16),
+        pltpu.SemaphoreType.DMA((2, 3)),
+        pltpu.SemaphoreType.DMA((1,)),
     ]
     scratch += Gather.sems(depth) + Scatter.scratch(depth, tokens, wide)
-    return call(kernel, out, scratch, 3, "experts", send, d_out_all, in_own, out_own)
+    return call(
+        kernel, out, scratch, 3, "experts", send, d_out_all, in_own, out_own, outside=(1,)
+    )
 
 
 def finish(
@@ -1317,8 +1314,6 @@
         for step in steps:
             attn.add_cores(step)
         query_.start()
-        swaps[1].start()
-        swaps[2].start()
         products(hidden_ref, hidden_there, keyval_ref, keyval_there, keyval_part)
         keyval_.start()
         for step in steps:
@@ -1345,6 +1340,8 @@
             keyval_.add_cores(step)
         attn.last(attn_out.own())
         attn_out.start()
+        swaps[1].start()
+        swaps[2].start()
         swaps[0].wait()
         small_out.own()[...] = (small_mine[:, side_columns(True)] + small_came[...]).astype(
             jnp.bfloat16
@@ -1426,7 +1423,7 @@
 
 
 def widen(query, keyval, attn, grad_in, in_there, grad_out, out_there):
-    half, quarter, features = query.shape[0], grad_out.shape[0], grad_out.shape[1]
+    quarter, features = grad_out.shape
     steps = 4
 
     def kernel(*refs):
@@ -1436,8 +1433,7 @@
         keyval_out[...] = keyval_ref[...].astype(jnp.float32)
         attn_out[...] = attn_ref[...].astype(jnp.float32)
         both = in_ref[...] + in_there_ref[...].astype(jnp.float32)
-        in_out[0, 0] = both[:, :quarter]
-        in_out[0, 1] = both[:, quarter:]
+        in_out[...] = both
         out_out[0] = out_ref[...] + out_there_ref[...].astype(jnp.float32)
 
     def rows(values):
@@ -1451,13 +1447,13 @@
             jax.ShapeDtypeStruct(query.shape, jnp.float32),
             jax.ShapeDtypeStruct(keyval.shape, jnp.float32),
             jax.ShapeDtypeStruct(attn.shape, jnp.float32),
-            jax.ShapeDtypeStruct((1, 2, features, quarter), jnp.float32),
+            jax.ShapeDtypeStruct(grad_in.shape, jnp.float32),
             jax.ShapeDtypeStruct((1, quarter, features), jnp.float32),
         ],
         in_specs=[rows(values) for values in operands],
         out_specs=[
             rows(query), rows(keyval), rows(attn),
-            pl.BlockSpec((1, 2, features // steps, quarter), lambda i: (0, 0, i, 0)),
+            rows(grad_in),
             pl.BlockSpec((1, quarter // steps, features), lambda i: (0, i, 0)),
         ],
         compiler_params=pltpu.CompilerParams(vmem_limit_bytes=VMEM_LIMIT),
@@ -1484,18 +1480,17 @@
     numbers = jnp.arange(128, dtype=jnp.int32)
     named = jnp.any(routes[0][:, :, None] == (numbers % experts)[None, None, :], axis=1)
     chosen = (named & (numbers < 2 * experts)[None, :]).astype(jnp.float32)
-    in_own = jnp.concatenate([w_in[0, 0], w_in[0, 1]], axis=1)
-
-    d_out_all, w_query_there, w_keyval_there, w_out_attn_there, small_there = front(
-        grad_out, w_query, w_keyval, w_out_attn, small
+    in_own = jnp.swapaxes(w_in[0], 1, 2).reshape(-1, D)
+
+    d_out_all, w_query_there, w_keyval_there, small_there = front(
+        grad_out, w_query, w_keyval, small
     )
     projections = (w_query, w_query_there, w_keyval, w_keyval_there)
     (
         query, keyval, level, mixed, hidden_own, hidden_there, mixed_own, mixed_there, middle,
-        send, gates,
+        send, gates, w_out_attn_there,
     ) = attend(
-        x, small, small_there, projections + (w_out_attn, w_out_attn_there), angles, docs, chosen,
-        experts,
+        x, small, small_there, projections, w_out_attn, angles, docs, chosen, experts
     )
     returned, results, grad_in, grad_in_other, grad_out_matrix, grad_out_other = run_experts(
         send, d_out_all, in_own, w_out[0], experts
@@ -1524,7 +1519,7 @@
         attn_sum,
         small_sum[experts + 1],
         small_sum[:experts].T,
-        grad_w_in,
+        jnp.swapaxes(grad_w_in.reshape(2, -1, D), 1, 2)[None],
         grad_w_out,
     )
 

time: 412 us -> 359 us (0.87)
  Pallas kernels: 393 us -> 346 us
  local copies, waits for them, and re-layouts: 12.4 us -> 7.13 us
    pallas_call x5, Pallas kernels: 383 us -> 337 us  [call(): pl.pallas_call(kernel, out_shape=out, in_specs=[spec(i, outside) for i in...]
where the time goes in v5:
time: 359 us; the launch traced here: 358 us
  Pallas kernels  346 us (96%)
  local copies, waits for them, and re-layouts  7.13 us (2%)
  other arithmetic  3.93 us (1%)
    pallas_call x5, Pallas kernels, call(): pl.pallas_call(kernel, out_shape=out, in_specs=[spec(i, outside) for i in...  337 us
    pallas_call x1, Pallas kernels, widen(): pl.pallas_call(kernel, grid=(steps,), out_shape=[jax.ShapeDtypeStruct(que...  9.26 us

profile of v5, /device:TPU:0, one launch (start us, length us, event | category | flops | bytes accessed | tf_op | source)
XLA Modules:
  0.0 358.1 jit_solution(309931541258817481)
XLA Ops:
  0.6 0.7 dynamic-slice_bitcast_fusion
  1.3 0.1 pad.7.clone
  1.4 0.7 broadcast_in_dim.25
  2.1 0.7 broadcast_in_dim.26
  2.8 0.8 compare_reduce_fusion
  3.6 1.4 maximum_maximum_fusion.small_ref
  5.0 0.6 and_convert_fusion.chosen_ref
  5.6 0.7 copy.25.doc_column
  6.4 0.3 fusion
  6.7 0.8 pad_maximum_fusion
  7.5 44.3 %front.1 = (bf16[2048,1536]{1,0:T(8,128)(2,1)}, bf16[768,1536]{1,0:T(8,128)(2,1)}, bf16[768,512]{1,0:T(8,128)(2,1)}, bf16[16,768]{1,0:T(8,128)(2,1)}) custom-call(bf16[128,1536]{1,0:T(8,128)(2,1)} %bitcast.23, bf16[768,1536]{1,0:T(8,128)(2,1)} %query_own.3, bf16[768,512]{1,0:T(8,128)(2,1)} %keyval_own.3, bf16[16,768]{1,0:T(8,128)(2,1)} %maximum_maximum_fusion.small_ref), custom_call_target="tpu_custom_call" | custom-call | tf_op jit(solution)/shard_map/front/pallas_call | solution.py:662
  51.8 45.0 %attend.1 = (bf16[128,1536]{1,0:T(8,128)(2,1)}, bf16[2048,512]{1,0:T(8,128)(2,1)}, f32[1536,1]{1,0:T(8,128)}, f32[128,1536]{1,0:T(8,128)}, bf16[128,768]{1,0:T(8...) custom-call(bf16[128,1536]{1,0:T(8,128)(2,1)} %bitcast.21, ...), custom_call_target="tpu_custom_call" | custom-call | tf_op jit(solution)/shard_map/attend/pallas_call | solution.py:662
  96.8 104.7 %experts.1 = (f32[128,1664]{1,0:T(8,128)}, bf16[8,128,1536]{2,1,0:T(8,128)(2,1)}, f32[384,1536]{1,0:T(8,128)}, bf16[384,1536]{1,0:T(8,128)(2,1)}, f32[192,1536]{1,0:T(8,128)}, /*index=5*/bf16[192,1536]{1,0:T(8,128)(2,1)}) custom-call(bf16[128,1664]{1,0:T(8,128)(2,1)} %get-tuple-element.56.send_ref, bf16[2048,1536]{1,0:T(8,128)(2,1)} %get-tuple-element.57.d_out_far, ...), custom_call_target="tpu_custom_call" | custom-call | tf_op jit(solution)/shard_map/experts/pallas_call | solution.py:662
  201.5 64.0 %attend_back.1 = (bf16[128,1536]{1,0:T(8,128)(2,1)}, f32[128,1536]{1,0:T(8,128)}, bf16[128,1536]{1,0:T(8,128)(2,1)}, bf16[128,1536]{1,0:T(8,128)(2,1)}, bf16[128...) custom-call(f32[128,1664]{1,0:T(8,128)} %get-tuple-element.58.return, ...), custom_call_target="tpu_custom_call" | custom-call | tf_op jit(solution)/shard_map/attend_back/pallas_call | solution.py:662
  265.5 79.0 %finish.1 = (bf16[768,1536]{1,0:T(8,128)(2,1)}, bf16[768,1536]{1,0:T(8,128)(2,1)}, bf16[768,512]{1,0:T(8,128)(2,1)}, f32[16,768]{1,0:T(8,128)}, bf16[128,1536]{1...) custom-call(bf16[128,1536]{1,0:T(8,128)(2,1)} %bitcast.22, ...), custom_call_target="tpu_custom_call" | custom-call | tf_op jit(solution)/shard_map/finish/pallas_call | solution.py:662
  344.5 1.4 slice_reduce_fusion
  346.0 1.3 slice_bitcast_fusion
  347.3 0.0 copy-start
  347.3 0.0 copy-start.1
  347.3 9.3 %widen.1 = (f32[768,1536]{1,0:T(8,128)}, f32[768,512]{1,0:T(8,128)}, f32[768,1536]{1,0:T(8,128)}, f32[384,1536]{1,0:T(8,128)}, f32[1,192,1536]{2,1,0:T(8,128)}) custom-call(bf16[768,1536]{1,0:T(8,128)(2,1)} %get-tuple-element.84.refs_0_, bf16[768,512]{1,0:T(8,128)(2,1)} %get-tuple-element.85.refs_1_, bf16[768,1536]{1,0:T(8,128)(2,1)} %get-tuple-element.86.refs_2_, ...), custom_call_target="tpu_custom_call" | custom-call | tf_op jit(solution)/shard_map/widen/pallas_call | solution.py:1443
  356.6 0.0 copy-done
  356.6 0.7 copy.29
  357.3 0.0 copy-done.1
  357.3 0.7 copy.30
  (5 shorter events, 0.0 us)
Async XLA Ops:
  347.3 9.3 %copy-start = (bf16[128,1536]{1,0:T(8,128)(2,1)S(1)}, bf16[128,1536]{1,0:T(8,128)(2,1)}, u32[]{:S(2)}) copy-start(bf16[128,1536]{1,0:T(8,128)(2,1)} %get-tuple-element.67) | copy-start | bytes 1179652
  347.3 10.0 %copy-start.1 = (bf16[128,1536]{1,0:T(8,128)(2,1)S(1)}, bf16[128,1536]{1,0:T(8,128)(2,1)}, u32[]{:S(2)}) copy-start(bf16[128,1536]{1,0:T(8,128)(2,1)} %get-tuple-element.82) | copy-start | bytes 1179652

commit v6 on v5

--- a/solution.py
+++ b/solution.py
@@ -444,8 +444,9 @@
 
 
 class Gather:
-    def __init__(self, out, rows, sems):
-        self.out, self.rows = out, rows
+    def __init__(self, out, rows, sems, part=0, parts=1):
+        self.out, self.block, self.rows = out, rows, rows // parts
+        self.first = part * self.rows
         self.z_sems, self.y_sems, self.c_sems = sems
         self.z, self.y, self.c, self.depth = chip_place()
 
@@ -458,7 +459,8 @@
         ]
 
     def slot(self, z, y, c):
-        return self.out.at[pl.ds(pl.multiple_of(ctx_of(z, y, c) * self.rows, 16), self.rows)]
+        start = ctx_of(z, y, c) * self.block + self.first
+        return self.out.at[pl.ds(pl.multiple_of(start, 16), self.rows)]
 
     def own(self):
         return self.slot(self.z, self.y, self.c)
@@ -482,6 +484,8 @@
 
     def start(self, source=None):
         z, depth = self.z, self.depth
+        if source is not None:
+            source = source.at[pl.ds(self.first, self.rows)]
         pl.when(z < depth - 1)(lambda: self.on_z(0, z, source).start())
         pl.when(z > 0)(lambda: self.on_z(1, z, source).start())
         self.on_y(z, source=source).start()
@@ -516,18 +520,33 @@
                 self.on_core(of_z, of_y).wait_send()
                 self.on_core(of_z, of_y, mine=False).wait_recv()
 
-    def run(self):
-        self.start()
-        self.follow()
-
-    def follow(self):
-        self.along_z(1)
-        self.along_y(0)
-        for step in range(1, self.depth):
-            if step + 1 < self.depth:
-                self.along_z(step + 1)
-            self.along_y(step)
-        self.finish()
+
+class Several:
+    def __init__(self, members):
+        self.members = members
+
+    def __getattr__(self, name):
+        def every(*given, **named):
+            for member in self.members:
+                getattr(member, name)(*given, **named)
+
+        return every
+
+
+def gather_parts(out, rows, sems, parts):
+    return Several(
+        [Gather(out, rows, sems[3 * i : 3 * i + 3], i, parts) for i in range(parts)]
+    )
+
+
+def follow(gather):
+    depth = chip_place()[3]
+    gather.along_z(1)
+    for step in range(depth):
+        if step >= 1 and step + 1 < depth:
+            gather.along_z(step + 1)
+        gather.along_y(step)
+    gather.finish()
 
 
 def add_into(target, terms, rows):
@@ -543,48 +562,65 @@
 
 
 class Scatter:
-    def __init__(self, part, scratch, sums=None):
+    def __init__(self, part, scratch, sums=None, piece=0, pieces=1):
         self.part = part
         self.from_core, self.totals, self.from_y, self.from_z = scratch[:4]
         self.sums = self.totals if sums is None else sums
         self.c_sems, self.y_sems, self.z_sems = scratch[4:]
-        self.rows = self.totals.shape[1]
+        self.block = self.totals.shape[1]
+        self.rows = self.block // pieces
+        self.first = piece * self.rows
         self.z, self.y, self.c, self.depth = chip_place()
 
     @staticmethod
-    def scratch(depth, rows, columns):
+    def sems(depth):
+        return [
+            pltpu.SemaphoreType.DMA((2, 2 * depth)),
+            pltpu.SemaphoreType.DMA((2, depth)),
+            pltpu.SemaphoreType.DMA((2, 2, depth)),
+        ]
+
+    @staticmethod
+    def scratch(depth, rows, columns, pieces=1):
         return [
             pltpu.VMEM((2 * depth, rows, columns), jnp.bfloat16),
             pltpu.VMEM((2 * depth, rows, columns), jnp.bfloat16),
             pltpu.VMEM((depth, rows, columns), jnp.bfloat16),
             pltpu.VMEM((depth + 1, rows, columns), jnp.bfloat16),
-            pltpu.SemaphoreType.DMA((2, 2 * depth)),
-            pltpu.SemaphoreType.DMA((2, depth)),
-            pltpu.SemaphoreType.DMA((2, 2, depth)),
-        ]
+        ] + Scatter.sems(depth) * pieces
+
+    def of(self, ref, place):
+        return ref.at[place, pl.ds(self.first, self.rows)]
 
     def split(self):
         return len(self.part.shape) == 3
 
     def share(self, chip, c):
-        return self.part.at[pl.ds(pl.multiple_of((chip * 2 + c) * self.rows, 16), self.rows)]
+        start = (chip * 2 + c) * self.block + self.first
+        return self.part.at[pl.ds(pl.multiple_of(start, 16), self.rows)]
 
     def on_core(self, chip):
         target = {"ctx": ctx_of(self.z, self.y, 1 - self.c)}
-        source = self.part.at[chip] if self.split() else self.share(chip, 1 - self.c)
-        return remote(source, self.from_core.at[chip], self.c_sems, (chip,), target)
+        source = self.of(self.part, chip) if self.split() else self.share(chip, 1 - self.c)
+        return remote(source, self.of(self.from_core, chip), self.c_sems, (chip,), target)
+
+    def send_core(self, chip):
+        self.on_core(chip).start()
+
+    def send_y(self, of_z):
+        self.on_y(of_z).start()
 
     def on_y(self, of_z):
         target = {"ctx": ctx_of(self.z, 1 - self.y, self.c)}
-        source = self.sums.at[of_z * 2 + 1 - self.y]
-        return remote(source, self.from_y.at[of_z], self.y_sems, (of_z,), target)
+        source = self.of(self.sums, of_z * 2 + 1 - self.y)
+        return remote(source, self.of(self.from_y, of_z), self.y_sems, (of_z,), target)
 
     def on_z(self, way, of_z):
         goal = jnp.minimum(self.z + 1, self.depth - 1) if way == 0 else jnp.maximum(self.z - 1, 0)
         place = of_z if way == 0 else jnp.where(of_z == goal, self.depth, of_z)
-        source = self.totals.at[of_z * 2 + self.y]
+        source = self.of(self.totals, of_z * 2 + self.y)
         target = {"ctx": ctx_of(goal, self.y, self.c)}
-        return remote(source, self.from_z.at[place], self.z_sems, (way, of_z), target)
+        return remote(source, self.of(self.from_z, place), self.z_sems, (way, of_z), target)
 
     def start(self):
         def send(of_z):
@@ -597,8 +633,9 @@
     def add_chip(self, of_z, other, send=True):
         chip = of_z * 2 + (1 - self.y if other else self.y)
         self.on_core(chip).wait_recv()
-        own = self.sums.at[chip] if self.split() else self.share(chip, self.c)
-        add_into(self.sums.at[chip], (own, self.from_core.at[chip]), self.rows)
+        total = self.of(self.sums, chip)
+        own = total if self.split() else self.share(chip, self.c)
+        add_into(total, (own, self.of(self.from_core, chip)), self.rows)
         if other and send:
             self.on_y(of_z).start()
 
@@ -613,14 +650,15 @@
         z, depth = self.z, self.depth
         self.on_y(of_z).wait_recv()
         place = of_z * 2 + self.y
-        total, own, other = self.totals.at[place], self.sums.at[place], self.from_y.at[of_z]
+        total, own = self.of(self.totals, place), self.of(self.sums, place)
+        other = self.of(self.from_y, of_z)
         upward, downward = (of_z > z) & (z > 0), (of_z < z) & (z < depth - 1)
         pl.when(upward)(lambda: self.on_z(0, of_z).wait_recv())
         pl.when(downward)(lambda: self.on_z(1, of_z).wait_recv())
 
         @pl.when(upward | downward)
         def _():
-            add_into(total, (own, other, self.from_z.at[of_z]), self.rows)
+            add_into(total, (own, other, self.of(self.from_z, of_z)), self.rows)
 
         @pl.when(jnp.logical_not(upward | downward))
         def _():
@@ -634,8 +672,9 @@
 
     def last(self, result):
         z, depth = self.z, self.depth
-        own = self.totals.at[z * 2 + self.y]
-        low, high = self.from_z.at[z], self.from_z.at[depth]
+        own = self.of(self.totals, z * 2 + self.y)
+        low, high = self.of(self.from_z, z), self.of(self.from_z, depth)
+        result = result.at[pl.ds(self.first, self.rows)]
         pl.when(z > 0)(lambda: self.on_z(0, z).wait_recv())
         pl.when(z < depth - 1)(lambda: self.on_z(1, z).wait_recv())
         inside = (z > 0) & (z < depth - 1)
@@ -653,16 +692,48 @@
             pl.when(of_z < self.z)(lambda: self.on_z(1, of_z).wait_send())
 
 
-def call(kernel, out, scratch, number, name, *operands, outside=(), outside_out=()):
+def scatter_parts(part, scratch, pieces, sums=None):
+    arrays, sems = tuple(scratch[:4]), tuple(scratch[4:])
+    return Several(
+        [
+            Scatter(part, arrays + sems[3 * i : 3 * i + 3], sums, i, pieces)
+            for i in range(pieces)
+        ]
+    )
+
+
+def call(kernel, out, scratch, number, name, *operands, outside=(), outside_out=(), late=()):
+    many = isinstance(out, (tuple, list))
+    count, results = len(operands), len(out) if many else 1
+    late = tuple(late)
+
     def spec(position, far):
         return pl.BlockSpec(memory_space=pl.ANY if position in far else pltpu.VMEM)
 
-    many = isinstance(out, (tuple, list))
-    out_specs = [spec(i, outside_out) for i in range(len(out) if many else 1)]
+    def with_late(*refs):
+        near, sems = refs[-len(late) - 1 : -1], refs[-1]
+        copies = {
+            i: pltpu.make_async_copy(refs[i], near[k], sems.at[k]) for k, i in enumerate(late)
+        }
+        for copy in copies.values():
+            copy.start()
+        held = [near[late.index(i)] if i in late else refs[i] for i in range(count)]
+
+        def arrive(*which):
+            for i in which:
+                copies[i].wait()
+
+        kernel(arrive, *held, *refs[count : -len(late) - 1])
+
+    if late:
+        scratch = list(scratch) + [pltpu.VMEM(operands[i].shape, operands[i].dtype) for i in late]
+        scratch.append(pltpu.SemaphoreType.DMA((len(late),)))
+    far = tuple(outside) + late
+    out_specs = [spec(i, outside_out) for i in range(results)]
     return pl.pallas_call(
-        kernel,
+        with_late if late else kernel,
         out_shape=out,
-        in_specs=[spec(i, outside) for i in range(len(operands))],
+        in_specs=[spec(i, far) for i in range(count)],
         out_specs=out_specs if many else out_specs[0],
         scratch_shapes=scratch,
         compiler_params=pltpu.CompilerParams(
@@ -720,13 +791,15 @@
         d_out_ref, query_ref, keyval_ref, small_ref,
         d_out_all, query_there, keyval_there, small_there, *sems,
     ):
-        gather = Gather(d_out_all, rows, sems[:3])
-        query_sems, keyval_sems, small_sems, own_sem = sems[3:]
+        gather = gather_parts(d_out_all, rows, sems[:6], 2)
+        query_sems, keyval_sems, small_sems, own_sem = sems[6:]
         query = Relay(query_ref, query_there, query_sems, parts=2)
         keyval = Relay(keyval_ref, keyval_there, keyval_sems)
         partner = {"wa": 1 - lax.axis_index("wa")}
         swap = remote(small_ref, small_there, small_sems, (0,), partner)
-        keep = pltpu.make_async_copy(d_out_ref, gather.own(), own_sem.at[0])
+        keep = pltpu.make_async_copy(
+            d_out_ref, Gather(d_out_all, rows, sems[:3]).own(), own_sem.at[0]
+        )
         keep.start()
         greet(across_x=True)
         swap.start()
@@ -756,7 +829,7 @@
         jax.ShapeDtypeStruct((count * rows, d_out.shape[1]), d_out.dtype),
         like(w_query), like(w_keyval), like(small),
     ]
-    scratch = Gather.sems(depth) + [Relay.semaphores()] * 2
+    scratch = Gather.sems(depth) * 2 + [Relay.semaphores()] * 2
     scratch += [pltpu.SemaphoreType.DMA((2, 1)), pltpu.SemaphoreType.DMA((1,))]
     every = range(4)
     return call(
@@ -816,24 +889,21 @@
 def attend(x, small, small_there, projections, w_out_attn, angles, docs, chosen, experts):
     count, tokens, features = lax.axis_size("ctx"), x.shape[0], x.shape[1]
     depth, length = count // 4, count * tokens
-    kv_columns, half = projections[2].shape[1], features // 2
+    kv_columns = projections[2].shape[1]
 
     def kernel(
-        x_ref, small_ref, small_there_ref, query_own, query_other, keyval_own, keyval_other,
-        attn_own, cosine_ref, sine_ref, doc_row, doc_column, chosen_ref,
-        query, keyval, level, mixed, hidden_own, hidden_there, mixed_own, mixed_there, middle,
-        send, gates_out, attn_other,
-        hidden, mixed_low, full, stacked, bias, x_sems, attn_sems, *sems,
+        arrive, x_ref, small_ref, small_there_ref, query_own, query_other, keyval_own, keyval_other,
+        attn_own, attn_own_far, cosine_ref, sine_ref, doc_row, doc_column, chosen_ref,
+        query, keyval, level, mixed, hidden, mixed_low, middle, send, gates_out, attn_other,
+        full, stacked, bias, attn_sems, *sems,
     ):
-        gather = Gather(keyval, tokens, sems)
-        attn = Relay(attn_own, attn_other, attn_sems, parts=2)
-        partner = {"wa": 1 - lax.axis_index("wa")}
+        gather = gather_parts(keyval, tokens, sems, 2)
+        attn = Relay(attn_own_far, attn_other, attn_sems, parts=2)
         greet(across_x=True)
         attn.start()
         fill_small(full, small_ref, small_there_ref)
         residual = x_ref[...].astype(jnp.float32)
         hidden[...] = normed(residual, full[experts : experts + 1]).astype(jnp.bfloat16)
-        hidden_own[...] = hidden[:, side_columns(True)]
         own, other = hidden[:, side_columns(True)], hidden[:, side_columns(False)]
         cosine, sine = cosine_ref[...], sine_ref[...]
 
@@ -842,19 +912,19 @@
                 other, matrix_other[...], preferred_element_type=jnp.float32
             )
 
+        arrive(5, 6)
         pre = onto(keyval_own, keyval_other)
         keys = turned(pre[:, : kv_columns // 2], cosine, sine)
         block = jnp.concatenate([keys, pre[:, kv_columns // 2 :]], axis=1)
-        gather.own()[...] = block.astype(jnp.bfloat16)
+        Gather(keyval, tokens, sems[:3]).own()[...] = block.astype(jnp.bfloat16)
         gather.start()
-        swap = remote(hidden.at[:, side_columns(False)], hidden_there, x_sems, (0,), partner)
-        swap.start()
+        arrive(3, 4)
         query[...] = turned(onto(query_own, query_other), cosine, sine).astype(jnp.bfloat16)
         bias[...] = allowed_bias(doc_row[...], doc_column[...], tokens)
         for head in range(HEADS):
             rows = slice(head * tokens, (head + 1) * tokens)
             stacked[rows, :] = query[:, head * 128 : (head + 1) * 128]
-        gather.follow()
+        follow(gather)
 
         @pl.loop(0, HEADS // 2)
         def _(pair):
@@ -867,22 +937,19 @@
             top = jnp.max(scores, axis=-1, keepdims=True)
             weights = jnp.exp(scores - top)
             total = jnp.sum(weights, axis=-1, keepdims=True)
-            probs = (weights / total).astype(jnp.bfloat16)
+            probs = (weights * (1 / total)).astype(jnp.bfloat16)
             mixture = jnp.dot(probs, val_part, preferred_element_type=jnp.float32)
             for part in range(2):
                 columns = pl.ds(pl.multiple_of((pair * 2 + part) * 128, 128), 128)
                 mixed[:, columns] = mixture[part * tokens : (part + 1) * tokens]
-            level[rows, :] = top + jnp.log(total)
+            column = jnp.broadcast_to(top + jnp.log(total), (2 * tokens, 128))
+            level[pl.ds(pair, 1), :] = jnp.transpose(column)[:1]
             pl.when(pair == HEADS // 4)(lambda: attn.pass_on(0))
 
         attn.pass_on(1)
         mixed_low[...] = mixed[...].astype(jnp.bfloat16)
-        mixed_own[...] = mixed_low[:, side_columns(True)]
-        swap_mixed = remote(
-            mixed_low.at[:, side_columns(False)], mixed_there, x_sems, (1,), partner
-        )
-        swap_mixed.start()
         attn.finish()
+        arrive(7)
         own, other = mixed_low[:, side_columns(True)], mixed_low[:, side_columns(False)]
         middle[...] = residual + onto(attn_own, attn_other)
         hidden_two = normed(middle[...], full[experts + 1 : experts + 2]).astype(jnp.bfloat16)
@@ -897,32 +964,27 @@
         carried = jnp.where(lane < experts, high, jnp.where(lane < 2 * experts, gates - high, 0.0))
         send[:, features:] = carried.astype(jnp.bfloat16)
         gates_out[...] = jnp.where(lane < experts, gates, 0.0)
-        swap.wait()
-        swap_mixed.wait()
 
     def shape(rows, columns, kind=jnp.bfloat16):
         return jax.ShapeDtypeStruct((rows, columns), kind)
 
     wide = features + 128
     out = [
-        shape(tokens, features), shape(length, kv_columns), shape(HEADS * tokens, 1, jnp.float32),
-        shape(tokens, features, jnp.float32),
-        shape(tokens, half), shape(tokens, half), shape(tokens, half), shape(tokens, half),
+        shape(tokens, features), shape(length, kv_columns), shape(8, 2 * tokens, jnp.float32),
+        shape(tokens, features, jnp.float32), shape(tokens, features), shape(tokens, features),
         shape(tokens, features, jnp.float32), shape(tokens, wide), shape(tokens, 128, jnp.float32),
         shape(*w_out_attn.shape),
     ]
     scratch = [
-        pltpu.VMEM((tokens, features), jnp.bfloat16),
-        pltpu.VMEM((tokens, features), jnp.bfloat16),
         pltpu.VMEM((small.shape[0], features), jnp.float32),
         pltpu.VMEM((HEADS * tokens, HEAD_DIM), jnp.bfloat16),
         pltpu.VMEM((tokens, length), jnp.float32),
-        pltpu.SemaphoreType.DMA((2, 2)),
         Relay.semaphores(),
-    ] + Gather.sems(depth)
+    ] + Gather.sems(depth) * 2
     return call(
         kernel, out, scratch, 2, "attend",
-        x, small, small_there, *projections, w_out_attn, *angles, *docs, chosen,
+        x, small, small_there, *projections, w_out_attn, w_out_attn, *angles, *docs, chosen,
+        outside=(8,), late=(5, 6, 3, 4, 7),
     )
 
 
@@ -935,41 +997,53 @@
 
 def attend_back(
     returned, gates, small, small_there, middle, d_out, send, attn_own, attn_other, query, keyval,
-    angles, docs, level, mixed, results, experts,
+    angles, docs, level, mixed, hidden, mixed_low, results, experts,
 ):
     count, tokens, features = lax.axis_size("ctx"), query.shape[0], query.shape[1]
     depth, length, kv_columns = count // 4, keyval.shape[0], keyval.shape[1]
 
     def kernel(
-        returned_ref, gates_ref, small_ref, small_there_ref, middle_ref, d_out_ref, send_ref,
+        arrive, returned_ref, gates_ref, small_ref, small_there_ref, middle_ref, d_out_ref, send_ref,
         attn_own_ref, attn_other_ref, query_ref, keyval_ref, cosine_ref, sine_ref, doc_row,
-        doc_column, level_ref, mixed_ref, results_ref,
+        doc_column, level_ref, mixed_ref, hidden_ref, mixed_low_ref, results_ref,
         output, grad_middle, grad_middle_low, grad_middle_there, grad_query, grad_query_there,
-        grad_keyval, grad_keyval_there, small_grads,
+        grad_keyval, grad_keyval_there, small_grads, hidden_own, hidden_there, mixed_own,
+        mixed_there,
         full, grad_mixed, turned_query, own_keyval, result_sum, stacked, grads, bias, delta, total,
         part, x_sems, *scratch,
     ):
-        result = Scatter(
-            None, (None,) + tuple(scratch[:3]) + (None,) + tuple(scratch[3:5]), results_ref
+        result = scatter_parts(
+            None, (None,) + tuple(scratch[:3]) + tuple(scratch[3:9]), 2, results_ref
         )
-        keyval_sum = Scatter(part, scratch[5:])
+        keyval_sum = scatter_parts(part, scratch[9:], 2)
         partner = {"wa": 1 - lax.axis_index("wa")}
         swaps = [
             remote(source, target, x_sems, (i,), partner)
             for i, (source, target) in enumerate(
                 [(grad_middle_low, grad_middle_there), (grad_query, grad_query_there),
-                 (grad_keyval, grad_keyval_there)]
+                 (grad_keyval, grad_keyval_there),
+                 (hidden_ref.at[:, side_columns(False)], hidden_there),
+                 (mixed_low_ref.at[:, side_columns(False)], mixed_there)]
             )
         ]
         greet(across_x=True)
-        for k in (depth - 1, depth - 2):
-            result.on_y(nearest(k)).start()
+        arrive(19)
+        for k in range(depth - 1, 0, -1):
+            result.send_y(nearest(k))
+        swaps[3].start()
+        swaps[4].start()
+        hidden_own[...] = hidden_ref[:, side_columns(True)]
+        mixed_own[...] = mixed_low_ref[:, side_columns(True)]
         fill_small(full, small_ref, small_there_ref)
+        arrive(0, 4, 5, 6)
         lane = lax.broadcasted_iota(jnp.int32, (tokens, 128), 1)
         gates = gates_ref[...]
         grad_gates = jnp.where(lane < experts, returned_ref[:, features:], 0.0)
         inner = jnp.sum(gates * grad_gates, axis=1, keepdims=True)
         grad_logits = (gates * (grad_gates - inner)).astype(jnp.bfloat16)
+        z = chip_place()[0]
+        at_end = (z == 0) | (z == depth - 1)
+        within = jnp.logical_not(at_end)
         grad_two = returned_ref[:, :features] + jnp.dot(
             grad_logits, router_block(full, experts), preferred_element_type=jnp.float32
         )
@@ -981,23 +1055,26 @@
         small_grads[:experts] = grad_router[:experts]
         row = lax.broadcasted_iota(jnp.int32, (small_grads.shape[0] - experts, 1), 0)
         small_grads[experts:] = jnp.where(row == 1, grad_gain, 0.0)
+        arrive(7, 8)
         grad_mixed[:, side_columns(True)] = rows_by_rows(
             grad_middle_low[...], attn_own_ref[...]
         ).astype(jnp.bfloat16)
         grad_mixed[:, side_columns(False)] = rows_by_rows(
             grad_middle_low[...], attn_other_ref[...]
         ).astype(jnp.bfloat16)
-        bias[...] = allowed_bias(doc_row[...], doc_column[...], tokens)
+        allowed = jnp.transpose(allowed_bias(doc_row[...], doc_column[...], tokens))
+        bias[:, :tokens] = allowed
+        bias[:, tokens:] = allowed
         total[...] = jnp.zeros_like(total)
+        arrive(9, 10, 16)
         for head in range(HEADS):
             rows = slice(head * tokens, (head + 1) * tokens)
             columns = slice(head * 128, head * 128 + 128)
             stacked[rows, :] = query_ref[:, columns]
             grads[rows, :] = grad_mixed[:, columns]
-            delta[rows, :] = jnp.sum(
-                grad_mixed[:, columns].astype(jnp.float32) * mixed_ref[:, columns],
-                axis=-1,
-                keepdims=True,
+            product = grad_mixed[:, columns].astype(jnp.float32) * mixed_ref[:, columns]
+            delta[head // 2 : head // 2 + 1, (head % 2) * tokens : (head % 2 + 1) * tokens] = (
+                jnp.sum(jnp.transpose(product), axis=0, keepdims=True)
             )
 
         @pl.loop(0, HEADS // 2)
@@ -1008,21 +1085,24 @@
             val_columns = pl.ds(pl.multiple_of(kind * 128 + 256, 128), 128)
             key_part, val_part = keyval_ref[:, key_columns], keyval_ref[:, val_columns]
             own, grad = stacked[rows, :], grads[rows, :]
-            scores = rows_by_rows(own, key_part) * HEAD_DIM**-0.5
-            scores = (scores.reshape(2, tokens, -1) + bias[...][None]).reshape(scores.shape)
-            probs = jnp.exp(scores - level_ref[rows, :])
-            grad_probs = rows_by_rows(grad, val_part)
-            grad_scores = (probs * (grad_probs - delta[rows, :])).astype(jnp.bfloat16)
-            own_grad = jnp.dot(grad_scores, key_part, preferred_element_type=jnp.float32)
+            pair_row = pl.ds(pair, 1)
+            scores = rows_by_rows(key_part, own) * HEAD_DIM**-0.5 + bias[...]
+            probs = jnp.exp(scores - level_ref[pair_row, :])
+            grad_probs = rows_by_rows(val_part, grad)
+            grad_scores = (probs * (grad_probs - delta[pair_row, :])).astype(jnp.bfloat16)
+            own_grad = jnp.transpose(columns_by_columns(key_part, grad_scores))
             for half in range(2):
                 columns = pl.ds(pl.multiple_of((pair * 2 + half) * 128, 128), 128)
                 turned_query[:, columns] = (
                     own_grad[half * tokens : (half + 1) * tokens] * HEAD_DIM**-0.5
                 )
-            total[:, key_columns] += columns_by_columns(grad_scores, own) * HEAD_DIM**-0.5
-            total[:, val_columns] += columns_by_columns(probs.astype(jnp.bfloat16), grad)
-            pl.when(pair == 1)(lambda: result.on_y(nearest(depth - 3)).start())
-            pl.when(pair == HEADS // 4)(lambda: result.add_y_of(nearest(depth - 1)))
+            total[:, key_columns] += (
+                jnp.dot(grad_scores, own, preferred_element_type=jnp.float32) * HEAD_DIM**-0.5
+            )
+            total[:, val_columns] += jnp.dot(
+                probs.astype(jnp.bfloat16), grad, preferred_element_type=jnp.float32
+            )
+            pl.when((pair == HEADS // 4) & at_end)(lambda: result.add_y_of(nearest(depth - 1)))
 
         part[...] = total[...].astype(jnp.bfloat16)
         keyval_sum.start()
@@ -1032,9 +1112,10 @@
         steps = range(depth - 1, -1, -1)
         for step in steps:
             keyval_sum.add_cores(step)
-        for k in range(depth - 4, -1, -1):
-            result.on_y(nearest(k)).start()
-        result.add_y_of(nearest(depth - 2))
+        result.send_y(nearest(0))
+        pl.when(within)(lambda: result.add_y_of(nearest(depth - 1)))
+        for k in range(depth - 2, 0, -1):
+            result.add_y_of(nearest(k))
         for step in steps:
             keyval_sum.add_y(step)
         keyval_sum.last(own_keyval)
@@ -1043,8 +1124,7 @@
             [keys, own_keyval[:, kv_columns // 2 :]], axis=1
         ).astype(jnp.bfloat16)
         swaps[2].start()
-        for k in range(depth - 3, -1, -1):
-            result.add_y_of(nearest(k))
+        result.add_y_of(nearest(0))
         result.last(result_sum)
         output[...] = (middle_ref[...] + result_sum[...]).astype(jnp.bfloat16)
         keyval_sum.finish()
@@ -1060,7 +1140,7 @@
     out = [
         shape(rows), shape(rows, jnp.float32), shape(rows), shape(rows), shape(rows), shape(rows),
         shape(narrow), shape(narrow), shape(small_shape, jnp.float32),
-    ]
+    ] + [shape((tokens, features // 2))] * 4
     scratch = [
         pltpu.VMEM(small_shape, jnp.float32),
         pltpu.VMEM(rows, jnp.bfloat16),
@@ -1069,18 +1149,19 @@
         pltpu.VMEM(rows, jnp.float32),
         pltpu.VMEM((HEADS * tokens, HEAD_DIM), jnp.bfloat16),
         pltpu.VMEM((HEADS * tokens, HEAD_DIM), jnp.bfloat16),
-        pltpu.VMEM((tokens, length), jnp.float32),
-        pltpu.VMEM((HEADS * tokens, 1), jnp.float32),
+        pltpu.VMEM((length, 2 * tokens), jnp.float32),
+        pltpu.VMEM((8, 2 * tokens), jnp.float32),
         pltpu.VMEM(keyval.shape, jnp.float32),
         pltpu.VMEM(keyval.shape, jnp.bfloat16),
-        pltpu.SemaphoreType.DMA((2, 3)),
+        pltpu.SemaphoreType.DMA((2, 5)),
     ]
     wide = Scatter.scratch(depth, tokens, features)
-    scratch += wide[1:4] + wide[5:] + Scatter.scratch(depth, tokens, kv_columns)
+    scratch += wide[1:4] + Scatter.sems(depth) * 2 + Scatter.scratch(depth, tokens, kv_columns, 2)
     return call(
         kernel, out, scratch, 4, "attend_back",
         returned, gates, small, small_there, middle, d_out, send, attn_own, attn_other, query,
-        keyval, *angles, *docs, level, mixed, results,
+        keyval, *angles, *docs, level, mixed, hidden, mixed_low, results,
+        late=(19, 0, 4, 5, 6, 7, 8, 9, 10, 16),
     )
 
 
@@ -1103,17 +1184,27 @@
 
     def kernel(
         send_ref, d_out_far, in_own_ref, out_own_ref,
-        returned, results, grad_in, grad_in_other, grad_out, grad_out_other,
+        returned, results_far, grad_in_far, grad_in_other_far, grad_out_far, grad_out_other_far,
         hidden_all, grad_both, gated_hidden, other_part, other_result, result_from, result_sems,
-        in_ref, out_ref, d_out_ref, x_sems, near_sem, *scratch,
+        in_ref, out_ref, d_out_ref, x_sems, near_sem, results, grad_in, grad_in_other, grad_out,
+        grad_out_other, far_sems, *scratch,
     ):
-        gather = Gather(hidden_all, tokens, scratch[:3])
-        scatter = Scatter(other_part, scratch[3:])
+        gather = gather_parts(hidden_all, tokens, scratch[:6], 2)
+        scatter = scatter_parts(other_part, scratch[6:], 2)
+        chip_sums = scratch[7]
         z, y, c, _ = chip_place()
         expert = lax.axis_index("ctx") // 2
         lane = lax.broadcasted_iota(jnp.int32, (1, 128), 1)
-        gather.own()[...] = send_ref[...]
+        Gather(hidden_all, tokens, scratch[:3]).own()[...] = send_ref[...]
         partner = {"wa": 1 - lax.axis_index("wa")}
+        stores = [
+            pltpu.make_async_copy(source, target, far_sems.at[i])
+            for i, (source, target) in enumerate(
+                [(results, results_far), (grad_in, grad_in_far),
+                 (grad_in_other, grad_in_other_far), (grad_out, grad_out_far),
+                 (grad_out_other, grad_out_other_far)]
+            )
+        ]
         near = pltpu.make_async_copy(d_out_far, d_out_ref, near_sem.at[0])
         near.start()
         swaps = [
@@ -1136,11 +1227,6 @@
         out_ref[:quarter] = out_own_ref[...]
         in_ref[:quarter] = in_own_ref[:quarter]
         in_ref[width : width + quarter] = in_own_ref[quarter:]
-        gather.follow()
-        near.wait()
-        for swap in swaps:
-            swap.wait()
-
         def chip_rows(chip):
             return pl.ds(pl.multiple_of(chip * 2 * tokens, 16), 2 * tokens)
 
@@ -1164,20 +1250,30 @@
             own, other = parted(
                 jnp.dot(grad_both[rows, :], in_ref[...], preferred_element_type=jnp.float32)
             )
-            scatter.sums[chip, :, :features] = own.astype(jnp.bfloat16)
+            chip_sums[chip, :, :features] = own.astype(jnp.bfloat16)
             other_part[chip, :, :features] = other.astype(jnp.bfloat16)
             own, other = parted(jnp.where(lane == expert, grad_gate, 0.0))
-            scatter.sums[chip, :, features:] = own.astype(jnp.bfloat16)
+            chip_sums[chip, :, features:] = own.astype(jnp.bfloat16)
             other_part[chip, :, features:] = other.astype(jnp.bfloat16)
-            scatter.on_core(chip).start()
-
-        @pl.loop(0, depth)
-        def _(turn):
-            of_z = nearest(depth - 1 - turn)
+            scatter.send_core(chip)
+
+        follow(gather)
+        near.wait()
+        for swap in swaps:
+            swap.wait()
+        backward(nearest(1) * 2 + 1 - y)
+        backward(nearest(1) * 2 + y)
+        scatter.add_chip(nearest(1), True)
+
+        def next_chip(turn, of_z):
             backward(of_z * 2 + 1 - y)
-            pl.when(turn > 0)(lambda: scatter.add_chip(nearest(depth - turn), False))
+            scatter.add_chip(nearest(jnp.where(turn == 0, 1, depth - turn)), False)
             backward(of_z * 2 + y)
             scatter.add_chip(of_z, True)
+
+        @pl.loop(0, depth - 1)
+        def _(turn):
+            next_chip(turn, nearest(jnp.where(turn == depth - 2, 0, depth - 1 - turn)))
 
         scatter.add_chip(nearest(0), False)
         scatter.add_y_of(nearest(depth - 1))
@@ -1207,6 +1303,8 @@
             grad_out[:, at] = grad[:quarter]
             grad_out_other[:, at] = grad[quarter:].astype(jnp.bfloat16)
 
+        stores[3].start()
+        stores[4].start()
         for k in range(depth - 3, 0, -1):
             scatter.add_y_of(nearest(k))
 
@@ -1220,17 +1318,22 @@
                 grad_in[rows, at] = grad[first : first + quarter]
                 grad_in_other[rows, at] = grad[first + quarter : first + width].astype(jnp.bfloat16)
 
-        scatter.add_y_of(nearest(0))
+        stores[1].start()
+        stores[2].start()
 
         @pl.loop(0, chips)
         def _(chip):
             result_copy(chip).wait_recv()
             add_into(results.at[chip], (results.at[chip], result_from.at[chip]), tokens)
 
+        stores[0].start()
+        scatter.add_y_of(nearest(0))
         scatter.last(returned)
         scatter.finish()
         for chip in range(chips):
             result_copy(chip).wait_send()
+        for store in stores:
+            store.wait()
 
     block = (chips, tokens, features)
     out = [
@@ -1255,9 +1358,12 @@
         pltpu.SemaphoreType.DMA((2, 3)),
         pltpu.SemaphoreType.DMA((1,)),
     ]
-    scratch += Gather.sems(depth) + Scatter.scratch(depth, tokens, wide)
+    scratch += [pltpu.VMEM(one.shape, one.dtype) for one in out[1:]]
+    scratch.append(pltpu.SemaphoreType.DMA((5,)))
+    scratch += Gather.sems(depth) * 2 + Scatter.scratch(depth, tokens, wide, 2)
     return call(
-        kernel, out, scratch, 3, "experts", send, d_out_all, in_own, out_own, outside=(1,)
+        kernel, out, scratch, 3, "experts", send, d_out_all, in_own, out_own, outside=(1,),
+        outside_out=range(1, 6),
     )
 
 
@@ -1271,7 +1377,7 @@
     experts = small.shape[0] // 2
 
     def kernel(
-        x_ref, grad_middle_ref, small_ref, small_there_ref, small_grads_ref,
+        arrive, x_ref, grad_middle_ref, small_ref, small_there_ref, small_grads_ref,
         query_own, query_other, keyval_own, keyval_other,
         hidden_ref, hidden_there, mixed_ref, mixed_there, middle_ref, middle_there,
         query_ref, query_there, keyval_ref, keyval_there, in_ref, out_ref,
@@ -1320,6 +1426,7 @@
             query_.add_cores(step)
         attn.add_y(depth - 1)
         fill_small(full, small_ref, small_there_ref)
+        arrive(0, 1, 5, 6, 7, 8)
         grad_one[:, side_columns(True)] = rows_by_rows(
             query_ref[...], query_own[...]
         ) + rows_by_rows(keyval_ref[...], keyval_own[...])
@@ -1419,6 +1526,7 @@
         kernel, out, scratch, 1, "finish",
         x, grad_middle, small, small_there, small_grads, *matrices, *hidden, *mixed, *middle,
         *query, *keyval, expert_in, expert_out, outside=(19, 20), outside_out=(5, 6),
+        late=(0, 1, 5, 6, 7, 8),
     )
 
 
@@ -1487,24 +1595,21 @@
     )
     projections = (w_query, w_query_there, w_keyval, w_keyval_there)
     (
-        query, keyval, level, mixed, hidden_own, hidden_there, mixed_own, mixed_there, middle,
-        send, gates, w_out_attn_there,
-    ) = attend(
-        x, small, small_there, projections, w_out_attn, angles, docs, chosen, experts
-    )
+        query, keyval, level, mixed, hidden, mixed_low, middle, send, gates, w_out_attn_there,
+    ) = attend(x, small, small_there, projections, w_out_attn, angles, docs, chosen, experts)
     returned, results, grad_in, grad_in_other, grad_out_matrix, grad_out_other = run_experts(
         send, d_out_all, in_own, w_out[0], experts
     )
     (
         output, grad_middle, middle_low, middle_there, grad_query, query_there, grad_keyval,
-        keyval_there, small_grads,
+        keyval_there, small_grads, *halves,
     ) = attend_back(
         returned, gates, small, small_there, middle, grad_out, send, w_out_attn, w_out_attn_there,
-        query, keyval, angles, docs, level, mixed, results, experts,
+        query, keyval, angles, docs, level, mixed, hidden, mixed_low, results, experts,
     )
     attn_sum, query_sum, keyval_sum, small_sum, grad_input, in_there, out_there = finish(
-        x, grad_middle, small, small_there, small_grads, projections, (hidden_own, hidden_there),
-        (mixed_own, mixed_there), (middle_low, middle_there), (grad_query, query_there),
+        x, grad_middle, small, small_there, small_grads, projections, halves[:2], halves[2:],
+        (middle_low, middle_there), (grad_query, query_there),
         (grad_keyval, keyval_there), grad_in_other, grad_out_other,
     )
     query_sum, keyval_sum, attn_sum, grad_w_in, grad_w_out = widen(

time: 359 us -> 335 us (0.933)
  Pallas kernels: 346 us -> 322 us
    pallas_call x5, Pallas kernels: 337 us -> 313 us  [call(): pl.pallas_call(with_late if late else kernel, out_shape=out, in_specs=[sp...]
where the time goes in v6:
time: 335 us; the launch traced here: 334 us
  Pallas kernels  322 us (96%)
  local copies, waits for them, and re-layouts  7.13 us (2%)
  other arithmetic  3.93 us (1%)
    pallas_call x5, Pallas kernels, call(): pl.pallas_call(with_late if late else kernel, out_shape=out, in_specs=[sp...  313 us
    pallas_call x1, Pallas kernels, widen(): pl.pallas_call(kernel, grid=(steps,), out_shape=[jax.ShapeDtypeStruct(que...  9.26 us

profile of v6, /device:TPU:0, one launch (start us, length us, event | category | flops | bytes accessed | tf_op | source)
XLA Modules:
  0.0 334.2 jit_solution(17675915187101089227)
XLA Ops:
  0.6 0.7 dynamic-slice_bitcast_fusion
  1.3 0.1 pad.7.clone
  1.4 0.7 broadcast_in_dim.25
  2.1 0.7 broadcast_in_dim.26
  2.8 0.8 compare_reduce_fusion
  3.6 1.4 maximum_maximum_fusion.small_ref.refs_1_.refs_2_
  5.0 0.6 and_convert_fusion.refs_13_
  5.6 0.7 copy.25.refs_12_.refs_14_
  6.4 0.3 fusion
  6.7 0.8 pad_maximum_fusion
  7.5 42.6 %front.1 = (bf16[2048,1536]{1,0:T(8,128)(2,1)}, bf16[768,1536]{1,0:T(8,128)(2,1)}, bf16[768,512]{1,0:T(8,128)(2,1)}, bf16[16,768]{1,0:T(8,128)(2,1)}) custom-call(bf16[128,1536]{1,0:T(8,128)(2,1)} %bitcast.23, bf16[768,1536]{1,0:T(8,128)(2,1)} %refs_5_.3, bf16[768,512]{1,0:T(8,128)(2,1)} %refs_7_.5, bf16[16,768]{1,0:T(8,128)(2,1)} %maximum_maximum_fusion.small_ref.refs_1_.refs_2_), custom_call_target="tpu_custom_call" | custom-call | tf_op jit(solution)/shard_map/front/pallas_call | solution.py:733
  50.1 36.3 %attend.1 = (bf16[128,1536]{1,0:T(8,128)(2,1)}, bf16[2048,512]{1,0:T(8,128)(2,1)}, f32[8,256]{1,0:T(8,128)}, f32[128,1536]{1,0:T(8,128)}, bf16[128,1536]{1,0:T(8...) custom-call(bf16[128,1536]{1,0:T(8,128)(2,1)} %bitcast.21, ...), custom_call_target="tpu_custom_call" | custom-call | tf_op jit(solution)/shard_map/attend/pallas_call | solution.py:733
  86.4 99.6 %experts.1 = (f32[128,1664]{1,0:T(8,128)}, bf16[8,128,1536]{2,1,0:T(8,128)(2,1)}, f32[384,1536]{1,0:T(8,128)}, bf16[384,1536]{1,0:T(8,128)(2,1)}, f32[192,1536]{1,0:T(8,128)}, /*index=5*/bf16[192,1536]{1,0:T(8,128)(2,1)}) custom-call(bf16[128,1664]{1,0:T(8,128)(2,1)} %get-tuple-element.58.send_ref.refs_6_, bf16[2048,1536]{1,0:T(8,128)(2,1)} %get-tuple-element.59.d_out_far, ...), custom_call_target="tpu_custom_call" | custom-call | tf_op jit(solution)/shard_map/experts/pallas_call | solution.py:733
  186.0 58.6 %attend_back.1 = (bf16[128,1536]{1,0:T(8,128)(2,1)}, f32[128,1536]{1,0:T(8,128)}, bf16[128,1536]{1,0:T(8,128)(2,1)}, bf16[128,1536]{1,0:T(8,128)(2,1)}, bf16[128...) custom-call(f32[128,1664]{1,0:T(8,128)} %get-tuple-element.60.refs_0, ...), custom_call_target="tpu_custom_call" | custom-call | tf_op jit(solution)/shard_map/attend_back/pallas_call | solution.py:733
  244.6 76.1 %finish.1 = (bf16[768,1536]{1,0:T(8,128)(2,1)}, bf16[768,1536]{1,0:T(8,128)(2,1)}, bf16[768,512]{1,0:T(8,128)(2,1)}, f32[16,768]{1,0:T(8,128)}, bf16[128,1536]{1...) custom-call(bf16[128,1536]{1,0:T(8,128)(2,1)} %bitcast.22, ...), custom_call_target="tpu_custom_call" | custom-call | tf_op jit(solution)/shard_map/finish/pallas_call | solution.py:733
  320.7 1.4 slice_reduce_fusion
  322.1 1.3 slice_bitcast_fusion
  323.4 0.0 copy-start
  323.4 0.0 copy-start.1
  323.4 9.3 %widen.1 = (f32[768,1536]{1,0:T(8,128)}, f32[768,512]{1,0:T(8,128)}, f32[768,1536]{1,0:T(8,128)}, f32[384,1536]{1,0:T(8,128)}, f32[1,192,1536]{2,1,0:T(8,128)}) custom-call(bf16[768,1536]{1,0:T(8,128)(2,1)} %get-tuple-element.88.refs_0_, bf16[768,512]{1,0:T(8,128)(2,1)} %get-tuple-element.89.refs_1_, bf16[768,1536]{1,0:T(8,128)(2,1)} %get-tuple-element.90.refs_2_, ...), custom_call_target="tpu_custom_call" | custom-call | tf_op jit(solution)/shard_map/widen/pallas_call | solution.py:1551
  332.7 0.0 copy-done
  332.7 0.7 copy.29
  333.5 0.0 copy-done.1
  333.5 0.7 copy.30
  (5 shorter events, 0.0 us)
Async XLA Ops:
  323.4 9.3 %copy-start = (bf16[128,1536]{1,0:T(8,128)(2,1)S(1)}, bf16[128,1536]{1,0:T(8,128)(2,1)}, u32[]{:S(2)}) copy-start(bf16[128,1536]{1,0:T(8,128)(2,1)} %get-tuple-element.71) | copy-start | bytes 1179652
  323.4 10.0 %copy-start.1 = (bf16[128,1536]{1,0:T(8,128)(2,1)S(1)}, bf16[128,1536]{1,0:T(8,128)(2,1)}, u32[]{:S(2)}) copy-start(bf16[128,1536]{1,0:T(8,128)(2,1)} %get-tuple-element.86) | copy-start | bytes 1179652

commit v7 on v6

--- a/solution.py
+++ b/solution.py
@@ -510,7 +510,11 @@
 
         each(step, across)
 
-    def finish(self):
+    def take_core(self, of_z):
+        for of_y in range(2):
+            self.on_core(of_z, of_y, mine=False).wait_recv()
+
+    def finish(self, *taken):
         z, depth = self.z, self.depth
         for of_z in range(depth):
             pl.when((z < depth - 1) & (of_z <= z))(lambda: self.on_z(0, of_z).wait_send())
@@ -518,7 +522,10 @@
             self.on_y(of_z).wait_send()
             for of_y in range(2):
                 self.on_core(of_z, of_y).wait_send()
-                self.on_core(of_z, of_y, mine=False).wait_recv()
+            open_still = of_z >= 0
+            for one in taken:
+                open_still = (of_z != one) & open_still
+            pl.when(open_still)(lambda: self.take_core(of_z))
 
 
 class Several:
@@ -746,27 +753,35 @@
 
 
 class Relay:
-    def __init__(self, source, out, sems, parts=1):
+    def __init__(self, source, out, sems, parts=1, paired=False):
         self.source, self.out, self.sems, self.parts = source, out, sems, parts
+        self.paired = paired
         self.z, self.y, self.c, _ = chip_place()
-        self.rows = source.shape[0] // (2 * parts)
+        self.odd = lax.rem(self.z, 2)
+        self.rows = source.shape[0] // ((4 if paired else 2) * parts)
 
     @staticmethod
     def semaphores():
-        return pltpu.SemaphoreType.DMA((2, 4))
-
-    def block(self, ref, part, c):
-        return ref.at[pl.ds(pl.multiple_of((c * self.parts + part) * self.rows, 16), self.rows)]
+        return pltpu.SemaphoreType.DMA((2, 8))
+
+    def block(self, ref, part, c, odd):
+        place = (c * 2 + odd if self.paired else c) * self.parts + part
+        return ref.at[pl.ds(pl.multiple_of(place * self.rows, 16), self.rows)]
 
     def on_x(self, part):
-        source, target = self.block(self.source, part, self.c), self.block(self.out, part, self.c)
+        source = self.block(self.source, part, self.c, self.odd)
+        target = self.block(self.out, part, self.c, self.odd)
         return remote(source, target, self.sems, (part,), {"wa": 1 - lax.axis_index("wa")})
 
-    def on_core(self, part, c):
-        block = self.block(self.out, part, c)
-        return remote(
-            block, block, self.sems, (2 + part,), {"ctx": ctx_of(self.z, self.y, 1 - self.c)}
-        )
+    def on_core(self, part, c, other_z=False):
+        block = self.block(self.out, part, c, 1 - self.odd if other_z else self.odd)
+        at = ((4 if other_z else 2) + part,)
+        return remote(block, block, self.sems, at, {"ctx": ctx_of(self.z, self.y, 1 - self.c)})
+
+    def on_pair(self, part, mine=True):
+        block = self.block(self.out, part, self.c, self.odd if mine else 1 - self.odd)
+        target = {"ctx": ctx_of(self.z + 1 - 2 * self.odd, self.y, self.c)}
+        return remote(block, block, self.sems, (6 + part,), target)
 
     def start(self):
         for part in range(self.parts):
@@ -774,13 +789,23 @@
 
     def pass_on(self, part=0):
         self.on_x(part).wait_recv()
+        if self.paired:
+            self.on_pair(part).start()
         self.on_core(part, self.c).start()
+
+    def pass_on_pair(self, part):
+        self.on_pair(part, mine=False).wait_recv()
+        self.on_core(part, self.c, other_z=True).start()
 
     def finish(self):
         for part in range(self.parts):
             self.on_x(part).wait_send()
             self.on_core(part, self.c).wait_send()
             self.on_core(part, 1 - self.c).wait_recv()
+            if self.paired:
+                self.on_pair(part).wait_send()
+                self.on_core(part, self.c, other_z=True).wait_send()
+                self.on_core(part, 1 - self.c, other_z=True).wait_recv()
 
 
 def front(d_out, w_query, w_keyval, small):
@@ -850,12 +875,24 @@
     )
 
 
-def allowed_bias(doc_row, doc_column, tokens):
-    keys = doc_row.shape[1]
-    query_block = lax.axis_index("ctx") * tokens // BLOCK
+def down(row):
+    return jnp.transpose(jnp.broadcast_to(row.astype(jnp.float32), (128, 128)))
+
+
+def allowed_bias(doc_row, tokens):
+    keys, me = doc_row.shape[1], lax.axis_index("ctx")
+    own = down(doc_row[:, pl.ds(pl.multiple_of(me * tokens, 128), tokens)])[:, :1]
     key_block = lax.broadcasted_iota(jnp.int32, (tokens, keys), 1) // BLOCK
-    allowed = (doc_row == doc_column) & (key_block <= query_block)
-    return jnp.where(allowed, 0.0, NEGATIVE)
+    same = doc_row[...].astype(jnp.float32) == own
+    return jnp.where(same & (key_block <= me * tokens // BLOCK), 0.0, NEGATIVE)
+
+
+def chosen_by(routes, lanes, experts):
+    numbers = lax.rem(lanes, experts).astype(jnp.float32)
+    found = down(routes[:1]) == numbers
+    for k in range(1, routes.shape[0]):
+        found = found | (down(routes[k : k + 1]) == numbers)
+    return found & (lanes < 2 * experts)
 
 
 def side_columns(own):
@@ -886,21 +923,27 @@
     return jnp.concatenate([rows, rows, spare], axis=0).astype(jnp.bfloat16)
 
 
-def attend(x, small, small_there, projections, w_out_attn, angles, docs, chosen, experts):
+def attend(
+    x, small, small_there, projections, w_out_attn, w_out, angles, doc_row, routes, experts
+):
     count, tokens, features = lax.axis_size("ctx"), x.shape[0], x.shape[1]
     depth, length = count // 4, count * tokens
     kv_columns = projections[2].shape[1]
 
     def kernel(
         arrive, x_ref, small_ref, small_there_ref, query_own, query_other, keyval_own, keyval_other,
-        attn_own, attn_own_far, cosine_ref, sine_ref, doc_row, doc_column, chosen_ref,
+        attn_own, attn_own_far, out_own, cosine_ref, sine_ref, doc_row_ref, routes_ref,
         query, keyval, level, mixed, hidden, mixed_low, middle, send, gates_out, attn_other,
-        full, stacked, bias, attn_sems, *sems,
+        out_other,
+        full, stacked, bias, x_sems, attn_sems, *sems,
     ):
         gather = gather_parts(keyval, tokens, sems, 2)
-        attn = Relay(attn_own_far, attn_other, attn_sems, parts=2)
+        attn = Relay(attn_own_far, attn_other, attn_sems, parts=2, paired=True)
         greet(across_x=True)
         attn.start()
+        partner = {"wa": 1 - lax.axis_index("wa")}
+        swap_out = remote(out_own, out_other, x_sems, (0,), partner)
+        swap_out.start()
         fill_small(full, small_ref, small_there_ref)
         residual = x_ref[...].astype(jnp.float32)
         hidden[...] = normed(residual, full[experts : experts + 1]).astype(jnp.bfloat16)
@@ -920,11 +963,20 @@
         gather.start()
         arrive(3, 4)
         query[...] = turned(onto(query_own, query_other), cosine, sine).astype(jnp.bfloat16)
-        bias[...] = allowed_bias(doc_row[...], doc_column[...], tokens)
+        bias[...] = allowed_bias(doc_row_ref, tokens)
         for head in range(HEADS):
             rows = slice(head * tokens, (head + 1) * tokens)
             stacked[rows, :] = query[:, head * 128 : (head + 1) * 128]
-        follow(gather)
+        gather.along_z(1)
+        gather.along_y(0)
+        gather.along_z(2)
+        gather.along_y(1)
+        gather.along_z(3)
+        attn.pass_on(0)
+        gather.along_y(2)
+        attn.pass_on(1)
+        gather.along_y(3)
+        gather.finish()
 
         @pl.loop(0, HEADS // 2)
         def _(pair):
@@ -944,9 +996,9 @@
                 mixed[:, columns] = mixture[part * tokens : (part + 1) * tokens]
             column = jnp.broadcast_to(top + jnp.log(total), (2 * tokens, 128))
             level[pl.ds(pair, 1), :] = jnp.transpose(column)[:1]
-            pl.when(pair == HEADS // 4)(lambda: attn.pass_on(0))
-
-        attn.pass_on(1)
+            pl.when(pair == HEADS // 4)(lambda: attn.pass_on_pair(0))
+
+        attn.pass_on_pair(1)
         mixed_low[...] = mixed[...].astype(jnp.bfloat16)
         attn.finish()
         arrive(7)
@@ -956,7 +1008,7 @@
         send[:, :features] = hidden_two
         logits = rows_by_rows(hidden_two, router_block(full, experts))
         lane = lax.broadcasted_iota(jnp.int32, logits.shape, 1)
-        masked = jnp.where(chosen_ref[...] > 0, logits, NEGATIVE)
+        masked = jnp.where(chosen_by(routes_ref[...], lane, experts), logits, NEGATIVE)
         weights = jnp.exp(masked - jnp.max(masked, axis=1, keepdims=True))
         total = jnp.sum(jnp.where(lane < experts, weights, 0.0), axis=1, keepdims=True)
         gates = weights / total
@@ -964,6 +1016,7 @@
         carried = jnp.where(lane < experts, high, jnp.where(lane < 2 * experts, gates - high, 0.0))
         send[:, features:] = carried.astype(jnp.bfloat16)
         gates_out[...] = jnp.where(lane < experts, gates, 0.0)
+        swap_out.wait()
 
     def shape(rows, columns, kind=jnp.bfloat16):
         return jax.ShapeDtypeStruct((rows, columns), kind)
@@ -973,18 +1026,19 @@
         shape(tokens, features), shape(length, kv_columns), shape(8, 2 * tokens, jnp.float32),
         shape(tokens, features, jnp.float32), shape(tokens, features), shape(tokens, features),
         shape(tokens, features, jnp.float32), shape(tokens, wide), shape(tokens, 128, jnp.float32),
-        shape(*w_out_attn.shape),
+        shape(*w_out_attn.shape), shape(*w_out.shape),
     ]
     scratch = [
         pltpu.VMEM((small.shape[0], features), jnp.float32),
         pltpu.VMEM((HEADS * tokens, HEAD_DIM), jnp.bfloat16),
         pltpu.VMEM((tokens, length), jnp.float32),
+        pltpu.SemaphoreType.DMA((2, 1)),
         Relay.semaphores(),
     ] + Gather.sems(depth) * 2
     return call(
         kernel, out, scratch, 2, "attend",
-        x, small, small_there, *projections, w_out_attn, w_out_attn, *angles, *docs, chosen,
-        outside=(8,), late=(5, 6, 3, 4, 7),
+        x, small, small_there, *projections, w_out_attn, w_out_attn, w_out, *angles, doc_row,
+        routes, outside=(8, 9), outside_out=(10,), late=(5, 6, 3, 4, 7),
     )
 
 
@@ -997,15 +1051,15 @@
 
 def attend_back(
     returned, gates, small, small_there, middle, d_out, send, attn_own, attn_other, query, keyval,
-    angles, docs, level, mixed, hidden, mixed_low, results, experts,
+    angles, doc_row, level, mixed, hidden, mixed_low, results, experts,
 ):
     count, tokens, features = lax.axis_size("ctx"), query.shape[0], query.shape[1]
     depth, length, kv_columns = count // 4, keyval.shape[0], keyval.shape[1]
 
     def kernel(
         arrive, returned_ref, gates_ref, small_ref, small_there_ref, middle_ref, d_out_ref, send_ref,
-        attn_own_ref, attn_other_ref, query_ref, keyval_ref, cosine_ref, sine_ref, doc_row,
-        doc_column, level_ref, mixed_ref, hidden_ref, mixed_low_ref, results_ref,
+        attn_own_ref, attn_other_ref, query_ref, keyval_ref, cosine_ref, sine_ref, doc_row_ref,
+        level_ref, mixed_ref, hidden_ref, mixed_low_ref, results_ref,
         output, grad_middle, grad_middle_low, grad_middle_there, grad_query, grad_query_there,
         grad_keyval, grad_keyval_there, small_grads, hidden_own, hidden_there, mixed_own,
         mixed_there,
@@ -1027,7 +1081,7 @@
             )
         ]
         greet(across_x=True)
-        arrive(19)
+        arrive(18)
         for k in range(depth - 1, 0, -1):
             result.send_y(nearest(k))
         swaps[3].start()
@@ -1062,11 +1116,11 @@
         grad_mixed[:, side_columns(False)] = rows_by_rows(
             grad_middle_low[...], attn_other_ref[...]
         ).astype(jnp.bfloat16)
-        allowed = jnp.transpose(allowed_bias(doc_row[...], doc_column[...], tokens))
+        allowed = jnp.transpose(allowed_bias(doc_row_ref, tokens))
         bias[:, :tokens] = allowed
         bias[:, tokens:] = allowed
         total[...] = jnp.zeros_like(total)
-        arrive(9, 10, 16)
+        arrive(9, 10, 15)
         for head in range(HEADS):
             rows = slice(head * tokens, (head + 1) * tokens)
             columns = slice(head * 128, head * 128 + 128)
@@ -1160,8 +1214,8 @@
     return call(
         kernel, out, scratch, 4, "attend_back",
         returned, gates, small, small_there, middle, d_out, send, attn_own, attn_other, query,
-        keyval, *angles, *docs, level, mixed, hidden, mixed_low, results,
-        late=(19, 0, 4, 5, 6, 7, 8, 9, 10, 16),
+        keyval, *angles, doc_row, level, mixed, hidden, mixed_low, results,
+        late=(18, 0, 4, 5, 6, 7, 8, 9, 10, 15),
     )
 
 
@@ -1175,7 +1229,7 @@
     return gelu * second, slope * second, gelu
 
 
-def run_experts(send, d_out_all, in_own, out_own, experts):
+def run_experts(send, d_out_all, in_own, out_own, out_other, experts):
     count, tokens = lax.axis_size("ctx"), send.shape[0]
     depth, chips, length = count // 4, count // 2, count * tokens
     wide, features = send.shape[1], d_out_all.shape[1]
@@ -1183,7 +1237,7 @@
     width = 2 * quarter
 
     def kernel(
-        send_ref, d_out_far, in_own_ref, out_own_ref,
+        send_ref, d_out_far, in_own_ref, out_own_ref, out_other_ref,
         returned, results_far, grad_in_far, grad_in_other_far, grad_out_far, grad_out_other_far,
         hidden_all, grad_both, gated_hidden, other_part, other_result, result_from, result_sems,
         in_ref, out_ref, d_out_ref, x_sems, near_sem, results, grad_in, grad_in_other, grad_out,
@@ -1217,14 +1271,12 @@
             )
             for part in range(2)
         ]
-        swaps.append(
-            remote(out_own_ref, out_ref.at[pl.ds(quarter, quarter)], x_sems, (2,), partner)
-        )
         greet(across_x=True)
         gather.start()
         for swap in swaps:
             swap.start()
         out_ref[:quarter] = out_own_ref[...]
+        out_ref[quarter:] = out_other_ref[...]
         in_ref[:quarter] = in_own_ref[:quarter]
         in_ref[width : width + quarter] = in_own_ref[quarter:]
         def chip_rows(chip):
@@ -1257,24 +1309,35 @@
             other_part[chip, :, features:] = other.astype(jnp.bfloat16)
             scatter.send_core(chip)
 
-        follow(gather)
+        gather.along_z(1)
+        for step in range(2, depth):
+            gather.along_y(step - 2)
+            gather.along_z(step)
         near.wait()
         for swap in swaps:
             swap.wait()
+        for of_z in (nearest(1), z):
+            gather.take_core(of_z)
         backward(nearest(1) * 2 + 1 - y)
         backward(nearest(1) * 2 + y)
         scatter.add_chip(nearest(1), True)
-
-        def next_chip(turn, of_z):
+        gather.along_y(depth - 2)
+        backward(z * 2 + 1 - y)
+        gather.along_y(depth - 1)
+        backward(z * 2 + y)
+        gather.finish(nearest(1), z)
+        scatter.add_chip(nearest(1), False)
+
+        @pl.loop(0, depth - 2)
+        def _(turn):
+            of_z = nearest(depth - 1 - turn)
             backward(of_z * 2 + 1 - y)
-            scatter.add_chip(nearest(jnp.where(turn == 0, 1, depth - turn)), False)
+            pl.when(turn > 0)(lambda: scatter.add_chip(nearest(depth - turn), False))
             backward(of_z * 2 + y)
             scatter.add_chip(of_z, True)
 
-        @pl.loop(0, depth - 1)
-        def _(turn):
-            next_chip(turn, nearest(jnp.where(turn == depth - 2, 0, depth - 1 - turn)))
-
+        scatter.add_chip(nearest(2), False)
+        scatter.add_chip(z, True)
         scatter.add_chip(nearest(0), False)
         scatter.add_y_of(nearest(depth - 1))
 
@@ -1355,14 +1418,14 @@
         pltpu.VMEM((2 * width, features), jnp.bfloat16),
         pltpu.VMEM((width, features), jnp.bfloat16),
         pltpu.VMEM(d_out_all.shape, jnp.bfloat16),
-        pltpu.SemaphoreType.DMA((2, 3)),
+        pltpu.SemaphoreType.DMA((2, 2)),
         pltpu.SemaphoreType.DMA((1,)),
     ]
     scratch += [pltpu.VMEM(one.shape, one.dtype) for one in out[1:]]
     scratch.append(pltpu.SemaphoreType.DMA((5,)))
     scratch += Gather.sems(depth) * 2 + Scatter.scratch(depth, tokens, wide, 2)
     return call(
-        kernel, out, scratch, 3, "experts", send, d_out_all, in_own, out_own, outside=(1,),
+        kernel, out, scratch, 3, "experts", send, d_out_all, in_own, out_own, out_other, outside=(1,),
         outside_out=range(1, 6),
     )
 
@@ -1584,10 +1647,6 @@
     angles = (
         jnp.concatenate([cosine, cosine], axis=1), jnp.concatenate([-sine, sine], axis=1)
     )
-    docs = (seq_ids, lax.dynamic_slice_in_dim(seq_ids[0], me * tokens, tokens, 0)[:, None])
-    numbers = jnp.arange(128, dtype=jnp.int32)
-    named = jnp.any(routes[0][:, :, None] == (numbers % experts)[None, None, :], axis=1)
-    chosen = (named & (numbers < 2 * experts)[None, :]).astype(jnp.float32)
     in_own = jnp.swapaxes(w_in[0], 1, 2).reshape(-1, D)
 
     d_out_all, w_query_there, w_keyval_there, small_there = front(
@@ -1596,16 +1655,20 @@
     projections = (w_query, w_query_there, w_keyval, w_keyval_there)
     (
         query, keyval, level, mixed, hidden, mixed_low, middle, send, gates, w_out_attn_there,
-    ) = attend(x, small, small_there, projections, w_out_attn, angles, docs, chosen, experts)
+        w_out_there,
+    ) = attend(
+        x, small, small_there, projections, w_out_attn, w_out[0], angles, seq_ids, routes[0].T,
+        experts,
+    )
     returned, results, grad_in, grad_in_other, grad_out_matrix, grad_out_other = run_experts(
-        send, d_out_all, in_own, w_out[0], experts
+        send, d_out_all, in_own, w_out[0], w_out_there, experts
     )
     (
         output, grad_middle, middle_low, middle_there, grad_query, query_there, grad_keyval,
         keyval_there, small_grads, *halves,
     ) = attend_back(
         returned, gates, small, small_there, middle, grad_out, send, w_out_attn, w_out_attn_there,
-        query, keyval, angles, docs, level, mixed, hidden, mixed_low, results, experts,
+        query, keyval, angles, seq_ids, level, mixed, hidden, mixed_low, results, experts,
     )
     attn_sum, query_sum, keyval_sum, small_sum, grad_input, in_there, out_there = finish(
         x, grad_middle, small, small_there, small_grads, projections, halves[:2], halves[2:],

time: 335 us -> 328 us (0.979); the launches traced: 334 us -> 323 us
  Pallas kernels: 322 us -> 313 us
    pallas_call x5, Pallas kernels: 313 us -> 304 us  [call(): pl.pallas_call(with_late if late else kernel, out_shape=out, in_specs=[sp...]
where the time goes in v7:
time: 328 us; the launch traced here: 323 us
  Pallas kernels  313 us (95%)
  local copies, waits for them, and re-layouts  5.73 us (2%)
    pallas_call x5, Pallas kernels, call(): pl.pallas_call(with_late if late else kernel, out_shape=out, in_specs=[sp...  304 us
    pallas_call x1, Pallas kernels, widen(): pl.pallas_call(kernel, grid=(steps,), out_shape=[jax.ShapeDtypeStruct(que...  9.26 us

profile of v7, /device:TPU:0, one launch (start us, length us, event | category | flops | bytes accessed | tf_op | source)
XLA Modules:
  0.0 322.6 jit_solution(5681221309682543133)
XLA Ops:
  0.7 0.1 pad.7.clone
  0.8 0.7 broadcast_in_dim.20
  1.4 0.7 broadcast_in_dim.21
  2.1 1.4 maximum_maximum_fusion.small_ref.refs_1_.refs_2_
  3.5 0.3 fusion
  3.8 0.8 pad_maximum_fusion
  4.6 42.8 %front.1 = (bf16[2048,1536]{1,0:T(8,128)(2,1)}, bf16[768,1536]{1,0:T(8,128)(2,1)}, bf16[768,512]{1,0:T(8,128)(2,1)}, bf16[16,768]{1,0:T(8,128)(2,1)}) custom-call(bf16[128,1536]{1,0:T(8,128)(2,1)} %bitcast.25, bf16[768,1536]{1,0:T(8,128)(2,1)} %refs_5_.3, bf16[768,512]{1,0:T(8,128)(2,1)} %refs_7_.5, bf16[16,768]{1,0:T(8,128)(2,1)} %maximum_maximum_fusion.small_ref.refs_1_.refs_2_), custom_call_target="tpu_custom_call" | custom-call | tf_op jit(solution)/shard_map/front/pallas_call | solution.py:740
  47.4 36.4 %attend.1 = (bf16[128,1536]{1,0:T(8,128)(2,1)}, bf16[2048,512]{1,0:T(8,128)(2,1)}, f32[8,256]{1,0:T(8,128)}, f32[128,1536]{1,0:T(8,128)}, bf16[128,1536]{1,0:T(8...) custom-call(bf16[128,1536]{1,0:T(8,128)(2,1)} %bitcast.23, ...), custom_call_target="tpu_custom_call" | custom-call | tf_op jit(solution)/shard_map/attend/pallas_call | solution.py:740
  83.8 92.3 %experts.1 = (f32[128,1664]{1,0:T(8,128)}, bf16[8,128,1536]{2,1,0:T(8,128)(2,1)}, f32[384,1536]{1,0:T(8,128)}, bf16[384,1536]{1,0:T(8,128)(2,1)}, f32[192,1536]{1,0:T(8,128)}, /*index=5*/bf16[192,1536]{1,0:T(8,128)(2,1)}) custom-call(bf16[128,1664]{1,0:T(8,128)(2,1)} %get-tuple-element.59.send_ref.refs_6_, bf16[2048,1536]{1,0:T(8,128)(2,1)} %get-tuple-element.60.d_out_far, ...), custom_call_target="tpu_custom_call" | custom-call | tf_op jit(solution)/shard_map/experts/pallas_call | solution.py:740
  176.1 57.5 %attend_back.1 = (bf16[128,1536]{1,0:T(8,128)(2,1)}, f32[128,1536]{1,0:T(8,128)}, bf16[128,1536]{1,0:T(8,128)(2,1)}, bf16[128,1536]{1,0:T(8,128)(2,1)}, bf16[128...) custom-call(f32[128,1664]{1,0:T(8,128)} %get-tuple-element.62.refs_0, ...), custom_call_target="tpu_custom_call" | custom-call | tf_op jit(solution)/shard_map/attend_back/pallas_call | solution.py:740
  233.7 74.9 %finish.1 = (bf16[768,1536]{1,0:T(8,128)(2,1)}, bf16[768,1536]{1,0:T(8,128)(2,1)}, bf16[768,512]{1,0:T(8,128)(2,1)}, f32[16,768]{1,0:T(8,128)}, bf16[128,1536]{1...) custom-call(bf16[128,1536]{1,0:T(8,128)(2,1)} %bitcast.24, ...), custom_call_target="tpu_custom_call" | custom-call | tf_op jit(solution)/shard_map/finish/pallas_call | solution.py:740
  308.6 1.4 slice_reduce_fusion
  310.0 1.3 slice_bitcast_fusion
  311.4 0.0 copy-start
  311.4 0.0 copy-start.1
  311.4 9.3 %widen.1 = (f32[768,1536]{1,0:T(8,128)}, f32[768,512]{1,0:T(8,128)}, f32[768,1536]{1,0:T(8,128)}, f32[384,1536]{1,0:T(8,128)}, f32[1,192,1536]{2,1,0:T(8,128)}) custom-call(bf16[768,1536]{1,0:T(8,128)(2,1)} %get-tuple-element.90.refs_0_, bf16[768,512]{1,0:T(8,128)(2,1)} %get-tuple-element.91.refs_1_, bf16[768,1536]{1,0:T(8,128)(2,1)} %get-tuple-element.92.refs_2_, ...), custom_call_target="tpu_custom_call" | custom-call | tf_op jit(solution)/shard_map/widen/pallas_call | solution.py:1614
  320.6 0.0 copy-done
  320.6 0.7 copy.24
  321.4 0.0 copy-done.1
  321.4 0.7 copy.25
  (3 shorter events, 0.0 us)
Async XLA Ops:
  311.4 9.3 %copy-start = (bf16[128,1536]{1,0:T(8,128)(2,1)S(1)}, bf16[128,1536]{1,0:T(8,128)(2,1)}, u32[]{:S(2)}) copy-start(bf16[128,1536]{1,0:T(8,128)(2,1)} %get-tuple-element.73) | copy-start | bytes 1179652
  311.4 10.0 %copy-start.1 = (bf16[128,1536]{1,0:T(8,128)(2,1)S(1)}, bf16[128,1536]{1,0:T(8,128)(2,1)}, u32[]{:S(2)}) copy-start(bf16[128,1536]{1,0:T(8,128)(2,1)} %get-tuple-element.88) | copy-start | bytes 1179652

commit v8 on v7

--- a/solution.py
+++ b/solution.py
@@ -808,61 +808,6 @@
                 self.on_core(part, 1 - self.c, other_z=True).wait_recv()
 
 
-def front(d_out, w_query, w_keyval, small):
-    count, rows = lax.axis_size("ctx"), d_out.shape[0]
-    depth = count // 4
-
-    def kernel(
-        d_out_ref, query_ref, keyval_ref, small_ref,
-        d_out_all, query_there, keyval_there, small_there, *sems,
-    ):
-        gather = gather_parts(d_out_all, rows, sems[:6], 2)
-        query_sems, keyval_sems, small_sems, own_sem = sems[6:]
-        query = Relay(query_ref, query_there, query_sems, parts=2)
-        keyval = Relay(keyval_ref, keyval_there, keyval_sems)
-        partner = {"wa": 1 - lax.axis_index("wa")}
-        swap = remote(small_ref, small_there, small_sems, (0,), partner)
-        keep = pltpu.make_async_copy(
-            d_out_ref, Gather(d_out_all, rows, sems[:3]).own(), own_sem.at[0]
-        )
-        keep.start()
-        greet(across_x=True)
-        swap.start()
-        query.start()
-        keyval.start()
-        gather.start(d_out_ref)
-        gather.along_z(1)
-        gather.along_y(0)
-        gather.along_z(2)
-        gather.along_y(1)
-        query.pass_on(0)
-        gather.along_z(3)
-        gather.along_y(2)
-        query.pass_on(1)
-        keyval.pass_on()
-        gather.along_y(3)
-        gather.finish()
-        query.finish()
-        keyval.finish()
-        swap.wait()
-        keep.wait()
-
-    def like(values):
-        return jax.ShapeDtypeStruct(values.shape, values.dtype)
-
-    out = [
-        jax.ShapeDtypeStruct((count * rows, d_out.shape[1]), d_out.dtype),
-        like(w_query), like(w_keyval), like(small),
-    ]
-    scratch = Gather.sems(depth) * 2 + [Relay.semaphores()] * 2
-    scratch += [pltpu.SemaphoreType.DMA((2, 1)), pltpu.SemaphoreType.DMA((1,))]
-    every = range(4)
-    return call(
-        kernel, out, scratch, 0, "front",
-        d_out, w_query, w_keyval, small, outside=every, outside_out=every,
-    )
-
-
 def rows_by_rows(left, right):
     return lax.dot_general(
         left, right, (((1,), (1,)), ((), ())), preferred_element_type=jnp.float32
@@ -924,27 +869,40 @@
 
 
 def attend(
-    x, small, small_there, projections, w_out_attn, w_out, angles, doc_row, routes, experts
+    x, d_out, small, w_query, w_keyval, w_out_attn, w_out, angles, doc_row, routes, experts
 ):
     count, tokens, features = lax.axis_size("ctx"), x.shape[0], x.shape[1]
     depth, length = count // 4, count * tokens
-    kv_columns = projections[2].shape[1]
+    kv_columns = w_keyval.shape[1]
 
     def kernel(
-        arrive, x_ref, small_ref, small_there_ref, query_own, query_other, keyval_own, keyval_other,
-        attn_own, attn_own_far, out_own, cosine_ref, sine_ref, doc_row_ref, routes_ref,
-        query, keyval, level, mixed, hidden, mixed_low, middle, send, gates_out, attn_other,
-        out_other,
-        full, stacked, bias, x_sems, attn_sems, *sems,
+        arrive, x_ref, small_ref, query_own, keyval_own, attn_own, d_out_far, query_far,
+        keyval_far, attn_far, out_far, cosine_ref, sine_ref, doc_row_ref, routes_ref,
+        query, keyval, level, mixed, hidden, mixed_low, middle, send, gates_out, query_other,
+        keyval_other, attn_other, small_there, d_out_all, out_other,
+        full, stacked, bias, query_sems, keyval_sems, attn_sems, small_sems, own_sem, *sems,
     ):
-        gather = gather_parts(keyval, tokens, sems, 2)
-        attn = Relay(attn_own_far, attn_other, attn_sems, parts=2, paired=True)
+        gather = gather_parts(keyval, tokens, sems[:6], 2)
+        spread = gather_parts(d_out_all, tokens, sems[6:], 2)
+        query_relay = Relay(query_far, query_other, query_sems, parts=2)
+        keyval_relay = Relay(keyval_far, keyval_other, keyval_sems)
+        attn = Relay(attn_far, attn_other, attn_sems, parts=2, paired=True)
+        partner = {"wa": 1 - lax.axis_index("wa")}
+        swap = remote(small_ref, small_there, small_sems, (0,), partner)
+        swap_out = remote(out_far, out_other, small_sems, (1,), partner)
+        keep = pltpu.make_async_copy(
+            d_out_far, Gather(d_out_all, tokens, sems[6:9]).own(), own_sem.at[0]
+        )
+        keep.start()
         greet(across_x=True)
+        swap.start()
+        keyval_relay.start()
+        query_relay.start()
         attn.start()
-        partner = {"wa": 1 - lax.axis_index("wa")}
-        swap_out = remote(out_own, out_other, x_sems, (0,), partner)
         swap_out.start()
-        fill_small(full, small_ref, small_there_ref)
+        spread.start(d_out_far)
+        swap.wait()
+        fill_small(full, small_ref, small_there)
         residual = x_ref[...].astype(jnp.float32)
         hidden[...] = normed(residual, full[experts : experts + 1]).astype(jnp.bfloat16)
         own, other = hidden[:, side_columns(True)], hidden[:, side_columns(False)]
@@ -955,26 +913,37 @@
                 other, matrix_other[...], preferred_element_type=jnp.float32
             )
 
-        arrive(5, 6)
+        bias[...] = allowed_bias(doc_row_ref, tokens)
+        spread.along_z(1)
+        spread.along_y(0)
+        keyval_relay.pass_on()
+        keyval_relay.finish()
+        arrive(3)
         pre = onto(keyval_own, keyval_other)
         keys = turned(pre[:, : kv_columns // 2], cosine, sine)
         block = jnp.concatenate([keys, pre[:, kv_columns // 2 :]], axis=1)
         Gather(keyval, tokens, sems[:3]).own()[...] = block.astype(jnp.bfloat16)
+        spread.along_z(2)
+        spread.along_y(1)
+        query_relay.pass_on(0)
+        spread.along_z(3)
         gather.start()
-        arrive(3, 4)
+        gather.along_z(1)
+        spread.along_y(2)
+        gather.along_y(0)
+        gather.along_z(2)
+        query_relay.pass_on(1)
+        spread.along_y(3)
+        gather.along_y(1)
+        gather.along_z(3)
+        query_relay.finish()
+        arrive(2)
         query[...] = turned(onto(query_own, query_other), cosine, sine).astype(jnp.bfloat16)
-        bias[...] = allowed_bias(doc_row_ref, tokens)
         for head in range(HEADS):
             rows = slice(head * tokens, (head + 1) * tokens)
             stacked[rows, :] = query[:, head * 128 : (head + 1) * 128]
-        gather.along_z(1)
-        gather.along_y(0)
-        gather.along_z(2)
-        gather.along_y(1)
-        gather.along_z(3)
         attn.pass_on(0)
         gather.along_y(2)
-        attn.pass_on(1)
         gather.along_y(3)
         gather.finish()
 
@@ -996,13 +965,14 @@
                 mixed[:, columns] = mixture[part * tokens : (part + 1) * tokens]
             column = jnp.broadcast_to(top + jnp.log(total), (2 * tokens, 128))
             level[pl.ds(pair, 1), :] = jnp.transpose(column)[:1]
-            pl.when(pair == HEADS // 4)(lambda: attn.pass_on_pair(0))
-
+            pl.when(pair == 1)(lambda: attn.pass_on(1))
+            pl.when(pair == 4)(lambda: attn.pass_on_pair(0))
+
+        mixed_low[...] = mixed[...].astype(jnp.bfloat16)
         attn.pass_on_pair(1)
-        mixed_low[...] = mixed[...].astype(jnp.bfloat16)
+        own, other = mixed_low[:, side_columns(True)], mixed_low[:, side_columns(False)]
+        arrive(4)
         attn.finish()
-        arrive(7)
-        own, other = mixed_low[:, side_columns(True)], mixed_low[:, side_columns(False)]
         middle[...] = residual + onto(attn_own, attn_other)
         hidden_two = normed(middle[...], full[experts + 1 : experts + 2]).astype(jnp.bfloat16)
         send[:, :features] = hidden_two
@@ -1016,6 +986,8 @@
         carried = jnp.where(lane < experts, high, jnp.where(lane < 2 * experts, gates - high, 0.0))
         send[:, features:] = carried.astype(jnp.bfloat16)
         gates_out[...] = jnp.where(lane < experts, gates, 0.0)
+        spread.finish()
+        keep.wait()
         swap_out.wait()
 
     def shape(rows, columns, kind=jnp.bfloat16):
@@ -1026,19 +998,23 @@
         shape(tokens, features), shape(length, kv_columns), shape(8, 2 * tokens, jnp.float32),
         shape(tokens, features, jnp.float32), shape(tokens, features), shape(tokens, features),
         shape(tokens, features, jnp.float32), shape(tokens, wide), shape(tokens, 128, jnp.float32),
-        shape(*w_out_attn.shape), shape(*w_out.shape),
+        shape(*w_query.shape), shape(*w_keyval.shape), shape(*w_out_attn.shape),
+        shape(*small.shape), shape(length, features), shape(*w_out.shape),
     ]
     scratch = [
         pltpu.VMEM((small.shape[0], features), jnp.float32),
         pltpu.VMEM((HEADS * tokens, HEAD_DIM), jnp.bfloat16),
         pltpu.VMEM((tokens, length), jnp.float32),
-        pltpu.SemaphoreType.DMA((2, 1)),
         Relay.semaphores(),
-    ] + Gather.sems(depth) * 2
+        Relay.semaphores(),
+        Relay.semaphores(),
+        pltpu.SemaphoreType.DMA((2, 2)),
+        pltpu.SemaphoreType.DMA((1,)),
+    ] + Gather.sems(depth) * 4
     return call(
         kernel, out, scratch, 2, "attend",
-        x, small, small_there, *projections, w_out_attn, w_out_attn, w_out, *angles, doc_row,
-        routes, outside=(8, 9), outside_out=(10,), late=(5, 6, 3, 4, 7),
+        x, small, w_query, w_keyval, w_out_attn, d_out, w_query, w_keyval, w_out_attn, w_out,
+        *angles, doc_row, routes, outside=(5, 6, 7, 8, 9), outside_out=(13, 14), late=(3, 2, 4),
     )
 
 
@@ -1649,17 +1625,14 @@
     )
     in_own = jnp.swapaxes(w_in[0], 1, 2).reshape(-1, D)
 
-    d_out_all, w_query_there, w_keyval_there, small_there = front(
-        grad_out, w_query, w_keyval, small
+    (
+        query, keyval, level, mixed, hidden, mixed_low, middle, send, gates, w_query_there,
+        w_keyval_there, w_out_attn_there, small_there, d_out_all, w_out_there,
+    ) = attend(
+        x, grad_out, small, w_query, w_keyval, w_out_attn, w_out[0], angles, seq_ids,
+        routes[0].T, experts,
     )
     projections = (w_query, w_query_there, w_keyval, w_keyval_there)
-    (
-        query, keyval, level, mixed, hidden, mixed_low, middle, send, gates, w_out_attn_there,
-        w_out_there,
-    ) = attend(
-        x, small, small_there, projections, w_out_attn, w_out[0], angles, seq_ids, routes[0].T,
-        experts,
-    )
     returned, results, grad_in, grad_in_other, grad_out_matrix, grad_out_other = run_experts(
         send, d_out_all, in_own, w_out[0], w_out_there, experts
     )

time: 328 us -> 321 us (0.979)
  Pallas kernels: 313 us -> 306 us
    pallas_call x5 -> x4, Pallas kernels: 304 us -> 297 us  [call(): pl.pallas_call(with_late if late else kernel, out_shape=out, in_specs=[sp...]
where the time goes in v8:
time: 321 us; the launch traced here: 315 us
  Pallas kernels  306 us (95%)
  local copies, waits for them, and re-layouts  5.73 us (2%)
    pallas_call x4, Pallas kernels, call(): pl.pallas_call(with_late if late else kernel, out_shape=out, in_specs=[sp...  297 us
    pallas_call x1, Pallas kernels, widen(): pl.pallas_call(kernel, grid=(steps,), out_shape=[jax.ShapeDtypeStruct(que...  9.26 us

profile of v8, /device:TPU:0, one launch (start us, length us, event | category | flops | bytes accessed | tf_op | source)
XLA Modules:
  0.0 315.4 jit_solution(11522924796010164888)
XLA Ops:
  0.7 0.1 pad.7.clone
  0.8 0.7 broadcast_in_dim.20
  1.4 0.7 broadcast_in_dim.21
  2.1 1.4 maximum_maximum_fusion.refs_1_.refs_2_
  3.5 0.3 fusion
  3.8 0.8 pad_maximum_fusion
  4.6 72.5 %attend.1 = (bf16[128,1536]{1,0:T(8,128)(2,1)}, bf16[2048,512]{1,0:T(8,128)(2,1)}, f32[8,256]{1,0:T(8,128)}, f32[128,1536]{1,0:T(8,128)}, bf16[128,1536]{1,0:T(8...) custom-call(bf16[128,1536]{1,0:T(8,128)(2,1)} %bitcast.23, ...), custom_call_target="tpu_custom_call" | custom-call | tf_op jit(solution)/shard_map/attend/pallas_call | solution.py:740
  77.1 91.3 %experts.1 = (f32[128,1664]{1,0:T(8,128)}, bf16[8,128,1536]{2,1,0:T(8,128)(2,1)}, f32[384,1536]{1,0:T(8,128)}, bf16[384,1536]{1,0:T(8,128)(2,1)}, f32[192,1536]{1,0:T(8,128)}, /*index=5*/bf16[192,1536]{1,0:T(8,128)(2,1)}) custom-call(bf16[128,1664]{1,0:T(8,128)(2,1)} %get-tuple-element.56.send_ref.refs_6_, bf16[2048,1536]{1,0:T(8,128)(2,1)} %get-tuple-element.57.d_out_far, ...), custom_call_target="tpu_custom_call" | custom-call | tf_op jit(solution)/shard_map/experts/pallas_call | solution.py:740
  168.4 57.8 %attend_back.1 = (bf16[128,1536]{1,0:T(8,128)(2,1)}, f32[128,1536]{1,0:T(8,128)}, bf16[128,1536]{1,0:T(8,128)(2,1)}, bf16[128,1536]{1,0:T(8,128)(2,1)}, bf16[128...) custom-call(f32[128,1664]{1,0:T(8,128)} %get-tuple-element.59.refs_0, ...), custom_call_target="tpu_custom_call" | custom-call | tf_op jit(solution)/shard_map/attend_back/pallas_call | solution.py:740
  226.2 75.3 %finish.1 = (bf16[768,1536]{1,0:T(8,128)(2,1)}, bf16[768,1536]{1,0:T(8,128)(2,1)}, bf16[768,512]{1,0:T(8,128)(2,1)}, f32[16,768]{1,0:T(8,128)}, bf16[128,1536]{1...) custom-call(bf16[128,1536]{1,0:T(8,128)(2,1)} %bitcast.24, ...), custom_call_target="tpu_custom_call" | custom-call | tf_op jit(solution)/shard_map/finish/pallas_call | solution.py:740
  301.5 1.4 slice_reduce_fusion
  302.9 1.3 slice_bitcast_fusion
  304.2 0.0 copy-start
  304.2 0.0 copy-start.1
  304.2 9.3 %widen.1 = (f32[768,1536]{1,0:T(8,128)}, f32[768,512]{1,0:T(8,128)}, f32[768,1536]{1,0:T(8,128)}, f32[384,1536]{1,0:T(8,128)}, f32[1,192,1536]{2,1,0:T(8,128)}) custom-call(bf16[768,1536]{1,0:T(8,128)(2,1)} %get-tuple-element.90.refs_0_, bf16[768,512]{1,0:T(8,128)(2,1)} %get-tuple-element.91.refs_1_, bf16[768,1536]{1,0:T(8,128)(2,1)} %get-tuple-element.92.refs_2_, ...), custom_call_target="tpu_custom_call" | custom-call | tf_op jit(solution)/shard_map/widen/pallas_call | solution.py:1590
  313.5 0.0 copy-done
  313.5 0.7 copy.24
  314.2 0.0 copy-done.1
  314.2 0.7 copy.25
  (3 shorter events, 0.0 us)
Async XLA Ops:
  304.2 9.3 %copy-start = (bf16[128,1536]{1,0:T(8,128)(2,1)S(1)}, bf16[128,1536]{1,0:T(8,128)(2,1)}, u32[]{:S(2)}) copy-start(bf16[128,1536]{1,0:T(8,128)(2,1)} %get-tuple-element.71) | copy-start | bytes 1179652
  304.2 10.0 %copy-start.1 = (bf16[128,1536]{1,0:T(8,128)(2,1)S(1)}, bf16[128,1536]{1,0:T(8,128)(2,1)}, u32[]{:S(2)}) copy-start(bf16[128,1536]{1,0:T(8,128)(2,1)} %get-tuple-element.88) | copy-start | bytes 1179652

commit v9 on v8

--- a/solution.py
+++ b/solution.py
@@ -709,36 +709,55 @@
     )
 
 
-def call(kernel, out, scratch, number, name, *operands, outside=(), outside_out=(), late=()):
+def call(
+    kernel, out, scratch, number, name, *operands, outside=(), outside_out=(), late=(), early=()
+):
     many = isinstance(out, (tuple, list))
     count, results = len(operands), len(out) if many else 1
-    late = tuple(late)
+    late, early = tuple(late), tuple(early)
+    more = len(late) + len(early) + 1
 
     def spec(position, far):
         return pl.BlockSpec(memory_space=pl.ANY if position in far else pltpu.VMEM)
 
-    def with_late(*refs):
-        near, sems = refs[-len(late) - 1 : -1], refs[-1]
-        copies = {
+    def moving(*refs):
+        near, sems = refs[-more:-1], refs[-1]
+        loads = {
             i: pltpu.make_async_copy(refs[i], near[k], sems.at[k]) for k, i in enumerate(late)
         }
-        for copy in copies.values():
+        stores = {
+            i: pltpu.make_async_copy(near[k], refs[count + i], sems.at[k])
+            for k, i in enumerate(early, len(late))
+        }
+        for copy in loads.values():
             copy.start()
         held = [near[late.index(i)] if i in late else refs[i] for i in range(count)]
+        given = [
+            near[len(late) + early.index(i)] if i in early else refs[count + i]
+            for i in range(results)
+        ]
 
         def arrive(*which):
             for i in which:
-                copies[i].wait()
-
-        kernel(arrive, *held, *refs[count : -len(late) - 1])
-
-    if late:
+                loads[i].wait()
+
+        def leave(*which):
+            for i in which:
+                stores[i].start()
+
+        helpers = (arrive, leave) if early else (arrive,)
+        kernel(*helpers, *held, *given, *refs[count + results : -more])
+        for copy in stores.values():
+            copy.wait()
+
+    if late or early:
         scratch = list(scratch) + [pltpu.VMEM(operands[i].shape, operands[i].dtype) for i in late]
-        scratch.append(pltpu.SemaphoreType.DMA((len(late),)))
-    far = tuple(outside) + late
-    out_specs = [spec(i, outside_out) for i in range(results)]
+        scratch += [pltpu.VMEM(out[i].shape, out[i].dtype) for i in early]
+        scratch.append(pltpu.SemaphoreType.DMA((more - 1,)))
+    far, far_out = tuple(outside) + late, tuple(outside_out) + early
+    out_specs = [spec(i, far_out) for i in range(results)]
     return pl.pallas_call(
-        with_late if late else kernel,
+        moving if late or early else kernel,
         out_shape=out,
         in_specs=[spec(i, far) for i in range(count)],
         out_specs=out_specs if many else out_specs[0],
@@ -869,18 +888,20 @@
 
 
 def attend(
-    x, d_out, small, w_query, w_keyval, w_out_attn, w_out, angles, doc_row, routes, experts
+    x, d_out, router, gains, w_query, w_keyval, w_out_attn, w_out, angles, doc_row, routes
 ):
     count, tokens, features = lax.axis_size("ctx"), x.shape[0], x.shape[1]
     depth, length = count // 4, count * tokens
-    kv_columns = w_keyval.shape[1]
+    kv_columns, experts = w_keyval.shape[1], router.shape[0]
+    small_shape = (2 * experts, router.shape[1])
 
     def kernel(
-        arrive, x_ref, small_ref, query_own, keyval_own, attn_own, d_out_far, query_far,
-        keyval_far, attn_far, out_far, cosine_ref, sine_ref, doc_row_ref, routes_ref,
+        arrive, leave, x_ref, router_ref, query_own, keyval_own, attn_own, d_out_far, query_far,
+        keyval_far, attn_far, out_far, cosine_ref, sine_ref, doc_row_ref, routes_ref, gain_one, gain_two,
         query, keyval, level, mixed, hidden, mixed_low, middle, send, gates_out, query_other,
         keyval_other, attn_other, small_there, d_out_all, out_other,
-        full, stacked, bias, query_sems, keyval_sems, attn_sems, small_sems, own_sem, *sems,
+        small_ref,
+        filled, full, stacked, bias, query_sems, keyval_sems, attn_sems, small_sems, own_sem, *sems,
     ):
         gather = gather_parts(keyval, tokens, sems[:6], 2)
         spread = gather_parts(d_out_all, tokens, sems[6:], 2)
@@ -894,6 +915,11 @@
             d_out_far, Gather(d_out_all, tokens, sems[6:9]).own(), own_sem.at[0]
         )
         keep.start()
+        filled[...] = jnp.zeros_like(filled)
+        filled[:experts] = router_ref[...].astype(jnp.float32)
+        filled[experts : experts + 1] = gain_one[...].astype(jnp.float32)
+        filled[experts + 1 : experts + 2] = gain_two[...].astype(jnp.float32)
+        small_ref[...] = filled[...].astype(jnp.bfloat16)
         greet(across_x=True)
         swap.start()
         keyval_relay.start()
@@ -923,6 +949,7 @@
         keys = turned(pre[:, : kv_columns // 2], cosine, sine)
         block = jnp.concatenate([keys, pre[:, kv_columns // 2 :]], axis=1)
         Gather(keyval, tokens, sems[:3]).own()[...] = block.astype(jnp.bfloat16)
+        leave(4, 10)
         spread.along_z(2)
         spread.along_y(1)
         query_relay.pass_on(0)
@@ -942,10 +969,12 @@
         for head in range(HEADS):
             rows = slice(head * tokens, (head + 1) * tokens)
             stacked[rows, :] = query[:, head * 128 : (head + 1) * 128]
+        leave(0, 9)
         attn.pass_on(0)
         gather.along_y(2)
         gather.along_y(3)
         gather.finish()
+        leave(1)
 
         @pl.loop(0, HEADS // 2)
         def _(pair):
@@ -969,10 +998,12 @@
             pl.when(pair == 4)(lambda: attn.pass_on_pair(0))
 
         mixed_low[...] = mixed[...].astype(jnp.bfloat16)
+        leave(3, 5)
         attn.pass_on_pair(1)
         own, other = mixed_low[:, side_columns(True)], mixed_low[:, side_columns(False)]
         arrive(4)
         attn.finish()
+        leave(11)
         middle[...] = residual + onto(attn_own, attn_other)
         hidden_two = normed(middle[...], full[experts + 1 : experts + 2]).astype(jnp.bfloat16)
         send[:, :features] = hidden_two
@@ -999,10 +1030,11 @@
         shape(tokens, features, jnp.float32), shape(tokens, features), shape(tokens, features),
         shape(tokens, features, jnp.float32), shape(tokens, wide), shape(tokens, 128, jnp.float32),
         shape(*w_query.shape), shape(*w_keyval.shape), shape(*w_out_attn.shape),
-        shape(*small.shape), shape(length, features), shape(*w_out.shape),
+        shape(*small_shape), shape(length, features), shape(*w_out.shape), shape(*small_shape),
     ]
     scratch = [
-        pltpu.VMEM((small.shape[0], features), jnp.float32),
+        pltpu.VMEM(small_shape, jnp.float32),
+        pltpu.VMEM((small_shape[0], features), jnp.float32),
         pltpu.VMEM((HEADS * tokens, HEAD_DIM), jnp.bfloat16),
         pltpu.VMEM((tokens, length), jnp.float32),
         Relay.semaphores(),
@@ -1013,8 +1045,9 @@
     ] + Gather.sems(depth) * 4
     return call(
         kernel, out, scratch, 2, "attend",
-        x, small, w_query, w_keyval, w_out_attn, d_out, w_query, w_keyval, w_out_attn, w_out,
-        *angles, doc_row, routes, outside=(5, 6, 7, 8, 9), outside_out=(13, 14), late=(3, 2, 4),
+        x, router, w_query, w_keyval, w_out_attn, d_out, w_query, w_keyval, w_out_attn, w_out,
+        *angles, doc_row, routes, *gains, outside=(5, 6, 7, 8, 9), outside_out=(13, 14), late=(3, 2, 4),
+        early=(0, 1, 3, 4, 5, 9, 10, 11),
     )
 
 
@@ -1033,7 +1066,7 @@
     depth, length, kv_columns = count // 4, keyval.shape[0], keyval.shape[1]
 
     def kernel(
-        arrive, returned_ref, gates_ref, small_ref, small_there_ref, middle_ref, d_out_ref, send_ref,
+        arrive, leave, returned_ref, gates_ref, small_ref, small_there_ref, middle_ref, d_out_ref, send_ref,
         attn_own_ref, attn_other_ref, query_ref, keyval_ref, cosine_ref, sine_ref, doc_row_ref,
         level_ref, mixed_ref, hidden_ref, mixed_low_ref, results_ref,
         output, grad_middle, grad_middle_low, grad_middle_there, grad_query, grad_query_there,
@@ -1064,6 +1097,7 @@
         swaps[4].start()
         hidden_own[...] = hidden_ref[:, side_columns(True)]
         mixed_own[...] = mixed_low_ref[:, side_columns(True)]
+        leave(9, 11)
         fill_small(full, small_ref, small_there_ref)
         arrive(0, 4, 5, 6)
         lane = lax.broadcasted_iota(jnp.int32, (tokens, 128), 1)
@@ -1082,6 +1116,7 @@
         grad_middle[...] = d_out_ref[...].astype(jnp.float32) + back
         grad_middle_low[...] = grad_middle[...].astype(jnp.bfloat16)
         swaps[0].start()
+        leave(1, 2)
         small_grads[:experts] = grad_router[:experts]
         row = lax.broadcasted_iota(jnp.int32, (small_grads.shape[0] - experts, 1), 0)
         small_grads[experts:] = jnp.where(row == 1, grad_gain, 0.0)
@@ -1139,6 +1174,7 @@
         cosine, sine = cosine_ref[...], -sine_ref[...]
         grad_query[...] = turned(turned_query[...], cosine, sine).astype(jnp.bfloat16)
         swaps[1].start()
+        leave(4)
         steps = range(depth - 1, -1, -1)
         for step in steps:
             keyval_sum.add_cores(step)
@@ -1191,7 +1227,7 @@
         kernel, out, scratch, 4, "attend_back",
         returned, gates, small, small_there, middle, d_out, send, attn_own, attn_other, query,
         keyval, *angles, doc_row, level, mixed, hidden, mixed_low, results,
-        late=(18, 0, 4, 5, 6, 7, 8, 9, 10, 15),
+        late=(18, 0, 4, 5, 6, 7, 8, 9, 10, 15), early=(1, 2, 4, 9, 11),
     )
 
 
@@ -1416,7 +1452,7 @@
     experts = small.shape[0] // 2
 
     def kernel(
-        arrive, x_ref, grad_middle_ref, small_ref, small_there_ref, small_grads_ref,
+        arrive, leave, x_ref, grad_middle_ref, small_ref, small_there_ref, small_grads_ref,
         query_own, query_other, keyval_own, keyval_other,
         hidden_ref, hidden_there, mixed_ref, mixed_there, middle_ref, middle_there,
         query_ref, query_there, keyval_ref, keyval_there, in_ref, out_ref,
@@ -1455,10 +1491,12 @@
         products(mixed_ref, mixed_there, middle_ref, middle_there, attn_part)
         greet(across_x=True)
         attn.start()
+        arrive(9, 10, 15, 16)
         products(hidden_ref, hidden_there, query_ref, query_there, query_part)
         for step in steps:
             attn.add_cores(step)
         query_.start()
+        arrive(17, 18)
         products(hidden_ref, hidden_there, keyval_ref, keyval_there, keyval_part)
         keyval_.start()
         for step in steps:
@@ -1477,6 +1515,7 @@
             x_ref[...].astype(jnp.float32), full[experts : experts + 1], grad_one[...]
         )
         grad_input[...] = (grad_middle_ref[...] + back).astype(jnp.bfloat16)
+        leave(4)
         row = lax.broadcasted_iota(jnp.int32, (small_mine.shape[0], 1), 0)
         small_mine[...] = jnp.where(row == experts, grad_gain, small_grads_ref[...])
         swaps[0].start()
@@ -1520,6 +1559,8 @@
         query_out.along_y(1)
         keyval_out.along_z(3)
         query_out.along_y(2)
+        attn_out.finish()
+        leave(0)
         small_out.along_y(0)
         keyval_out.along_y(0)
         small_out.along_y(1)
@@ -1529,7 +1570,11 @@
         keyval_out.along_y(2)
         small_out.along_y(3)
         keyval_out.along_y(3)
-        for one in [small_out] + gathers + scatters:
+        query_out.finish()
+        leave(1)
+        keyval_out.finish()
+        leave(2)
+        for one in [small_out] + scatters:
             one.finish()
         small_rows = small_came.shape[0]
         total = small_all[:small_rows].astype(jnp.float32)
@@ -1565,17 +1610,18 @@
         kernel, out, scratch, 1, "finish",
         x, grad_middle, small, small_there, small_grads, *matrices, *hidden, *mixed, *middle,
         *query, *keyval, expert_in, expert_out, outside=(19, 20), outside_out=(5, 6),
-        late=(0, 1, 5, 6, 7, 8),
-    )
-
-
-def widen(query, keyval, attn, grad_in, in_there, grad_out, out_there):
+        late=(9, 10, 15, 16, 17, 18, 5, 6, 7, 8, 0, 1), early=(0, 1, 2, 4),
+    )
+
+
+def widen(query, keyval, attn, grad_in, in_there, grad_out, out_there, small):
     quarter, features = grad_out.shape
-    steps = 4
+    steps, experts = 4, small.shape[0] // 2
 
     def kernel(*refs):
         query_ref, keyval_ref, attn_ref, in_ref, in_there_ref, out_ref, out_there_ref = refs[:7]
-        query_out, keyval_out, attn_out, in_out, out_out = refs[7:]
+        small_ref, query_out, keyval_out, attn_out, in_out, out_out, router_out = refs[7:]
+        router_out[...] = small_ref[:experts]
         query_out[...] = query_ref[...].astype(jnp.float32)
         keyval_out[...] = keyval_ref[...].astype(jnp.float32)
         attn_out[...] = attn_ref[...].astype(jnp.float32)
@@ -1596,16 +1642,19 @@
             jax.ShapeDtypeStruct(attn.shape, jnp.float32),
             jax.ShapeDtypeStruct(grad_in.shape, jnp.float32),
             jax.ShapeDtypeStruct((1, quarter, features), jnp.float32),
+            jax.ShapeDtypeStruct((experts, small.shape[1]), jnp.float32),
         ],
-        in_specs=[rows(values) for values in operands],
+        in_specs=[rows(values) for values in operands]
+        + [pl.BlockSpec(small.shape, lambda i: (0, 0))],
         out_specs=[
             rows(query), rows(keyval), rows(attn),
             rows(grad_in),
             pl.BlockSpec((1, quarter // steps, features), lambda i: (0, i, 0)),
+            pl.BlockSpec((experts, small.shape[1]), lambda i: (0, 0)),
         ],
         compiler_params=pltpu.CompilerParams(vmem_limit_bytes=VMEM_LIMIT),
         name="widen",
-    )(*operands)
+    )(*operands, small)
 
 
 def gathered_body(
@@ -1615,9 +1664,6 @@
     me = lax.axis_index("ctx")
     tokens, experts = layer_input.shape[1], router.shape[1]
     x, grad_out = layer_input[0], d_out[0]
-    small = jnp.concatenate(
-        [router.T, gain_attn[None], gain_ffn[None], jnp.zeros((experts - 2, D // 2), jnp.bfloat16)]
-    )
     turns = angle_table(me * tokens + jnp.arange(tokens, dtype=jnp.int32))[:, 0]
     cosine, sine = jnp.cos(turns), jnp.sin(turns)
     angles = (
@@ -1627,10 +1673,10 @@
 
     (
         query, keyval, level, mixed, hidden, mixed_low, middle, send, gates, w_query_there,
-        w_keyval_there, w_out_attn_there, small_there, d_out_all, w_out_there,
+        w_keyval_there, w_out_attn_there, small_there, d_out_all, w_out_there, small,
     ) = attend(
-        x, grad_out, small, w_query, w_keyval, w_out_attn, w_out[0], angles, seq_ids,
-        routes[0].T, experts,
+        x, grad_out, router.T, (gain_attn[None], gain_ffn[None]), w_query, w_keyval, w_out_attn,
+        w_out[0], angles, seq_ids, routes[0].T,
     )
     projections = (w_query, w_query_there, w_keyval, w_keyval_there)
     returned, results, grad_in, grad_in_other, grad_out_matrix, grad_out_other = run_experts(
@@ -1648,8 +1694,8 @@
         (middle_low, middle_there), (grad_query, query_there),
         (grad_keyval, keyval_there), grad_in_other, grad_out_other,
     )
-    query_sum, keyval_sum, attn_sum, grad_w_in, grad_w_out = widen(
-        query_sum, keyval_sum, attn_sum, grad_in, in_there, grad_out_matrix, out_there
+    query_sum, keyval_sum, attn_sum, grad_w_in, grad_w_out, grad_router = widen(
+        query_sum, keyval_sum, attn_sum, grad_in, in_there, grad_out_matrix, out_there, small_sum
     )
     return (
         output[None],
@@ -1659,7 +1705,7 @@
         keyval_sum,
         attn_sum,
         small_sum[experts + 1],
-        small_sum[:experts].T,
+        grad_router.T,
         jnp.swapaxes(grad_w_in.reshape(2, -1, D), 1, 2)[None],
         grad_w_out,
     )

time: 321 us -> 315 us (0.981)
  Pallas kernels: 306 us -> 302 us
    pallas_call x4, Pallas kernels: 297 us -> 292 us  [call(): pl.pallas_call(moving if late or early else kernel, out_shape=out, in_spe...]
where the time goes in v9:
time: 315 us; the launch traced here: 310 us
  Pallas kernels  302 us (96%)
  local copies, waits for them, and re-layouts  5.46 us (2%)
    pallas_call x4, Pallas kernels, call(): pl.pallas_call(moving if late or early else kernel, out_shape=out, in_spe...  292 us
    pallas_call x1, Pallas kernels, widen(): pl.pallas_call(kernel, grid=(steps,), out_shape=[jax.ShapeDtypeStruct(que...  9.97 us

profile of v9, /device:TPU:0, one launch (start us, length us, event | category | flops | bytes accessed | tf_op | source)
XLA Modules:
  0.0 309.6 jit_solution(14337792594259026195)
XLA Ops:
  0.7 1.3 broadcast_in_dim.17.refs_14_
  1.9 1.3 broadcast_in_dim.18.refs_15_
  3.2 0.3 fusion
  3.5 0.8 pad_maximum_fusion
  4.3 69.7 %attend.1 = (bf16[128,1536]{1,0:T(8,128)(2,1)}, bf16[2048,512]{1,0:T(8,128)(2,1)}, f32[8,256]{1,0:T(8,128)}, f32[128,1536]{1,0:T(8,128)}, bf16[128,1536]{1,0:T(8...) custom-call(bf16[128,1536]{1,0:T(8,128)(2,1)} %bitcast.22, ...), custom_call_target="tpu_custom_call" | custom-call | tf_op jit(solution)/shard_map/attend/pallas_call | solution.py:759
  74.0 91.3 %experts.1 = (f32[128,1664]{1,0:T(8,128)}, bf16[8,128,1536]{2,1,0:T(8,128)(2,1)}, f32[384,1536]{1,0:T(8,128)}, bf16[384,1536]{1,0:T(8,128)(2,1)}, f32[192,1536]{1,0:T(8,128)}, /*index=5*/bf16[192,1536]{1,0:T(8,128)(2,1)}) custom-call(bf16[128,1664]{1,0:T(8,128)(2,1)} %get-tuple-element.58.send_ref.refs_6_, bf16[2048,1536]{1,0:T(8,128)(2,1)} %get-tuple-element.59.d_out_far, ...), custom_call_target="tpu_custom_call" | custom-call | tf_op jit(solution)/shard_map/experts/pallas_call | solution.py:759
  165.3 57.4 %attend_back.1 = (bf16[128,1536]{1,0:T(8,128)(2,1)}, f32[128,1536]{1,0:T(8,128)}, bf16[128,1536]{1,0:T(8,128)(2,1)}, bf16[128,1536]{1,0:T(8,128)(2,1)}, bf16[128...) custom-call(f32[128,1664]{1,0:T(8,128)} %get-tuple-element.61.refs_0, ...), custom_call_target="tpu_custom_call" | custom-call | tf_op jit(solution)/shard_map/attend_back/pallas_call | solution.py:759
  222.8 73.5 %finish.1 = (bf16[768,1536]{1,0:T(8,128)(2,1)}, bf16[768,1536]{1,0:T(8,128)(2,1)}, bf16[768,512]{1,0:T(8,128)(2,1)}, f32[16,768]{1,0:T(8,128)}, bf16[128,1536]{1...) custom-call(bf16[128,1536]{1,0:T(8,128)(2,1)} %bitcast.23, ...), custom_call_target="tpu_custom_call" | custom-call | tf_op jit(solution)/shard_map/finish/pallas_call | solution.py:759
  296.3 1.4 slice_reduce_fusion
  297.7 0.0 copy-start
  297.7 0.0 copy-start.1
  297.7 10.0 %widen.1 = (f32[768,1536]{1,0:T(8,128)}, f32[768,512]{1,0:T(8,128)}, f32[768,1536]{1,0:T(8,128)}, f32[384,1536]{1,0:T(8,128)}, f32[1,192,1536]{2,1,0:T(8,128)}, /*index=5*/f32[8,768]{1,0:T(8,128)}) custom-call(bf16[768,1536]{1,0:T(8,128)(2,1)} %get-tuple-element.93.refs_0_, bf16[768,512]{1,0:T(8,128)(2,1)} %get-tuple-element.94.refs_1_, ...), custom_call_target="tpu_custom_call" | custom-call | tf_op jit(solution)/shard_map/widen/pallas_call | solution.py:1636
  307.7 0.0 copy-done
  307.7 0.7 copy.24
  308.4 0.0 copy-done.1
  308.4 0.7 copy.25
  (2 shorter events, 0.0 us)
Async XLA Ops:
  297.7 10.0 %copy-start = (bf16[128,1536]{1,0:T(8,128)(2,1)S(1)}, bf16[128,1536]{1,0:T(8,128)(2,1)}, u32[]{:S(2)}) copy-start(bf16[128,1536]{1,0:T(8,128)(2,1)} %get-tuple-element.74) | copy-start | bytes 1179652
  297.7 10.7 %copy-start.1 = (bf16[128,1536]{1,0:T(8,128)(2,1)S(1)}, bf16[128,1536]{1,0:T(8,128)(2,1)}, u32[]{:S(2)}) copy-start(bf16[128,1536]{1,0:T(8,128)(2,1)} %get-tuple-element.91) | copy-start | bytes 1179652

commit v10 on v9

--- a/solution.py
+++ b/solution.py
@@ -1182,7 +1182,8 @@
         pl.when(within)(lambda: result.add_y_of(nearest(depth - 1)))
         for k in range(depth - 2, 0, -1):
             result.add_y_of(nearest(k))
-        for step in steps:
+            keyval_sum.add_y(k + 1)
+        for step in (1, 0):
             keyval_sum.add_y(step)
         keyval_sum.last(own_keyval)
         keys = turned(own_keyval[:, : kv_columns // 2], cosine, sine)
@@ -1371,6 +1372,9 @@
 
         scatter.add_y_of(nearest(depth - 2))
 
+        for k in range(depth - 3, 0, -1):
+            scatter.add_y_of(nearest(k))
+
         @pl.loop(0, features // 512)
         def _(turn):
             at = pl.ds(pl.multiple_of(turn * 512, 512), 512)
@@ -1380,8 +1384,6 @@
 
         stores[3].start()
         stores[4].start()
-        for k in range(depth - 3, 0, -1):
-            scatter.add_y_of(nearest(k))
 
         @pl.loop(0, features // 512)
         def _(turn):

time: 315 us -> 314 us (level)
  no operation moved by 1% of the time
where the time goes in v10:
time: 314 us; the launch traced here: 309 us
  Pallas kernels  301 us (96%)
  local copies, waits for them, and re-layouts  5.46 us (2%)
    pallas_call x4, Pallas kernels, call(): pl.pallas_call(moving if late or early else kernel, out_shape=out, in_spe...  291 us
    pallas_call x1, Pallas kernels, widen(): pl.pallas_call(kernel, grid=(steps,), out_shape=[jax.ShapeDtypeStruct(que...  9.97 us

profile of v10, /device:TPU:0, one launch (start us, length us, event | category | flops | bytes accessed | tf_op | source)
XLA Modules:
  0.0 308.8 jit_solution(12843651868588492939)
XLA Ops:
  0.7 1.3 broadcast_in_dim.17.refs_14_
  1.9 1.3 broadcast_in_dim.18.refs_15_
  3.2 0.3 fusion
  3.5 0.8 pad_maximum_fusion
  4.3 69.7 %attend.1 = (bf16[128,1536]{1,0:T(8,128)(2,1)}, bf16[2048,512]{1,0:T(8,128)(2,1)}, f32[8,256]{1,0:T(8,128)}, f32[128,1536]{1,0:T(8,128)}, bf16[128,1536]{1,0:T(8...) custom-call(bf16[128,1536]{1,0:T(8,128)(2,1)} %bitcast.22, ...), custom_call_target="tpu_custom_call" | custom-call | tf_op jit(solution)/shard_map/attend/pallas_call | solution.py:759
  74.0 88.3 %experts.1 = (f32[128,1664]{1,0:T(8,128)}, bf16[8,128,1536]{2,1,0:T(8,128)(2,1)}, f32[384,1536]{1,0:T(8,128)}, bf16[384,1536]{1,0:T(8,128)(2,1)}, f32[192,1536]{1,0:T(8,128)}, /*index=5*/bf16[192,1536]{1,0:T(8,128)(2,1)}) custom-call(bf16[128,1664]{1,0:T(8,128)(2,1)} %get-tuple-element.58.send_ref.refs_6_, bf16[2048,1536]{1,0:T(8,128)(2,1)} %get-tuple-element.59.d_out_far, ...), custom_call_target="tpu_custom_call" | custom-call | tf_op jit(solution)/shard_map/experts/pallas_call | solution.py:759
  162.3 58.7 %attend_back.1 = (bf16[128,1536]{1,0:T(8,128)(2,1)}, f32[128,1536]{1,0:T(8,128)}, bf16[128,1536]{1,0:T(8,128)(2,1)}, bf16[128,1536]{1,0:T(8,128)(2,1)}, bf16[128...) custom-call(f32[128,1664]{1,0:T(8,128)} %get-tuple-element.61.refs_0, ...), custom_call_target="tpu_custom_call" | custom-call | tf_op jit(solution)/shard_map/attend_back/pallas_call | solution.py:759
  221.0 74.4 %finish.1 = (bf16[768,1536]{1,0:T(8,128)(2,1)}, bf16[768,1536]{1,0:T(8,128)(2,1)}, bf16[768,512]{1,0:T(8,128)(2,1)}, f32[16,768]{1,0:T(8,128)}, bf16[128,1536]{1...) custom-call(bf16[128,1536]{1,0:T(8,128)(2,1)} %bitcast.23, ...), custom_call_target="tpu_custom_call" | custom-call | tf_op jit(solution)/shard_map/finish/pallas_call | solution.py:759
  295.4 1.4 slice_reduce_fusion
  296.8 0.0 copy-start
  296.8 0.0 copy-start.1
  296.8 10.0 %widen.1 = (f32[768,1536]{1,0:T(8,128)}, f32[768,512]{1,0:T(8,128)}, f32[768,1536]{1,0:T(8,128)}, f32[384,1536]{1,0:T(8,128)}, f32[1,192,1536]{2,1,0:T(8,128)}, /*index=5*/f32[8,768]{1,0:T(8,128)}) custom-call(bf16[768,1536]{1,0:T(8,128)(2,1)} %get-tuple-element.93.refs_0_, bf16[768,512]{1,0:T(8,128)(2,1)} %get-tuple-element.94.refs_1_, ...), custom_call_target="tpu_custom_call" | custom-call | tf_op jit(solution)/shard_map/widen/pallas_call | solution.py:1638
  306.8 0.0 copy-done
  306.8 0.7 copy.24
  307.6 0.0 copy-done.1
  307.6 0.7 copy.25
  (2 shorter events, 0.0 us)
Async XLA Ops:
  296.8 10.0 %copy-start = (bf16[128,1536]{1,0:T(8,128)(2,1)S(1)}, bf16[128,1536]{1,0:T(8,128)(2,1)}, u32[]{:S(2)}) copy-start(bf16[128,1536]{1,0:T(8,128)(2,1)} %get-tuple-element.74) | copy-start | bytes 1179652
  296.8 10.7 %copy-start.1 = (bf16[128,1536]{1,0:T(8,128)(2,1)S(1)}, bf16[128,1536]{1,0:T(8,128)(2,1)}, u32[]{:S(2)}) copy-start(bf16[128,1536]{1,0:T(8,128)(2,1)} %get-tuple-element.91) | copy-start | bytes 1179652

commit v11 on v10

--- a/solution.py
+++ b/solution.py
@@ -1093,6 +1093,7 @@
         arrive(18)
         for k in range(depth - 1, 0, -1):
             result.send_y(nearest(k))
+        arrive(16, 17)
         swaps[3].start()
         swaps[4].start()
         hidden_own[...] = hidden_ref[:, side_columns(True)]
@@ -1228,7 +1229,7 @@
         kernel, out, scratch, 4, "attend_back",
         returned, gates, small, small_there, middle, d_out, send, attn_own, attn_other, query,
         keyval, *angles, doc_row, level, mixed, hidden, mixed_low, results,
-        late=(18, 0, 4, 5, 6, 7, 8, 9, 10, 15), early=(1, 2, 4, 9, 11),
+        late=(18, 16, 17, 0, 4, 5, 6, 7, 8, 9, 10, 15), early=(1, 2, 4, 9, 11),
     )
 
 
@@ -1250,7 +1251,7 @@
     width = 2 * quarter
 
     def kernel(
-        send_ref, d_out_far, in_own_ref, out_own_ref, out_other_ref,
+        arrive, send_ref, d_out_far, in_own_ref, out_own_ref, out_other_ref,
         returned, results_far, grad_in_far, grad_in_other_far, grad_out_far, grad_out_other_far,
         hidden_all, grad_both, gated_hidden, other_part, other_result, result_from, result_sems,
         in_ref, out_ref, d_out_ref, x_sems, near_sem, results, grad_in, grad_in_other, grad_out,
@@ -1286,8 +1287,10 @@
         ]
         greet(across_x=True)
         gather.start()
+        arrive(2)
         for swap in swaps:
             swap.start()
+        arrive(3, 4)
         out_ref[:quarter] = out_own_ref[...]
         out_ref[quarter:] = out_other_ref[...]
         in_ref[:quarter] = in_own_ref[:quarter]
@@ -1440,7 +1443,7 @@
     scratch += Gather.sems(depth) * 2 + Scatter.scratch(depth, tokens, wide, 2)
     return call(
         kernel, out, scratch, 3, "experts", send, d_out_all, in_own, out_own, out_other, outside=(1,),
-        outside_out=range(1, 6),
+        outside_out=range(1, 6), late=(2, 3, 4),
     )
 
 

time: 314 us -> 313 us (level)
  no operation moved by 1% of the time
where the time goes in v11:
time: 313 us; the launch traced here: 308 us
  Pallas kernels  300 us (96%)
  local copies, waits for them, and re-layouts  5.46 us (2%)
    pallas_call x4, Pallas kernels, call(): pl.pallas_call(moving if late or early else kernel, out_shape=out, in_spe...  290 us
    pallas_call x1, Pallas kernels, widen(): pl.pallas_call(kernel, grid=(steps,), out_shape=[jax.ShapeDtypeStruct(que...  9.97 us

profile of v11, /device:TPU:0, one launch (start us, length us, event | category | flops | bytes accessed | tf_op | source)
XLA Modules:
  0.0 307.6 jit_solution(10533215111518376309)
XLA Ops:
  0.7 1.3 broadcast_in_dim.17.refs_14_
  1.9 1.3 broadcast_in_dim.18.refs_15_
  3.2 0.3 fusion
  3.5 0.8 pad_maximum_fusion
  4.3 69.7 %attend.1 = (bf16[128,1536]{1,0:T(8,128)(2,1)}, bf16[2048,512]{1,0:T(8,128)(2,1)}, f32[8,256]{1,0:T(8,128)}, f32[128,1536]{1,0:T(8,128)}, bf16[128,1536]{1,0:T(8...) custom-call(bf16[128,1536]{1,0:T(8,128)(2,1)} %bitcast.22, ...), custom_call_target="tpu_custom_call" | custom-call | tf_op jit(solution)/shard_map/attend/pallas_call | solution.py:759
  74.0 87.6 %experts.1 = (f32[128,1664]{1,0:T(8,128)}, bf16[8,128,1536]{2,1,0:T(8,128)(2,1)}, f32[384,1536]{1,0:T(8,128)}, bf16[384,1536]{1,0:T(8,128)(2,1)}, f32[192,1536]{1,0:T(8,128)}, /*index=5*/bf16[192,1536]{1,0:T(8,128)(2,1)}) custom-call(bf16[128,1664]{1,0:T(8,128)(2,1)} %get-tuple-element.58.refs_0_.refs_6_, bf16[2048,1536]{1,0:T(8,128)(2,1)} %get-tuple-element.59.refs_1_, ...), custom_call_target="tpu_custom_call" | custom-call | tf_op jit(solution)/shard_map/experts/pallas_call | solution.py:759
  161.6 58.4 %attend_back.1 = (bf16[128,1536]{1,0:T(8,128)(2,1)}, f32[128,1536]{1,0:T(8,128)}, bf16[128,1536]{1,0:T(8,128)(2,1)}, bf16[128,1536]{1,0:T(8,128)(2,1)}, bf16[128...) custom-call(f32[128,1664]{1,0:T(8,128)} %get-tuple-element.61.refs_0, ...), custom_call_target="tpu_custom_call" | custom-call | tf_op jit(solution)/shard_map/attend_back/pallas_call | solution.py:759
  220.0 74.3 %finish.1 = (bf16[768,1536]{1,0:T(8,128)(2,1)}, bf16[768,1536]{1,0:T(8,128)(2,1)}, bf16[768,512]{1,0:T(8,128)(2,1)}, f32[16,768]{1,0:T(8,128)}, bf16[128,1536]{1...) custom-call(bf16[128,1536]{1,0:T(8,128)(2,1)} %bitcast.23, ...), custom_call_target="tpu_custom_call" | custom-call | tf_op jit(solution)/shard_map/finish/pallas_call | solution.py:759
  294.3 1.4 slice_reduce_fusion
  295.7 0.0 copy-start
  295.7 0.0 copy-start.1
  295.7 10.0 %widen.1 = (f32[768,1536]{1,0:T(8,128)}, f32[768,512]{1,0:T(8,128)}, f32[768,1536]{1,0:T(8,128)}, f32[384,1536]{1,0:T(8,128)}, f32[1,192,1536]{2,1,0:T(8,128)}, /*index=5*/f32[8,768]{1,0:T(8,128)}) custom-call(bf16[768,1536]{1,0:T(8,128)(2,1)} %get-tuple-element.93.refs_0_, bf16[768,512]{1,0:T(8,128)(2,1)} %get-tuple-element.94.refs_1_, ...), custom_call_target="tpu_custom_call" | custom-call | tf_op jit(solution)/shard_map/widen/pallas_call | solution.py:1641
  305.7 0.0 copy-done
  305.7 0.7 copy.24
  306.5 0.0 copy-done.1
  306.5 0.7 copy.25
  (2 shorter events, 0.0 us)
Async XLA Ops:
  295.7 10.0 %copy-start = (bf16[128,1536]{1,0:T(8,128)(2,1)S(1)}, bf16[128,1536]{1,0:T(8,128)(2,1)}, u32[]{:S(2)}) copy-start(bf16[128,1536]{1,0:T(8,128)(2,1)} %get-tuple-element.74) | copy-start | bytes 1179652
  295.7 10.7 %copy-start.1 = (bf16[128,1536]{1,0:T(8,128)(2,1)S(1)}, bf16[128,1536]{1,0:T(8,128)(2,1)}, u32[]{:S(2)}) copy-start(bf16[128,1536]{1,0:T(8,128)(2,1)} %get-tuple-element.91) | copy-start | bytes 1179652
